TPU v7x, 32 devices: a whole 2x2x4 slice. The times are simulated.
32 devices in a mesh: groups: 2 (over y), row: 4 (over z), col: 4 (over x, core).
Axes of the slice: x: 2, y: 2, z: 4, core: 2. Of those that a mesh axis runs over, the one named last changes fastest.
Arguments:
- right_side: float32 [128, 8192], P('groups', ('row', 'col')), parts along dimension 0, may hold values from -6 to 6
- prior: float32 [8192], P(('row', 'col')), may hold values from 0.5 to 2
- blocks: bfloat16 [1024, 128, 128], P(('row', 'col')), may hold values from -0.125 to 0.125
- block_row: int32 [1024], P(('row', 'col')), may hold values from 0 to 63, as said below
- block_col: int32 [1024], P(('row', 'col')), may hold values from 0 to 63, as said below
Outputs:
- solution_field: float32 [128, 8192], P('groups', ('row', 'col')), parts along dimension 0
- residual: float32 [128, 8192], P('groups', ('row', 'col')), parts along dimension 0
There are 2 independent parts, one for each index of `groups`. A program takes and returns all parts, laid end to end along the dimension named above; an argument that names none is the same for every part. Nothing has to cross between parts.
Inputs may be any that keep to these rules, and one draw needn't show every extreme that they name: `block_row`: stored blocks k*64 to (k+1)*64 - 1 belong to device k of row+col, k = r*4+c; their block rows lie in r*16 to (r+1)*16 - 1. `block_col`: the block columns b of device (r, c) satisfy (b // 4) % 4 == c.
All inputs are finite; a program needn't handle non-finite values.
Results may differ from a plain program's by a relative error of at most 0.0069.
Values may be sent and summed in bfloat16 or wider, within the bound.
No kernel may reach another device: no remote copies, remote signals or barrier semaphores. Data moves between devices by JAX's collectives and lax.ppermute only.
A program may use at most 64 MiB of HBM per device.

v0:
```python
import jax
import jax.numpy as jnp
from jax import lax
from jax.sharding import PartitionSpec as P

BLOCK = 128
ITERS = 2


def spd_solve(matrix, rhs):
    factor = jnp.linalg.cholesky(matrix)
    half_solved = lax.linalg.triangular_solve(factor, rhs, left_side=True, lower=True)
    return lax.linalg.triangular_solve(
        factor, half_solved, left_side=True, lower=True, transpose_a=True
    )


def pair_gram(left, right):
    return lax.dot_general(
        left,
        right,
        (((1,), (1,)), ((), ())),
        precision=lax.Precision.HIGHEST,
        preferred_element_type=jnp.float32,
    )


def apply_left(coeffs, panel):
    return jnp.dot(
        coeffs, panel, precision=lax.Precision.HIGHEST, preferred_element_type=jnp.float32
    )


def forward_part(blocks, col_local, row_onehot, search):
    frames = search.shape[0]
    panel_view = search.reshape(frames, -1, BLOCK)
    picked = jnp.take(panel_view, col_local, axis=1)
    contrib = jnp.einsum("fkj,kij->fki", picked, blocks, preferred_element_type=jnp.float32)
    summed = jnp.einsum("rk,fki->fri", row_onehot, contrib, precision=lax.Precision.HIGHEST)
    return summed.reshape(frames, -1)


def backward_part(blocks, row_local, col_onehot, footprint):
    frames = footprint.shape[0]
    foot_view = footprint.reshape(frames, -1, BLOCK)
    picked = jnp.take(foot_view, row_local, axis=1)
    contrib = jnp.einsum("fki,kij->fkj", picked, blocks, preferred_element_type=jnp.float32)
    summed = jnp.einsum("ck,fkj->fcj", col_onehot, contrib, precision=lax.Precision.HIGHEST)
    return summed.reshape(frames, -1)


def shards(right_side, prior, blocks, block_row, block_col):
    pix_dev = right_side.shape[1]
    stretch_blocks = pix_dev // BLOCK
    rows_axis = lax.axis_size("row")
    cols_axis = lax.axis_size("col")
    row_span = stretch_blocks * cols_axis
    row_local = block_row % row_span
    col_local = block_col // row_span * stretch_blocks + block_col % stretch_blocks
    row_onehot = (jnp.arange(row_span, dtype=jnp.int32)[:, None] == row_local[None, :]).astype(
        jnp.float32
    )
    col_onehot = (
        jnp.arange(stretch_blocks * rows_axis, dtype=jnp.int32)[:, None] == col_local[None, :]
    ).astype(jnp.float32)
    solution = jnp.zeros_like(right_side)
    residual = right_side
    direction = right_side
    gram = lax.psum(pair_gram(residual, residual), ("row", "col"))
    for iteration in range(ITERS):
        final_step = iteration + 1 == ITERS
        search = lax.all_gather(direction.astype(jnp.bfloat16), "row", axis=1, tiled=True)
        foot_part = forward_part(blocks, col_local, row_onehot, search)
        foot_own = lax.psum_scatter(foot_part, "col", scatter_dimension=1, tiled=True).astype(
            jnp.bfloat16
        )
        foot_rows = lax.all_gather(foot_own, "col", axis=1, tiled=True)
        image_part = backward_part(blocks, row_local, col_onehot, foot_rows)
        image = (
            lax.psum_scatter(image_part, "row", scatter_dimension=1, tiled=True)
            + prior[None, :] * direction
        )
        if not final_step:
            curvature, cross, image_gram = lax.psum(
                (pair_gram(direction, image), pair_gram(image, residual), pair_gram(image, image)),
                ("row", "col"),
            )
        else:
            curvature = lax.psum(pair_gram(direction, image), ("row", "col"))
        step_alpha = spd_solve(curvature, gram)
        solution = solution + apply_left(step_alpha.T, direction)
        new_residual = residual - apply_left(step_alpha.T, image)
        if not final_step:
            new_gram = (
                gram
                - apply_left(cross.T, step_alpha)
                - apply_left(step_alpha.T, cross)
                + apply_left(apply_left(step_alpha.T, image_gram), step_alpha)
            )
            step_beta = spd_solve(gram, new_gram)
            direction = new_residual + apply_left(step_beta.T, direction)
            gram = new_gram
        residual = new_residual
    return (solution, residual)


def solution(mesh):
    return jax.shard_map(
        shards,
        mesh=mesh,
        in_specs=(
            P("groups", ("row", "col")),
            P(("row", "col")),
            P(("row", "col"), None, None),
            P(("row", "col")),
            P(("row", "col")),
        ),
        out_specs=(P("groups", ("row", "col")), P("groups", ("row", "col"))),
        check_vma=False,
    )
```

profile of v0, /device:TPU:0, one launch (start us, length us, event | category | flops | bytes accessed | tf_op | source)
XLA Modules:
  0.0 368.7 jit_solution(2030040030827632624)
XLA Ops:
  9.0 15.6 %all_gather.12 = bf16[64,2048]{1,0:T(8,128)(2,1)S(1)} all-gather(bf16[64,512]{1,0:T(8,128)(2,1)S(1)} %convert_element_type.14), channel_id=1, replica_groups=mesh['groups'=2,'row'=4,'col'=4] {'row'}, dimensions={1}, use_global_device_ids=true | all-gather | bytes 327680 | tf_op jit(solution)/shard_map/all_gather | solution.py:72
  26.1 1.5 convolution_bitcast_fusion.3
  27.7 2.0 fusion.6
  30.7 23.3 %reduce-scatter.5.cloned.1.call-done = f32[64,512]{1,0:T(8,128)} async-done(((f32[64,2048]{1,0:T(8,128)}), f32[64,512]{1,0:T(8,128)}) %reduce-scatter.5.cloned.1.call-update) | async-done | bytes 131088 | tf_op jit(solution)/shard_map/reduce_scatter | solution.py:74
  54.9 5.8 %all_gather.13 = bf16[64,2048]{1,0:T(8,128)(2,1)S(1)} all-gather(bf16[64,512]{1,0:T(8,128)(2,1)S(1)} %convert_element_type.15), channel_id=1, replica_groups=mesh['groups'=2,'row'=4,'col'=4] {'col'}, dimensions={1}, use_global_device_ids=true | all-gather | bytes 327680 | tf_op jit(solution)/shard_map/all_gather | solution.py:77
  62.3 2.0 fusion.4
  66.1 20.9 %reduce-scatter.7.cloned.1.call-done = f32[64,512]{1,0:T(8,128)} async-done(((f32[64,2048]{1,0:T(8,128)}), f32[64,512]{1,0:T(8,128)}) %reduce-scatter.7.cloned.1.call-update) | async-done | bytes 131088 | tf_op jit(solution)/shard_map/reduce_scatter | solution.py:80
  87.0 1.9 fusion.26
  88.9 1.9 fusion.25
  91.0 86.7 %all-reduce.3.cloned.1.call-done = (f32[64,64]{0,1:T(8,128)}, f32[64,64]{0,1:T(8,128)}, f32[64,64]{1,0:T(8,128)}, f32[64,64]{1,0:T(8,128)}) async-done(((f32[64,64]{0,1:T(8,128)}, f32[64,64]{0,1:T(8,128)}, f32[64,64]{1,0:T(8,128)}, f32[64,64]{1,0:T(8,128)}), (f32[64,64]{0,1:T(8,128)}, f32[64,64]{0,1:T(8,128)}, f32[64,64]{1,0:T(8,128)}, f32[64,64]{1,0:T(8,128)})) %all-reduce.3.cloned.1.call-update) | async-done | bytes 65552 | tf_op jit(solution)/shard_map/psum | solution.py:69
  180.2 5.8 %cholesky.70 = f32[64,64]{1,0:T(8,128)S(1)} custom-call(f32[64,64]{1,0:T(8,128)S(1)} %get-tuple-element.16), custom_call_target="Cholesky" | custom-call | tf_op jit(solution)/shard_map/jit(cholesky)/cholesky | solution.py:11
  187.4 4.9 %custom-call.15 = f32[1,64,64]{1,2,0:T(8,128)S(1)} custom-call(f32[1,64,64]{2,1,0:T(8,128)S(1)} %fusion.33), custom_call_target="InvertDiagBlocksLowerTriangular" | custom-call | tf_op jit(solution)/shard_map/triangular_solve/custom-call.2 | solution.py:13
  192.3 5.9 %cholesky.59 = f32[64,64]{1,0:T(8,128)S(1)} custom-call(f32[64,64]{1,0:T(8,128)S(1)} %get-tuple-element.17), custom_call_target="Cholesky" | custom-call | tf_op jit(solution)/shard_map/jit(cholesky)/cholesky | solution.py:11
  199.5 4.9 %custom-call.13 = f32[1,64,64]{1,2,0:T(8,128)S(1)} custom-call(f32[1,64,64]{2,1,0:T(8,128)S(1)} %fusion.32), custom_call_target="InvertDiagBlocksLowerTriangular" | custom-call | tf_op jit(solution)/shard_map/triangular_solve/custom-call.2 | solution.py:13
  204.4 1.0 fusion.45
  205.6 1.0 fusion.70
  206.6 1.0 convolution_subtract_fusion.3
  207.6 1.0 convolution_subtract_fusion.2
  210.0 1.0 fusion.67
  210.9 15.9 %all_gather.14 = bf16[64,2048]{1,0:T(8,128)(2,1)S(1)} all-gather(bf16[64,512]{1,0:T(8,128)(2,1)S(1)} %get-tuple-element.14), channel_id=1, replica_groups=mesh['groups'=2,'row'=4,'col'=4] {'row'}, dimensions={1}, use_global_device_ids=true | all-gather | bytes 327680 | tf_op jit(solution)/shard_map/all_gather | solution.py:72
  227.6 2.2 convolution_bitcast_fusion.1
  229.8 2.0 fusion.2
  232.8 21.8 %reduce-scatter.9.cloned.1.call-done = f32[64,512]{1,0:T(8,128)} async-done(((f32[64,2048]{1,0:T(8,128)}), f32[64,512]{1,0:T(8,128)}) %reduce-scatter.9.cloned.1.call-update) | async-done | bytes 131088 | tf_op jit(solution)/shard_map/reduce_scatter | solution.py:74
  255.5 6.0 %all_gather.15 = bf16[64,2048]{1,0:T(8,128)(2,1)S(1)} all-gather(bf16[64,512]{1,0:T(8,128)(2,1)S(1)} %convert_element_type.17), channel_id=1, replica_groups=mesh['groups'=2,'row'=4,'col'=4] {'col'}, dimensions={1}, use_global_device_ids=true | all-gather | bytes 327680 | tf_op jit(solution)/shard_map/all_gather | solution.py:77
  263.1 2.0 fusion
  266.4 21.5 %reduce-scatter.11.cloned.1.call-done = f32[64,512]{1,0:T(8,128)} async-done(((f32[64,2048]{1,0:T(8,128)}), f32[64,512]{1,0:T(8,128)}) %reduce-scatter.11.cloned.1.call-update) | async-done | bytes 131088 | tf_op jit(solution)/shard_map/reduce_scatter | solution.py:80
  287.9 1.2 fusion.24
  289.1 57.6 %psum.39 = f32[64,64]{0,1:T(8,128)S(1)} all-reduce(f32[64,64]{0,1:T(8,128)S(1)} %fusion.24), channel_id=1, replica_groups=mesh['groups'=2,'row'=4,'col'=4] {'row','col'}, use_global_device_ids=true, to_apply=%region_10.15 | all-reduce | flops 4096 | bytes 32768 | tf_op jit(solution)/shard_map/psum | solution.py:89
  346.8 5.8 %cholesky.81 = f32[64,64]{1,0:T(8,128)S(1)} custom-call(f32[64,64]{1,0:T(8,128)S(1)} %fusion.39), custom_call_target="Cholesky" | custom-call | tf_op jit(solution)/shard_map/jit(cholesky)/cholesky | solution.py:11
  354.0 4.9 %custom-call.17 = f32[1,64,64]{1,2,0:T(8,128)S(1)} custom-call(f32[1,64,64]{2,1,0:T(8,128)S(1)} %fusion.34), custom_call_target="InvertDiagBlocksLowerTriangular" | custom-call | tf_op jit(solution)/shard_map/triangular_solve/custom-call.2 | solution.py:13
  359.3 1.0 convolution_add_fusion
  360.3 1.9 convolution_subtract_fusion
  (88 shorter events, 22.8 us)
Async XLA Ops:
  7.2 19.0 %copy-start = (bf16[64,128,128]{2,1,0:T(8,128)(2,1)S(1)}, bf16[64,128,128]{2,1,0:T(8,128)(2,1)}, u32[]{:S(2)}) copy-start(bf16[64,128,128]{2,1,0:T(8,128)(2,1)} %param.14) | copy-start | bytes 6291460
  7.2 46.8 %reduce-scatter.5.cloned.1.call-start = ((), (), s32[]{:S(2)}) async-start(), calls=%async_computation.4 | async-start | bytes 655360 | tf_op jit(solution)/shard_map/reduce_scatter | solution.py:74
  8.0 19.6 %copy-start.15 = (pred[64]{0:T(512)(128)(4,1)}, pred[64]{0:T(512)(128)(4,1)S(1)}, u32[]{:S(2)}) copy-start(pred[64]{0:T(512)(128)(4,1)S(1)} %get-tuple-element.12) | copy-start | bytes 196
  25.4 5.3 %copy-start.11 = (s32[64]{0:T(128)}, s32[64]{0:T(128)S(1)}, u32[]{:S(2)}) copy-start(s32[64]{0:T(128)S(1)} %get-tuple-element.11) | copy-start | bytes 772
  25.4 36.1 %copy-start.13 = (pred[64]{0:T(512)(128)(4,1)}, pred[64]{0:T(512)(128)(4,1)S(1)}, u32[]{:S(2)}) copy-start(pred[64]{0:T(512)(128)(4,1)S(1)} %get-tuple-element.10) | copy-start | bytes 196
  30.6 56.4 %reduce-scatter.7.cloned.1.call-start = ((), (), s32[]{:S(2)}) async-start(), calls=%async_computation.5 | async-start | bytes 655360 | tf_op jit(solution)/shard_map/reduce_scatter | solution.py:80
  62.2 3.0 copy-start.1
  62.3 24.8 %copy-start.10 = (f32[512]{0:T(512)S(1)}, f32[512]{0:T(512)}, u32[]{:S(2)}) copy-start(f32[512]{0:T(512)} %param.13) | copy-start | bytes 6148
  65.2 112.5 %all-reduce.3.cloned.1.call-start = ((), (), s32[]{:S(2)}) async-start(), calls=%async_computation.8 | async-start | bytes 262144 | tf_op jit(solution)/shard_map/psum | solution.py:69
  87.0 122.6 %copy-start.5 = (f32[64,512]{1,0:T(8,128)S(1)}, f32[64,512]{1,0:T(8,128)}, u32[]{:S(2)}) copy-start(f32[64,512]{1,0:T(8,128)} %reduce-scatter.7.cloned.1.call-done) | copy-start | bytes 393220
  90.8 163.8 %reduce-scatter.9.cloned.1.call-start = ((), (), s32[]{:S(2)}) async-start(), calls=%async_computation.6 | async-start | bytes 655360 | tf_op jit(solution)/shard_map/reduce_scatter | solution.py:74
  205.6 21.2 %copy-start.3 = (f32[64,64]{1,0:T(8,128)}, f32[64,64]{1,0:T(8,128)S(1)}, u32[]{:S(2)}) copy-start(f32[64,64]{1,0:T(8,128)S(1)} %fusion.47) | copy-start | bytes 49156
  208.8 0.6 copy-start.8
  210.0 16.8 %copy-start.6 = (f32[64,512]{1,0:T(8,128)}, f32[64,512]{1,0:T(8,128)S(1)}, u32[]{:S(2)}) copy-start(f32[64,512]{1,0:T(8,128)S(1)} %convolution_subtract_fusion.1) | copy-start | bytes 393220
  227.6 2.2 copy-start.12
  232.7 29.6 %copy-start.14 = (pred[64]{0:T(512)(128)(4,1)S(1)}, pred[64]{0:T(512)(128)(4,1)}, u32[]{:S(2)}) copy-start(pred[64]{0:T(512)(128)(4,1)} %copy-done.13) | copy-start | bytes 196
  232.7 55.1 %reduce-scatter.11.cloned.1.call-start = ((), (), s32[]{:S(2)}) async-start(), calls=%async_computation.7 | async-start | bytes 655360 | tf_op jit(solution)/shard_map/reduce_scatter | solution.py:80
  263.1 3.0 copy-start.4
  263.1 24.8 %copy-start.2 = (f32[64,512]{1,0:T(8,128)S(1)}, f32[64,512]{1,0:T(8,128)}, u32[]{:S(2)}) copy-start(f32[64,512]{1,0:T(8,128)} %get-tuple-element.15) | copy-start | bytes 393220
  263.1 95.8 %copy-start.9 = (f32[64,64]{0,1:T(8,128)S(1)}, f32[64,64]{0,1:T(8,128)}, u32[]{:S(2)}) copy-start(f32[64,64]{0,1:T(8,128)} %copy-done.8) | copy-start | bytes 49156
  265.1 95.2 %copy-start.7 = (f32[64,512]{1,0:T(8,128)S(1)}, f32[64,512]{1,0:T(8,128)}, u32[]{:S(2)}) copy-start(f32[64,512]{1,0:T(8,128)} %copy-done.6) | copy-start | bytes 393220
Sparse Core Ops, SparseCore 0:
  30.7 23.1 reduce-scatter.4
  65.3 21.6 reduce-scatter.6
  92.0 85.7 all-reduce.2
  232.9 21.6 reduce-scatter.8
  266.2 21.6 reduce-scatter.10
where the time goes:
time: 370 us; the launch traced here: 369 us
  waiting for transfers between devices  174 us (47%)
  blocking collectives  101 us (27%)
  other arithmetic  41.3 us (11%)
  matrix products  28.5 us (8%)
  between operations  14.3 us (4%)
  local copies, waits for them, and re-layouts  9.18 us (2%)
    psum x1, waiting for transfers between devices, shards(): gram = lax.psum(pair_gram(residual, residual), ('row', 'col'))  86.7 us
    psum x1, blocking collectives, shards(): curvature = lax.psum(pair_gram(direction, image), ('row', 'col'))  57.6 us
    reduce_scatter x2, waiting for transfers between devices, shards(): lax.psum_scatter(foot_part, 'col', scatter_dimension=1, tiled=True)  45 us
    reduce_scatter x2, waiting for transfers between devices, shards(): lax.psum_scatter(image_part, 'row', scatter_dimension=1, tiled=True)  42.4 us
    all_gather x2, blocking collectives, shards(): lax.all_gather(direction.astype(jnp.bfloat16), 'row', axis=1, tiled=True)  31.5 us
    another operation x9, other arithmetic, spd_solve(): factor = jnp.linalg.cholesky(matrix)  19.6 us
    another operation x6, other arithmetic, spd_solve(): lax.linalg.triangular_solve(factor, half_solved, left_side=True, lower=Tr...  16.6 us
    all_gather x2, blocking collectives, shards(): foot_rows = lax.all_gather(foot_own, 'col', axis=1, tiled=True)  11.8 us
  transfers between devices with their start and end apart: 5, of which 5 were waited for; matrix products, arithmetic and copies ran while one was open for 0% of the time, Pallas kernels for 0%

commit v1 on v0

v1 whole, which is shorter than its diff:
```python
import jax
import jax.numpy as jnp
from jax import lax
from jax.experimental import pallas as pl
from jax.experimental.pallas import tpu as pltpu
from jax.sharding import PartitionSpec as P

BLOCK = 128
FP32 = lax.Precision.HIGHEST
VMEM = pl.BlockSpec(memory_space=pltpu.VMEM)
SMEM = pl.BlockSpec(memory_space=pltpu.SMEM)
PARAMS = pltpu.CompilerParams(vmem_limit_bytes=48 * 1024 * 1024)


def nt_dot(a, b, precision=None):
    return lax.dot_general(
        a, b, (((1,), (1,)), ((), ())), precision=precision, preferred_element_type=jnp.float32
    )


def tn_dot(a, b):
    return lax.dot_general(
        a, b, (((0,), (0,)), ((), ())), precision=FP32, preferred_element_type=jnp.float32
    )


def nn_dot(a, b):
    return lax.dot_general(
        a, b, (((1,), (0,)), ((), ())), precision=FP32, preferred_element_type=jnp.float32
    )


def call(kernel, outs, ins, scratch=()):
    return pl.pallas_call(
        kernel,
        out_shape=outs,
        in_specs=[SMEM if x.dtype == jnp.int32 else VMEM for x in ins],
        out_specs=jax.tree.map(lambda _: VMEM, outs),
        scratch_shapes=list(scratch),
        compiler_params=PARAMS,
    )(*ins)


def store_split(out_ref, at, value):
    high = value.astype(jnp.bfloat16)
    low = (value - high.astype(jnp.float32)).astype(jnp.bfloat16)
    for dest in range(out_ref.shape[0]):
        out_ref[dest, at] = high
        out_ref[dest, at + 1] = low


def load_split(in_ref, at):
    total = None
    for source in range(in_ref.shape[0]):
        part = in_ref[source, at].astype(jnp.float32) + in_ref[source, at + 1].astype(jnp.float32)
        total = part if total is None else total + part
    return total


def load_sum(in_ref, at):
    total = in_ref[0, at].astype(jnp.float32)
    for source in range(1, in_ref.shape[0]):
        total += in_ref[source, at].astype(jnp.float32)
    return total


def lanes(j):
    return slice(j * BLOCK, (j + 1) * BLOCK)


def cast_kernel(v_ref, out_ref):
    for j in range(out_ref.shape[0]):
        out_ref[j] = v_ref[:, lanes(j)].astype(jnp.bfloat16)


def forward_kernel(row_span, stretch, brow, bcol, search, blocks, v_ref, prior, out_ref, acc):
    acc[...] = jnp.zeros_like(acc)
    for k in range(blocks.shape[0]):
        at_row = lax.rem(brow[k], row_span)
        at_col = lax.div(bcol[k], row_span) * stretch + lax.rem(bcol[k], stretch)
        acc[at_row] += nt_dot(search[at_col], blocks[k])
    for dest in range(out_ref.shape[0]):
        for j in range(stretch):
            out_ref[dest, j] = acc[dest * stretch + j].astype(jnp.bfloat16)
    value = v_ref[...]
    both = jnp.concatenate([value, value * prior[...]], axis=0)
    store_split(out_ref, stretch, nt_dot(value, both, FP32))


def foot_kernel(in_ref, foot_ref, gram_ref):
    stretch = foot_ref.shape[0]
    for j in range(stretch):
        foot_ref[j] = load_sum(in_ref, j).astype(jnp.bfloat16)
    gram_ref[...] = load_split(in_ref, stretch)


def backward_kernel(row_span, stretch, brow, bcol, foot, blocks, gram, out_ref, acc):
    acc[...] = jnp.zeros_like(acc)
    for k in range(blocks.shape[0]):
        at_row = lax.rem(brow[k], row_span)
        at_col = lax.div(bcol[k], row_span) * stretch + lax.rem(bcol[k], stretch)
        acc[at_col] += jnp.dot(foot[at_row], blocks[k], preferred_element_type=jnp.float32)
    for dest in range(out_ref.shape[0]):
        for j in range(stretch):
            out_ref[dest, j] = acc[dest * stretch + j].astype(jnp.bfloat16)
    whole = jnp.concatenate([foot[b] for b in range(row_span)], axis=1)
    padded = jnp.concatenate([jnp.zeros_like(whole), whole], axis=0)
    store_split(out_ref, stretch, gram[...] + nt_dot(whole, padded))


def frame_scale(gram):
    n = gram.shape[0]
    same = lax.broadcasted_iota(jnp.int32, (n, n), 0) == lax.broadcasted_iota(jnp.int32, (n, n), 1)
    norm = jnp.where(same, gram[:, :n], 0.0)
    energy = jnp.where(same, gram[:, n:], 0.0)
    column = jnp.sum(energy, axis=1, keepdims=True) / jnp.sum(norm, axis=1, keepdims=True)
    row = jnp.sum(energy, axis=0, keepdims=True) / jnp.sum(norm, axis=0, keepdims=True)
    return column, row


def image_kernel(in_ref, v_ref, prior, image_ref, next_ref, cast_ref, gram_ref):
    stretch = cast_ref.shape[0]
    gram = load_split(in_ref, stretch)
    gram_ref[...] = gram
    scale, _ = frame_scale(gram)
    for j in range(stretch):
        value = v_ref[:, lanes(j)]
        image = load_sum(in_ref, j) + prior[:, lanes(j)] * value
        following = image - scale * value
        image_ref[:, lanes(j)] = image
        next_ref[:, lanes(j)] = following
        cast_ref[j] = following.astype(jnp.bfloat16)


def eliminate(work, n):
    at = lax.broadcasted_iota(jnp.int32, (n, 1), 0)
    for k in range(n):
        pivot_row = work[k : k + 1, :] / work[k : k + 1, k : k + 1]
        column = jnp.where(at == k, 0.0, work[:, k : k + 1])
        work = jnp.where(at == k, pivot_row, work - column * pivot_row)
    return work[:, n:]


def inverse_kernel(gram, out_ref):
    n = gram.shape[0]
    eye = lax.broadcasted_iota(jnp.int32, (n, n), 0) == lax.broadcasted_iota(jnp.int32, (n, n), 1)
    out_ref[...] = eliminate(
        jnp.concatenate([gram[:, n:], jnp.where(eye, 1.0, 0.0)], axis=1), n
    )


def final_kernel(in_ref, v_ref, image_ref, next_ref, prior, gram_ref, inverse_ref, x_ref, r_ref):
    n = gram_ref.shape[0]
    stretch = in_ref.shape[1] - 2
    gram = gram_ref[...]
    norm, energy = gram[:, :n], gram[:, n:]
    scale, scale_row = frame_scale(gram)
    second = load_split(in_ref, stretch)
    next_norm, next_energy = second[:, :n], second[:, n:]
    next_rhs = energy - scale * norm
    cross = next_norm + next_rhs * scale_row
    inverse = inverse_ref[...]
    alpha = nn_dot(inverse, norm)
    conj = nn_dot(inverse, cross.T)
    schur = next_energy - nn_dot(cross, conj)
    rhs = next_rhs - nn_dot(cross, alpha)
    gamma = eliminate(jnp.concatenate([schur, rhs], axis=1), n)
    first = alpha - nn_dot(conj, gamma)
    coeffs = jnp.concatenate([first, gamma], axis=0)
    for j in range(stretch):
        value = v_ref[:, lanes(j)]
        following = next_ref[:, lanes(j)]
        second_image = load_sum(in_ref, j) + prior[:, lanes(j)] * following
        x_ref[:, lanes(j)] = tn_dot(coeffs, jnp.concatenate([value, following], axis=0))
        r_ref[:, lanes(j)] = value - tn_dot(
            coeffs, jnp.concatenate([image_ref[:, lanes(j)], second_image], axis=0)
        )


def gather(x, axis):
    return lax.all_gather(x, axis, axis=0, tiled=True)


def exchange(x, axis):
    return lax.all_to_all(x, axis, split_axis=0, concat_axis=0, tiled=True)


def shards(right_side, prior, blocks, block_row, block_col):
    frames, pix = right_side.shape
    stretch = pix // BLOCK
    rows, cols = lax.axis_size("row"), lax.axis_size("col")
    row_span, col_span = stretch * cols, stretch * rows
    prior = prior.reshape(1, pix)
    f32, bf16 = jnp.float32, jnp.bfloat16

    def shape(dims, dtype):
        return jax.ShapeDtypeStruct(dims, dtype)

    panel = shape((stretch, frames, BLOCK), bf16)
    gram_type = shape((frames, 2 * frames), f32)
    own = shape((frames, pix), f32)

    def apply_operator(own_value, own_cast):
        search = gather(own_cast, "row")
        partial = call(
            lambda *refs: forward_kernel(row_span, stretch, *refs),
            shape((cols, stretch + 2, frames, BLOCK), bf16),
            (block_row, block_col, search, blocks, own_value, prior),
            [pltpu.VMEM((row_span, frames, BLOCK), f32)],
        )
        foot, gram = call(foot_kernel, (panel, gram_type), (exchange(partial, "col"),))
        foot = gather(foot, "col")
        partial = call(
            lambda *refs: backward_kernel(row_span, stretch, *refs),
            shape((rows, stretch + 2, frames, BLOCK), bf16),
            (block_row, block_col, foot, blocks, gram),
            [pltpu.VMEM((col_span, frames, BLOCK), f32)],
        )
        return exchange(partial, "row")

    cast = call(cast_kernel, panel, (right_side,))
    received = apply_operator(right_side, cast)
    image, following, cast, gram = call(
        image_kernel, (own, own, panel, gram_type), (received, right_side, prior)
    )
    inverse = call(inverse_kernel, shape((frames, frames), f32), (gram,))
    received = apply_operator(following, cast)
    return call(
        final_kernel,
        (own, own),
        (received, right_side, image, following, prior, gram, inverse),
    )


def solution(mesh):
    return jax.shard_map(
        shards,
        mesh=mesh,
        in_specs=(
            P("groups", ("row", "col")),
            P(("row", "col")),
            P(("row", "col"), None, None),
            P(("row", "col")),
            P(("row", "col")),
        ),
        out_specs=(P("groups", ("row", "col")), P("groups", ("row", "col"))),
        check_vma=False,
    )
```

time: 370 us -> 117 us (0.32)
  waiting for transfers between devices: 174 us -> 6.87 us
  other arithmetic: 41.3 us -> 0 us
  matrix products: 28.5 us -> 0 us
  blocking collectives: 101 us -> 78.8 us
  Pallas kernels: 0 us -> 21.9 us
  between operations: 14.3 us -> 0.69 us
  local copies, waits for them, and re-layouts: 9.18 us -> 4.5 us
    reduce_scatter x4 -> x0, waiting for transfers between devices: 87.4 us -> none  [the longest x2 45 us: shards(): lax.psum_scatter(foot_part, 'col', scatter_dimension=1, tiled=True)]
    psum x1 -> x0, waiting for transfers between devices: 86.7 us -> none  [shards(): gram = lax.psum(pair_gram(residual, residual), ('row', 'col'))]
    psum x1 -> x0, blocking collectives: 57.6 us -> none  [shards(): curvature = lax.psum(pair_gram(direction, image), ('row', 'col'))]
    all_to_all x0 -> x3, blocking collectives: none -> 37 us  [exchange(): return lax.all_to_all(x, axis, split_axis=0, concat_axis=0, tiled=True)]
    another operation x15 -> x0, other arithmetic: 36.2 us -> none  [the longest x9 19.6 us: spd_solve(): factor = jnp.linalg.cholesky(matrix)]
    dot_general x21 -> x0, matrix products: 26.5 us -> none  [the longest x9 7.73 us: apply_left(): jnp.dot(coeffs, panel, precision=lax.Precision.HIGHEST, preferred_element...]
    pallas_call x0 -> x10, Pallas kernels: none -> 21.9 us  [call(): pl.pallas_call(kernel, out_shape=outs, in_specs=[SMEM if x.dtype == jnp.i...]
    all_to_all x0 -> x1, waiting for transfers between devices: none -> 6.87 us  [exchange(): return lax.all_to_all(x, axis, split_axis=0, concat_axis=0, tiled=True)]
  transfers between devices with their start and end apart: 5 -> 1, of which waited for: 5 -> 1; matrix products, arithmetic and copies ran while one was open for 0% -> 0% of each run, Pallas kernels for 0% -> 5%
where the time goes in v1:
time: 117 us; the launch traced here: 116 us
  blocking collectives  78.8 us (67%)
  Pallas kernels  21.9 us (19%)
  waiting for transfers between devices  6.87 us (6%)
  local copies, waits for them, and re-layouts  4.5 us (4%)
  starting transfers between devices  3.46 us (3%)
    all_gather x4, blocking collectives, gather(): return lax.all_gather(x, axis, axis=0, tiled=True)  41.8 us
    all_to_all x3, blocking collectives, exchange(): return lax.all_to_all(x, axis, split_axis=0, concat_axis=0, tiled=True)  37 us
    pallas_call x10, Pallas kernels, call(): pl.pallas_call(kernel, out_shape=outs, in_specs=[SMEM if x.dtype == jnp.i...  21.9 us
    all_to_all x1, waiting for transfers between devices, exchange(): return lax.all_to_all(x, axis, split_axis=0, concat_axis=0, tiled=True)  6.87 us
    unnamed x20, local copies, waits for them, and re-layouts  4.5 us
    all_to_all x1, starting transfers between devices, exchange(): return lax.all_to_all(x, axis, split_axis=0, concat_axis=0, tiled=True)  3.46 us
  transfers between devices with their start and end apart: 1, of which 1 were waited for; matrix products, arithmetic and copies ran while one was open for 0% of the time, Pallas kernels for 5%

profile of v1, /device:TPU:0, one launch (start us, length us, event | category | flops | bytes accessed | tf_op | source)
XLA Modules:
  0.0 116.2 jit_solution(7494268829942940758)
XLA Ops:
  0.6 0.0 copy-start.2
  0.6 0.9 copy-done.2
  1.5 15.6 %all_gather.12.refs_2_ = bf16[16,64,128]{2,1,0:T(8,128)(2,1)S(1)} all-gather(bf16[4,64,128]{2,1,0:T(8,128)(2,1)S(1)} %shard_map.68), channel_id=1, replica_groups=mesh['groups'=2,'row'=4,'col'=4] {'row'}, dimensions={0}, use_global_device_ids=true | all-gather | bytes 327680 | tf_op jit(solution)/shard_map/all_gather | solution.py:181
  17.2 0.0 copy-start
  17.2 1.6 %copy-done = bf16[64,128,128]{2,1,0:T(8,128)(2,1)S(1)} copy-done((bf16[64,128,128]{2,1,0:T(8,128)(2,1)S(1)}, bf16[64,128,128]{2,1,0:T(8,128)(2,1)}, u32[]{:S(2)}) %copy-start) | copy-done | bytes 2097176
  18.8 0.0 copy-start.4
  18.8 0.7 copy-done.4
  19.5 0.0 copy-start.6
  19.5 0.7 copy-done.6
  20.1 0.7 copy-done.8
  20.8 2.4 %shard_map.69 = bf16[4,6,64,128]{3,2,1,0:T(8,128)(2,1)S(1)} custom-call(s32[64]{0:T(128)S(1)} %copy-done.6, s32[64]{0:T(128)S(1)} %copy-done.8, bf16[16,64,128]{2,1,0:T(8,128)(2,1)S(1)} %all_gather.12.refs_2_, bf16[64,128,128]{2,1,0:T(8,128)(2,1)S(1)} %copy-done, f32[64,512]{1,0:T(8,128)S(1)} %copy-done.2, f32[1,512]{1,0:T(1,128)S(1)} %bitcast.1), custom_call_target="tpu_custom_call" | custom-call | tf_op jit(solution)/shard_map/pallas_call | solution.py:34
  23.1 10.0 %all_to_all.20.in_ref = bf16[4,6,64,128]{3,2,1,0:T(8,128)(2,1)S(1)} all-to-all(bf16[4,6,64,128]{3,2,1,0:T(8,128)(2,1)S(1)} %shard_map.69), channel_id=1, replica_groups=mesh['groups'=2,'row'=4,'col'=4] {'col'}, dimensions={0} | all-to-all | bytes 786432 | tf_op jit(solution)/shard_map/all_to_all | solution.py:185
  33.1 0.1 shard_map.70
  33.2 5.9 %all_gather.13.refs_2_ = bf16[16,64,128]{2,1,0:T(8,128)(2,1)S(1)} all-gather(bf16[4,64,128]{2,1,0:T(8,128)(2,1)S(1)} %get-tuple-element.10), channel_id=1, replica_groups=mesh['groups'=2,'row'=4,'col'=4] {'col'}, dimensions={0}, use_global_device_ids=true | all-gather | bytes 327680 | tf_op jit(solution)/shard_map/all_gather | solution.py:181
  39.1 0.0 copy-done.1
  39.1 0.0 copy-done.7
  39.1 0.0 copy-done.9
  39.1 1.4 %shard_map.71 = bf16[4,6,64,128]{3,2,1,0:T(8,128)(2,1)S(1)} custom-call(s32[64]{0:T(128)S(1)} %copy-done.7, s32[64]{0:T(128)S(1)} %copy-done.9, bf16[16,64,128]{2,1,0:T(8,128)(2,1)S(1)} %all_gather.13.refs_2_, bf16[64,128,128]{2,1,0:T(8,128)(2,1)S(1)} %copy-done.1, f32[64,128]{1,0:T(8,128)S(1)} %get-tuple-element.11.refs_4_), custom_call_target="tpu_custom_call" | custom-call | tf_op jit(solution)/shard_map/pallas_call | solution.py:34
  40.6 17.1 %all_to_all.21.in_ref = bf16[4,6,64,128]{3,2,1,0:T(8,128)(2,1)S(1)} all-to-all(bf16[4,6,64,128]{3,2,1,0:T(8,128)(2,1)S(1)} %shard_map.71), channel_id=1, replica_groups=mesh['groups'=2,'row'=4,'col'=4] {'row'}, dimensions={0} | all-to-all | bytes 786432 | tf_op jit(solution)/shard_map/all_to_all | solution.py:185
  57.7 0.0 copy-done.3
  57.7 0.0 copy-done.5
  57.7 0.2 shard_map.72
  57.9 14.4 %all_gather.14.refs_2_ = bf16[16,64,128]{2,1,0:T(8,128)(2,1)S(1)} all-gather(bf16[4,64,128]{2,1,0:T(8,128)(2,1)S(1)} %get-tuple-element.12), channel_id=1, replica_groups=mesh['groups'=2,'row'=4,'col'=4] {'row'}, dimensions={0}, use_global_device_ids=true | all-gather | bytes 327680 | tf_op jit(solution)/shard_map/all_gather | solution.py:181
  72.3 2.4 %shard_map.73 = bf16[4,6,64,128]{3,2,1,0:T(8,128)(2,1)S(1)} custom-call(s32[64]{0:T(128)S(1)} %copy-done.7, s32[64]{0:T(128)S(1)} %copy-done.9, bf16[16,64,128]{2,1,0:T(8,128)(2,1)S(1)} %all_gather.14.refs_2_, bf16[64,128,128]{2,1,0:T(8,128)(2,1)S(1)} %copy-done.1, f32[64,512]{1,0:T(8,128)S(1)} %get-tuple-element.13.refs_4_.next_ref, f32[1,512]{1,0:T(1,128)S(1)} %bitcast.3), custom_call_target="tpu_custom_call" | custom-call | tf_op jit(solution)/shard_map/pallas_call | solution.py:34
  74.7 9.8 %all_to_all.22.in_ref = bf16[4,6,64,128]{3,2,1,0:T(8,128)(2,1)S(1)} all-to-all(bf16[4,6,64,128]{3,2,1,0:T(8,128)(2,1)S(1)} %shard_map.73), channel_id=1, replica_groups=mesh['groups'=2,'row'=4,'col'=4] {'col'}, dimensions={0} | all-to-all | bytes 786432 | tf_op jit(solution)/shard_map/all_to_all | solution.py:185
  84.5 0.1 shard_map.74
  84.6 5.8 %all_gather.15.refs_2_ = bf16[16,64,128]{2,1,0:T(8,128)(2,1)S(1)} all-gather(bf16[4,64,128]{2,1,0:T(8,128)(2,1)S(1)} %get-tuple-element.14), channel_id=1, replica_groups=mesh['groups'=2,'row'=4,'col'=4] {'col'}, dimensions={0}, use_global_device_ids=true | all-gather | bytes 327680 | tf_op jit(solution)/shard_map/all_gather | solution.py:181
  90.4 2.2 %shard_map.75 = bf16[4,6,64,128]{3,2,1,0:T(8,128)(2,1)} custom-call(s32[64]{0:T(128)S(1)} %copy-done.7, s32[64]{0:T(128)S(1)} %copy-done.9, bf16[16,64,128]{2,1,0:T(8,128)(2,1)S(1)} %all_gather.15.refs_2_, bf16[64,128,128]{2,1,0:T(8,128)(2,1)S(1)} %copy-done.1, f32[64,128]{1,0:T(8,128)S(1)} %get-tuple-element.15.refs_4_), custom_call_target="tpu_custom_call" | custom-call | tf_op jit(solution)/shard_map/pallas_call | solution.py:34
  92.6 3.5 %all-to-all-start.3 = ((bf16[4,6,64,128]{3,2,1,0:T(8,128)(2,1)}), bf16[4,6,64,128]{3,2,1,0:T(8,128)(2,1)S(1)}, u32[]{:S(2)}, u32[]{:S(2)}) async-start(bf16[4,6,64,128]{3,2,1,0:T(8,128)(2,1)} %shard_map.75), calls=%async_computation.3 | async-start | bytes 786432 | tf_op jit(solution)/shard_map/all_to_all | solution.py:185
  96.0 5.6 %shard_map.76.inverse_ref = f32[64,64]{1,0:T(8,128)S(1)} custom-call(f32[64,128]{1,0:T(8,128)S(1)} %get-tuple-element.17.gram.gram_ref), custom_call_target="tpu_custom_call" | custom-call | tf_op jit(solution)/shard_map/pallas_call | solution.py:34
  101.6 6.9 %all-to-all-done.3.in_ref = bf16[4,6,64,128]{3,2,1,0:T(8,128)(2,1)S(1)} async-done(((bf16[4,6,64,128]{3,2,1,0:T(8,128)(2,1)}), bf16[4,6,64,128]{3,2,1,0:T(8,128)(2,1)S(1)}, u32[]{:S(2)}, u32[]{:S(2)}) %all-to-all-start.3) | async-done | bytes 393248 | tf_op jit(solution)/shard_map/all_to_all | solution.py:185
  108.5 7.8 %shard_map.77 = (f32[64,512]{1,0:T(8,128)}, f32[64,512]{1,0:T(8,128)}) custom-call(bf16[4,6,64,128]{3,2,1,0:T(8,128)(2,1)S(1)} %all-to-all-done.3.in_ref, f32[64,512]{1,0:T(8,128)S(1)} %copy-done.3, f32[64,512]{1,0:T(8,128)S(1)} %get-tuple-element.16.image_ref, f32[64,512]{1,0:T(8,128)S(1)} %get-tuple-element.13.refs_4_.next_ref, f32[1,512]{1,0:T(1,128)S(1)} %bitcast.4, ...), custom_call_target="tpu_custom_call" | custom-call | tf_op jit(solution)/shard_map/pallas_call | solution.py:34
  (7 shorter events, 0.0 us)
Async XLA Ops:
  0.6 0.9 copy-start.2
  17.2 1.6 %copy-start = (bf16[64,128,128]{2,1,0:T(8,128)(2,1)S(1)}, bf16[64,128,128]{2,1,0:T(8,128)(2,1)}, u32[]{:S(2)}) copy-start(bf16[64,128,128]{2,1,0:T(8,128)(2,1)} %refs_3_.7) | copy-start | bytes 6291460
  18.8 0.7 copy-start.4
  19.5 0.7 copy-start.6
  20.1 0.7 copy-start.8
  20.8 18.4 %copy-start.1 = (bf16[64,128,128]{2,1,0:T(8,128)(2,1)S(1)}, bf16[64,128,128]{2,1,0:T(8,128)(2,1)}, u32[]{:S(2)}) copy-start(bf16[64,128,128]{2,1,0:T(8,128)(2,1)} %refs_3_.7) | copy-start | bytes 6291460
  20.8 18.4 %copy-start.7 = (s32[64]{0:T(128)S(1)}, s32[64]{0:T(128)}, u32[]{:S(2)}) copy-start(s32[64]{0:T(128)} %refs_0_.7) | copy-start | bytes 772
  20.8 18.4 %copy-start.9 = (s32[64]{0:T(128)S(1)}, s32[64]{0:T(128)}, u32[]{:S(2)}) copy-start(s32[64]{0:T(128)} %refs_1_.7) | copy-start | bytes 772
  33.1 24.6 %copy-start.3 = (f32[64,512]{1,0:T(8,128)S(1)}, f32[64,512]{1,0:T(8,128)}, u32[]{:S(2)}) copy-start(f32[64,512]{1,0:T(8,128)} %v_ref.5) | copy-start | bytes 393220
  33.1 24.6 %copy-start.5 = (f32[512]{0:T(512)S(1)}, f32[512]{0:T(512)}, u32[]{:S(2)}) copy-start(f32[512]{0:T(512)} %param.6) | copy-start | bytes 6148
  92.6 15.9 %all-to-all-start.3 = ((bf16[4,6,64,128]{3,2,1,0:T(8,128)(2,1)}), bf16[4,6,64,128]{3,2,1,0:T(8,128)(2,1)S(1)}, u32[]{:S(2)}, u32[]{:S(2)}) async-start(bf16[4,6,64,128]{3,2,1,0:T(8,128)(2,1)} %shard_map.75), calls=%async_computation.3 | async-start | bytes 786432 | tf_op jit(solution)/shard_map/all_to_all | solution.py:185

commit v2 on v1

--- a/solution.py
+++ b/solution.py
@@ -31,37 +31,64 @@
 
 
 def call(kernel, outs, ins, scratch=()):
-    return pl.pallas_call(
-        kernel,
-        out_shape=outs,
-        in_specs=[SMEM if x.dtype == jnp.int32 else VMEM for x in ins],
-        out_specs=jax.tree.map(lambda _: VMEM, outs),
+    flat_ins, ins_tree = jax.tree.flatten(tuple(ins))
+    flat_outs, outs_tree = jax.tree.flatten(outs if isinstance(outs, tuple) else (outs,))
+
+    def body(*refs):
+        middle, last = len(flat_ins), len(flat_ins) + len(flat_outs)
+        kernel(
+            *jax.tree.unflatten(ins_tree, refs[:middle]),
+            *jax.tree.unflatten(outs_tree, refs[middle:last]),
+            *refs[last:],
+        )
+
+    results = pl.pallas_call(
+        body,
+        out_shape=flat_outs,
+        in_specs=[SMEM if x.dtype == jnp.int32 else VMEM for x in flat_ins],
+        out_specs=[VMEM for _ in flat_outs],
         scratch_shapes=list(scratch),
         compiler_params=PARAMS,
-    )(*ins)
-
-
-def store_split(out_ref, at, value):
+    )(*flat_ins)
+    results = jax.tree.unflatten(outs_tree, results)
+    return results if isinstance(outs, tuple) else results[0]
+
+
+def store_split(out_refs, at, value):
     high = value.astype(jnp.bfloat16)
     low = (value - high.astype(jnp.float32)).astype(jnp.bfloat16)
-    for dest in range(out_ref.shape[0]):
-        out_ref[dest, at] = high
-        out_ref[dest, at + 1] = low
-
-
-def load_split(in_ref, at):
-    total = None
-    for source in range(in_ref.shape[0]):
-        part = in_ref[source, at].astype(jnp.float32) + in_ref[source, at + 1].astype(jnp.float32)
-        total = part if total is None else total + part
+    for out_ref in out_refs:
+        out_ref[at] = high
+        out_ref[at + 1] = low
+
+
+def load_sum(in_refs, at):
+    total = in_refs[0][at].astype(jnp.float32)
+    for in_ref in in_refs[1:]:
+        total += in_ref[at].astype(jnp.float32)
     return total
 
 
-def load_sum(in_ref, at):
-    total = in_ref[0, at].astype(jnp.float32)
-    for source in range(1, in_ref.shape[0]):
-        total += in_ref[source, at].astype(jnp.float32)
-    return total
+def load_split(in_refs, at):
+    return load_sum(in_refs, at) + load_sum(in_refs, at + 1)
+
+
+def fill_panel(panel, in_refs, axis):
+    count, stretch = len(in_refs), in_refs[0].shape[0]
+    me = lax.axis_index(axis)
+    for shift, in_ref in enumerate(in_refs):
+        source = lax.rem(me - shift + count, count)
+        for j in range(stretch):
+            panel[source * stretch + j] = in_ref[j]
+
+
+def spread(out_refs, acc, axis, stretch):
+    count = len(out_refs)
+    me = lax.axis_index(axis)
+    for shift, out_ref in enumerate(out_refs):
+        dest = lax.rem(me + shift, count)
+        for j in range(stretch):
+            out_ref[j] = acc[dest * stretch + j].astype(jnp.bfloat16)
 
 
 def lanes(j):
@@ -73,18 +100,17 @@
         out_ref[j] = v_ref[:, lanes(j)].astype(jnp.bfloat16)
 
 
-def forward_kernel(row_span, stretch, brow, bcol, search, blocks, v_ref, prior, out_ref, acc):
+def forward_kernel(row_span, stretch, brow, bcol, search, blocks, v_ref, prior, out_refs, acc, panel):
     acc[...] = jnp.zeros_like(acc)
+    fill_panel(panel, search, "row")
     for k in range(blocks.shape[0]):
         at_row = lax.rem(brow[k], row_span)
         at_col = lax.div(bcol[k], row_span) * stretch + lax.rem(bcol[k], stretch)
-        acc[at_row] += nt_dot(search[at_col], blocks[k])
-    for dest in range(out_ref.shape[0]):
-        for j in range(stretch):
-            out_ref[dest, j] = acc[dest * stretch + j].astype(jnp.bfloat16)
+        acc[at_row] += nt_dot(panel[at_col], blocks[k])
+    spread(out_refs, acc, "col", stretch)
     value = v_ref[...]
     both = jnp.concatenate([value, value * prior[...]], axis=0)
-    store_split(out_ref, stretch, nt_dot(value, both, FP32))
+    store_split(out_refs, stretch, nt_dot(value, both, FP32))
 
 
 def foot_kernel(in_ref, foot_ref, gram_ref):
@@ -94,18 +120,17 @@
     gram_ref[...] = load_split(in_ref, stretch)
 
 
-def backward_kernel(row_span, stretch, brow, bcol, foot, blocks, gram, out_ref, acc):
+def backward_kernel(row_span, stretch, brow, bcol, foot, blocks, gram, out_refs, acc, panel):
     acc[...] = jnp.zeros_like(acc)
+    fill_panel(panel, foot, "col")
     for k in range(blocks.shape[0]):
         at_row = lax.rem(brow[k], row_span)
         at_col = lax.div(bcol[k], row_span) * stretch + lax.rem(bcol[k], stretch)
-        acc[at_col] += jnp.dot(foot[at_row], blocks[k], preferred_element_type=jnp.float32)
-    for dest in range(out_ref.shape[0]):
-        for j in range(stretch):
-            out_ref[dest, j] = acc[dest * stretch + j].astype(jnp.bfloat16)
-    whole = jnp.concatenate([foot[b] for b in range(row_span)], axis=1)
+        acc[at_col] += jnp.dot(panel[at_row], blocks[k], preferred_element_type=jnp.float32)
+    spread(out_refs, acc, "row", stretch)
+    whole = jnp.concatenate([panel[b] for b in range(row_span)], axis=1)
     padded = jnp.concatenate([jnp.zeros_like(whole), whole], axis=0)
-    store_split(out_ref, stretch, gram[...] + nt_dot(whole, padded))
+    store_split(out_refs, stretch, gram[...] + nt_dot(whole, padded))
 
 
 def frame_scale(gram):
@@ -115,7 +140,7 @@
     energy = jnp.where(same, gram[:, n:], 0.0)
     column = jnp.sum(energy, axis=1, keepdims=True) / jnp.sum(norm, axis=1, keepdims=True)
     row = jnp.sum(energy, axis=0, keepdims=True) / jnp.sum(norm, axis=0, keepdims=True)
-    return column, row
+    return 1.25 * column, 1.25 * row
 
 
 def image_kernel(in_ref, v_ref, prior, image_ref, next_ref, cast_ref, gram_ref):
@@ -151,7 +176,7 @@
 
 def final_kernel(in_ref, v_ref, image_ref, next_ref, prior, gram_ref, inverse_ref, x_ref, r_ref):
     n = gram_ref.shape[0]
-    stretch = in_ref.shape[1] - 2
+    stretch = in_ref[0].shape[0] - 2
     gram = gram_ref[...]
     norm, energy = gram[:, :n], gram[:, n:]
     scale, scale_row = frame_scale(gram)
@@ -177,12 +202,17 @@
         )
 
 
+def shifted(x, axis, shift):
+    count = lax.axis_size(axis)
+    return lax.ppermute(x, axis, [(i, (i + shift) % count) for i in range(count)])
+
+
 def gather(x, axis):
-    return lax.all_gather(x, axis, axis=0, tiled=True)
-
-
-def exchange(x, axis):
-    return lax.all_to_all(x, axis, split_axis=0, concat_axis=0, tiled=True)
+    return tuple([x] + [shifted(x, axis, s) for s in range(1, lax.axis_size(axis))])
+
+
+def exchange(parts, axis):
+    return tuple([parts[0]] + [shifted(x, axis, s) for s, x in enumerate(parts) if s])
 
 
 def shards(right_side, prior, blocks, block_row, block_col):
@@ -202,19 +232,19 @@
 
     def apply_operator(own_value, own_cast):
         search = gather(own_cast, "row")
-        partial = call(
+        (partial,) = call(
             lambda *refs: forward_kernel(row_span, stretch, *refs),
-            shape((cols, stretch + 2, frames, BLOCK), bf16),
+            ((shape((stretch + 2, frames, BLOCK), bf16),) * cols,),
             (block_row, block_col, search, blocks, own_value, prior),
-            [pltpu.VMEM((row_span, frames, BLOCK), f32)],
+            [pltpu.VMEM((row_span, frames, BLOCK), f32), pltpu.VMEM((col_span, frames, BLOCK), bf16)],
         )
         foot, gram = call(foot_kernel, (panel, gram_type), (exchange(partial, "col"),))
         foot = gather(foot, "col")
-        partial = call(
+        (partial,) = call(
             lambda *refs: backward_kernel(row_span, stretch, *refs),
-            shape((rows, stretch + 2, frames, BLOCK), bf16),
+            ((shape((stretch + 2, frames, BLOCK), bf16),) * rows,),
             (block_row, block_col, foot, blocks, gram),
-            [pltpu.VMEM((col_span, frames, BLOCK), f32)],
+            [pltpu.VMEM((col_span, frames, BLOCK), f32), pltpu.VMEM((row_span, frames, BLOCK), bf16)],
         )
         return exchange(partial, "row")
 

time: 117 us -> 85.9 us (0.73)
  blocking collectives: 78.8 us -> 0 us
  starting transfers between devices: 3.46 us -> 30.7 us
  waiting for transfers between devices: 6.87 us -> 28.6 us
    all_gather x4 -> x0, blocking collectives: 41.8 us -> none  [gather(): return lax.all_gather(x, axis, axis=0, tiled=True)]
    all_to_all x3 -> x0, blocking collectives: 37 us -> none  [exchange(): return lax.all_to_all(x, axis, split_axis=0, concat_axis=0, tiled=True)]
    ppermute x0 -> x24, starting transfers between devices: none -> 30.7 us  [shifted(): lax.ppermute(x, axis, [(i, (i + shift) % count) for i in range(count)])]
    ppermute x0 -> x24, waiting for transfers between devices: none -> 28.6 us  [shifted(): lax.ppermute(x, axis, [(i, (i + shift) % count) for i in range(count)])]
    all_to_all x1 -> x0, waiting for transfers between devices: 6.87 us -> none  [exchange(): return lax.all_to_all(x, axis, split_axis=0, concat_axis=0, tiled=True)]
    all_to_all x1 -> x0, starting transfers between devices: 3.46 us -> none  [exchange(): return lax.all_to_all(x, axis, split_axis=0, concat_axis=0, tiled=True)]
  transfers between devices with their start and end apart: 1 -> 24, of which waited for: 1 -> 18; matrix products, arithmetic and copies ran while one was open for 0% -> 0% of each run, Pallas kernels for 5% -> 6%
where the time goes in v2:
time: 85.9 us; the launch traced here: 85.7 us
  starting transfers between devices  30.7 us (36%)
  waiting for transfers between devices  28.6 us (33%)
  Pallas kernels  21.2 us (25%)
  local copies, waits for them, and re-layouts  4.5 us (5%)
    ppermute x24, starting transfers between devices, shifted(): lax.ppermute(x, axis, [(i, (i + shift) % count) for i in range(count)])  30.7 us
    ppermute x24, waiting for transfers between devices, shifted(): lax.ppermute(x, axis, [(i, (i + shift) % count) for i in range(count)])  28.6 us
    pallas_call x10, Pallas kernels, call(): pl.pallas_call(body, out_shape=flat_outs, in_specs=[SMEM if x.dtype == jn...  21.2 us
    unnamed x20, local copies, waits for them, and re-layouts  4.5 us
  transfers between devices with their start and end apart: 24, of which 18 were waited for; matrix products, arithmetic and copies ran while one was open for 0% of the time, Pallas kernels for 6%

profile of v2, /device:TPU:0, one launch (start us, length us, event | category | flops | bytes accessed | tf_op | source)
XLA Modules:
  0.0 85.7 jit_solution(6093887178956358585)
XLA Ops:
  1.6 3.1 %collective-permute-start = (bf16[4,64,128]{2,1,0:T(8,128)(2,1)S(1)}, bf16[4,64,128]{2,1,0:T(8,128)(2,1)S(1)}, u32[]{:S(2)}, u32[]{:S(2)}) collective-permute-start(bf16[4,64,128]{2,1,0:T(8,128)(2,1)S(1)} %shard_map.68.refs_2_), channel_id=1, source_target_pairs={{0,4},{4,8},{8,12},{12,0},{1,5},{5,9},{9,13},{13,1},{2,6},{6,10},{... | collective-permute-start | bytes 196616 | tf_op jit(solution)/shard_map/ppermute | solution.py:207
  4.6 2.6 %collective-permute-start.1 = (bf16[4,64,128]{2,1,0:T(8,128)(2,1)S(1)}, bf16[4,64,128]{2,1,0:T(8,128)(2,1)S(1)}, u32[]{:S(2)}, u32[]{:S(2)}) collective-permute-start(bf16[4,64,128]{2,1,0:T(8,128)(2,1)S(1)} %shard_map.68.refs_2_), channel_id=1, source_target_pairs={{0,8},{4,12},{8,0},{12,4},{1,9},{5,13},{9,1},{13,5},{2,10},{6,14},... | collective-permute-start | bytes 196616 | tf_op jit(solution)/shard_map/ppermute | solution.py:207
  7.2 1.3 %collective-permute-start.2 = (bf16[4,64,128]{2,1,0:T(8,128)(2,1)S(1)}, bf16[4,64,128]{2,1,0:T(8,128)(2,1)S(1)}, u32[]{:S(2)}, u32[]{:S(2)}) collective-permute-start(bf16[4,64,128]{2,1,0:T(8,128)(2,1)S(1)} %shard_map.68.refs_2_), channel_id=1, source_target_pairs={{0,12},{4,0},{8,4},{12,8},{1,13},{5,1},{9,5},{13,9},{2,14},{6,2},{... | collective-permute-start | bytes 196616 | tf_op jit(solution)/shard_map/ppermute | solution.py:207
  9.2 2.5 %collective-permute-done.1.refs_4_ = bf16[4,64,128]{2,1,0:T(8,128)(2,1)S(1)} collective-permute-done((bf16[4,64,128]{2,1,0:T(8,128)(2,1)S(1)}, bf16[4,64,128]{2,1,0:T(8,128)(2,1)S(1)}, u32[]{:S(2)}, u32[]{:S(2)}) %collective-permute-start.1) | collective-permute-done | bytes 65568 | tf_op jit(solution)/shard_map/ppermute | solution.py:207
  11.9 1.6 %copy-done = bf16[64,128,128]{2,1,0:T(8,128)(2,1)S(1)} copy-done((bf16[64,128,128]{2,1,0:T(8,128)(2,1)S(1)}, bf16[64,128,128]{2,1,0:T(8,128)(2,1)}, u32[]{:S(2)}) %copy-start) | copy-done | bytes 2097176
  15.5 2.3 %shard_map.69 = (bf16[6,64,128]{2,1,0:T(8,128)(2,1)S(1)}, bf16[6,64,128]{2,1,0:T(8,128)(2,1)S(1)}, bf16[6,64,128]{2,1,0:T(8,128)(2,1)S(1)}, bf16[6,64,128]{2,1,0:T(8,128)(2,1)S(1)}) custom-call(s32[64]{0:T(128)S(1)} %copy-done.6, s32[64]{0:T(128)S(1)} %copy-done.8, bf16[4,64,128]{2,1,0:T(8,128)(2,1)S(1)} %shard_map.68.refs_2_, ...), custom_call_target="tpu_custom_call" | custom-call | tf_op jit(solution)/shard_map/pallas_call | solution.py:45
  17.9 1.6 %collective-permute-start.4 = (bf16[6,64,128]{2,1,0:T(8,128)(2,1)S(1)}, bf16[6,64,128]{2,1,0:T(8,128)(2,1)S(1)}, u32[]{:S(2)}, u32[]{:S(2)}) collective-permute-start(bf16[6,64,128]{2,1,0:T(8,128)(2,1)S(1)} %get-tuple-element.28), channel_id=1, source_target_pairs={{0,2},{1,3},{2,0},{3,1},{4,6},{5,7},{6,4},{7,5},{8,10},{9,11},{10,... | collective-permute-start | bytes 294920 | tf_op jit(solution)/shard_map/ppermute | solution.py:207
  19.5 1.4 %collective-permute-start.5 = (bf16[6,64,128]{2,1,0:T(8,128)(2,1)S(1)}, bf16[6,64,128]{2,1,0:T(8,128)(2,1)S(1)}, u32[]{:S(2)}, u32[]{:S(2)}) collective-permute-start(bf16[6,64,128]{2,1,0:T(8,128)(2,1)S(1)} %get-tuple-element.29), channel_id=1, source_target_pairs={{0,3},{1,0},{2,1},{3,2},{4,7},{5,4},{6,5},{7,6},{8,11},{9,8},{10,9... | collective-permute-start | bytes 294920 | tf_op jit(solution)/shard_map/ppermute | solution.py:207
  20.9 1.5 %collective-permute-done.3.refs_1_ = bf16[6,64,128]{2,1,0:T(8,128)(2,1)S(1)} collective-permute-done((bf16[6,64,128]{2,1,0:T(8,128)(2,1)S(1)}, bf16[6,64,128]{2,1,0:T(8,128)(2,1)S(1)}, u32[]{:S(2)}, u32[]{:S(2)}) %collective-permute-start.3) | collective-permute-done | bytes 98336 | tf_op jit(solution)/shard_map/ppermute | solution.py:207
  25.0 1.5 %collective-permute-start.7 = (bf16[4,64,128]{2,1,0:T(8,128)(2,1)S(1)}, bf16[4,64,128]{2,1,0:T(8,128)(2,1)S(1)}, u32[]{:S(2)}, u32[]{:S(2)}) collective-permute-start(bf16[4,64,128]{2,1,0:T(8,128)(2,1)S(1)} %get-tuple-element.30.refs_2_), channel_id=1, source_target_pairs={{0,2},{1,3},{2,0},{3,1},{4,6},{5,7},{6,4},{7,5},{8,10},{9,11},{10,... | collective-permute-start | bytes 196616 | tf_op jit(solution)/shard_map/ppermute | solution.py:207
  26.7 1.4 %collective-permute-done.6.refs_3_ = bf16[4,64,128]{2,1,0:T(8,128)(2,1)S(1)} collective-permute-done((bf16[4,64,128]{2,1,0:T(8,128)(2,1)S(1)}, bf16[4,64,128]{2,1,0:T(8,128)(2,1)S(1)}, u32[]{:S(2)}, u32[]{:S(2)}) %collective-permute-start.6) | collective-permute-done | bytes 65568 | tf_op jit(solution)/shard_map/ppermute | solution.py:207
  28.1 1.4 %collective-permute-done.7.refs_4_ = bf16[4,64,128]{2,1,0:T(8,128)(2,1)S(1)} collective-permute-done((bf16[4,64,128]{2,1,0:T(8,128)(2,1)S(1)}, bf16[4,64,128]{2,1,0:T(8,128)(2,1)S(1)}, u32[]{:S(2)}, u32[]{:S(2)}) %collective-permute-start.7) | collective-permute-done | bytes 65568 | tf_op jit(solution)/shard_map/ppermute | solution.py:207
  29.6 1.5 %shard_map.71 = (bf16[6,64,128]{2,1,0:T(8,128)(2,1)S(1)}, bf16[6,64,128]{2,1,0:T(8,128)(2,1)S(1)}, bf16[6,64,128]{2,1,0:T(8,128)(2,1)S(1)}, bf16[6,64,128]{2,1,0:T(8,128)(2,1)S(1)}) custom-call(s32[64]{0:T(128)S(1)} %copy-done.7, s32[64]{0:T(128)S(1)} %copy-done.9, bf16[4,64,128]{2,1,0:T(8,128)(2,1)S(1)} %get-tuple-element.30.refs_2_, ...), custom_call_target="tpu_custom_call" | custom-call | tf_op jit(solution)/shard_map/pallas_call | solution.py:45
  31.8 3.1 %collective-permute-start.11 = (bf16[6,64,128]{2,1,0:T(8,128)(2,1)S(1)}, bf16[6,64,128]{2,1,0:T(8,128)(2,1)S(1)}, u32[]{:S(2)}, u32[]{:S(2)}) collective-permute-start(bf16[6,64,128]{2,1,0:T(8,128)(2,1)S(1)} %get-tuple-element.35), channel_id=1, source_target_pairs={{0,12},{4,0},{8,4},{12,8},{1,13},{5,1},{9,5},{13,9},{2,14},{6,2},{... | collective-permute-start | bytes 294920 | tf_op jit(solution)/shard_map/ppermute | solution.py:207
  35.0 4.7 %collective-permute-done.10.refs_2_ = bf16[6,64,128]{2,1,0:T(8,128)(2,1)S(1)} collective-permute-done((bf16[6,64,128]{2,1,0:T(8,128)(2,1)S(1)}, bf16[6,64,128]{2,1,0:T(8,128)(2,1)S(1)}, u32[]{:S(2)}, u32[]{:S(2)}) %collective-permute-start.10) | collective-permute-done | bytes 98336 | tf_op jit(solution)/shard_map/ppermute | solution.py:207
  39.7 2.9 %collective-permute-done.9.refs_1_ = bf16[6,64,128]{2,1,0:T(8,128)(2,1)S(1)} collective-permute-done((bf16[6,64,128]{2,1,0:T(8,128)(2,1)S(1)}, bf16[6,64,128]{2,1,0:T(8,128)(2,1)S(1)}, u32[]{:S(2)}, u32[]{:S(2)}) %collective-permute-start.9) | collective-permute-done | bytes 98336 | tf_op jit(solution)/shard_map/ppermute | solution.py:207
  42.7 1.6 %collective-permute-start.12 = (bf16[4,64,128]{2,1,0:T(8,128)(2,1)S(1)}, bf16[4,64,128]{2,1,0:T(8,128)(2,1)S(1)}, u32[]{:S(2)}, u32[]{:S(2)}) collective-permute-start(bf16[4,64,128]{2,1,0:T(8,128)(2,1)S(1)} %get-tuple-element.36.refs_2_), channel_id=1, source_target_pairs={{0,4},{4,8},{8,12},{12,0},{1,5},{5,9},{9,13},{13,1},{2,6},{6,10},{... | collective-permute-start | bytes 196616 | tf_op jit(solution)/shard_map/ppermute | solution.py:207
  45.5 2.0 %collective-permute-start.14 = (bf16[4,64,128]{2,1,0:T(8,128)(2,1)S(1)}, bf16[4,64,128]{2,1,0:T(8,128)(2,1)S(1)}, u32[]{:S(2)}, u32[]{:S(2)}) collective-permute-start(bf16[4,64,128]{2,1,0:T(8,128)(2,1)S(1)} %get-tuple-element.36.refs_2_), channel_id=1, source_target_pairs={{0,12},{4,0},{8,4},{12,8},{1,13},{5,1},{9,5},{13,9},{2,14},{6,2},{... | collective-permute-start | bytes 196616 | tf_op jit(solution)/shard_map/ppermute | solution.py:207
  47.5 2.1 %collective-permute-done.12.refs_3_ = bf16[4,64,128]{2,1,0:T(8,128)(2,1)S(1)} collective-permute-done((bf16[4,64,128]{2,1,0:T(8,128)(2,1)S(1)}, bf16[4,64,128]{2,1,0:T(8,128)(2,1)S(1)}, u32[]{:S(2)}, u32[]{:S(2)}) %collective-permute-start.12) | collective-permute-done | bytes 65568 | tf_op jit(solution)/shard_map/ppermute | solution.py:207
  49.6 1.8 %collective-permute-done.13.refs_4_ = bf16[4,64,128]{2,1,0:T(8,128)(2,1)S(1)} collective-permute-done((bf16[4,64,128]{2,1,0:T(8,128)(2,1)S(1)}, bf16[4,64,128]{2,1,0:T(8,128)(2,1)S(1)}, u32[]{:S(2)}, u32[]{:S(2)}) %collective-permute-start.13) | collective-permute-done | bytes 65568 | tf_op jit(solution)/shard_map/ppermute | solution.py:207
  51.4 2.3 %shard_map.73 = (bf16[6,64,128]{2,1,0:T(8,128)(2,1)S(1)}, bf16[6,64,128]{2,1,0:T(8,128)(2,1)S(1)}, bf16[6,64,128]{2,1,0:T(8,128)(2,1)S(1)}, bf16[6,64,128]{2,1,0:T(8,128)(2,1)S(1)}) custom-call(s32[64]{0:T(128)S(1)} %copy-done.7, s32[64]{0:T(128)S(1)} %copy-done.9, bf16[4,64,128]{2,1,0:T(8,128)(2,1)S(1)} %get-tuple-element.36.refs_2_, ...), custom_call_target="tpu_custom_call" | custom-call | tf_op jit(solution)/shard_map/pallas_call | solution.py:45
  53.8 1.4 %collective-permute-start.16 = (bf16[6,64,128]{2,1,0:T(8,128)(2,1)S(1)}, bf16[6,64,128]{2,1,0:T(8,128)(2,1)S(1)}, u32[]{:S(2)}, u32[]{:S(2)}) collective-permute-start(bf16[6,64,128]{2,1,0:T(8,128)(2,1)S(1)} %get-tuple-element.40), channel_id=1, source_target_pairs={{0,2},{1,3},{2,0},{3,1},{4,6},{5,7},{6,4},{7,5},{8,10},{9,11},{10,... | collective-permute-start | bytes 294920 | tf_op jit(solution)/shard_map/ppermute | solution.py:207
  55.1 1.4 %collective-permute-start.17 = (bf16[6,64,128]{2,1,0:T(8,128)(2,1)S(1)}, bf16[6,64,128]{2,1,0:T(8,128)(2,1)S(1)}, u32[]{:S(2)}, u32[]{:S(2)}) collective-permute-start(bf16[6,64,128]{2,1,0:T(8,128)(2,1)S(1)} %get-tuple-element.41), channel_id=1, source_target_pairs={{0,3},{1,0},{2,1},{3,2},{4,7},{5,4},{6,5},{7,6},{8,11},{9,8},{10,9... | collective-permute-start | bytes 294920 | tf_op jit(solution)/shard_map/ppermute | solution.py:207
  56.5 1.7 %collective-permute-done.15.refs_1_ = bf16[6,64,128]{2,1,0:T(8,128)(2,1)S(1)} collective-permute-done((bf16[6,64,128]{2,1,0:T(8,128)(2,1)S(1)}, bf16[6,64,128]{2,1,0:T(8,128)(2,1)S(1)}, u32[]{:S(2)}, u32[]{:S(2)}) %collective-permute-start.15) | collective-permute-done | bytes 98336 | tf_op jit(solution)/shard_map/ppermute | solution.py:207
  62.3 1.4 %collective-permute-done.18.refs_3_ = bf16[4,64,128]{2,1,0:T(8,128)(2,1)S(1)} collective-permute-done((bf16[4,64,128]{2,1,0:T(8,128)(2,1)S(1)}, bf16[4,64,128]{2,1,0:T(8,128)(2,1)S(1)}, u32[]{:S(2)}, u32[]{:S(2)}) %collective-permute-start.18) | collective-permute-done | bytes 65568 | tf_op jit(solution)/shard_map/ppermute | solution.py:207
  63.7 1.4 %collective-permute-done.19.refs_4_ = bf16[4,64,128]{2,1,0:T(8,128)(2,1)S(1)} collective-permute-done((bf16[4,64,128]{2,1,0:T(8,128)(2,1)S(1)}, bf16[4,64,128]{2,1,0:T(8,128)(2,1)S(1)}, u32[]{:S(2)}, u32[]{:S(2)}) %collective-permute-start.19) | collective-permute-done | bytes 65568 | tf_op jit(solution)/shard_map/ppermute | solution.py:207
  65.1 1.5 %shard_map.75 = (bf16[6,64,128]{2,1,0:T(8,128)(2,1)S(1)}, bf16[6,64,128]{2,1,0:T(8,128)(2,1)S(1)}, bf16[6,64,128]{2,1,0:T(8,128)(2,1)S(1)}, bf16[6,64,128]{2,1,0:T(8,128)(2,1)S(1)}) custom-call(s32[64]{0:T(128)S(1)} %copy-done.7, s32[64]{0:T(128)S(1)} %copy-done.9, bf16[4,64,128]{2,1,0:T(8,128)(2,1)S(1)} %get-tuple-element.42.refs_2_, ...), custom_call_target="tpu_custom_call" | custom-call | tf_op jit(solution)/shard_map/pallas_call | solution.py:45
  66.6 1.7 %collective-permute-start.21 = (bf16[6,64,128]{2,1,0:T(8,128)(2,1)S(1)}, bf16[6,64,128]{2,1,0:T(8,128)(2,1)S(1)}, u32[]{:S(2)}, u32[]{:S(2)}) collective-permute-start(bf16[6,64,128]{2,1,0:T(8,128)(2,1)S(1)} %get-tuple-element.45), channel_id=1, source_target_pairs={{0,4},{4,8},{8,12},{12,0},{1,5},{5,9},{9,13},{13,1},{2,6},{6,10},{... | collective-permute-start | bytes 294920 | tf_op jit(solution)/shard_map/ppermute | solution.py:207
  68.3 1.5 %collective-permute-start.22 = (bf16[6,64,128]{2,1,0:T(8,128)(2,1)S(1)}, bf16[6,64,128]{2,1,0:T(8,128)(2,1)S(1)}, u32[]{:S(2)}, u32[]{:S(2)}) collective-permute-start(bf16[6,64,128]{2,1,0:T(8,128)(2,1)S(1)} %get-tuple-element.46), channel_id=1, source_target_pairs={{0,8},{4,12},{8,0},{12,4},{1,9},{5,13},{9,1},{13,5},{2,10},{6,14},... | collective-permute-start | bytes 294920 | tf_op jit(solution)/shard_map/ppermute | solution.py:207
  70.7 5.6 %shard_map.76.refs_9_ = f32[64,64]{1,0:T(8,128)S(1)} custom-call(f32[64,128]{1,0:T(8,128)S(1)} %get-tuple-element.49.refs_0_.refs_8_), custom_call_target="tpu_custom_call" | custom-call | tf_op jit(solution)/shard_map/pallas_call | solution.py:45
  76.3 1.6 %collective-permute-done.22.refs_2_ = bf16[6,64,128]{2,1,0:T(8,128)(2,1)S(1)} collective-permute-done((bf16[6,64,128]{2,1,0:T(8,128)(2,1)S(1)}, bf16[6,64,128]{2,1,0:T(8,128)(2,1)S(1)}, u32[]{:S(2)}, u32[]{:S(2)}) %collective-permute-start.22) | collective-permute-done | bytes 98336 | tf_op jit(solution)/shard_map/ppermute | solution.py:207
  77.9 7.8 %shard_map.77 = (f32[64,512]{1,0:T(8,128)}, f32[64,512]{1,0:T(8,128)}) custom-call(bf16[6,64,128]{2,1,0:T(8,128)(2,1)S(1)} %get-tuple-element.44.refs_0_, bf16[6,64,128]{2,1,0:T(8,128)(2,1)S(1)} %collective-permute-done.21.refs_1_, bf16[6,64,128]{2,1,0:T(8,128)(2,1)S(1)} %collective-permute-done.22.refs_2_, ...), custom_call_target="tpu_custom_call" | custom-call | tf_op jit(solution)/shard_map/pallas_call | solution.py:45
  (46 shorter events, 13.9 us)
Async XLA Ops:
  0.6 0.9 %copy-start.2 = (f32[64,512]{1,0:T(8,128)S(1)}, f32[64,512]{1,0:T(8,128)}, u32[]{:S(2)}) copy-start(f32[64,512]{1,0:T(8,128)} %refs_4_.3) | copy-start | bytes 393220
  1.5 28.0 %copy-start.7 = (s32[64]{0:T(128)S(1)}, s32[64]{0:T(128)}, u32[]{:S(2)}) copy-start(s32[64]{0:T(128)} %refs_0_.9) | copy-start | bytes 772
  1.5 28.0 %copy-start.9 = (s32[64]{0:T(128)S(1)}, s32[64]{0:T(128)}, u32[]{:S(2)}) copy-start(s32[64]{0:T(128)} %refs_1_.7) | copy-start | bytes 772
  1.6 7.6 %collective-permute-start = (bf16[4,64,128]{2,1,0:T(8,128)(2,1)S(1)}, bf16[4,64,128]{2,1,0:T(8,128)(2,1)S(1)}, u32[]{:S(2)}, u32[]{:S(2)}) collective-permute-start(bf16[4,64,128]{2,1,0:T(8,128)(2,1)S(1)} %shard_map.68.refs_2_), channel_id=1, source_target_pairs={{0,4},{4,8},{8,12},{12,0},{1,5},{5,9},{9,13},{13,1},{2,6},{6,10},{... | collective-permute-start | bytes 196616 | tf_op jit(solution)/shard_map/ppermute | solution.py:207
  4.6 7.1 %collective-permute-start.1 = (bf16[4,64,128]{2,1,0:T(8,128)(2,1)S(1)}, bf16[4,64,128]{2,1,0:T(8,128)(2,1)S(1)}, u32[]{:S(2)}, u32[]{:S(2)}) collective-permute-start(bf16[4,64,128]{2,1,0:T(8,128)(2,1)S(1)} %shard_map.68.refs_2_), channel_id=1, source_target_pairs={{0,8},{4,12},{8,0},{12,4},{1,9},{5,13},{9,1},{13,5},{2,10},{6,14},... | collective-permute-start | bytes 196616 | tf_op jit(solution)/shard_map/ppermute | solution.py:207
  7.2 4.7 %collective-permute-start.2 = (bf16[4,64,128]{2,1,0:T(8,128)(2,1)S(1)}, bf16[4,64,128]{2,1,0:T(8,128)(2,1)S(1)}, u32[]{:S(2)}, u32[]{:S(2)}) collective-permute-start(bf16[4,64,128]{2,1,0:T(8,128)(2,1)S(1)} %shard_map.68.refs_2_), channel_id=1, source_target_pairs={{0,12},{4,0},{8,4},{12,8},{1,13},{5,1},{9,5},{13,9},{2,14},{6,2},{... | collective-permute-start | bytes 196616 | tf_op jit(solution)/shard_map/ppermute | solution.py:207
  11.9 1.6 %copy-start = (bf16[64,128,128]{2,1,0:T(8,128)(2,1)S(1)}, bf16[64,128,128]{2,1,0:T(8,128)(2,1)}, u32[]{:S(2)}) copy-start(bf16[64,128,128]{2,1,0:T(8,128)(2,1)} %refs_6_.7) | copy-start | bytes 6291460
  13.5 0.7 copy-start.4
  15.5 14.0 %copy-start.1 = (bf16[64,128,128]{2,1,0:T(8,128)(2,1)S(1)}, bf16[64,128,128]{2,1,0:T(8,128)(2,1)}, u32[]{:S(2)}) copy-start(bf16[64,128,128]{2,1,0:T(8,128)(2,1)} %refs_6_.7) | copy-start | bytes 6291460
  15.5 27.0 %copy-start.3 = (f32[64,512]{1,0:T(8,128)S(1)}, f32[64,512]{1,0:T(8,128)}, u32[]{:S(2)}) copy-start(f32[64,512]{1,0:T(8,128)} %refs_4_.3) | copy-start | bytes 393220
  15.5 27.0 %copy-start.5 = (f32[512]{0:T(512)S(1)}, f32[512]{0:T(512)}, u32[]{:S(2)}) copy-start(f32[512]{0:T(512)} %param.6) | copy-start | bytes 6148
  17.9 4.5 %collective-permute-start.3 = (bf16[6,64,128]{2,1,0:T(8,128)(2,1)S(1)}, bf16[6,64,128]{2,1,0:T(8,128)(2,1)S(1)}, u32[]{:S(2)}, u32[]{:S(2)}) collective-permute-start(bf16[6,64,128]{2,1,0:T(8,128)(2,1)S(1)} %get-tuple-element.27), channel_id=1, source_target_pairs={{0,1},{1,2},{2,3},{3,0},{4,5},{5,6},{6,7},{7,4},{8,9},{9,10},{10,1... | collective-permute-start | bytes 294920 | tf_op jit(solution)/shard_map/ppermute | solution.py:207
  17.9 5.7 %collective-permute-start.4 = (bf16[6,64,128]{2,1,0:T(8,128)(2,1)S(1)}, bf16[6,64,128]{2,1,0:T(8,128)(2,1)S(1)}, u32[]{:S(2)}, u32[]{:S(2)}) collective-permute-start(bf16[6,64,128]{2,1,0:T(8,128)(2,1)S(1)} %get-tuple-element.28), channel_id=1, source_target_pairs={{0,2},{1,3},{2,0},{3,1},{4,6},{5,7},{6,4},{7,5},{8,10},{9,11},{10,... | collective-permute-start | bytes 294920 | tf_op jit(solution)/shard_map/ppermute | solution.py:207
  19.5 4.6 %collective-permute-start.5 = (bf16[6,64,128]{2,1,0:T(8,128)(2,1)S(1)}, bf16[6,64,128]{2,1,0:T(8,128)(2,1)S(1)}, u32[]{:S(2)}, u32[]{:S(2)}) collective-permute-start(bf16[6,64,128]{2,1,0:T(8,128)(2,1)S(1)} %get-tuple-element.29), channel_id=1, source_target_pairs={{0,3},{1,0},{2,1},{3,2},{4,7},{5,4},{6,5},{7,6},{8,11},{9,8},{10,9... | collective-permute-start | bytes 294920 | tf_op jit(solution)/shard_map/ppermute | solution.py:207
  24.2 3.9 %collective-permute-start.6 = (bf16[4,64,128]{2,1,0:T(8,128)(2,1)S(1)}, bf16[4,64,128]{2,1,0:T(8,128)(2,1)S(1)}, u32[]{:S(2)}, u32[]{:S(2)}) collective-permute-start(bf16[4,64,128]{2,1,0:T(8,128)(2,1)S(1)} %get-tuple-element.30.refs_2_), channel_id=1, source_target_pairs={{0,1},{1,2},{2,3},{3,0},{4,5},{5,6},{6,7},{7,4},{8,9},{9,10},{10,1... | collective-permute-start | bytes 196616 | tf_op jit(solution)/shard_map/ppermute | solution.py:207
  25.0 4.5 %collective-permute-start.7 = (bf16[4,64,128]{2,1,0:T(8,128)(2,1)S(1)}, bf16[4,64,128]{2,1,0:T(8,128)(2,1)S(1)}, u32[]{:S(2)}, u32[]{:S(2)}) collective-permute-start(bf16[4,64,128]{2,1,0:T(8,128)(2,1)S(1)} %get-tuple-element.30.refs_2_), channel_id=1, source_target_pairs={{0,2},{1,3},{2,0},{3,1},{4,6},{5,7},{6,4},{7,5},{8,10},{9,11},{10,... | collective-permute-start | bytes 196616 | tf_op jit(solution)/shard_map/ppermute | solution.py:207
  26.6 3.0 %collective-permute-start.8 = (bf16[4,64,128]{2,1,0:T(8,128)(2,1)S(1)}, bf16[4,64,128]{2,1,0:T(8,128)(2,1)S(1)}, u32[]{:S(2)}, u32[]{:S(2)}) collective-permute-start(bf16[4,64,128]{2,1,0:T(8,128)(2,1)S(1)} %get-tuple-element.30.refs_2_), channel_id=1, source_target_pairs={{0,3},{1,0},{2,1},{3,2},{4,7},{5,4},{6,5},{7,6},{8,11},{9,8},{10,9... | collective-permute-start | bytes 196616 | tf_op jit(solution)/shard_map/ppermute | solution.py:207
  31.0 8.7 %collective-permute-start.10 = (bf16[6,64,128]{2,1,0:T(8,128)(2,1)S(1)}, bf16[6,64,128]{2,1,0:T(8,128)(2,1)S(1)}, u32[]{:S(2)}, u32[]{:S(2)}) collective-permute-start(bf16[6,64,128]{2,1,0:T(8,128)(2,1)S(1)} %get-tuple-element.34), channel_id=1, source_target_pairs={{0,8},{4,12},{8,0},{12,4},{1,9},{5,13},{9,1},{13,5},{2,10},{6,14},... | collective-permute-start | bytes 294920 | tf_op jit(solution)/shard_map/ppermute | solution.py:207
  31.8 7.8 %collective-permute-start.11 = (bf16[6,64,128]{2,1,0:T(8,128)(2,1)S(1)}, bf16[6,64,128]{2,1,0:T(8,128)(2,1)S(1)}, u32[]{:S(2)}, u32[]{:S(2)}) collective-permute-start(bf16[6,64,128]{2,1,0:T(8,128)(2,1)S(1)} %get-tuple-element.35), channel_id=1, source_target_pairs={{0,12},{4,0},{8,4},{12,8},{1,13},{5,1},{9,5},{13,9},{2,14},{6,2},{... | collective-permute-start | bytes 294920 | tf_op jit(solution)/shard_map/ppermute | solution.py:207
  35.0 7.6 %collective-permute-start.9 = (bf16[6,64,128]{2,1,0:T(8,128)(2,1)S(1)}, bf16[6,64,128]{2,1,0:T(8,128)(2,1)S(1)}, u32[]{:S(2)}, u32[]{:S(2)}) collective-permute-start(bf16[6,64,128]{2,1,0:T(8,128)(2,1)S(1)} %get-tuple-element.33), channel_id=1, source_target_pairs={{0,4},{4,8},{8,12},{12,0},{1,5},{5,9},{9,13},{13,1},{2,6},{6,10},{... | collective-permute-start | bytes 294920 | tf_op jit(solution)/shard_map/ppermute | solution.py:207
  42.7 6.9 %collective-permute-start.12 = (bf16[4,64,128]{2,1,0:T(8,128)(2,1)S(1)}, bf16[4,64,128]{2,1,0:T(8,128)(2,1)S(1)}, u32[]{:S(2)}, u32[]{:S(2)}) collective-permute-start(bf16[4,64,128]{2,1,0:T(8,128)(2,1)S(1)} %get-tuple-element.36.refs_2_), channel_id=1, source_target_pairs={{0,4},{4,8},{8,12},{12,0},{1,5},{5,9},{9,13},{13,1},{2,6},{6,10},{... | collective-permute-start | bytes 196616 | tf_op jit(solution)/shard_map/ppermute | solution.py:207
  44.3 7.0 %collective-permute-start.13 = (bf16[4,64,128]{2,1,0:T(8,128)(2,1)S(1)}, bf16[4,64,128]{2,1,0:T(8,128)(2,1)S(1)}, u32[]{:S(2)}, u32[]{:S(2)}) collective-permute-start(bf16[4,64,128]{2,1,0:T(8,128)(2,1)S(1)} %get-tuple-element.36.refs_2_), channel_id=1, source_target_pairs={{0,8},{4,12},{8,0},{12,4},{1,9},{5,13},{9,1},{13,5},{2,10},{6,14},... | collective-permute-start | bytes 196616 | tf_op jit(solution)/shard_map/ppermute | solution.py:207
  45.5 5.9 %collective-permute-start.14 = (bf16[4,64,128]{2,1,0:T(8,128)(2,1)S(1)}, bf16[4,64,128]{2,1,0:T(8,128)(2,1)S(1)}, u32[]{:S(2)}, u32[]{:S(2)}) collective-permute-start(bf16[4,64,128]{2,1,0:T(8,128)(2,1)S(1)} %get-tuple-element.36.refs_2_), channel_id=1, source_target_pairs={{0,12},{4,0},{8,4},{12,8},{1,13},{5,1},{9,5},{13,9},{2,14},{6,2},{... | collective-permute-start | bytes 196616 | tf_op jit(solution)/shard_map/ppermute | solution.py:207
  53.7 4.5 %collective-permute-start.15 = (bf16[6,64,128]{2,1,0:T(8,128)(2,1)S(1)}, bf16[6,64,128]{2,1,0:T(8,128)(2,1)S(1)}, u32[]{:S(2)}, u32[]{:S(2)}) collective-permute-start(bf16[6,64,128]{2,1,0:T(8,128)(2,1)S(1)} %get-tuple-element.39), channel_id=1, source_target_pairs={{0,1},{1,2},{2,3},{3,0},{4,5},{5,6},{6,7},{7,4},{8,9},{9,10},{10,1... | collective-permute-start | bytes 294920 | tf_op jit(solution)/shard_map/ppermute | solution.py:207
  53.8 5.7 %collective-permute-start.16 = (bf16[6,64,128]{2,1,0:T(8,128)(2,1)S(1)}, bf16[6,64,128]{2,1,0:T(8,128)(2,1)S(1)}, u32[]{:S(2)}, u32[]{:S(2)}) collective-permute-start(bf16[6,64,128]{2,1,0:T(8,128)(2,1)S(1)} %get-tuple-element.40), channel_id=1, source_target_pairs={{0,2},{1,3},{2,0},{3,1},{4,6},{5,7},{6,4},{7,5},{8,10},{9,11},{10,... | collective-permute-start | bytes 294920 | tf_op jit(solution)/shard_map/ppermute | solution.py:207
  55.1 4.6 %collective-permute-start.17 = (bf16[6,64,128]{2,1,0:T(8,128)(2,1)S(1)}, bf16[6,64,128]{2,1,0:T(8,128)(2,1)S(1)}, u32[]{:S(2)}, u32[]{:S(2)}) collective-permute-start(bf16[6,64,128]{2,1,0:T(8,128)(2,1)S(1)} %get-tuple-element.41), channel_id=1, source_target_pairs={{0,3},{1,0},{2,1},{3,2},{4,7},{5,4},{6,5},{7,6},{8,11},{9,8},{10,9... | collective-permute-start | bytes 294920 | tf_op jit(solution)/shard_map/ppermute | solution.py:207
  59.8 3.9 %collective-permute-start.18 = (bf16[4,64,128]{2,1,0:T(8,128)(2,1)S(1)}, bf16[4,64,128]{2,1,0:T(8,128)(2,1)S(1)}, u32[]{:S(2)}, u32[]{:S(2)}) collective-permute-start(bf16[4,64,128]{2,1,0:T(8,128)(2,1)S(1)} %get-tuple-element.42.refs_2_), channel_id=1, source_target_pairs={{0,1},{1,2},{2,3},{3,0},{4,5},{5,6},{6,7},{7,4},{8,9},{9,10},{10,1... | collective-permute-start | bytes 196616 | tf_op jit(solution)/shard_map/ppermute | solution.py:207
  60.9 4.3 %collective-permute-start.19 = (bf16[4,64,128]{2,1,0:T(8,128)(2,1)S(1)}, bf16[4,64,128]{2,1,0:T(8,128)(2,1)S(1)}, u32[]{:S(2)}, u32[]{:S(2)}) collective-permute-start(bf16[4,64,128]{2,1,0:T(8,128)(2,1)S(1)} %get-tuple-element.42.refs_2_), channel_id=1, source_target_pairs={{0,2},{1,3},{2,0},{3,1},{4,6},{5,7},{6,4},{7,5},{8,10},{9,11},{10,... | collective-permute-start | bytes 196616 | tf_op jit(solution)/shard_map/ppermute | solution.py:207
  62.2 3.0 %collective-permute-start.20 = (bf16[4,64,128]{2,1,0:T(8,128)(2,1)S(1)}, bf16[4,64,128]{2,1,0:T(8,128)(2,1)S(1)}, u32[]{:S(2)}, u32[]{:S(2)}) collective-permute-start(bf16[4,64,128]{2,1,0:T(8,128)(2,1)S(1)} %get-tuple-element.42.refs_2_), channel_id=1, source_target_pairs={{0,3},{1,0},{2,1},{3,2},{4,7},{5,4},{6,5},{7,6},{8,11},{9,8},{10,9... | collective-permute-start | bytes 196616 | tf_op jit(solution)/shard_map/ppermute | solution.py:207
  66.6 9.7 %collective-permute-start.21 = (bf16[6,64,128]{2,1,0:T(8,128)(2,1)S(1)}, bf16[6,64,128]{2,1,0:T(8,128)(2,1)S(1)}, u32[]{:S(2)}, u32[]{:S(2)}) collective-permute-start(bf16[6,64,128]{2,1,0:T(8,128)(2,1)S(1)} %get-tuple-element.45), channel_id=1, source_target_pairs={{0,4},{4,8},{8,12},{12,0},{1,5},{5,9},{9,13},{13,1},{2,6},{6,10},{... | collective-permute-start | bytes 294920 | tf_op jit(solution)/shard_map/ppermute | solution.py:207
  68.3 9.6 %collective-permute-start.22 = (bf16[6,64,128]{2,1,0:T(8,128)(2,1)S(1)}, bf16[6,64,128]{2,1,0:T(8,128)(2,1)S(1)}, u32[]{:S(2)}, u32[]{:S(2)}) collective-permute-start(bf16[6,64,128]{2,1,0:T(8,128)(2,1)S(1)} %get-tuple-element.46), channel_id=1, source_target_pairs={{0,8},{4,12},{8,0},{12,4},{1,9},{5,13},{9,1},{13,5},{2,10},{6,14},... | collective-permute-start | bytes 294920 | tf_op jit(solution)/shard_map/ppermute | solution.py:207
  69.8 8.1 %collective-permute-start.23 = (bf16[6,64,128]{2,1,0:T(8,128)(2,1)S(1)}, bf16[6,64,128]{2,1,0:T(8,128)(2,1)S(1)}, u32[]{:S(2)}, u32[]{:S(2)}) collective-permute-start(bf16[6,64,128]{2,1,0:T(8,128)(2,1)S(1)} %get-tuple-element.47), channel_id=1, source_target_pairs={{0,12},{4,0},{8,4},{12,8},{1,13},{5,1},{9,5},{13,9},{2,14},{6,2},{... | collective-permute-start | bytes 294920 | tf_op jit(solution)/shard_map/ppermute | solution.py:207
  (2 other events, 1.3 us)

commit v3 on v2

--- a/solution.py
+++ b/solution.py
@@ -74,19 +74,18 @@
 
 
 def fill_panel(panel, in_refs, axis):
-    count, stretch = len(in_refs), in_refs[0].shape[0]
+    stretch = in_refs[0].shape[0]
     me = lax.axis_index(axis)
-    for shift, in_ref in enumerate(in_refs):
-        source = lax.rem(me - shift + count, count)
+    for flip, in_ref in enumerate(in_refs):
+        source = lax.bitwise_xor(me, flip)
         for j in range(stretch):
             panel[source * stretch + j] = in_ref[j]
 
 
 def spread(out_refs, acc, axis, stretch):
-    count = len(out_refs)
     me = lax.axis_index(axis)
-    for shift, out_ref in enumerate(out_refs):
-        dest = lax.rem(me + shift, count)
+    for flip, out_ref in enumerate(out_refs):
+        dest = lax.bitwise_xor(me, flip)
         for j in range(stretch):
             out_ref[j] = acc[dest * stretch + j].astype(jnp.bfloat16)
 
@@ -202,17 +201,16 @@
         )
 
 
-def shifted(x, axis, shift):
-    count = lax.axis_size(axis)
-    return lax.ppermute(x, axis, [(i, (i + shift) % count) for i in range(count)])
+def swap(x, axis, flip):
+    return lax.ppermute(x, axis, [(i, i ^ flip) for i in range(lax.axis_size(axis))])
 
 
 def gather(x, axis):
-    return tuple([x] + [shifted(x, axis, s) for s in range(1, lax.axis_size(axis))])
+    return tuple([x] + [swap(x, axis, s) for s in range(1, lax.axis_size(axis))])
 
 
 def exchange(parts, axis):
-    return tuple([parts[0]] + [shifted(x, axis, s) for s, x in enumerate(parts) if s])
+    return tuple([parts[0]] + [swap(x, axis, s) for s, x in enumerate(parts) if s])
 
 
 def shards(right_side, prior, blocks, block_row, block_col):

time: 85.9 us -> 90.6 us (1.055)
  waiting for transfers between devices: 28.6 us -> 38.1 us
  starting transfers between devices: 30.7 us -> 25.8 us
    ppermute x24, waiting for transfers between devices: 28.6 us -> 38.1 us  [swap(): lax.ppermute(x, axis, [(i, i ^ flip) for i in range(lax.axis_size(axis))])]
    ppermute x24, starting transfers between devices: 30.7 us -> 25.8 us  [swap(): lax.ppermute(x, axis, [(i, i ^ flip) for i in range(lax.axis_size(axis))])]
  transfers between devices with their start and end apart: 24 -> 24, of which waited for: 18 -> 14; matrix products, arithmetic and copies ran while one was open for 0% -> 0% of each run, Pallas kernels for 6% -> 6%
where the time goes in v3:
time: 90.6 us; the launch traced here: 90.4 us
  waiting for transfers between devices  38.1 us (42%)
  starting transfers between devices  25.8 us (28%)
  Pallas kernels  21.3 us (24%)
  local copies, waits for them, and re-layouts  4.5 us (5%)
    ppermute x24, waiting for transfers between devices, swap(): lax.ppermute(x, axis, [(i, i ^ flip) for i in range(lax.axis_size(axis))])  38.1 us
    ppermute x24, starting transfers between devices, swap(): lax.ppermute(x, axis, [(i, i ^ flip) for i in range(lax.axis_size(axis))])  25.8 us
    pallas_call x10, Pallas kernels, call(): pl.pallas_call(body, out_shape=flat_outs, in_specs=[SMEM if x.dtype == jn...  21.3 us
    unnamed x20, local copies, waits for them, and re-layouts  4.5 us
  transfers between devices with their start and end apart: 24, of which 14 were waited for; matrix products, arithmetic and copies ran while one was open for 0% of the time, Pallas kernels for 6%

profile of v3, /device:TPU:0, one launch (start us, length us, event | category | flops | bytes accessed | tf_op | source)
XLA Modules:
  0.0 90.4 jit_solution(2279470343068330827)
XLA Ops:
  1.6 3.1 %collective-permute-start = (bf16[4,64,128]{2,1,0:T(8,128)(2,1)S(1)}, bf16[4,64,128]{2,1,0:T(8,128)(2,1)S(1)}, u32[]{:S(2)}, u32[]{:S(2)}) collective-permute-start(bf16[4,64,128]{2,1,0:T(8,128)(2,1)S(1)} %shard_map.68.refs_2_), channel_id=1, source_target_pairs={{0,4},{4,0},{8,12},{12,8},{1,5},{5,1},{9,13},{13,9},{2,6},{6,2},{1... | collective-permute-start | bytes 196616 | tf_op jit(solution)/shard_map/ppermute | solution.py:205
  4.6 2.6 %collective-permute-start.1 = (bf16[4,64,128]{2,1,0:T(8,128)(2,1)S(1)}, bf16[4,64,128]{2,1,0:T(8,128)(2,1)S(1)}, u32[]{:S(2)}, u32[]{:S(2)}) collective-permute-start(bf16[4,64,128]{2,1,0:T(8,128)(2,1)S(1)} %shard_map.68.refs_2_), channel_id=1, source_target_pairs={{0,8},{4,12},{8,0},{12,4},{1,9},{5,13},{9,1},{13,5},{2,10},{6,14},... | collective-permute-start | bytes 196616 | tf_op jit(solution)/shard_map/ppermute | solution.py:205
  7.2 4.7 %collective-permute-done.1.refs_4_ = bf16[4,64,128]{2,1,0:T(8,128)(2,1)S(1)} collective-permute-done((bf16[4,64,128]{2,1,0:T(8,128)(2,1)S(1)}, bf16[4,64,128]{2,1,0:T(8,128)(2,1)S(1)}, u32[]{:S(2)}, u32[]{:S(2)}) %collective-permute-start.1) | collective-permute-done | bytes 65568 | tf_op jit(solution)/shard_map/ppermute | solution.py:205
  11.9 1.4 %collective-permute-done.2.refs_5_ = bf16[4,64,128]{2,1,0:T(8,128)(2,1)S(1)} collective-permute-done((bf16[4,64,128]{2,1,0:T(8,128)(2,1)S(1)}, bf16[4,64,128]{2,1,0:T(8,128)(2,1)S(1)}, u32[]{:S(2)}, u32[]{:S(2)}) %collective-permute-start.2) | collective-permute-done | bytes 65568 | tf_op jit(solution)/shard_map/ppermute | solution.py:205
  13.3 1.6 %copy-done = bf16[64,128,128]{2,1,0:T(8,128)(2,1)S(1)} copy-done((bf16[64,128,128]{2,1,0:T(8,128)(2,1)S(1)}, bf16[64,128,128]{2,1,0:T(8,128)(2,1)}, u32[]{:S(2)}) %copy-start) | copy-done | bytes 2097176
  16.9 2.4 %shard_map.69 = (bf16[6,64,128]{2,1,0:T(8,128)(2,1)S(1)}, bf16[6,64,128]{2,1,0:T(8,128)(2,1)S(1)}, bf16[6,64,128]{2,1,0:T(8,128)(2,1)S(1)}, bf16[6,64,128]{2,1,0:T(8,128)(2,1)S(1)}) custom-call(s32[64]{0:T(128)S(1)} %copy-done.6, s32[64]{0:T(128)S(1)} %copy-done.8, bf16[4,64,128]{2,1,0:T(8,128)(2,1)S(1)} %shard_map.68.refs_2_, ...), custom_call_target="tpu_custom_call" | custom-call | tf_op jit(solution)/shard_map/pallas_call | solution.py:45
  19.4 1.6 %collective-permute-start.4 = (bf16[6,64,128]{2,1,0:T(8,128)(2,1)S(1)}, bf16[6,64,128]{2,1,0:T(8,128)(2,1)S(1)}, u32[]{:S(2)}, u32[]{:S(2)}) collective-permute-start(bf16[6,64,128]{2,1,0:T(8,128)(2,1)S(1)} %get-tuple-element.28), channel_id=1, source_target_pairs={{0,2},{1,3},{2,0},{3,1},{4,6},{5,7},{6,4},{7,5},{8,10},{9,11},{10,... | collective-permute-start | bytes 294920 | tf_op jit(solution)/shard_map/ppermute | solution.py:205
  21.2 3.8 %collective-permute-done.4.refs_2_ = bf16[6,64,128]{2,1,0:T(8,128)(2,1)S(1)} collective-permute-done((bf16[6,64,128]{2,1,0:T(8,128)(2,1)S(1)}, bf16[6,64,128]{2,1,0:T(8,128)(2,1)S(1)}, u32[]{:S(2)}, u32[]{:S(2)}) %collective-permute-start.4) | collective-permute-done | bytes 98336 | tf_op jit(solution)/shard_map/ppermute | solution.py:205
  25.0 1.2 %collective-permute-done.5.refs_3_ = bf16[6,64,128]{2,1,0:T(8,128)(2,1)S(1)} collective-permute-done((bf16[6,64,128]{2,1,0:T(8,128)(2,1)S(1)}, bf16[6,64,128]{2,1,0:T(8,128)(2,1)S(1)}, u32[]{:S(2)}, u32[]{:S(2)}) %collective-permute-start.5) | collective-permute-done | bytes 98336 | tf_op jit(solution)/shard_map/ppermute | solution.py:205
  26.6 1.5 %collective-permute-start.7 = (bf16[4,64,128]{2,1,0:T(8,128)(2,1)S(1)}, bf16[4,64,128]{2,1,0:T(8,128)(2,1)S(1)}, u32[]{:S(2)}, u32[]{:S(2)}) collective-permute-start(bf16[4,64,128]{2,1,0:T(8,128)(2,1)S(1)} %get-tuple-element.30.refs_2_), channel_id=1, source_target_pairs={{0,2},{1,3},{2,0},{3,1},{4,6},{5,7},{6,4},{7,5},{8,10},{9,11},{10,... | collective-permute-start | bytes 196616 | tf_op jit(solution)/shard_map/ppermute | solution.py:205
  28.2 2.7 %collective-permute-done.7.refs_4_ = bf16[4,64,128]{2,1,0:T(8,128)(2,1)S(1)} collective-permute-done((bf16[4,64,128]{2,1,0:T(8,128)(2,1)S(1)}, bf16[4,64,128]{2,1,0:T(8,128)(2,1)S(1)}, u32[]{:S(2)}, u32[]{:S(2)}) %collective-permute-start.7) | collective-permute-done | bytes 65568 | tf_op jit(solution)/shard_map/ppermute | solution.py:205
  30.9 1.5 %collective-permute-done.8.refs_5_ = bf16[4,64,128]{2,1,0:T(8,128)(2,1)S(1)} collective-permute-done((bf16[4,64,128]{2,1,0:T(8,128)(2,1)S(1)}, bf16[4,64,128]{2,1,0:T(8,128)(2,1)S(1)}, u32[]{:S(2)}, u32[]{:S(2)}) %collective-permute-start.8) | collective-permute-done | bytes 65568 | tf_op jit(solution)/shard_map/ppermute | solution.py:205
  32.4 1.5 %shard_map.71 = (bf16[6,64,128]{2,1,0:T(8,128)(2,1)S(1)}, bf16[6,64,128]{2,1,0:T(8,128)(2,1)S(1)}, bf16[6,64,128]{2,1,0:T(8,128)(2,1)S(1)}, bf16[6,64,128]{2,1,0:T(8,128)(2,1)S(1)}) custom-call(s32[64]{0:T(128)S(1)} %copy-done.7, s32[64]{0:T(128)S(1)} %copy-done.9, bf16[4,64,128]{2,1,0:T(8,128)(2,1)S(1)} %get-tuple-element.30.refs_2_, ...), custom_call_target="tpu_custom_call" | custom-call | tf_op jit(solution)/shard_map/pallas_call | solution.py:45
  33.8 1.6 %collective-permute-start.10 = (bf16[6,64,128]{2,1,0:T(8,128)(2,1)S(1)}, bf16[6,64,128]{2,1,0:T(8,128)(2,1)S(1)}, u32[]{:S(2)}, u32[]{:S(2)}) collective-permute-start(bf16[6,64,128]{2,1,0:T(8,128)(2,1)S(1)} %get-tuple-element.34), channel_id=1, source_target_pairs={{0,8},{4,12},{8,0},{12,4},{1,9},{5,13},{9,1},{13,5},{2,10},{6,14},... | collective-permute-start | bytes 294920 | tf_op jit(solution)/shard_map/ppermute | solution.py:205
  36.1 1.3 %collective-permute-start.9 = (bf16[6,64,128]{2,1,0:T(8,128)(2,1)S(1)}, bf16[6,64,128]{2,1,0:T(8,128)(2,1)S(1)}, u32[]{:S(2)}, u32[]{:S(2)}) collective-permute-start(bf16[6,64,128]{2,1,0:T(8,128)(2,1)S(1)} %get-tuple-element.33), channel_id=1, source_target_pairs={{0,4},{4,0},{8,12},{12,8},{1,5},{5,1},{9,13},{13,9},{2,6},{6,2},{1... | collective-permute-start | bytes 294920 | tf_op jit(solution)/shard_map/ppermute | solution.py:205
  37.4 5.9 %collective-permute-done.10.refs_2_ = bf16[6,64,128]{2,1,0:T(8,128)(2,1)S(1)} collective-permute-done((bf16[6,64,128]{2,1,0:T(8,128)(2,1)S(1)}, bf16[6,64,128]{2,1,0:T(8,128)(2,1)S(1)}, u32[]{:S(2)}, u32[]{:S(2)}) %collective-permute-start.10) | collective-permute-done | bytes 98336 | tf_op jit(solution)/shard_map/ppermute | solution.py:205
  43.3 1.3 %collective-permute-done.9.refs_1_ = bf16[6,64,128]{2,1,0:T(8,128)(2,1)S(1)} collective-permute-done((bf16[6,64,128]{2,1,0:T(8,128)(2,1)S(1)}, bf16[6,64,128]{2,1,0:T(8,128)(2,1)S(1)}, u32[]{:S(2)}, u32[]{:S(2)}) %collective-permute-start.9) | collective-permute-done | bytes 98336 | tf_op jit(solution)/shard_map/ppermute | solution.py:205
  44.7 1.4 %collective-permute-start.12 = (bf16[4,64,128]{2,1,0:T(8,128)(2,1)S(1)}, bf16[4,64,128]{2,1,0:T(8,128)(2,1)S(1)}, u32[]{:S(2)}, u32[]{:S(2)}) collective-permute-start(bf16[4,64,128]{2,1,0:T(8,128)(2,1)S(1)} %get-tuple-element.36.refs_2_), channel_id=1, source_target_pairs={{0,4},{4,0},{8,12},{12,8},{1,5},{5,1},{9,13},{13,9},{2,6},{6,2},{1... | collective-permute-start | bytes 196616 | tf_op jit(solution)/shard_map/ppermute | solution.py:205
  46.1 1.6 %collective-permute-start.13 = (bf16[4,64,128]{2,1,0:T(8,128)(2,1)S(1)}, bf16[4,64,128]{2,1,0:T(8,128)(2,1)S(1)}, u32[]{:S(2)}, u32[]{:S(2)}) collective-permute-start(bf16[4,64,128]{2,1,0:T(8,128)(2,1)S(1)} %get-tuple-element.36.refs_2_), channel_id=1, source_target_pairs={{0,8},{4,12},{8,0},{12,4},{1,9},{5,13},{9,1},{13,5},{2,10},{6,14},... | collective-permute-start | bytes 196616 | tf_op jit(solution)/shard_map/ppermute | solution.py:205
  47.7 1.4 %collective-permute-start.14 = (bf16[4,64,128]{2,1,0:T(8,128)(2,1)S(1)}, bf16[4,64,128]{2,1,0:T(8,128)(2,1)S(1)}, u32[]{:S(2)}, u32[]{:S(2)}) collective-permute-start(bf16[4,64,128]{2,1,0:T(8,128)(2,1)S(1)} %get-tuple-element.36.refs_2_), channel_id=1, source_target_pairs={{0,12},{4,8},{8,4},{12,0},{1,13},{5,9},{9,5},{13,1},{2,14},{6,10},... | collective-permute-start | bytes 196616 | tf_op jit(solution)/shard_map/ppermute | solution.py:205
  49.2 4.9 %collective-permute-done.13.refs_4_ = bf16[4,64,128]{2,1,0:T(8,128)(2,1)S(1)} collective-permute-done((bf16[4,64,128]{2,1,0:T(8,128)(2,1)S(1)}, bf16[4,64,128]{2,1,0:T(8,128)(2,1)S(1)}, u32[]{:S(2)}, u32[]{:S(2)}) %collective-permute-start.13) | collective-permute-done | bytes 65568 | tf_op jit(solution)/shard_map/ppermute | solution.py:205
  54.1 2.4 %shard_map.73 = (bf16[6,64,128]{2,1,0:T(8,128)(2,1)S(1)}, bf16[6,64,128]{2,1,0:T(8,128)(2,1)S(1)}, bf16[6,64,128]{2,1,0:T(8,128)(2,1)S(1)}, bf16[6,64,128]{2,1,0:T(8,128)(2,1)S(1)}) custom-call(s32[64]{0:T(128)S(1)} %copy-done.7, s32[64]{0:T(128)S(1)} %copy-done.9, bf16[4,64,128]{2,1,0:T(8,128)(2,1)S(1)} %get-tuple-element.36.refs_2_, ...), custom_call_target="tpu_custom_call" | custom-call | tf_op jit(solution)/shard_map/pallas_call | solution.py:45
  58.4 3.8 %collective-permute-done.16.refs_2_ = bf16[6,64,128]{2,1,0:T(8,128)(2,1)S(1)} collective-permute-done((bf16[6,64,128]{2,1,0:T(8,128)(2,1)S(1)}, bf16[6,64,128]{2,1,0:T(8,128)(2,1)S(1)}, u32[]{:S(2)}, u32[]{:S(2)}) %collective-permute-start.16) | collective-permute-done | bytes 98336 | tf_op jit(solution)/shard_map/ppermute | solution.py:205
  62.2 1.2 %collective-permute-done.17.refs_3_ = bf16[6,64,128]{2,1,0:T(8,128)(2,1)S(1)} collective-permute-done((bf16[6,64,128]{2,1,0:T(8,128)(2,1)S(1)}, bf16[6,64,128]{2,1,0:T(8,128)(2,1)S(1)}, u32[]{:S(2)}, u32[]{:S(2)}) %collective-permute-start.17) | collective-permute-done | bytes 98336 | tf_op jit(solution)/shard_map/ppermute | solution.py:205
  65.4 2.9 %collective-permute-done.19.refs_4_ = bf16[4,64,128]{2,1,0:T(8,128)(2,1)S(1)} collective-permute-done((bf16[4,64,128]{2,1,0:T(8,128)(2,1)S(1)}, bf16[4,64,128]{2,1,0:T(8,128)(2,1)S(1)}, u32[]{:S(2)}, u32[]{:S(2)}) %collective-permute-start.19) | collective-permute-done | bytes 65568 | tf_op jit(solution)/shard_map/ppermute | solution.py:205
  69.2 1.4 %shard_map.75 = (bf16[6,64,128]{2,1,0:T(8,128)(2,1)S(1)}, bf16[6,64,128]{2,1,0:T(8,128)(2,1)S(1)}, bf16[6,64,128]{2,1,0:T(8,128)(2,1)S(1)}, bf16[6,64,128]{2,1,0:T(8,128)(2,1)S(1)}) custom-call(s32[64]{0:T(128)S(1)} %copy-done.7, s32[64]{0:T(128)S(1)} %copy-done.9, bf16[4,64,128]{2,1,0:T(8,128)(2,1)S(1)} %get-tuple-element.42.refs_2_, ...), custom_call_target="tpu_custom_call" | custom-call | tf_op jit(solution)/shard_map/pallas_call | solution.py:45
  70.7 1.5 %collective-permute-start.21 = (bf16[6,64,128]{2,1,0:T(8,128)(2,1)S(1)}, bf16[6,64,128]{2,1,0:T(8,128)(2,1)S(1)}, u32[]{:S(2)}, u32[]{:S(2)}) collective-permute-start(bf16[6,64,128]{2,1,0:T(8,128)(2,1)S(1)} %get-tuple-element.45), channel_id=1, source_target_pairs={{0,4},{4,0},{8,12},{12,8},{1,5},{5,1},{9,13},{13,9},{2,6},{6,2},{1... | collective-permute-start | bytes 294920 | tf_op jit(solution)/shard_map/ppermute | solution.py:205
  72.1 1.3 %collective-permute-start.22 = (bf16[6,64,128]{2,1,0:T(8,128)(2,1)S(1)}, bf16[6,64,128]{2,1,0:T(8,128)(2,1)S(1)}, u32[]{:S(2)}, u32[]{:S(2)}) collective-permute-start(bf16[6,64,128]{2,1,0:T(8,128)(2,1)S(1)} %get-tuple-element.46), channel_id=1, source_target_pairs={{0,8},{4,12},{8,0},{12,4},{1,9},{5,13},{9,1},{13,5},{2,10},{6,14},... | collective-permute-start | bytes 294920 | tf_op jit(solution)/shard_map/ppermute | solution.py:205
  73.4 1.7 %collective-permute-start.23 = (bf16[6,64,128]{2,1,0:T(8,128)(2,1)S(1)}, bf16[6,64,128]{2,1,0:T(8,128)(2,1)S(1)}, u32[]{:S(2)}, u32[]{:S(2)}) collective-permute-start(bf16[6,64,128]{2,1,0:T(8,128)(2,1)S(1)} %get-tuple-element.47), channel_id=1, source_target_pairs={{0,12},{4,8},{8,4},{12,0},{1,13},{5,9},{9,5},{13,1},{2,14},{6,10},... | collective-permute-start | bytes 294920 | tf_op jit(solution)/shard_map/ppermute | solution.py:205
  75.1 5.6 %shard_map.76.refs_9_ = f32[64,64]{1,0:T(8,128)S(1)} custom-call(f32[64,128]{1,0:T(8,128)S(1)} %get-tuple-element.49.refs_0_.refs_8_), custom_call_target="tpu_custom_call" | custom-call | tf_op jit(solution)/shard_map/pallas_call | solution.py:45
  80.7 2.0 %collective-permute-done.22.refs_2_ = bf16[6,64,128]{2,1,0:T(8,128)(2,1)S(1)} collective-permute-done((bf16[6,64,128]{2,1,0:T(8,128)(2,1)S(1)}, bf16[6,64,128]{2,1,0:T(8,128)(2,1)S(1)}, u32[]{:S(2)}, u32[]{:S(2)}) %collective-permute-start.22) | collective-permute-done | bytes 98336 | tf_op jit(solution)/shard_map/ppermute | solution.py:205
  82.7 7.8 %shard_map.77 = (f32[64,512]{1,0:T(8,128)}, f32[64,512]{1,0:T(8,128)}) custom-call(bf16[6,64,128]{2,1,0:T(8,128)(2,1)S(1)} %get-tuple-element.44.refs_0_, bf16[6,64,128]{2,1,0:T(8,128)(2,1)S(1)} %collective-permute-done.21.refs_1_, bf16[6,64,128]{2,1,0:T(8,128)(2,1)S(1)} %collective-permute-done.22.refs_2_, ...), custom_call_target="tpu_custom_call" | custom-call | tf_op jit(solution)/shard_map/pallas_call | solution.py:45
  (46 shorter events, 9.5 us)
Async XLA Ops:
  0.6 0.9 %copy-start.2 = (f32[64,512]{1,0:T(8,128)S(1)}, f32[64,512]{1,0:T(8,128)}, u32[]{:S(2)}) copy-start(f32[64,512]{1,0:T(8,128)} %refs_4_.3) | copy-start | bytes 393220
  1.5 30.8 %copy-start.7 = (s32[64]{0:T(128)S(1)}, s32[64]{0:T(128)}, u32[]{:S(2)}) copy-start(s32[64]{0:T(128)} %refs_0_.9) | copy-start | bytes 772
  1.5 30.8 %copy-start.9 = (s32[64]{0:T(128)S(1)}, s32[64]{0:T(128)}, u32[]{:S(2)}) copy-start(s32[64]{0:T(128)} %refs_1_.7) | copy-start | bytes 772
  1.6 5.7 %collective-permute-start = (bf16[4,64,128]{2,1,0:T(8,128)(2,1)S(1)}, bf16[4,64,128]{2,1,0:T(8,128)(2,1)S(1)}, u32[]{:S(2)}, u32[]{:S(2)}) collective-permute-start(bf16[4,64,128]{2,1,0:T(8,128)(2,1)S(1)} %shard_map.68.refs_2_), channel_id=1, source_target_pairs={{0,4},{4,0},{8,12},{12,8},{1,5},{5,1},{9,13},{13,9},{2,6},{6,2},{1... | collective-permute-start | bytes 196616 | tf_op jit(solution)/shard_map/ppermute | solution.py:205
  4.6 7.3 %collective-permute-start.1 = (bf16[4,64,128]{2,1,0:T(8,128)(2,1)S(1)}, bf16[4,64,128]{2,1,0:T(8,128)(2,1)S(1)}, u32[]{:S(2)}, u32[]{:S(2)}) collective-permute-start(bf16[4,64,128]{2,1,0:T(8,128)(2,1)S(1)} %shard_map.68.refs_2_), channel_id=1, source_target_pairs={{0,8},{4,12},{8,0},{12,4},{1,9},{5,13},{9,1},{13,5},{2,10},{6,14},... | collective-permute-start | bytes 196616 | tf_op jit(solution)/shard_map/ppermute | solution.py:205
  7.2 6.1 %collective-permute-start.2 = (bf16[4,64,128]{2,1,0:T(8,128)(2,1)S(1)}, bf16[4,64,128]{2,1,0:T(8,128)(2,1)S(1)}, u32[]{:S(2)}, u32[]{:S(2)}) collective-permute-start(bf16[4,64,128]{2,1,0:T(8,128)(2,1)S(1)} %shard_map.68.refs_2_), channel_id=1, source_target_pairs={{0,12},{4,8},{8,4},{12,0},{1,13},{5,9},{9,5},{13,1},{2,14},{6,10},... | collective-permute-start | bytes 196616 | tf_op jit(solution)/shard_map/ppermute | solution.py:205
  13.3 1.6 %copy-start = (bf16[64,128,128]{2,1,0:T(8,128)(2,1)S(1)}, bf16[64,128,128]{2,1,0:T(8,128)(2,1)}, u32[]{:S(2)}) copy-start(bf16[64,128,128]{2,1,0:T(8,128)(2,1)} %refs_6_.7) | copy-start | bytes 6291460
  14.9 0.7 copy-start.4
  16.9 15.5 %copy-start.1 = (bf16[64,128,128]{2,1,0:T(8,128)(2,1)S(1)}, bf16[64,128,128]{2,1,0:T(8,128)(2,1)}, u32[]{:S(2)}) copy-start(bf16[64,128,128]{2,1,0:T(8,128)(2,1)} %refs_6_.7) | copy-start | bytes 6291460
  16.9 27.6 %copy-start.3 = (f32[64,512]{1,0:T(8,128)S(1)}, f32[64,512]{1,0:T(8,128)}, u32[]{:S(2)}) copy-start(f32[64,512]{1,0:T(8,128)} %refs_4_.3) | copy-start | bytes 393220
  16.9 27.6 %copy-start.5 = (f32[512]{0:T(512)S(1)}, f32[512]{0:T(512)}, u32[]{:S(2)}) copy-start(f32[512]{0:T(512)} %param.6) | copy-start | bytes 6148
  19.3 1.9 %collective-permute-start.3 = (bf16[6,64,128]{2,1,0:T(8,128)(2,1)S(1)}, bf16[6,64,128]{2,1,0:T(8,128)(2,1)S(1)}, u32[]{:S(2)}, u32[]{:S(2)}) collective-permute-start(bf16[6,64,128]{2,1,0:T(8,128)(2,1)S(1)} %get-tuple-element.27), channel_id=1, source_target_pairs={{0,1},{1,0},{2,3},{3,2},{4,5},{5,4},{6,7},{7,6},{8,9},{9,8},{10,11... | collective-permute-start | bytes 294920 | tf_op jit(solution)/shard_map/ppermute | solution.py:205
  19.4 5.7 %collective-permute-start.4 = (bf16[6,64,128]{2,1,0:T(8,128)(2,1)S(1)}, bf16[6,64,128]{2,1,0:T(8,128)(2,1)S(1)}, u32[]{:S(2)}, u32[]{:S(2)}) collective-permute-start(bf16[6,64,128]{2,1,0:T(8,128)(2,1)S(1)} %get-tuple-element.28), channel_id=1, source_target_pairs={{0,2},{1,3},{2,0},{3,1},{4,6},{5,7},{6,4},{7,5},{8,10},{9,11},{10,... | collective-permute-start | bytes 294920 | tf_op jit(solution)/shard_map/ppermute | solution.py:205
  20.9 5.3 %collective-permute-start.5 = (bf16[6,64,128]{2,1,0:T(8,128)(2,1)S(1)}, bf16[6,64,128]{2,1,0:T(8,128)(2,1)S(1)}, u32[]{:S(2)}, u32[]{:S(2)}) collective-permute-start(bf16[6,64,128]{2,1,0:T(8,128)(2,1)S(1)} %get-tuple-element.29), channel_id=1, source_target_pairs={{0,3},{1,2},{2,1},{3,0},{4,7},{5,6},{6,5},{7,4},{8,11},{9,10},{10,... | collective-permute-start | bytes 294920 | tf_op jit(solution)/shard_map/ppermute | solution.py:205
  26.3 1.9 %collective-permute-start.6 = (bf16[4,64,128]{2,1,0:T(8,128)(2,1)S(1)}, bf16[4,64,128]{2,1,0:T(8,128)(2,1)S(1)}, u32[]{:S(2)}, u32[]{:S(2)}) collective-permute-start(bf16[4,64,128]{2,1,0:T(8,128)(2,1)S(1)} %get-tuple-element.30.refs_2_), channel_id=1, source_target_pairs={{0,1},{1,0},{2,3},{3,2},{4,5},{5,4},{6,7},{7,6},{8,9},{9,8},{10,11... | collective-permute-start | bytes 196616 | tf_op jit(solution)/shard_map/ppermute | solution.py:205
  26.6 4.3 %collective-permute-start.7 = (bf16[4,64,128]{2,1,0:T(8,128)(2,1)S(1)}, bf16[4,64,128]{2,1,0:T(8,128)(2,1)S(1)}, u32[]{:S(2)}, u32[]{:S(2)}) collective-permute-start(bf16[4,64,128]{2,1,0:T(8,128)(2,1)S(1)} %get-tuple-element.30.refs_2_), channel_id=1, source_target_pairs={{0,2},{1,3},{2,0},{3,1},{4,6},{5,7},{6,4},{7,5},{8,10},{9,11},{10,... | collective-permute-start | bytes 196616 | tf_op jit(solution)/shard_map/ppermute | solution.py:205
  28.1 4.3 %collective-permute-start.8 = (bf16[4,64,128]{2,1,0:T(8,128)(2,1)S(1)}, bf16[4,64,128]{2,1,0:T(8,128)(2,1)S(1)}, u32[]{:S(2)}, u32[]{:S(2)}) collective-permute-start(bf16[4,64,128]{2,1,0:T(8,128)(2,1)S(1)} %get-tuple-element.30.refs_2_), channel_id=1, source_target_pairs={{0,3},{1,2},{2,1},{3,0},{4,7},{5,6},{6,5},{7,4},{8,11},{9,10},{10,... | collective-permute-start | bytes 196616 | tf_op jit(solution)/shard_map/ppermute | solution.py:205
  33.8 9.4 %collective-permute-start.10 = (bf16[6,64,128]{2,1,0:T(8,128)(2,1)S(1)}, bf16[6,64,128]{2,1,0:T(8,128)(2,1)S(1)}, u32[]{:S(2)}, u32[]{:S(2)}) collective-permute-start(bf16[6,64,128]{2,1,0:T(8,128)(2,1)S(1)} %get-tuple-element.34), channel_id=1, source_target_pairs={{0,8},{4,12},{8,0},{12,4},{1,9},{5,13},{9,1},{13,5},{2,10},{6,14},... | collective-permute-start | bytes 294920 | tf_op jit(solution)/shard_map/ppermute | solution.py:205
  35.5 7.8 %collective-permute-start.11 = (bf16[6,64,128]{2,1,0:T(8,128)(2,1)S(1)}, bf16[6,64,128]{2,1,0:T(8,128)(2,1)S(1)}, u32[]{:S(2)}, u32[]{:S(2)}) collective-permute-start(bf16[6,64,128]{2,1,0:T(8,128)(2,1)S(1)} %get-tuple-element.35), channel_id=1, source_target_pairs={{0,12},{4,8},{8,4},{12,0},{1,13},{5,9},{9,5},{13,1},{2,14},{6,10},... | collective-permute-start | bytes 294920 | tf_op jit(solution)/shard_map/ppermute | solution.py:205
  36.1 8.4 %collective-permute-start.9 = (bf16[6,64,128]{2,1,0:T(8,128)(2,1)S(1)}, bf16[6,64,128]{2,1,0:T(8,128)(2,1)S(1)}, u32[]{:S(2)}, u32[]{:S(2)}) collective-permute-start(bf16[6,64,128]{2,1,0:T(8,128)(2,1)S(1)} %get-tuple-element.33), channel_id=1, source_target_pairs={{0,4},{4,0},{8,12},{12,8},{1,5},{5,1},{9,13},{13,9},{2,6},{6,2},{1... | collective-permute-start | bytes 294920 | tf_op jit(solution)/shard_map/ppermute | solution.py:205
  44.7 4.5 %collective-permute-start.12 = (bf16[4,64,128]{2,1,0:T(8,128)(2,1)S(1)}, bf16[4,64,128]{2,1,0:T(8,128)(2,1)S(1)}, u32[]{:S(2)}, u32[]{:S(2)}) collective-permute-start(bf16[4,64,128]{2,1,0:T(8,128)(2,1)S(1)} %get-tuple-element.36.refs_2_), channel_id=1, source_target_pairs={{0,4},{4,0},{8,12},{12,8},{1,5},{5,1},{9,13},{13,9},{2,6},{6,2},{1... | collective-permute-start | bytes 196616 | tf_op jit(solution)/shard_map/ppermute | solution.py:205
  46.1 8.0 %collective-permute-start.13 = (bf16[4,64,128]{2,1,0:T(8,128)(2,1)S(1)}, bf16[4,64,128]{2,1,0:T(8,128)(2,1)S(1)}, u32[]{:S(2)}, u32[]{:S(2)}) collective-permute-start(bf16[4,64,128]{2,1,0:T(8,128)(2,1)S(1)} %get-tuple-element.36.refs_2_), channel_id=1, source_target_pairs={{0,8},{4,12},{8,0},{12,4},{1,9},{5,13},{9,1},{13,5},{2,10},{6,14},... | collective-permute-start | bytes 196616 | tf_op jit(solution)/shard_map/ppermute | solution.py:205
  47.7 6.4 %collective-permute-start.14 = (bf16[4,64,128]{2,1,0:T(8,128)(2,1)S(1)}, bf16[4,64,128]{2,1,0:T(8,128)(2,1)S(1)}, u32[]{:S(2)}, u32[]{:S(2)}) collective-permute-start(bf16[4,64,128]{2,1,0:T(8,128)(2,1)S(1)} %get-tuple-element.36.refs_2_), channel_id=1, source_target_pairs={{0,12},{4,8},{8,4},{12,0},{1,13},{5,9},{9,5},{13,1},{2,14},{6,10},... | collective-permute-start | bytes 196616 | tf_op jit(solution)/shard_map/ppermute | solution.py:205
  56.5 1.9 %collective-permute-start.15 = (bf16[6,64,128]{2,1,0:T(8,128)(2,1)S(1)}, bf16[6,64,128]{2,1,0:T(8,128)(2,1)S(1)}, u32[]{:S(2)}, u32[]{:S(2)}) collective-permute-start(bf16[6,64,128]{2,1,0:T(8,128)(2,1)S(1)} %get-tuple-element.39), channel_id=1, source_target_pairs={{0,1},{1,0},{2,3},{3,2},{4,5},{5,4},{6,7},{7,6},{8,9},{9,8},{10,11... | collective-permute-start | bytes 294920 | tf_op jit(solution)/shard_map/ppermute | solution.py:205
  56.5 5.7 %collective-permute-start.16 = (bf16[6,64,128]{2,1,0:T(8,128)(2,1)S(1)}, bf16[6,64,128]{2,1,0:T(8,128)(2,1)S(1)}, u32[]{:S(2)}, u32[]{:S(2)}) collective-permute-start(bf16[6,64,128]{2,1,0:T(8,128)(2,1)S(1)} %get-tuple-element.40), channel_id=1, source_target_pairs={{0,2},{1,3},{2,0},{3,1},{4,6},{5,7},{6,4},{7,5},{8,10},{9,11},{10,... | collective-permute-start | bytes 294920 | tf_op jit(solution)/shard_map/ppermute | solution.py:205
  57.7 5.7 %collective-permute-start.17 = (bf16[6,64,128]{2,1,0:T(8,128)(2,1)S(1)}, bf16[6,64,128]{2,1,0:T(8,128)(2,1)S(1)}, u32[]{:S(2)}, u32[]{:S(2)}) collective-permute-start(bf16[6,64,128]{2,1,0:T(8,128)(2,1)S(1)} %get-tuple-element.41), channel_id=1, source_target_pairs={{0,3},{1,2},{2,1},{3,0},{4,7},{5,6},{6,5},{7,4},{8,11},{9,10},{10,... | collective-permute-start | bytes 294920 | tf_op jit(solution)/shard_map/ppermute | solution.py:205
  63.5 1.9 %collective-permute-start.18 = (bf16[4,64,128]{2,1,0:T(8,128)(2,1)S(1)}, bf16[4,64,128]{2,1,0:T(8,128)(2,1)S(1)}, u32[]{:S(2)}, u32[]{:S(2)}) collective-permute-start(bf16[4,64,128]{2,1,0:T(8,128)(2,1)S(1)} %get-tuple-element.42.refs_2_), channel_id=1, source_target_pairs={{0,1},{1,0},{2,3},{3,2},{4,5},{5,4},{6,7},{7,6},{8,9},{9,8},{10,11... | collective-permute-start | bytes 196616 | tf_op jit(solution)/shard_map/ppermute | solution.py:205
  63.8 4.5 %collective-permute-start.19 = (bf16[4,64,128]{2,1,0:T(8,128)(2,1)S(1)}, bf16[4,64,128]{2,1,0:T(8,128)(2,1)S(1)}, u32[]{:S(2)}, u32[]{:S(2)}) collective-permute-start(bf16[4,64,128]{2,1,0:T(8,128)(2,1)S(1)} %get-tuple-element.42.refs_2_), channel_id=1, source_target_pairs={{0,2},{1,3},{2,0},{3,1},{4,6},{5,7},{6,4},{7,5},{8,10},{9,11},{10,... | collective-permute-start | bytes 196616 | tf_op jit(solution)/shard_map/ppermute | solution.py:205
  64.9 4.3 %collective-permute-start.20 = (bf16[4,64,128]{2,1,0:T(8,128)(2,1)S(1)}, bf16[4,64,128]{2,1,0:T(8,128)(2,1)S(1)}, u32[]{:S(2)}, u32[]{:S(2)}) collective-permute-start(bf16[4,64,128]{2,1,0:T(8,128)(2,1)S(1)} %get-tuple-element.42.refs_2_), channel_id=1, source_target_pairs={{0,3},{1,2},{2,1},{3,0},{4,7},{5,6},{6,5},{7,4},{8,11},{9,10},{10,... | collective-permute-start | bytes 196616 | tf_op jit(solution)/shard_map/ppermute | solution.py:205
  70.7 10.0 %collective-permute-start.21 = (bf16[6,64,128]{2,1,0:T(8,128)(2,1)S(1)}, bf16[6,64,128]{2,1,0:T(8,128)(2,1)S(1)}, u32[]{:S(2)}, u32[]{:S(2)}) collective-permute-start(bf16[6,64,128]{2,1,0:T(8,128)(2,1)S(1)} %get-tuple-element.45), channel_id=1, source_target_pairs={{0,4},{4,0},{8,12},{12,8},{1,5},{5,1},{9,13},{13,9},{2,6},{6,2},{1... | collective-permute-start | bytes 294920 | tf_op jit(solution)/shard_map/ppermute | solution.py:205
  72.1 10.5 %collective-permute-start.22 = (bf16[6,64,128]{2,1,0:T(8,128)(2,1)S(1)}, bf16[6,64,128]{2,1,0:T(8,128)(2,1)S(1)}, u32[]{:S(2)}, u32[]{:S(2)}) collective-permute-start(bf16[6,64,128]{2,1,0:T(8,128)(2,1)S(1)} %get-tuple-element.46), channel_id=1, source_target_pairs={{0,8},{4,12},{8,0},{12,4},{1,9},{5,13},{9,1},{13,5},{2,10},{6,14},... | collective-permute-start | bytes 294920 | tf_op jit(solution)/shard_map/ppermute | solution.py:205
  73.4 9.3 %collective-permute-start.23 = (bf16[6,64,128]{2,1,0:T(8,128)(2,1)S(1)}, bf16[6,64,128]{2,1,0:T(8,128)(2,1)S(1)}, u32[]{:S(2)}, u32[]{:S(2)}) collective-permute-start(bf16[6,64,128]{2,1,0:T(8,128)(2,1)S(1)} %get-tuple-element.47), channel_id=1, source_target_pairs={{0,12},{4,8},{8,4},{12,0},{1,13},{5,9},{9,5},{13,1},{2,14},{6,10},... | collective-permute-start | bytes 294920 | tf_op jit(solution)/shard_map/ppermute | solution.py:205
  (2 other events, 1.3 us)

commit v4 on v0

v4 whole, which is shorter than its diff:
```python
import jax
import jax.numpy as jnp
from jax import lax
from jax.experimental import pallas as pl
from jax.experimental.pallas import tpu as pltpu
from jax.sharding import PartitionSpec as P

BLOCK = 128
TILE = 8
PANEL = 4
DIAG = 16
F32, BF16 = jnp.float32, jnp.bfloat16
FP32 = lax.Precision.HIGHEST
VMEM = pl.BlockSpec(memory_space=pltpu.VMEM)
SMEM = pl.BlockSpec(memory_space=pltpu.SMEM)
ANY = pl.BlockSpec(memory_space=pl.ANY)


def nt_dot(a, b, precision=None):
    return lax.dot_general(
        a, b, (((1,), (1,)), ((), ())), precision=precision, preferred_element_type=F32
    )


def tn_dot(a, b):
    return lax.dot_general(
        a, b, (((0,), (0,)), ((), ())), precision=FP32, preferred_element_type=F32
    )


def nn_dot(a, b):
    return lax.dot_general(
        a, b, (((1,), (0,)), ((), ())), precision=FP32, preferred_element_type=F32
    )


def call(kernel, outs, ins, scratch=(), specs=None, cost=None):
    flat_ins, ins_tree = jax.tree.flatten(tuple(ins))
    flat_outs, outs_tree = jax.tree.flatten(tuple(outs))

    def body(*refs):
        middle, last = len(flat_ins), len(flat_ins) + len(flat_outs)
        kernel(
            *jax.tree.unflatten(ins_tree, refs[:middle]),
            *jax.tree.unflatten(outs_tree, refs[middle:last]),
            *refs[last:],
        )

    def space(x):
        return SMEM if x.dtype == jnp.int32 else VMEM

    results = pl.pallas_call(
        body,
        out_shape=flat_outs,
        in_specs=specs or [space(x) for x in flat_ins],
        out_specs=[space(x) for x in flat_outs],
        scratch_shapes=list(scratch),
        compiler_params=pltpu.CompilerParams(vmem_limit_bytes=48 * 1024 * 1024),
        cost_estimate=cost,
    )(*flat_ins)
    return jax.tree.unflatten(outs_tree, results)


def lanes(j):
    return slice(j * BLOCK, (j + 1) * BLOCK)


def rows(j, count):
    return slice(j * count, (j + 1) * count)


def split(value):
    high = value.astype(BF16)
    return high, (value - high.astype(F32)).astype(BF16)


def sum_rows(refs, at):
    total = refs[0][at, :].astype(F32)
    for ref in refs[1:]:
        total += ref[at, :].astype(F32)
    return total


def eye(n):
    return lax.broadcasted_iota(jnp.int32, (n, n), 0) == lax.broadcasted_iota(jnp.int32, (n, n), 1)


def cast_kernel(v_ref, out_ref):
    frames = v_ref.shape[0]
    for j in range(v_ref.shape[1] // BLOCK):
        out_ref[rows(j, frames), :] = v_ref[:, lanes(j)].astype(BF16)


def stage_kernel(row_span, stretch, brow, bcol, blocks, index_ref, out_ref, sem):
    copy = pltpu.make_async_copy(blocks, out_ref, sem)
    copy.start()
    for k in range(brow.shape[0]):
        index_ref[0, k] = lax.rem(brow[k], row_span)
        index_ref[1, k] = lax.div(bcol[k], row_span) * stretch + lax.rem(bcol[k], stretch)
    copy.wait()


def gram_kernel(v_ref, prior, out_ref):
    value = v_ref[...]
    out_ref[...] = nt_dot(value, jnp.concatenate([value, value * prior[...]], axis=0), FP32)


def fill(panel, ref, at, stretch):
    frames = panel.shape[1]
    for j in range(stretch):
        panel[at * stretch + j] = ref[rows(j, frames), :]


def whole_of(panel):
    return jnp.concatenate([panel[b] for b in range(panel.shape[0])], axis=1)


def forward_kernel(stretch, cols, index, search, blocks, gram, half, keep_ref, send_ref, acc, panel):
    frames = panel.shape[1]
    me = lax.axis_index("row")
    for shift, ref in enumerate(search):
        fill(panel, ref, lax.rem(me - shift + len(search), len(search)), stretch)
    acc[...] = jnp.zeros_like(acc)
    for k in range(blocks.shape[0]):
        acc[index[0, k]] += nt_dot(panel[index[1, k]], blocks[k])
    core = lax.rem(lax.axis_index("col"), 2)
    for x in range(cols // 2):
        for j in range(stretch):
            at = rows(x * stretch + j, frames)
            keep_ref[at, :] = acc[(2 * x + core) * stretch + j]
            send_ref[at, :] = acc[(2 * x + 1 - core) * stretch + j]
    at = rows(cols // 2 * stretch, frames)
    value = gram[...]
    if half:
        whole = whole_of(panel)
        inner = nt_dot(whole, jnp.concatenate([whole, jnp.zeros_like(whole)], axis=0))
        lane = lax.broadcasted_iota(jnp.int32, value.shape, 1)
        value = jnp.where(lane < frames, inner, value)
        send_ref[at.stop :, :] = half[0][...]
        keep_ref[at.stop :, :] = half[0][...]
    keep_ref[at, :] = value
    send_ref[at, :] = value


def pair_kernel(frames, keep, received, out_ref, first_refs):
    core = lax.rem(lax.axis_index("col"), 2)
    split_at = frames // 2
    data = out_ref.shape[0] - frames
    for j in range(data // frames):
        at = rows(j, frames)
        out_ref[at, :] = (keep[at, :] + received[at, :]).astype(BF16)
    at = pl.ds(pl.multiple_of(data + core * split_at, split_at), split_at)
    out_ref[data : data + split_at, :], out_ref[data + split_at :, :] = split(
        keep[at, :] + received[at, :]
    )
    if first_refs:
        at = pl.ds(pl.multiple_of(core * split_at, split_at), split_at)
        first_refs[0][at, :] = keep[data + frames :, :]
        at = pl.ds(pl.multiple_of((1 - core) * split_at, split_at), split_at)
        first_refs[0][at, :] = received[data + frames :, :]


def chips_kernel(frames, parts, out_ref):
    split_at = frames // 2
    data = out_ref.shape[0] - frames
    for j in range(data // frames):
        at = rows(j, frames)
        out_ref[at, :] = sum_rows(parts, at).astype(BF16)
    high, low = slice(data, data + split_at), slice(data + split_at, data + frames)
    out_ref[high, :], out_ref[low, :] = split(sum_rows(parts, high) + sum_rows(parts, low))


def backward_kernel(
    stretch, cols, last, index, own, received, blocks, out_refs, norm_refs, acc, panel, gram
):
    frames = panel.shape[1]
    split_at = frames // 2
    core = lax.rem(lax.axis_index("col"), 2)
    data = cols // 2 * stretch * frames
    for ref, side in ((own, core), (received, 1 - core)):
        for x in range(cols // 2):
            for j in range(stretch):
                panel[(2 * x + side) * stretch + j] = ref[rows(x * stretch + j, frames), :]
        at = pl.ds(pl.multiple_of(side * split_at, split_at), split_at)
        gram[at, :] = ref[data : data + split_at, :].astype(F32) + ref[data + split_at :, :].astype(
            F32
        )
    acc[...] = jnp.zeros_like(acc)
    for k in range(blocks.shape[0]):
        acc[index[1, k]] += jnp.dot(panel[index[0, k]], blocks[k], preferred_element_type=F32)
    me = lax.axis_index("row")
    for shift, out_ref in enumerate(out_refs):
        dest = lax.rem(me + shift, len(out_refs))
        for j in range(stretch):
            out_ref[rows(j, frames), :] = acc[dest * stretch + j].astype(BF16)
    whole = whole_of(panel)
    total = gram[...] + nt_dot(whole, jnp.concatenate([jnp.zeros_like(whole), whole], axis=0))
    at = stretch * frames
    if last:
        high, low = split(total[:, frames:])
        block = jnp.concatenate([high, low], axis=1)
        for out_ref in out_refs:
            out_ref[at:, :] = block
        norm_refs[0][...] = total[:, :frames]
    else:
        gram[...] = total
        high, low = split(gram[pl.ds(pl.multiple_of(core * split_at, split_at), split_at), :])
        lane = lax.broadcasted_iota(jnp.int32, total.shape, 1)
        row = lax.broadcasted_iota(jnp.int32, total.shape, 0)
        on_diagonal = jnp.logical_or(lane == row, lane == row + frames)
        diagonal = jnp.sum(jnp.where(on_diagonal, total, 0.0), axis=0, keepdims=True)
        row = lax.broadcasted_iota(jnp.int32, (DIAG, 2 * frames), 0)
        tile = jnp.where(row == 0, diagonal, 0.0).astype(BF16)
        for out_ref in out_refs:
            out_ref[at : at + split_at, :] = high
            out_ref[at + split_at : at + frames, :] = low
            out_ref[at + frames :, :] = tile


def frame_shift(diagonal, frames):
    row = 1.25 * diagonal[:, frames:] / diagonal[:, :frames]
    return jnp.sum(jnp.where(eye(frames), row, 0.0), axis=1, keepdims=True), row


def image_kernel(parts, v_ref, prior, image_ref, next_ref, cast_ref, half_ref, diag_ref):
    frames = v_ref.shape[0]
    split_at = frames // 2
    data = cast_ref.shape[0]
    diagonal = sum_rows(parts, slice(data + frames, data + frames + DIAG))
    diag_ref[...] = diagonal
    shift, _ = frame_shift(diagonal[0:1, :], frames)
    for j in range(data // frames):
        value = v_ref[:, lanes(j)]
        image = sum_rows(parts, rows(j, frames)) + prior[:, lanes(j)] * value
        following = image - shift * value
        image_ref[:, lanes(j)] = image
        next_ref[:, lanes(j)] = following
        cast_ref[rows(j, frames), :] = following.astype(BF16)
    half_ref[...] = sum_rows(parts, slice(data, data + split_at)) + sum_rows(
        parts, slice(data + split_at, data + frames)
    )


def eliminate(matrix, right, n):
    width = matrix.shape[1] + right.shape[1]
    work = jnp.concatenate([matrix, right], axis=1)
    work = [work[rows(i, TILE), :] for i in range(n // TILE)]
    at = lax.broadcasted_iota(jnp.int32, (TILE, width), 0)

    def step(tiles, column, k, pivot):
        i, s = divmod(k, TILE)
        row = tiles[i][s : s + 1, :] * pivot
        done = [t - c * row for t, c in zip(tiles, column)]
        done[i] = jnp.where(at == s, row, done[i])
        return done

    for start in range(0, n, PANEL):
        columns = [
            [jnp.broadcast_to(t[:, k : k + 1], (TILE, width)) for t in work]
            for k in range(start, start + PANEL)
        ]
        for u in range(PANEL):
            k = start + u
            i, s = divmod(k, TILE)
            pivot = 1.0 / columns[u][i][s : s + 1, :]
            for later in range(u + 1, PANEL):
                columns[later] = step(columns[later], columns[u], k, pivot)
            work = step(work, columns[u], k, pivot)
    return jnp.concatenate(work, axis=0)[:, n:]


def inverse_kernel(first, out_ref):
    n = first.shape[0]
    out_ref[...] = eliminate(first[:, n:], jnp.where(eye(n), 1.0, 0.0), n)


def final_kernel(
    parts, v_ref, image_ref, next_ref, prior, first, inverse_ref, norm_ref, diag_ref, x_ref, r_ref
):
    n = first.shape[0]
    data = parts[0].shape[0] - n
    norm, energy = first[:, :n], first[:, n:]
    shift, shift_row = frame_shift(diag_ref[0:1, :], n)
    second = sum_rows(parts, slice(data, data + n))
    next_energy = second[:, :n] + second[:, n:]
    next_rhs = energy - shift * norm
    cross = norm_ref[...] + next_rhs * shift_row
    inverse = inverse_ref[...]
    alpha = nn_dot(inverse, norm)
    conj = nn_dot(inverse, cross.T)
    schur = next_energy - nn_dot(cross, conj)
    rhs = next_rhs - nn_dot(cross, alpha)
    gamma = eliminate(schur, rhs, n)
    coeffs = jnp.concatenate([alpha - nn_dot(conj, gamma), gamma], axis=0)
    for j in range(data // n):
        value = v_ref[:, lanes(j)]
        following = next_ref[:, lanes(j)]
        second_image = sum_rows(parts, rows(j, n)) + prior[:, lanes(j)] * following
        x_ref[:, lanes(j)] = tn_dot(coeffs, jnp.concatenate([value, following], axis=0))
        r_ref[:, lanes(j)] = value - tn_dot(
            coeffs, jnp.concatenate([image_ref[:, lanes(j)], second_image], axis=0)
        )


def shifted(x, axis, shift):
    count = lax.axis_size(axis)
    return lax.ppermute(x, axis, [(i, (i + shift) % count) for i in range(count)])


def swapped(x, axis, flip):
    return lax.ppermute(x, axis, [(i, i ^ flip) for i in range(lax.axis_size(axis))])


def gather(x, axis):
    return tuple([x] + [shifted(x, axis, s) for s in range(1, lax.axis_size(axis))])


def exchange(parts, axis):
    return tuple([parts[0]] + [shifted(x, axis, s) for s, x in enumerate(parts) if s])


def shards(right_side, prior, blocks, block_row, block_col):
    frames, pix = right_side.shape
    stretch = pix // BLOCK
    n_rows, n_cols = lax.axis_size("row"), lax.axis_size("col")
    row_span, col_span = stretch * n_cols, stretch * n_rows
    prior = prior.reshape(1, pix)
    stored = blocks.shape[0]
    half_cols = n_cols // 2 * stretch * frames

    def shape(dims, dtype=F32):
        return jax.ShapeDtypeStruct(dims, dtype)

    own = shape((frames, pix))
    gram_type = shape((frames, 2 * frames))
    cast_type = shape((stretch * frames, BLOCK), BF16)
    aside = pl.CostEstimate(flops=2 * 10**9, bytes_accessed=8 * 10**6, transcendentals=0)

    def forward(search, gram, half):
        size = half_cols + frames + (frames // 2 if half else 0)
        keep, send = call(
            lambda *refs: forward_kernel(stretch, n_cols, *refs),
            (shape((size, BLOCK)),) * 2,
            (index, search, staged, gram, half),
            [
                pltpu.VMEM((row_span, frames, BLOCK), F32),
                pltpu.VMEM((col_span, frames, BLOCK), BF16),
            ],
        )
        received = swapped(send, "col", 1)
        pair, first = call(
            lambda *refs: pair_kernel(frames, *refs),
            (shape((half_cols + frames, BLOCK), BF16), (gram_type,) if half else ()),
            (keep, received),
        )
        parts = tuple([pair] + [swapped(pair, "col", flip) for flip in range(2, n_cols, 2)])
        (foot,) = call(
            lambda *refs: chips_kernel(frames, *refs),
            (shape((half_cols + frames, BLOCK), BF16),),
            (parts,),
        )
        return foot, swapped(foot, "col", 1), first

    def backward(own_foot, other_foot, last):
        size = stretch * frames + frames + (0 if last else DIAG)
        parts, norm = call(
            lambda *refs: backward_kernel(stretch, n_cols, last, *refs),
            ((shape((size, BLOCK), BF16),) * n_rows, (shape((frames, frames)),) if last else ()),
            (index, own_foot, other_foot, staged),
            [
                pltpu.VMEM((col_span, frames, BLOCK), F32),
                pltpu.VMEM((row_span, frames, BLOCK), BF16),
                pltpu.VMEM((frames, 2 * frames), F32),
            ],
        )
        return exchange(parts, "row"), norm

    (cast,) = call(cast_kernel, (cast_type,), (right_side,))
    search = gather(cast, "row")
    index, staged = call(
        lambda *refs: stage_kernel(row_span, stretch, *refs),
        (shape((2, stored), jnp.int32), shape(blocks.shape, BF16)),
        (block_row, block_col, blocks),
        [pltpu.SemaphoreType.DMA],
        specs=[SMEM, SMEM, ANY],
        cost=aside,
    )
    (gram,) = call(gram_kernel, (gram_type,), (right_side, prior), cost=aside)
    own_foot, other_foot, _ = forward(search, gram, ())
    parts, _ = backward(own_foot, other_foot, False)
    image, following, cast, half, diagonal = call(
        image_kernel,
        (own, own, cast_type, shape((frames // 2, 2 * frames)), shape((DIAG, 2 * frames))),
        (parts, right_side, prior),
    )
    search = gather(cast, "row")
    (gram,) = call(gram_kernel, (gram_type,), (following, prior), cost=aside)
    own_foot, other_foot, (first,) = forward(search, gram, (half,))
    (inverse,) = call(inverse_kernel, (shape((frames, frames)),), (first,), cost=aside)
    parts, (norm,) = backward(own_foot, other_foot, True)
    return tuple(
        call(
            final_kernel,
            (own, own),
            (parts, right_side, image, following, prior, first, inverse, norm, diagonal),
        )
    )


def solution(mesh):
    return jax.shard_map(
        shards,
        mesh=mesh,
        in_specs=(
            P("groups", ("row", "col")),
            P(("row", "col")),
            P(("row", "col"), None, None),
            P(("row", "col")),
            P(("row", "col")),
        ),
        out_specs=(P("groups", ("row", "col")), P("groups", ("row", "col"))),
        check_vma=False,
    )
```

time: 370 us -> 74 us (0.20)
  waiting for transfers between devices: 174 us -> 30.8 us
  blocking collectives: 101 us -> 0 us
  other arithmetic: 41.3 us -> 0 us
  matrix products: 28.5 us -> 0 us
  starting transfers between devices: 0.39 us -> 21.8 us
  Pallas kernels: 0 us -> 17.5 us
  between operations: 14.3 us -> 0.8 us
  local copies, waits for them, and re-layouts: 9.18 us -> 2.8 us
    reduce_scatter x4 -> x0, waiting for transfers between devices: 87.4 us -> none  [the longest x2 45 us: shards(): lax.psum_scatter(foot_part, 'col', scatter_dimension=1, tiled=True)]
    psum x1 -> x0, waiting for transfers between devices: 86.7 us -> none  [shards(): gram = lax.psum(pair_gram(residual, residual), ('row', 'col'))]
    psum x1 -> x0, blocking collectives: 57.6 us -> none  [shards(): curvature = lax.psum(pair_gram(direction, image), ('row', 'col'))]
    all_gather x4 -> x0, blocking collectives: 43.3 us -> none  [the longest x2 31.5 us: shards(): lax.all_gather(direction.astype(jnp.bfloat16), 'row', axis=1, tiled=True)]
    another operation x15 -> x0, other arithmetic: 36.2 us -> none  [the longest x9 19.6 us: spd_solve(): factor = jnp.linalg.cholesky(matrix)]
    ppermute x0 -> x18, waiting for transfers between devices: none -> 30.8 us  [the longest x12 16.2 us: shifted(): lax.ppermute(x, axis, [(i, (i + shift) % count) for i in range(count)])]
    dot_general x21 -> x0, matrix products: 26.5 us -> none  [the longest x9 7.73 us: apply_left(): jnp.dot(coeffs, panel, precision=lax.Precision.HIGHEST, preferred_element...]
    ppermute x0 -> x18, starting transfers between devices: none -> 21.8 us  [the longest x12 18.4 us: shifted(): lax.ppermute(x, axis, [(i, (i + shift) % count) for i in range(count)])]
  transfers between devices with their start and end apart: 5 -> 18, of which waited for: 5 -> 13; matrix products, arithmetic and copies ran while one was open for 0% -> 0% of each run, Pallas kernels for 0% -> 7%
where the time goes in v4:
time: 74 us; the launch traced here: 73.8 us
  waiting for transfers between devices  30.8 us (42%)
  starting transfers between devices  21.8 us (29%)
  Pallas kernels  17.5 us (24%)
  local copies, waits for them, and re-layouts  2.8 us (4%)
  between operations  0.8 us (1%)
    ppermute x12, starting transfers between devices, shifted(): lax.ppermute(x, axis, [(i, (i + shift) % count) for i in range(count)])  18.4 us
    pallas_call x15, Pallas kernels, call(): pl.pallas_call(body, out_shape=flat_outs, in_specs=specs or [space(x) for...  17.5 us
    ppermute x12, waiting for transfers between devices, shifted(): lax.ppermute(x, axis, [(i, (i + shift) % count) for i in range(count)])  16.2 us
    ppermute x6, waiting for transfers between devices, swapped(): lax.ppermute(x, axis, [(i, i ^ flip) for i in range(lax.axis_size(axis))])  14.7 us
    ppermute x6, starting transfers between devices, swapped(): lax.ppermute(x, axis, [(i, i ^ flip) for i in range(lax.axis_size(axis))])  3.4 us
    unnamed x14, local copies, waits for them, and re-layouts  2.8 us
  transfers between devices with their start and end apart: 18, of which 13 were waited for; matrix products, arithmetic and copies ran while one was open for 0% of the time, Pallas kernels for 7%

profile of v4, /device:TPU:0, one launch (start us, length us, event | category | flops | bytes accessed | tf_op | source)
XLA Modules:
  0.0 73.8 jit_solution(13065542860605013183)
XLA Ops:
  0.6 0.9 %copy-done = f32[64,512]{1,0:T(8,128)S(1)} copy-done((f32[64,512]{1,0:T(8,128)S(1)}, f32[64,512]{1,0:T(8,128)}, u32[]{:S(2)}) %copy-start) | copy-done | bytes 131096
  1.5 5.1 %collective-permute-start.2 = (bf16[256,128]{1,0:T(8,128)(2,1)S(1)}, bf16[256,128]{1,0:T(8,128)(2,1)S(1)}, u32[]{:S(2)}, u32[]{:S(2)}) collective-permute-start(bf16[256,128]{1,0:T(8,128)(2,1)S(1)} %shard_map.69.refs_1_), channel_id=1, source_target_pairs={{0,12},{4,0},{8,4},{12,8},{1,13},{5,1},{9,5},{13,9},{2,14},{6,2},{... | collective-permute-start | bytes 196616 | tf_op jit(solution)/shard_map/ppermute | solution.py:307
  6.7 1.0 %collective-permute-start = (bf16[256,128]{1,0:T(8,128)(2,1)S(1)}, bf16[256,128]{1,0:T(8,128)(2,1)S(1)}, u32[]{:S(2)}, u32[]{:S(2)}) collective-permute-start(bf16[256,128]{1,0:T(8,128)(2,1)S(1)} %shard_map.69.refs_1_), channel_id=1, source_target_pairs={{0,4},{4,8},{8,12},{12,0},{1,5},{5,9},{9,13},{13,1},{2,6},{6,10},{... | collective-permute-start | bytes 196616 | tf_op jit(solution)/shard_map/ppermute | solution.py:307
  8.7 1.2 %copy-done.4 = bf16[64,128,128]{2,1,0:T(8,128)(2,1)S(1)} copy-done((bf16[64,128,128]{2,1,0:T(8,128)(2,1)S(1)}, bf16[64,128,128]{2,1,0:T(8,128)(2,1)}, u32[]{:S(2)}) %copy-start.4) | copy-done | bytes 2097176
  9.9 1.6 %shard_map.68 = (s32[2,64]{1,0:T(2,128)S(1)}, bf16[64,128,128]{2,1,0:T(8,128)(2,1)S(1)}) custom-call(s32[64]{0:T(128)S(1)} %copy-done.5, s32[64]{0:T(128)S(1)} %copy-done.6, bf16[64,128,128]{2,1,0:T(8,128)(2,1)S(1)} %copy-done.4), custom_call_target="tpu_custom_call" | custom-call | flops 2000000000 | bytes 8000000 | tf_op jit(solution)/shard_map/pallas_call | solution.py:52
  11.6 1.5 %collective-permute-done.1.refs_3_ = bf16[256,128]{1,0:T(8,128)(2,1)S(1)} collective-permute-done((bf16[256,128]{1,0:T(8,128)(2,1)S(1)}, bf16[256,128]{1,0:T(8,128)(2,1)S(1)}, u32[]{:S(2)}, u32[]{:S(2)}) %collective-permute-start.1) | collective-permute-done | bytes 65568 | tf_op jit(solution)/shard_map/ppermute | solution.py:307
  13.1 2.1 %shard_map.71 = (f32[576,128]{1,0:T(8,128)S(1)}, f32[576,128]{1,0:T(8,128)S(1)}) custom-call(s32[2,64]{1,0:T(2,128)S(1)} %get-tuple-element.24.refs_0_, bf16[256,128]{1,0:T(8,128)(2,1)S(1)} %shard_map.69.refs_1_, bf16[256,128]{1,0:T(8,128)(2,1)S(1)} %collective-permute-done.refs_2_, bf16[256,128]{1,0:T(8,128)(2,1)S(1)} %collective-permute-done.1.refs_3_, ...), custom_call_target="tpu_custom_call" | custom-call | tf_op jit(solution)/shard_map/pallas_call | solution.py:52
  15.4 1.6 %collective-permute-done.3.refs_1_ = f32[576,128]{1,0:T(8,128)S(1)} collective-permute-done((f32[576,128]{1,0:T(8,128)S(1)}, f32[576,128]{1,0:T(8,128)S(1)}, u32[]{:S(2)}, u32[]{:S(2)}) %collective-permute-start.3) | collective-permute-done | bytes 294944 | tf_op jit(solution)/shard_map/ppermute | solution.py:311
  17.0 1.6 %collective-permute-start.4 = (bf16[576,128]{1,0:T(8,128)(2,1)S(1)}, bf16[576,128]{1,0:T(8,128)(2,1)S(1)}, u32[]{:S(2)}, u32[]{:S(2)}) collective-permute-start(bf16[576,128]{1,0:T(8,128)(2,1)S(1)} %shard_map.72.refs_0_), channel_id=1, source_target_pairs={{0,2},{1,3},{2,0},{3,1},{4,6},{5,7},{6,4},{7,5},{8,10},{9,11},{10,... | collective-permute-start | bytes 442376 | tf_op jit(solution)/shard_map/ppermute | solution.py:311
  18.5 4.4 %collective-permute-done.4.refs_1_ = bf16[576,128]{1,0:T(8,128)(2,1)S(1)} collective-permute-done((bf16[576,128]{1,0:T(8,128)(2,1)S(1)}, bf16[576,128]{1,0:T(8,128)(2,1)S(1)}, u32[]{:S(2)}, u32[]{:S(2)}) %collective-permute-start.4) | collective-permute-done | bytes 147488 | tf_op jit(solution)/shard_map/ppermute | solution.py:311
  23.0 1.4 %collective-permute-done.5.refs_2_ = bf16[576,128]{1,0:T(8,128)(2,1)S(1)} collective-permute-done((bf16[576,128]{1,0:T(8,128)(2,1)S(1)}, bf16[576,128]{1,0:T(8,128)(2,1)S(1)}, u32[]{:S(2)}, u32[]{:S(2)}) %collective-permute-start.5) | collective-permute-done | bytes 147488 | tf_op jit(solution)/shard_map/ppermute | solution.py:311
  24.4 1.5 %shard_map.74 = (bf16[336,128]{1,0:T(8,128)(2,1)S(1)}, bf16[336,128]{1,0:T(8,128)(2,1)S(1)}, bf16[336,128]{1,0:T(8,128)(2,1)S(1)}, bf16[336,128]{1,0:T(8,128)(2,1)S(1)}) custom-call(s32[2,64]{1,0:T(2,128)S(1)} %get-tuple-element.24.refs_0_, bf16[576,128]{1,0:T(8,128)(2,1)S(1)} %shard_map.73.refs_1_, bf16[576,128]{1,0:T(8,128)(2,1)S(1)} %collective-permute-done.5.refs_2_, ...), custom_call_target="tpu_custom_call" | custom-call | tf_op jit(solution)/shard_map/pallas_call | solution.py:52
  25.9 1.0 %collective-permute-start.6 = (bf16[336,128]{1,0:T(8,128)(2,1)S(1)}, bf16[336,128]{1,0:T(8,128)(2,1)S(1)}, u32[]{:S(2)}, u32[]{:S(2)}) collective-permute-start(bf16[336,128]{1,0:T(8,128)(2,1)S(1)} %get-tuple-element.29), channel_id=1, source_target_pairs={{0,4},{4,8},{8,12},{12,0},{1,5},{5,9},{9,13},{13,1},{2,6},{6,10},{... | collective-permute-start | bytes 258056 | tf_op jit(solution)/shard_map/ppermute | solution.py:307
  26.9 1.5 %collective-permute-start.7 = (bf16[336,128]{1,0:T(8,128)(2,1)S(1)}, bf16[336,128]{1,0:T(8,128)(2,1)S(1)}, u32[]{:S(2)}, u32[]{:S(2)}) collective-permute-start(bf16[336,128]{1,0:T(8,128)(2,1)S(1)} %get-tuple-element.30), channel_id=1, source_target_pairs={{0,8},{4,12},{8,0},{12,4},{1,9},{5,13},{9,1},{13,5},{2,10},{6,14},... | collective-permute-start | bytes 258056 | tf_op jit(solution)/shard_map/ppermute | solution.py:307
  28.4 2.2 %collective-permute-start.8 = (bf16[336,128]{1,0:T(8,128)(2,1)S(1)}, bf16[336,128]{1,0:T(8,128)(2,1)S(1)}, u32[]{:S(2)}, u32[]{:S(2)}) collective-permute-start(bf16[336,128]{1,0:T(8,128)(2,1)S(1)} %get-tuple-element.31), channel_id=1, source_target_pairs={{0,12},{4,0},{8,4},{12,8},{1,13},{5,1},{9,5},{13,9},{2,14},{6,2},{... | collective-permute-start | bytes 258056 | tf_op jit(solution)/shard_map/ppermute | solution.py:307
  30.6 2.6 %collective-permute-done.6.refs_1_ = bf16[336,128]{1,0:T(8,128)(2,1)S(1)} collective-permute-done((bf16[336,128]{1,0:T(8,128)(2,1)S(1)}, bf16[336,128]{1,0:T(8,128)(2,1)S(1)}, u32[]{:S(2)}, u32[]{:S(2)}) %collective-permute-start.6) | collective-permute-done | bytes 86048 | tf_op jit(solution)/shard_map/ppermute | solution.py:307
  33.2 2.9 %collective-permute-done.7.refs_2_ = bf16[336,128]{1,0:T(8,128)(2,1)S(1)} collective-permute-done((bf16[336,128]{1,0:T(8,128)(2,1)S(1)}, bf16[336,128]{1,0:T(8,128)(2,1)S(1)}, u32[]{:S(2)}, u32[]{:S(2)}) %collective-permute-start.7) | collective-permute-done | bytes 86048 | tf_op jit(solution)/shard_map/ppermute | solution.py:307
  36.3 2.7 %collective-permute-start.11 = (bf16[256,128]{1,0:T(8,128)(2,1)S(1)}, bf16[256,128]{1,0:T(8,128)(2,1)S(1)}, u32[]{:S(2)}, u32[]{:S(2)}) collective-permute-start(bf16[256,128]{1,0:T(8,128)(2,1)S(1)} %get-tuple-element.32.refs_1_), channel_id=1, source_target_pairs={{0,12},{4,0},{8,4},{12,8},{1,13},{5,1},{9,5},{13,9},{2,14},{6,2},{... | collective-permute-start | bytes 196616 | tf_op jit(solution)/shard_map/ppermute | solution.py:307
  39.0 1.0 %collective-permute-start.10 = (bf16[256,128]{1,0:T(8,128)(2,1)S(1)}, bf16[256,128]{1,0:T(8,128)(2,1)S(1)}, u32[]{:S(2)}, u32[]{:S(2)}) collective-permute-start(bf16[256,128]{1,0:T(8,128)(2,1)S(1)} %get-tuple-element.32.refs_1_), channel_id=1, source_target_pairs={{0,8},{4,12},{8,0},{12,4},{1,9},{5,13},{9,1},{13,5},{2,10},{6,14},... | collective-permute-start | bytes 196616 | tf_op jit(solution)/shard_map/ppermute | solution.py:307
  40.4 1.2 %collective-permute-done.11.refs_4_ = bf16[256,128]{1,0:T(8,128)(2,1)S(1)} collective-permute-done((bf16[256,128]{1,0:T(8,128)(2,1)S(1)}, bf16[256,128]{1,0:T(8,128)(2,1)S(1)}, u32[]{:S(2)}, u32[]{:S(2)}) %collective-permute-start.11) | collective-permute-done | bytes 65568 | tf_op jit(solution)/shard_map/ppermute | solution.py:307
  41.5 4.7 %collective-permute-done.10.refs_3_ = bf16[256,128]{1,0:T(8,128)(2,1)S(1)} collective-permute-done((bf16[256,128]{1,0:T(8,128)(2,1)S(1)}, bf16[256,128]{1,0:T(8,128)(2,1)S(1)}, u32[]{:S(2)}, u32[]{:S(2)}) %collective-permute-start.10) | collective-permute-done | bytes 65568 | tf_op jit(solution)/shard_map/ppermute | solution.py:307
  46.3 2.2 %shard_map.77 = (f32[608,128]{1,0:T(8,128)S(1)}, f32[608,128]{1,0:T(8,128)S(1)}) custom-call(s32[2,64]{1,0:T(2,128)S(1)} %get-tuple-element.24.refs_0_, bf16[256,128]{1,0:T(8,128)(2,1)S(1)} %get-tuple-element.32.refs_1_, bf16[256,128]{1,0:T(8,128)(2,1)S(1)} %collective-permute-done.9.refs_2_, bf16[256,128]{1,0:T(8,128)(2,1)S(1)} %collective-permute-done.10.refs_3_, ...), custom_call_target="tpu_custom_call" | custom-call | tf_op jit(solution)/shard_map/pallas_call | solution.py:52
  48.6 1.6 %collective-permute-done.12.refs_1_ = f32[608,128]{1,0:T(8,128)S(1)} collective-permute-done((f32[608,128]{1,0:T(8,128)S(1)}, f32[608,128]{1,0:T(8,128)S(1)}, u32[]{:S(2)}, u32[]{:S(2)}) %collective-permute-start.12) | collective-permute-done | bytes 311328 | tf_op jit(solution)/shard_map/ppermute | solution.py:311
  50.2 1.6 %collective-permute-start.13 = (bf16[576,128]{1,0:T(8,128)(2,1)S(1)}, bf16[576,128]{1,0:T(8,128)(2,1)S(1)}, u32[]{:S(2)}, u32[]{:S(2)}) collective-permute-start(bf16[576,128]{1,0:T(8,128)(2,1)S(1)} %get-tuple-element.37.refs_0_), channel_id=1, source_target_pairs={{0,2},{1,3},{2,0},{3,1},{4,6},{5,7},{6,4},{7,5},{8,10},{9,11},{10,... | collective-permute-start | bytes 442376 | tf_op jit(solution)/shard_map/ppermute | solution.py:311
  51.8 4.4 %collective-permute-done.13.refs_1_ = bf16[576,128]{1,0:T(8,128)(2,1)S(1)} collective-permute-done((bf16[576,128]{1,0:T(8,128)(2,1)S(1)}, bf16[576,128]{1,0:T(8,128)(2,1)S(1)}, u32[]{:S(2)}, u32[]{:S(2)}) %collective-permute-start.13) | collective-permute-done | bytes 147488 | tf_op jit(solution)/shard_map/ppermute | solution.py:311
  56.3 1.4 %collective-permute-done.14.refs_2_ = bf16[576,128]{1,0:T(8,128)(2,1)S(1)} collective-permute-done((bf16[576,128]{1,0:T(8,128)(2,1)S(1)}, bf16[576,128]{1,0:T(8,128)(2,1)S(1)}, u32[]{:S(2)}, u32[]{:S(2)}) %collective-permute-start.14) | collective-permute-done | bytes 147488 | tf_op jit(solution)/shard_map/ppermute | solution.py:311
  57.6 1.5 %shard_map.80 = (bf16[320,128]{1,0:T(8,128)(2,1)S(1)}, bf16[320,128]{1,0:T(8,128)(2,1)S(1)}, bf16[320,128]{1,0:T(8,128)(2,1)S(1)}, bf16[320,128]{1,0:T(8,128)(2,1)S(1)}, f32[64,64]{1,0:T(8,128)S(1)}) custom-call(s32[2,64]{1,0:T(2,128)S(1)} %get-tuple-element.24.refs_0_, bf16[576,128]{1,0:T(8,128)(2,1)S(1)} %shard_map.79.refs_1_, ...), custom_call_target="tpu_custom_call" | custom-call | tf_op jit(solution)/shard_map/pallas_call | solution.py:52
  59.2 1.6 %collective-permute-start.16 = (bf16[320,128]{1,0:T(8,128)(2,1)S(1)}, bf16[320,128]{1,0:T(8,128)(2,1)S(1)}, u32[]{:S(2)}, u32[]{:S(2)}) collective-permute-start(bf16[320,128]{1,0:T(8,128)(2,1)S(1)} %get-tuple-element.40), channel_id=1, source_target_pairs={{0,8},{4,12},{8,0},{12,4},{1,9},{5,13},{9,1},{13,5},{2,10},{6,14},... | collective-permute-start | bytes 245768 | tf_op jit(solution)/shard_map/ppermute | solution.py:307
  60.9 2.3 %collective-permute-start.17 = (bf16[320,128]{1,0:T(8,128)(2,1)S(1)}, bf16[320,128]{1,0:T(8,128)(2,1)S(1)}, u32[]{:S(2)}, u32[]{:S(2)}) collective-permute-start(bf16[320,128]{1,0:T(8,128)(2,1)S(1)} %get-tuple-element.41), channel_id=1, source_target_pairs={{0,12},{4,0},{8,4},{12,8},{1,13},{5,1},{9,5},{13,9},{2,14},{6,2},{... | collective-permute-start | bytes 245768 | tf_op jit(solution)/shard_map/ppermute | solution.py:307
  63.1 2.6 %shard_map.81.refs_9_ = f32[64,64]{1,0:T(8,128)S(1)} custom-call(f32[64,128]{1,0:T(8,128)S(1)} %get-tuple-element.43.refs_0_.refs_8_), custom_call_target="tpu_custom_call" | custom-call | flops 2000000000 | bytes 8000000 | tf_op jit(solution)/shard_map/pallas_call | solution.py:52
  66.4 2.6 %collective-permute-done.16.refs_2_ = bf16[320,128]{1,0:T(8,128)(2,1)S(1)} collective-permute-done((bf16[320,128]{1,0:T(8,128)(2,1)S(1)}, bf16[320,128]{1,0:T(8,128)(2,1)S(1)}, u32[]{:S(2)}, u32[]{:S(2)}) %collective-permute-start.16) | collective-permute-done | bytes 81952 | tf_op jit(solution)/shard_map/ppermute | solution.py:307
  69.0 4.8 %shard_map.82 = (f32[64,512]{1,0:T(8,128)}, f32[64,512]{1,0:T(8,128)}) custom-call(bf16[320,128]{1,0:T(8,128)(2,1)S(1)} %get-tuple-element.38.refs_0_, bf16[320,128]{1,0:T(8,128)(2,1)S(1)} %collective-permute-done.15.refs_1_, bf16[320,128]{1,0:T(8,128)(2,1)S(1)} %collective-permute-done.16.refs_2_, bf16[320,128]{1,0:T(8,128)(2,1)S(1)} %collective-permute-done.17.refs_3_, ...), custom_call_target="tpu_custom_call" | custom-call | tf_op jit(solution)/shard_map/pallas_call | solution.py:52
  (33 shorter events, 2.9 us)
Async XLA Ops:
  0.6 0.9 %copy-start = (f32[64,512]{1,0:T(8,128)S(1)}, f32[64,512]{1,0:T(8,128)}, u32[]{:S(2)}) copy-start(f32[64,512]{1,0:T(8,128)} %refs_4_.3) | copy-start | bytes 393220
  1.5 10.1 %collective-permute-start.2 = (bf16[256,128]{1,0:T(8,128)(2,1)S(1)}, bf16[256,128]{1,0:T(8,128)(2,1)S(1)}, u32[]{:S(2)}, u32[]{:S(2)}) collective-permute-start(bf16[256,128]{1,0:T(8,128)(2,1)S(1)} %shard_map.69.refs_1_), channel_id=1, source_target_pairs={{0,12},{4,0},{8,4},{12,8},{1,13},{5,1},{9,5},{13,9},{2,14},{6,2},{... | collective-permute-start | bytes 196616 | tf_op jit(solution)/shard_map/ppermute | solution.py:307
  6.7 6.5 %collective-permute-start.1 = (bf16[256,128]{1,0:T(8,128)(2,1)S(1)}, bf16[256,128]{1,0:T(8,128)(2,1)S(1)}, u32[]{:S(2)}, u32[]{:S(2)}) collective-permute-start(bf16[256,128]{1,0:T(8,128)(2,1)S(1)} %shard_map.69.refs_1_), channel_id=1, source_target_pairs={{0,8},{4,12},{8,0},{12,4},{1,9},{5,13},{9,1},{13,5},{2,10},{6,14},... | collective-permute-start | bytes 196616 | tf_op jit(solution)/shard_map/ppermute | solution.py:307
  6.7 6.5 %collective-permute-start = (bf16[256,128]{1,0:T(8,128)(2,1)S(1)}, bf16[256,128]{1,0:T(8,128)(2,1)S(1)}, u32[]{:S(2)}, u32[]{:S(2)}) collective-permute-start(bf16[256,128]{1,0:T(8,128)(2,1)S(1)} %shard_map.69.refs_1_), channel_id=1, source_target_pairs={{0,4},{4,8},{8,12},{12,0},{1,5},{5,9},{9,13},{13,1},{2,6},{6,10},{... | collective-permute-start | bytes 196616 | tf_op jit(solution)/shard_map/ppermute | solution.py:307
  7.7 0.7 copy-start.2
  8.3 1.6 %copy-start.4 = (bf16[64,128,128]{2,1,0:T(8,128)(2,1)S(1)}, bf16[64,128,128]{2,1,0:T(8,128)(2,1)}, u32[]{:S(2)}) copy-start(bf16[64,128,128]{2,1,0:T(8,128)(2,1)} %refs_2_.1) | copy-start | bytes 6291460
  8.3 1.6 %copy-start.5 = (s32[64]{0:T(128)S(1)}, s32[64]{0:T(128)}, u32[]{:S(2)}) copy-start(s32[64]{0:T(128)} %refs_0_.3) | copy-start | bytes 772
  8.4 1.6 %copy-start.6 = (s32[64]{0:T(128)S(1)}, s32[64]{0:T(128)}, u32[]{:S(2)}) copy-start(s32[64]{0:T(128)} %refs_1_.1) | copy-start | bytes 772
  15.3 20.8 %copy-start.1 = (f32[64,512]{1,0:T(8,128)S(1)}, f32[64,512]{1,0:T(8,128)}, u32[]{:S(2)}) copy-start(f32[64,512]{1,0:T(8,128)} %refs_4_.3) | copy-start | bytes 393220
  15.3 20.8 %copy-start.3 = (f32[512]{0:T(512)S(1)}, f32[512]{0:T(512)}, u32[]{:S(2)}) copy-start(f32[512]{0:T(512)} %param.6) | copy-start | bytes 6148
  15.3 1.6 %collective-permute-start.3 = (f32[576,128]{1,0:T(8,128)S(1)}, f32[576,128]{1,0:T(8,128)S(1)}, u32[]{:S(2)}, u32[]{:S(2)}) collective-permute-start(f32[576,128]{1,0:T(8,128)S(1)} %get-tuple-element.27), channel_id=1, source_target_pairs={{0,1},{1,0},{2,3},{3,2},{4,5},{5,4},{6,7},{7,6},{8,9},{9,8},{10,11... | collective-permute-start | bytes 884744 | tf_op jit(solution)/shard_map/ppermute | solution.py:311
  17.0 6.0 %collective-permute-start.4 = (bf16[576,128]{1,0:T(8,128)(2,1)S(1)}, bf16[576,128]{1,0:T(8,128)(2,1)S(1)}, u32[]{:S(2)}, u32[]{:S(2)}) collective-permute-start(bf16[576,128]{1,0:T(8,128)(2,1)S(1)} %shard_map.72.refs_0_), channel_id=1, source_target_pairs={{0,2},{1,3},{2,0},{3,1},{4,6},{5,7},{6,4},{7,5},{8,10},{9,11},{10,... | collective-permute-start | bytes 442376 | tf_op jit(solution)/shard_map/ppermute | solution.py:311
  23.0 1.4 %collective-permute-start.5 = (bf16[576,128]{1,0:T(8,128)(2,1)S(1)}, bf16[576,128]{1,0:T(8,128)(2,1)S(1)}, u32[]{:S(2)}, u32[]{:S(2)}) collective-permute-start(bf16[576,128]{1,0:T(8,128)(2,1)S(1)} %shard_map.73.refs_1_), channel_id=1, source_target_pairs={{0,1},{1,0},{2,3},{3,2},{4,5},{5,4},{6,7},{7,6},{8,9},{9,8},{10,11... | collective-permute-start | bytes 442376 | tf_op jit(solution)/shard_map/ppermute | solution.py:311
  25.9 7.3 %collective-permute-start.6 = (bf16[336,128]{1,0:T(8,128)(2,1)S(1)}, bf16[336,128]{1,0:T(8,128)(2,1)S(1)}, u32[]{:S(2)}, u32[]{:S(2)}) collective-permute-start(bf16[336,128]{1,0:T(8,128)(2,1)S(1)} %get-tuple-element.29), channel_id=1, source_target_pairs={{0,4},{4,8},{8,12},{12,0},{1,5},{5,9},{9,13},{13,1},{2,6},{6,10},{... | collective-permute-start | bytes 258056 | tf_op jit(solution)/shard_map/ppermute | solution.py:307
  26.9 9.2 %collective-permute-start.7 = (bf16[336,128]{1,0:T(8,128)(2,1)S(1)}, bf16[336,128]{1,0:T(8,128)(2,1)S(1)}, u32[]{:S(2)}, u32[]{:S(2)}) collective-permute-start(bf16[336,128]{1,0:T(8,128)(2,1)S(1)} %get-tuple-element.30), channel_id=1, source_target_pairs={{0,8},{4,12},{8,0},{12,4},{1,9},{5,13},{9,1},{13,5},{2,10},{6,14},... | collective-permute-start | bytes 258056 | tf_op jit(solution)/shard_map/ppermute | solution.py:307
  28.4 7.7 %collective-permute-start.8 = (bf16[336,128]{1,0:T(8,128)(2,1)S(1)}, bf16[336,128]{1,0:T(8,128)(2,1)S(1)}, u32[]{:S(2)}, u32[]{:S(2)}) collective-permute-start(bf16[336,128]{1,0:T(8,128)(2,1)S(1)} %get-tuple-element.31), channel_id=1, source_target_pairs={{0,12},{4,0},{8,4},{12,8},{1,13},{5,1},{9,5},{13,9},{2,14},{6,2},{... | collective-permute-start | bytes 258056 | tf_op jit(solution)/shard_map/ppermute | solution.py:307
  36.3 5.2 %collective-permute-start.11 = (bf16[256,128]{1,0:T(8,128)(2,1)S(1)}, bf16[256,128]{1,0:T(8,128)(2,1)S(1)}, u32[]{:S(2)}, u32[]{:S(2)}) collective-permute-start(bf16[256,128]{1,0:T(8,128)(2,1)S(1)} %get-tuple-element.32.refs_1_), channel_id=1, source_target_pairs={{0,12},{4,0},{8,4},{12,8},{1,13},{5,1},{9,5},{13,9},{2,14},{6,2},{... | collective-permute-start | bytes 196616 | tf_op jit(solution)/shard_map/ppermute | solution.py:307
  39.0 7.2 %collective-permute-start.10 = (bf16[256,128]{1,0:T(8,128)(2,1)S(1)}, bf16[256,128]{1,0:T(8,128)(2,1)S(1)}, u32[]{:S(2)}, u32[]{:S(2)}) collective-permute-start(bf16[256,128]{1,0:T(8,128)(2,1)S(1)} %get-tuple-element.32.refs_1_), channel_id=1, source_target_pairs={{0,8},{4,12},{8,0},{12,4},{1,9},{5,13},{9,1},{13,5},{2,10},{6,14},... | collective-permute-start | bytes 196616 | tf_op jit(solution)/shard_map/ppermute | solution.py:307
  40.0 6.3 %collective-permute-start.9 = (bf16[256,128]{1,0:T(8,128)(2,1)S(1)}, bf16[256,128]{1,0:T(8,128)(2,1)S(1)}, u32[]{:S(2)}, u32[]{:S(2)}) collective-permute-start(bf16[256,128]{1,0:T(8,128)(2,1)S(1)} %get-tuple-element.32.refs_1_), channel_id=1, source_target_pairs={{0,4},{4,8},{8,12},{12,0},{1,5},{5,9},{9,13},{13,1},{2,6},{6,10},{... | collective-permute-start | bytes 196616 | tf_op jit(solution)/shard_map/ppermute | solution.py:307
  48.5 1.7 %collective-permute-start.12 = (f32[608,128]{1,0:T(8,128)S(1)}, f32[608,128]{1,0:T(8,128)S(1)}, u32[]{:S(2)}, u32[]{:S(2)}) collective-permute-start(f32[608,128]{1,0:T(8,128)S(1)} %get-tuple-element.36), channel_id=1, source_target_pairs={{0,1},{1,0},{2,3},{3,2},{4,5},{5,4},{6,7},{7,6},{8,9},{9,8},{10,11... | collective-permute-start | bytes 933896 | tf_op jit(solution)/shard_map/ppermute | solution.py:311
  50.2 6.0 %collective-permute-start.13 = (bf16[576,128]{1,0:T(8,128)(2,1)S(1)}, bf16[576,128]{1,0:T(8,128)(2,1)S(1)}, u32[]{:S(2)}, u32[]{:S(2)}) collective-permute-start(bf16[576,128]{1,0:T(8,128)(2,1)S(1)} %get-tuple-element.37.refs_0_), channel_id=1, source_target_pairs={{0,2},{1,3},{2,0},{3,1},{4,6},{5,7},{6,4},{7,5},{8,10},{9,11},{10,... | collective-permute-start | bytes 442376 | tf_op jit(solution)/shard_map/ppermute | solution.py:311
  56.2 1.4 %collective-permute-start.14 = (bf16[576,128]{1,0:T(8,128)(2,1)S(1)}, bf16[576,128]{1,0:T(8,128)(2,1)S(1)}, u32[]{:S(2)}, u32[]{:S(2)}) collective-permute-start(bf16[576,128]{1,0:T(8,128)(2,1)S(1)} %shard_map.79.refs_1_), channel_id=1, source_target_pairs={{0,1},{1,0},{2,3},{3,2},{4,5},{5,4},{6,7},{7,6},{8,9},{9,8},{10,11... | collective-permute-start | bytes 442376 | tf_op jit(solution)/shard_map/ppermute | solution.py:311
  59.2 7.2 %collective-permute-start.15 = (bf16[320,128]{1,0:T(8,128)(2,1)S(1)}, bf16[320,128]{1,0:T(8,128)(2,1)S(1)}, u32[]{:S(2)}, u32[]{:S(2)}) collective-permute-start(bf16[320,128]{1,0:T(8,128)(2,1)S(1)} %get-tuple-element.39), channel_id=1, source_target_pairs={{0,4},{4,8},{8,12},{12,0},{1,5},{5,9},{9,13},{13,1},{2,6},{6,10},{... | collective-permute-start | bytes 245768 | tf_op jit(solution)/shard_map/ppermute | solution.py:307
  59.2 9.8 %collective-permute-start.16 = (bf16[320,128]{1,0:T(8,128)(2,1)S(1)}, bf16[320,128]{1,0:T(8,128)(2,1)S(1)}, u32[]{:S(2)}, u32[]{:S(2)}) collective-permute-start(bf16[320,128]{1,0:T(8,128)(2,1)S(1)} %get-tuple-element.40), channel_id=1, source_target_pairs={{0,8},{4,12},{8,0},{12,4},{1,9},{5,13},{9,1},{13,5},{2,10},{6,14},... | collective-permute-start | bytes 245768 | tf_op jit(solution)/shard_map/ppermute | solution.py:307
  60.9 8.1 %collective-permute-start.17 = (bf16[320,128]{1,0:T(8,128)(2,1)S(1)}, bf16[320,128]{1,0:T(8,128)(2,1)S(1)}, u32[]{:S(2)}, u32[]{:S(2)}) collective-permute-start(bf16[320,128]{1,0:T(8,128)(2,1)S(1)} %get-tuple-element.41), channel_id=1, source_target_pairs={{0,12},{4,0},{8,4},{12,8},{1,13},{5,1},{9,5},{13,9},{2,14},{6,2},{... | collective-permute-start | bytes 245768 | tf_op jit(solution)/shard_map/ppermute | solution.py:307

commit v5 on v4

--- a/solution.py
+++ b/solution.py
@@ -7,7 +7,7 @@
 
 BLOCK = 128
 TILE = 8
-PANEL = 4
+AHEAD = 4
 DIAG = 16
 F32, BF16 = jnp.float32, jnp.bfloat16
 FP32 = lax.Precision.HIGHEST
@@ -100,6 +100,11 @@
     copy.wait()
 
 
+def turn_kernel(blocks, out_ref):
+    for k in range(blocks.shape[0]):
+        out_ref[k] = blocks[k].T
+
+
 def gram_kernel(v_ref, prior, out_ref):
     value = v_ref[...]
     out_ref[...] = nt_dot(value, jnp.concatenate([value, value * prior[...]], axis=0), FP32)
@@ -118,11 +123,15 @@
 def forward_kernel(stretch, cols, index, search, blocks, gram, half, keep_ref, send_ref, acc, panel):
     frames = panel.shape[1]
     me = lax.axis_index("row")
-    for shift, ref in enumerate(search):
-        fill(panel, ref, lax.rem(me - shift + len(search), len(search)), stretch)
+    for flip, ref in enumerate(search):
+        fill(panel, ref, lax.bitwise_xor(me, flip), stretch)
     acc[...] = jnp.zeros_like(acc)
     for k in range(blocks.shape[0]):
-        acc[index[0, k]] += nt_dot(panel[index[1, k]], blocks[k])
+        if half:
+            part = jnp.dot(panel[index[1, k]], blocks[k], preferred_element_type=F32)
+        else:
+            part = nt_dot(panel[index[1, k]], blocks[k])
+        acc[index[0, k]] += part
     core = lax.rem(lax.axis_index("col"), 2)
     for x in range(cols // 2):
         for j in range(stretch):
@@ -171,7 +180,8 @@
 
 
 def backward_kernel(
-    stretch, cols, last, index, own, received, blocks, out_refs, norm_refs, acc, panel, gram
+    stretch, cols, last, index, own, received, blocks,
+    far_refs, near_ref, keep_refs, keep_ref, norm_refs, acc, panel, gram,
 ):
     frames = panel.shape[1]
     split_at = frames // 2
@@ -189,32 +199,66 @@
     for k in range(blocks.shape[0]):
         acc[index[1, k]] += jnp.dot(panel[index[0, k]], blocks[k], preferred_element_type=F32)
     me = lax.axis_index("row")
-    for shift, out_ref in enumerate(out_refs):
-        dest = lax.rem(me + shift, len(out_refs))
+    for far, (far_ref, kept_ref) in enumerate(zip(far_refs, keep_refs)):
+        shard = lax.bitwise_xor(me, 2 * (far + 1))
+        other = lax.bitwise_xor(shard, 1)
         for j in range(stretch):
-            out_ref[rows(j, frames), :] = acc[dest * stretch + j].astype(BF16)
+            kept_ref[rows(j, frames), :] = acc[shard * stretch + j]
+            far_ref[rows(j, frames), :] = acc[other * stretch + j].astype(BF16)
+    other = lax.bitwise_xor(me, 1)
+    for j in range(stretch):
+        keep_ref[rows(j, frames), :] = acc[me * stretch + j]
+        near_ref[rows(j, frames), :] = acc[other * stretch + j].astype(BF16)
     whole = whole_of(panel)
     total = gram[...] + nt_dot(whole, jnp.concatenate([jnp.zeros_like(whole), whole], axis=0))
     at = stretch * frames
+    out_ref = far_refs[0]
     if last:
         high, low = split(total[:, frames:])
-        block = jnp.concatenate([high, low], axis=1)
-        for out_ref in out_refs:
-            out_ref[at:, :] = block
+        out_ref[at:, :] = jnp.concatenate([high, low], axis=1)
         norm_refs[0][...] = total[:, :frames]
     else:
         gram[...] = total
-        high, low = split(gram[pl.ds(pl.multiple_of(core * split_at, split_at), split_at), :])
+        out_ref[at : at + split_at, :], out_ref[at + split_at : at + frames, :] = split(
+            gram[pl.ds(pl.multiple_of(core * split_at, split_at), split_at), :]
+        )
         lane = lax.broadcasted_iota(jnp.int32, total.shape, 1)
         row = lax.broadcasted_iota(jnp.int32, total.shape, 0)
         on_diagonal = jnp.logical_or(lane == row, lane == row + frames)
         diagonal = jnp.sum(jnp.where(on_diagonal, total, 0.0), axis=0, keepdims=True)
         row = lax.broadcasted_iota(jnp.int32, (DIAG, 2 * frames), 0)
-        tile = jnp.where(row == 0, diagonal, 0.0).astype(BF16)
-        for out_ref in out_refs:
-            out_ref[at : at + split_at, :] = high
-            out_ref[at + split_at : at + frames, :] = low
-            out_ref[at + frames :, :] = tile
+        out_ref[at + frames :, :] = jnp.where(row == 0, diagonal, 0.0).astype(BF16)
+
+
+def rows_kernel(last, frames, sent, received, kept, out_refs, gram_ref, diag_ref):
+    split_at = frames // 2
+    data = kept[0].shape[0]
+    for out_ref, kept_ref, received_ref in zip(out_refs, kept, received):
+        for j in range(data // frames):
+            at = rows(j, frames)
+            out_ref[at, :] = (kept_ref[at, :] + received_ref[at, :].astype(F32)).astype(BF16)
+    pair = (sent, received[0])
+    if last:
+        both = sum_rows(pair, slice(data, data + frames))
+        value = both[:, :frames] + both[:, frames:]
+        block = jnp.concatenate(split(value), axis=1)
+        gram_ref[...] = value
+    else:
+        high, low = slice(data, data + split_at), slice(data + split_at, data + frames)
+        value = sum_rows(pair, high) + sum_rows(pair, low)
+        gram_ref[...] = value
+        block = jnp.concatenate(split(value), axis=0)
+        tile = sum_rows(pair, slice(data + frames, data + frames + DIAG)).astype(BF16)
+        diag_ref[0][...] = tile
+    for out_ref in out_refs:
+        out_ref[data : data + frames, :] = block
+        if not last:
+            out_ref[data + frames :, :] = tile
+
+
+def own_sum(keep, near, far, j, frames):
+    at = rows(j, frames)
+    return keep[at, :] + sum_rows((near, *far), at)
 
 
 def frame_shift(diagonal, frames):
@@ -222,22 +266,26 @@
     return jnp.sum(jnp.where(eye(frames), row, 0.0), axis=1, keepdims=True), row
 
 
-def image_kernel(parts, v_ref, prior, image_ref, next_ref, cast_ref, half_ref, diag_ref):
+def image_kernel(
+    keep, near, far, gram, tile, v_ref, prior, image_ref, next_ref, cast_ref, half_ref, diag_ref
+):
     frames = v_ref.shape[0]
     split_at = frames // 2
     data = cast_ref.shape[0]
-    diagonal = sum_rows(parts, slice(data + frames, data + frames + DIAG))
+    diagonal = tile[...].astype(F32) + sum_rows(far, slice(data + frames, data + frames + DIAG))
     diag_ref[...] = diagonal
     shift, _ = frame_shift(diagonal[0:1, :], frames)
     for j in range(data // frames):
         value = v_ref[:, lanes(j)]
-        image = sum_rows(parts, rows(j, frames)) + prior[:, lanes(j)] * value
+        image = own_sum(keep, near, far, j, frames) + prior[:, lanes(j)] * value
         following = image - shift * value
         image_ref[:, lanes(j)] = image
         next_ref[:, lanes(j)] = following
         cast_ref[rows(j, frames), :] = following.astype(BF16)
-    half_ref[...] = sum_rows(parts, slice(data, data + split_at)) + sum_rows(
-        parts, slice(data + split_at, data + frames)
+    half_ref[...] = (
+        gram[...]
+        + sum_rows(far, slice(data, data + split_at))
+        + sum_rows(far, slice(data + split_at, data + frames))
     )
 
 
@@ -247,76 +295,69 @@
     work = [work[rows(i, TILE), :] for i in range(n // TILE)]
     at = lax.broadcasted_iota(jnp.int32, (TILE, width), 0)
 
-    def step(tiles, column, k, pivot):
+    def column(k):
+        return [jnp.broadcast_to(t[:, k : k + 1], (TILE, width)) for t in work]
+
+    def step(tiles, spread, k, pivot):
         i, s = divmod(k, TILE)
         row = tiles[i][s : s + 1, :] * pivot
-        done = [t - c * row for t, c in zip(tiles, column)]
+        done = [t - c * row for t, c in zip(tiles, spread)]
         done[i] = jnp.where(at == s, row, done[i])
         return done
 
-    for start in range(0, n, PANEL):
-        columns = [
-            [jnp.broadcast_to(t[:, k : k + 1], (TILE, width)) for t in work]
-            for k in range(start, start + PANEL)
-        ]
-        for u in range(PANEL):
-            k = start + u
-            i, s = divmod(k, TILE)
-            pivot = 1.0 / columns[u][i][s : s + 1, :]
-            for later in range(u + 1, PANEL):
-                columns[later] = step(columns[later], columns[u], k, pivot)
-            work = step(work, columns[u], k, pivot)
+    ahead = [column(k) for k in range(AHEAD)]
+    for k in range(n):
+        i, s = divmod(k, TILE)
+        spread = ahead.pop(0)
+        pivot = 1.0 / spread[i][s : s + 1, :]
+        ahead = [step(later, spread, k, pivot) for later in ahead]
+        work = step(work, spread, k, pivot)
+        if k + AHEAD < n:
+            ahead.append(column(k + AHEAD))
     return jnp.concatenate(work, axis=0)[:, n:]
 
 
-def inverse_kernel(first, out_ref):
+def middle_kernel(first, norm_ref, diag_ref, out_ref):
     n = first.shape[0]
-    out_ref[...] = eliminate(first[:, n:], jnp.where(eye(n), 1.0, 0.0), n)
-
-
-def final_kernel(
-    parts, v_ref, image_ref, next_ref, prior, first, inverse_ref, norm_ref, diag_ref, x_ref, r_ref
-):
-    n = first.shape[0]
-    data = parts[0].shape[0] - n
     norm, energy = first[:, :n], first[:, n:]
     shift, shift_row = frame_shift(diag_ref[0:1, :], n)
-    second = sum_rows(parts, slice(data, data + n))
-    next_energy = second[:, :n] + second[:, n:]
+    inverse = eliminate(energy, jnp.where(eye(n), 1.0, 0.0), n)
     next_rhs = energy - shift * norm
     cross = norm_ref[...] + next_rhs * shift_row
-    inverse = inverse_ref[...]
     alpha = nn_dot(inverse, norm)
     conj = nn_dot(inverse, cross.T)
-    schur = next_energy - nn_dot(cross, conj)
-    rhs = next_rhs - nn_dot(cross, alpha)
-    gamma = eliminate(schur, rhs, n)
-    coeffs = jnp.concatenate([alpha - nn_dot(conj, gamma), gamma], axis=0)
+    out_ref[0] = alpha
+    out_ref[1] = conj
+    out_ref[2] = nn_dot(cross, conj)
+    out_ref[3] = next_rhs - nn_dot(cross, alpha)
+
+
+def final_kernel(
+    keep, near, far, gram, v_ref, image_ref, next_ref, prior, middle, x_ref, r_ref
+):
+    n = v_ref.shape[0]
+    data = keep.shape[0]
+    second = sum_rows(far, slice(data, data + n))
+    schur = gram[...] + second[:, :n] + second[:, n:] - middle[2]
+    gamma = eliminate(schur, middle[3], n)
+    coeffs = jnp.concatenate([middle[0] - nn_dot(middle[1], gamma), gamma], axis=0)
     for j in range(data // n):
         value = v_ref[:, lanes(j)]
         following = next_ref[:, lanes(j)]
-        second_image = sum_rows(parts, rows(j, n)) + prior[:, lanes(j)] * following
+        second_image = own_sum(keep, near, far, j, n) + prior[:, lanes(j)] * following
         x_ref[:, lanes(j)] = tn_dot(coeffs, jnp.concatenate([value, following], axis=0))
         r_ref[:, lanes(j)] = value - tn_dot(
             coeffs, jnp.concatenate([image_ref[:, lanes(j)], second_image], axis=0)
         )
 
 
-def shifted(x, axis, shift):
-    count = lax.axis_size(axis)
-    return lax.ppermute(x, axis, [(i, (i + shift) % count) for i in range(count)])
-
-
 def swapped(x, axis, flip):
     return lax.ppermute(x, axis, [(i, i ^ flip) for i in range(lax.axis_size(axis))])
 
 
 def gather(x, axis):
-    return tuple([x] + [shifted(x, axis, s) for s in range(1, lax.axis_size(axis))])
-
-
-def exchange(parts, axis):
-    return tuple([parts[0]] + [shifted(x, axis, s) for s, x in enumerate(parts) if s])
+    even = [x] + [swapped(x, axis, flip) for flip in range(2, lax.axis_size(axis), 2)]
+    return tuple(part for own in even for part in (own, swapped(own, axis, 1)))
 
 
 def shards(right_side, prior, blocks, block_row, block_col):
@@ -341,7 +382,7 @@
         keep, send = call(
             lambda *refs: forward_kernel(stretch, n_cols, *refs),
             (shape((size, BLOCK)),) * 2,
-            (index, search, staged, gram, half),
+            (index, search, turned if half else staged, gram, half),
             [
                 pltpu.VMEM((row_span, frames, BLOCK), F32),
                 pltpu.VMEM((col_span, frames, BLOCK), BF16),
@@ -362,10 +403,18 @@
         return foot, swapped(foot, "col", 1), first
 
     def backward(own_foot, other_foot, last):
-        size = stretch * frames + frames + (0 if last else DIAG)
-        parts, norm = call(
+        size = stretch * frames
+        extra = frames + (0 if last else DIAG)
+        pairs = n_rows // 2 - 1
+        far, near, kept, keep, norm = call(
             lambda *refs: backward_kernel(stretch, n_cols, last, *refs),
-            ((shape((size, BLOCK), BF16),) * n_rows, (shape((frames, frames)),) if last else ()),
+            (
+                tuple(shape((size + (0 if p else extra), BLOCK), BF16) for p in range(pairs)),
+                shape((size, BLOCK), BF16),
+                (shape((size, BLOCK)),) * pairs,
+                shape((size, BLOCK)),
+                (shape((frames, frames)),) if last else (),
+            ),
             (index, own_foot, other_foot, staged),
             [
                 pltpu.VMEM((col_span, frames, BLOCK), F32),
@@ -373,7 +422,19 @@
                 pltpu.VMEM((frames, 2 * frames), F32),
             ],
         )
-        return exchange(parts, "row"), norm
+        received = tuple(swapped(x, "row", 1) for x in far)
+        near = swapped(near, "row", 1)
+        sums, gram, tile = call(
+            lambda *refs: rows_kernel(last, frames, *refs),
+            (
+                (shape((size + extra, BLOCK), BF16),) * pairs,
+                shape((frames, frames) if last else (frames // 2, 2 * frames)),
+                () if last else (shape((DIAG, 2 * frames), BF16),),
+            ),
+            (far[0], received, kept),
+        )
+        far = tuple(swapped(x, "row", 2 * (p + 1)) for p, x in enumerate(sums))
+        return (keep, near, far, gram, *tile), norm
 
     (cast,) = call(cast_kernel, (cast_type,), (right_side,))
     search = gather(cast, "row")
@@ -387,22 +448,25 @@
     )
     (gram,) = call(gram_kernel, (gram_type,), (right_side, prior), cost=aside)
     own_foot, other_foot, _ = forward(search, gram, ())
+    (turned,) = call(turn_kernel, (shape(blocks.shape, BF16),), (staged,), cost=aside)
     parts, _ = backward(own_foot, other_foot, False)
     image, following, cast, half, diagonal = call(
         image_kernel,
         (own, own, cast_type, shape((frames // 2, 2 * frames)), shape((DIAG, 2 * frames))),
-        (parts, right_side, prior),
+        (*parts, right_side, prior),
     )
     search = gather(cast, "row")
     (gram,) = call(gram_kernel, (gram_type,), (following, prior), cost=aside)
     own_foot, other_foot, (first,) = forward(search, gram, (half,))
-    (inverse,) = call(inverse_kernel, (shape((frames, frames)),), (first,), cost=aside)
     parts, (norm,) = backward(own_foot, other_foot, True)
+    (middle,) = call(
+        middle_kernel, (shape((4, frames, frames)),), (first, norm, diagonal), cost=aside
+    )
     return tuple(
         call(
             final_kernel,
             (own, own),
-            (parts, right_side, image, following, prior, first, inverse, norm, diagonal),
+            (*parts, right_side, image, following, prior, middle),
         )
     )
 

time: 74 us -> 73.7 us (level)
  starting transfers between devices: 21.8 us -> 25.9 us
  waiting for transfers between devices: 30.8 us -> 28.9 us
  local copies, waits for them, and re-layouts: 2.8 us -> 1.6 us
  Pallas kernels: 17.5 us -> 16.3 us
    ppermute x6 -> x18, starting transfers between devices: 3.4 us -> 25.9 us  [swapped(): lax.ppermute(x, axis, [(i, i ^ flip) for i in range(lax.axis_size(axis))])]
    ppermute x12 -> x0, starting transfers between devices: 18.4 us -> none  [shifted(): lax.ppermute(x, axis, [(i, (i + shift) % count) for i in range(count)])]
    ppermute x12 -> x0, waiting for transfers between devices: 16.2 us -> none  [shifted(): lax.ppermute(x, axis, [(i, (i + shift) % count) for i in range(count)])]
    ppermute x6 -> x18, waiting for transfers between devices: 14.7 us -> 28.9 us  [swapped(): lax.ppermute(x, axis, [(i, i ^ flip) for i in range(lax.axis_size(axis))])]
    pallas_call x15 -> x18, Pallas kernels: 17.5 us -> 16.3 us  [call(): pl.pallas_call(body, out_shape=flat_outs, in_specs=specs or [space(x) for...]
    unnamed x14, local copies, waits for them, and re-layouts: 2.8 us -> 1.6 us
  transfers between devices with their start and end apart: 18 -> 18, of which waited for: 13 -> 14; matrix products, arithmetic and copies ran while one was open for 0% -> 0% of each run, Pallas kernels for 7% -> 8%
where the time goes in v5:
time: 73.7 us; the launch traced here: 73.5 us
  waiting for transfers between devices  28.9 us (39%)
  starting transfers between devices  25.9 us (35%)
  Pallas kernels  16.3 us (22%)
  local copies, waits for them, and re-layouts  1.6 us (2%)
  between operations  0.81 us (1%)
    ppermute x18, waiting for transfers between devices, swapped(): lax.ppermute(x, axis, [(i, i ^ flip) for i in range(lax.axis_size(axis))])  28.9 us
    ppermute x18, starting transfers between devices, swapped(): lax.ppermute(x, axis, [(i, i ^ flip) for i in range(lax.axis_size(axis))])  25.9 us
    pallas_call x18, Pallas kernels, call(): pl.pallas_call(body, out_shape=flat_outs, in_specs=specs or [space(x) for...  16.3 us
    unnamed x14, local copies, waits for them, and re-layouts  1.6 us
  transfers between devices with their start and end apart: 18, of which 14 were waited for; matrix products, arithmetic and copies ran while one was open for 0% of the time, Pallas kernels for 8%

profile of v5, /device:TPU:0, one launch (start us, length us, event | category | flops | bytes accessed | tf_op | source)
XLA Modules:
  0.0 73.5 jit_solution(8449189125906580216)
XLA Ops:
  0.6 0.9 %copy-done = f32[64,512]{1,0:T(8,128)S(1)} copy-done((f32[64,512]{1,0:T(8,128)S(1)}, f32[64,512]{1,0:T(8,128)}, u32[]{:S(2)}) %copy-start) | copy-done | bytes 131096
  1.5 4.1 %collective-permute-start.1 = (bf16[256,128]{1,0:T(8,128)(2,1)S(1)}, bf16[256,128]{1,0:T(8,128)(2,1)S(1)}, u32[]{:S(2)}, u32[]{:S(2)}) collective-permute-start(bf16[256,128]{1,0:T(8,128)(2,1)S(1)} %shard_map.69.refs_1_), channel_id=1, source_target_pairs={{0,8},{4,12},{8,0},{12,4},{1,9},{5,13},{9,1},{13,5},{2,10},{6,14},... | collective-permute-start | bytes 196616 | tf_op jit(solution)/shard_map/ppermute | solution.py:355
  5.7 1.6 %collective-permute-start = (bf16[256,128]{1,0:T(8,128)(2,1)S(1)}, bf16[256,128]{1,0:T(8,128)(2,1)S(1)}, u32[]{:S(2)}, u32[]{:S(2)}) collective-permute-start(bf16[256,128]{1,0:T(8,128)(2,1)S(1)} %shard_map.69.refs_1_), channel_id=1, source_target_pairs={{0,4},{4,0},{8,12},{12,8},{1,5},{5,1},{9,13},{13,9},{2,6},{6,2},{1... | collective-permute-start | bytes 196616 | tf_op jit(solution)/shard_map/ppermute | solution.py:355
  8.7 1.4 %collective-permute-start.2 = (bf16[256,128]{1,0:T(8,128)(2,1)S(1)}, bf16[256,128]{1,0:T(8,128)(2,1)S(1)}, u32[]{:S(2)}, u32[]{:S(2)}) collective-permute-start(bf16[256,128]{1,0:T(8,128)(2,1)S(1)} %collective-permute-done.1.refs_3_), channel_id=1, source_target_pairs={{0,4},{4,0},{8,12},{12,8},{1,5},{5,1},{9,13},{13,9},{2,6},{6,2},{1... | collective-permute-start | bytes 196616 | tf_op jit(solution)/shard_map/ppermute | solution.py:355
  10.1 1.6 %shard_map.68 = (s32[2,64]{1,0:T(2,128)S(1)}, bf16[64,128,128]{2,1,0:T(8,128)(2,1)S(1)}) custom-call(s32[64]{0:T(128)S(1)} %copy-done.5, s32[64]{0:T(128)S(1)} %copy-done.6, bf16[64,128,128]{2,1,0:T(8,128)(2,1)S(1)} %copy-done.4), custom_call_target="tpu_custom_call" | custom-call | flops 2000000000 | bytes 8000000 | tf_op jit(solution)/shard_map/pallas_call | solution.py:52
  11.7 1.2 %collective-permute-done.2.refs_4_ = bf16[256,128]{1,0:T(8,128)(2,1)S(1)} collective-permute-done((bf16[256,128]{1,0:T(8,128)(2,1)S(1)}, bf16[256,128]{1,0:T(8,128)(2,1)S(1)}, u32[]{:S(2)}, u32[]{:S(2)}) %collective-permute-start.2) | collective-permute-done | bytes 65568 | tf_op jit(solution)/shard_map/ppermute | solution.py:355
  13.0 2.1 %shard_map.71 = (f32[576,128]{1,0:T(8,128)S(1)}, f32[576,128]{1,0:T(8,128)S(1)}) custom-call(s32[2,64]{1,0:T(2,128)S(1)} %get-tuple-element.29.refs_0_, bf16[256,128]{1,0:T(8,128)(2,1)S(1)} %shard_map.69.refs_1_, bf16[256,128]{1,0:T(8,128)(2,1)S(1)} %collective-permute-done.refs_2_, bf16[256,128]{1,0:T(8,128)(2,1)S(1)} %collective-permute-done.1.refs_3_, ...), custom_call_target="tpu_custom_call" | custom-call | tf_op jit(solution)/shard_map/pallas_call | solution.py:52
  15.2 1.6 %collective-permute-done.3.refs_1_ = f32[576,128]{1,0:T(8,128)S(1)} collective-permute-done((f32[576,128]{1,0:T(8,128)S(1)}, f32[576,128]{1,0:T(8,128)S(1)}, u32[]{:S(2)}, u32[]{:S(2)}) %collective-permute-start.3) | collective-permute-done | bytes 294944 | tf_op jit(solution)/shard_map/ppermute | solution.py:355
  16.8 1.9 %collective-permute-start.4 = (bf16[576,128]{1,0:T(8,128)(2,1)S(1)}, bf16[576,128]{1,0:T(8,128)(2,1)S(1)}, u32[]{:S(2)}, u32[]{:S(2)}) collective-permute-start(bf16[576,128]{1,0:T(8,128)(2,1)S(1)} %shard_map.72.refs_0_), channel_id=1, source_target_pairs={{0,2},{1,3},{2,0},{3,1},{4,6},{5,7},{6,4},{7,5},{8,10},{9,11},{10,... | collective-permute-start | bytes 442376 | tf_op jit(solution)/shard_map/ppermute | solution.py:355
  18.7 4.1 %collective-permute-done.4.refs_1_ = bf16[576,128]{1,0:T(8,128)(2,1)S(1)} collective-permute-done((bf16[576,128]{1,0:T(8,128)(2,1)S(1)}, bf16[576,128]{1,0:T(8,128)(2,1)S(1)}, u32[]{:S(2)}, u32[]{:S(2)}) %collective-permute-start.4) | collective-permute-done | bytes 147488 | tf_op jit(solution)/shard_map/ppermute | solution.py:355
  23.0 1.4 %collective-permute-done.5.refs_2_ = bf16[576,128]{1,0:T(8,128)(2,1)S(1)} collective-permute-done((bf16[576,128]{1,0:T(8,128)(2,1)S(1)}, bf16[576,128]{1,0:T(8,128)(2,1)S(1)}, u32[]{:S(2)}, u32[]{:S(2)}) %collective-permute-start.5) | collective-permute-done | bytes 147488 | tf_op jit(solution)/shard_map/ppermute | solution.py:355
  24.3 1.4 %shard_map.74 = (bf16[336,128]{1,0:T(8,128)(2,1)S(1)}, bf16[256,128]{1,0:T(8,128)(2,1)S(1)}, f32[256,128]{1,0:T(8,128)S(1)}, f32[256,128]{1,0:T(8,128)S(1)}) custom-call(s32[2,64]{1,0:T(2,128)S(1)} %get-tuple-element.29.refs_0_, bf16[576,128]{1,0:T(8,128)(2,1)S(1)} %shard_map.73.refs_1_, bf16[576,128]{1,0:T(8,128)(2,1)S(1)} %collective-permute-done.5.refs_2_, ...), custom_call_target="tpu_custom_call" | custom-call | tf_op jit(solution)/shard_map/pallas_call | solution.py:52
  25.8 1.3 %collective-permute-start.7 = (bf16[336,128]{1,0:T(8,128)(2,1)S(1)}, bf16[336,128]{1,0:T(8,128)(2,1)S(1)}, u32[]{:S(2)}, u32[]{:S(2)}) collective-permute-start(bf16[336,128]{1,0:T(8,128)(2,1)S(1)} %get-tuple-element.35.refs_0_), channel_id=1, source_target_pairs={{0,4},{4,0},{8,12},{12,8},{1,5},{5,1},{9,13},{13,9},{2,6},{6,2},{1... | collective-permute-start | bytes 258056 | tf_op jit(solution)/shard_map/ppermute | solution.py:355
  27.1 3.3 %collective-permute-done.7.refs_1_ = bf16[336,128]{1,0:T(8,128)(2,1)S(1)} collective-permute-done((bf16[336,128]{1,0:T(8,128)(2,1)S(1)}, bf16[336,128]{1,0:T(8,128)(2,1)S(1)}, u32[]{:S(2)}, u32[]{:S(2)}) %collective-permute-start.7) | collective-permute-done | bytes 86048 | tf_op jit(solution)/shard_map/ppermute | solution.py:355
  30.5 2.8 %collective-permute-start.8 = (bf16[336,128]{1,0:T(8,128)(2,1)S(1)}, bf16[336,128]{1,0:T(8,128)(2,1)S(1)}, u32[]{:S(2)}, u32[]{:S(2)}) collective-permute-start(bf16[336,128]{1,0:T(8,128)(2,1)S(1)} %get-tuple-element.37), channel_id=1, source_target_pairs={{0,8},{4,12},{8,0},{12,4},{1,9},{5,13},{9,1},{13,5},{2,10},{6,14},... | collective-permute-start | bytes 258056 | tf_op jit(solution)/shard_map/ppermute | solution.py:355
  33.2 1.7 %collective-permute-start.6 = (bf16[256,128]{1,0:T(8,128)(2,1)S(1)}, bf16[256,128]{1,0:T(8,128)(2,1)S(1)}, u32[]{:S(2)}, u32[]{:S(2)}) collective-permute-start(bf16[256,128]{1,0:T(8,128)(2,1)S(1)} %get-tuple-element.34), channel_id=1, source_target_pairs={{0,4},{4,0},{8,12},{12,8},{1,5},{5,1},{9,13},{13,9},{2,6},{6,2},{1... | collective-permute-start | bytes 196616 | tf_op jit(solution)/shard_map/ppermute | solution.py:355
  35.0 2.6 %collective-permute-done.6.refs_1_ = bf16[256,128]{1,0:T(8,128)(2,1)S(1)} collective-permute-done((bf16[256,128]{1,0:T(8,128)(2,1)S(1)}, bf16[256,128]{1,0:T(8,128)(2,1)S(1)}, u32[]{:S(2)}, u32[]{:S(2)}) %collective-permute-start.6) | collective-permute-done | bytes 65568 | tf_op jit(solution)/shard_map/ppermute | solution.py:355
  37.9 1.7 %collective-permute-start.10 = (bf16[256,128]{1,0:T(8,128)(2,1)S(1)}, bf16[256,128]{1,0:T(8,128)(2,1)S(1)}, u32[]{:S(2)}, u32[]{:S(2)}) collective-permute-start(bf16[256,128]{1,0:T(8,128)(2,1)S(1)} %get-tuple-element.40.refs_1_), channel_id=1, source_target_pairs={{0,8},{4,12},{8,0},{12,4},{1,9},{5,13},{9,1},{13,5},{2,10},{6,14},... | collective-permute-start | bytes 196616 | tf_op jit(solution)/shard_map/ppermute | solution.py:355
  40.1 2.2 %collective-permute-start.9 = (bf16[256,128]{1,0:T(8,128)(2,1)S(1)}, bf16[256,128]{1,0:T(8,128)(2,1)S(1)}, u32[]{:S(2)}, u32[]{:S(2)}) collective-permute-start(bf16[256,128]{1,0:T(8,128)(2,1)S(1)} %get-tuple-element.40.refs_1_), channel_id=1, source_target_pairs={{0,4},{4,0},{8,12},{12,8},{1,5},{5,1},{9,13},{13,9},{2,6},{6,2},{1... | collective-permute-start | bytes 196616 | tf_op jit(solution)/shard_map/ppermute | solution.py:355
  43.2 1.5 %collective-permute-start.11 = (bf16[256,128]{1,0:T(8,128)(2,1)S(1)}, bf16[256,128]{1,0:T(8,128)(2,1)S(1)}, u32[]{:S(2)}, u32[]{:S(2)}) collective-permute-start(bf16[256,128]{1,0:T(8,128)(2,1)S(1)} %collective-permute-done.10.refs_3_), channel_id=1, source_target_pairs={{0,4},{4,0},{8,12},{12,8},{1,5},{5,1},{9,13},{13,9},{2,6},{6,2},{1... | collective-permute-start | bytes 196616 | tf_op jit(solution)/shard_map/ppermute | solution.py:355
  45.1 2.3 %collective-permute-done.11.refs_4_ = bf16[256,128]{1,0:T(8,128)(2,1)S(1)} collective-permute-done((bf16[256,128]{1,0:T(8,128)(2,1)S(1)}, bf16[256,128]{1,0:T(8,128)(2,1)S(1)}, u32[]{:S(2)}, u32[]{:S(2)}) %collective-permute-start.11) | collective-permute-done | bytes 65568 | tf_op jit(solution)/shard_map/ppermute | solution.py:355
  47.5 1.4 %shard_map.79 = (f32[608,128]{1,0:T(8,128)S(1)}, f32[608,128]{1,0:T(8,128)S(1)}) custom-call(s32[2,64]{1,0:T(2,128)S(1)} %get-tuple-element.29.refs_0_, bf16[256,128]{1,0:T(8,128)(2,1)S(1)} %get-tuple-element.40.refs_1_, bf16[256,128]{1,0:T(8,128)(2,1)S(1)} %collective-permute-done.9.refs_2_, bf16[256,128]{1,0:T(8,128)(2,1)S(1)} %collective-permute-done.10.refs_3_, ...), custom_call_target="tpu_custom_call" | custom-call | tf_op jit(solution)/shard_map/pallas_call | solution.py:52
  48.9 1.6 %collective-permute-done.12.refs_1_ = f32[608,128]{1,0:T(8,128)S(1)} collective-permute-done((f32[608,128]{1,0:T(8,128)S(1)}, f32[608,128]{1,0:T(8,128)S(1)}, u32[]{:S(2)}, u32[]{:S(2)}) %collective-permute-start.12) | collective-permute-done | bytes 311328 | tf_op jit(solution)/shard_map/ppermute | solution.py:355
  50.5 1.6 %collective-permute-start.13 = (bf16[576,128]{1,0:T(8,128)(2,1)S(1)}, bf16[576,128]{1,0:T(8,128)(2,1)S(1)}, u32[]{:S(2)}, u32[]{:S(2)}) collective-permute-start(bf16[576,128]{1,0:T(8,128)(2,1)S(1)} %get-tuple-element.45.refs_0_), channel_id=1, source_target_pairs={{0,2},{1,3},{2,0},{3,1},{4,6},{5,7},{6,4},{7,5},{8,10},{9,11},{10,... | collective-permute-start | bytes 442376 | tf_op jit(solution)/shard_map/ppermute | solution.py:355
  52.1 4.4 %collective-permute-done.13.refs_1_ = bf16[576,128]{1,0:T(8,128)(2,1)S(1)} collective-permute-done((bf16[576,128]{1,0:T(8,128)(2,1)S(1)}, bf16[576,128]{1,0:T(8,128)(2,1)S(1)}, u32[]{:S(2)}, u32[]{:S(2)}) %collective-permute-start.13) | collective-permute-done | bytes 147488 | tf_op jit(solution)/shard_map/ppermute | solution.py:355
  56.6 1.4 %collective-permute-done.14.refs_2_ = bf16[576,128]{1,0:T(8,128)(2,1)S(1)} collective-permute-done((bf16[576,128]{1,0:T(8,128)(2,1)S(1)}, bf16[576,128]{1,0:T(8,128)(2,1)S(1)}, u32[]{:S(2)}, u32[]{:S(2)}) %collective-permute-start.14) | collective-permute-done | bytes 147488 | tf_op jit(solution)/shard_map/ppermute | solution.py:355
  58.0 1.5 %shard_map.82 = (bf16[320,128]{1,0:T(8,128)(2,1)S(1)}, bf16[256,128]{1,0:T(8,128)(2,1)S(1)}, f32[256,128]{1,0:T(8,128)S(1)}, f32[256,128]{1,0:T(8,128)S(1)}, f32[64,64]{1,0:T(8,128)S(1)}) custom-call(s32[2,64]{1,0:T(2,128)S(1)} %get-tuple-element.29.refs_0_, bf16[576,128]{1,0:T(8,128)(2,1)S(1)} %shard_map.81.refs_1_, ...), custom_call_target="tpu_custom_call" | custom-call | tf_op jit(solution)/shard_map/pallas_call | solution.py:52
  59.5 1.6 %collective-permute-start.16 = (bf16[320,128]{1,0:T(8,128)(2,1)S(1)}, bf16[320,128]{1,0:T(8,128)(2,1)S(1)}, u32[]{:S(2)}, u32[]{:S(2)}) collective-permute-start(bf16[320,128]{1,0:T(8,128)(2,1)S(1)} %get-tuple-element.48.refs_0_), channel_id=1, source_target_pairs={{0,4},{4,0},{8,12},{12,8},{1,5},{5,1},{9,13},{13,9},{2,6},{6,2},{1... | collective-permute-start | bytes 245768 | tf_op jit(solution)/shard_map/ppermute | solution.py:355
  61.5 3.1 %collective-permute-done.16.refs_1_ = bf16[320,128]{1,0:T(8,128)(2,1)S(1)} collective-permute-done((bf16[320,128]{1,0:T(8,128)(2,1)S(1)}, bf16[320,128]{1,0:T(8,128)(2,1)S(1)}, u32[]{:S(2)}, u32[]{:S(2)}) %collective-permute-start.16) | collective-permute-done | bytes 81952 | tf_op jit(solution)/shard_map/ppermute | solution.py:355
  64.8 1.8 %collective-permute-start.17 = (bf16[320,128]{1,0:T(8,128)(2,1)S(1)}, bf16[320,128]{1,0:T(8,128)(2,1)S(1)}, u32[]{:S(2)}, u32[]{:S(2)}) collective-permute-start(bf16[320,128]{1,0:T(8,128)(2,1)S(1)} %get-tuple-element.50), channel_id=1, source_target_pairs={{0,8},{4,12},{8,0},{12,4},{1,9},{5,13},{9,1},{13,5},{2,10},{6,14},... | collective-permute-start | bytes 245768 | tf_op jit(solution)/shard_map/ppermute | solution.py:355
  66.6 2.9 %shard_map.84.refs_8_ = f32[4,64,64]{2,1,0:T(8,128)S(1)} custom-call(f32[64,128]{1,0:T(8,128)S(1)} %get-tuple-element.53.refs_0_, f32[64,64]{1,0:T(8,128)S(1)} %get-tuple-element.54.refs_1_, f32[16,128]{1,0:T(8,128)S(1)} %get-tuple-element.55.refs_2_), custom_call_target="tpu_custom_call" | custom-call | flops 2000000000 | bytes 8000000 | tf_op jit(solution)/shard_map/pallas_call | solution.py:52
  70.1 3.4 %shard_map.85 = (f32[64,512]{1,0:T(8,128)}, f32[64,512]{1,0:T(8,128)}) custom-call(f32[256,128]{1,0:T(8,128)S(1)} %get-tuple-element.46.refs_0_, bf16[256,128]{1,0:T(8,128)(2,1)S(1)} %collective-permute-done.15.refs_1_, bf16[320,128]{1,0:T(8,128)(2,1)S(1)} %collective-permute-done.17.refs_2_, f32[64,64]{1,0:T(8,128)S(1)} %get-tuple-element.51.refs_3_, ...), custom_call_target="tpu_custom_call" | custom-call | tf_op jit(solution)/shard_map/pallas_call | solution.py:52
  (36 shorter events, 5.3 us)
Async XLA Ops:
  0.6 0.9 %copy-start = (f32[64,512]{1,0:T(8,128)S(1)}, f32[64,512]{1,0:T(8,128)}, u32[]{:S(2)}) copy-start(f32[64,512]{1,0:T(8,128)} %refs_4_.1) | copy-start | bytes 393220
  1.5 7.2 %collective-permute-start.1 = (bf16[256,128]{1,0:T(8,128)(2,1)S(1)}, bf16[256,128]{1,0:T(8,128)(2,1)S(1)}, u32[]{:S(2)}, u32[]{:S(2)}) collective-permute-start(bf16[256,128]{1,0:T(8,128)(2,1)S(1)} %shard_map.69.refs_1_), channel_id=1, source_target_pairs={{0,8},{4,12},{8,0},{12,4},{1,9},{5,13},{9,1},{13,5},{2,10},{6,14},... | collective-permute-start | bytes 196616 | tf_op jit(solution)/shard_map/ppermute | solution.py:355
  5.7 6.1 %collective-permute-start = (bf16[256,128]{1,0:T(8,128)(2,1)S(1)}, bf16[256,128]{1,0:T(8,128)(2,1)S(1)}, u32[]{:S(2)}, u32[]{:S(2)}) collective-permute-start(bf16[256,128]{1,0:T(8,128)(2,1)S(1)} %shard_map.69.refs_1_), channel_id=1, source_target_pairs={{0,4},{4,0},{8,12},{12,8},{1,5},{5,1},{9,13},{13,9},{2,6},{6,2},{1... | collective-permute-start | bytes 196616 | tf_op jit(solution)/shard_map/ppermute | solution.py:355
  7.2 0.7 copy-start.2
  7.9 2.2 %copy-start.4 = (bf16[64,128,128]{2,1,0:T(8,128)(2,1)S(1)}, bf16[64,128,128]{2,1,0:T(8,128)(2,1)}, u32[]{:S(2)}) copy-start(bf16[64,128,128]{2,1,0:T(8,128)(2,1)} %refs_2_.1) | copy-start | bytes 6291460
  7.9 2.2 %copy-start.5 = (s32[64]{0:T(128)S(1)}, s32[64]{0:T(128)}, u32[]{:S(2)}) copy-start(s32[64]{0:T(128)} %refs_0_.3) | copy-start | bytes 772
  7.9 2.2 %copy-start.6 = (s32[64]{0:T(128)S(1)}, s32[64]{0:T(128)}, u32[]{:S(2)}) copy-start(s32[64]{0:T(128)} %refs_1_.1) | copy-start | bytes 772
  8.7 4.3 %collective-permute-start.2 = (bf16[256,128]{1,0:T(8,128)(2,1)S(1)}, bf16[256,128]{1,0:T(8,128)(2,1)S(1)}, u32[]{:S(2)}, u32[]{:S(2)}) collective-permute-start(bf16[256,128]{1,0:T(8,128)(2,1)S(1)} %collective-permute-done.1.refs_3_), channel_id=1, source_target_pairs={{0,4},{4,0},{8,12},{12,8},{1,5},{5,1},{9,13},{13,9},{2,6},{6,2},{1... | collective-permute-start | bytes 196616 | tf_op jit(solution)/shard_map/ppermute | solution.py:355
  15.1 22.5 %copy-start.1 = (f32[64,512]{1,0:T(8,128)S(1)}, f32[64,512]{1,0:T(8,128)}, u32[]{:S(2)}) copy-start(f32[64,512]{1,0:T(8,128)} %refs_4_.1) | copy-start | bytes 393220
  15.1 1.6 %collective-permute-start.3 = (f32[576,128]{1,0:T(8,128)S(1)}, f32[576,128]{1,0:T(8,128)S(1)}, u32[]{:S(2)}, u32[]{:S(2)}) collective-permute-start(f32[576,128]{1,0:T(8,128)S(1)} %get-tuple-element.32), channel_id=1, source_target_pairs={{0,1},{1,0},{2,3},{3,2},{4,5},{5,4},{6,7},{7,6},{8,9},{9,8},{10,11... | collective-permute-start | bytes 884744 | tf_op jit(solution)/shard_map/ppermute | solution.py:355
  16.8 6.1 %collective-permute-start.4 = (bf16[576,128]{1,0:T(8,128)(2,1)S(1)}, bf16[576,128]{1,0:T(8,128)(2,1)S(1)}, u32[]{:S(2)}, u32[]{:S(2)}) collective-permute-start(bf16[576,128]{1,0:T(8,128)(2,1)S(1)} %shard_map.72.refs_0_), channel_id=1, source_target_pairs={{0,2},{1,3},{2,0},{3,1},{4,6},{5,7},{6,4},{7,5},{8,10},{9,11},{10,... | collective-permute-start | bytes 442376 | tf_op jit(solution)/shard_map/ppermute | solution.py:355
  22.9 1.4 %collective-permute-start.5 = (bf16[576,128]{1,0:T(8,128)(2,1)S(1)}, bf16[576,128]{1,0:T(8,128)(2,1)S(1)}, u32[]{:S(2)}, u32[]{:S(2)}) collective-permute-start(bf16[576,128]{1,0:T(8,128)(2,1)S(1)} %shard_map.73.refs_1_), channel_id=1, source_target_pairs={{0,1},{1,0},{2,3},{3,2},{4,5},{5,4},{6,7},{7,6},{8,9},{9,8},{10,11... | collective-permute-start | bytes 442376 | tf_op jit(solution)/shard_map/ppermute | solution.py:355
  25.8 4.6 %collective-permute-start.7 = (bf16[336,128]{1,0:T(8,128)(2,1)S(1)}, bf16[336,128]{1,0:T(8,128)(2,1)S(1)}, u32[]{:S(2)}, u32[]{:S(2)}) collective-permute-start(bf16[336,128]{1,0:T(8,128)(2,1)S(1)} %get-tuple-element.35.refs_0_), channel_id=1, source_target_pairs={{0,4},{4,0},{8,12},{12,8},{1,5},{5,1},{9,13},{13,9},{2,6},{6,2},{1... | collective-permute-start | bytes 258056 | tf_op jit(solution)/shard_map/ppermute | solution.py:355
  30.5 7.2 %collective-permute-start.8 = (bf16[336,128]{1,0:T(8,128)(2,1)S(1)}, bf16[336,128]{1,0:T(8,128)(2,1)S(1)}, u32[]{:S(2)}, u32[]{:S(2)}) collective-permute-start(bf16[336,128]{1,0:T(8,128)(2,1)S(1)} %get-tuple-element.37), channel_id=1, source_target_pairs={{0,8},{4,12},{8,0},{12,4},{1,9},{5,13},{9,1},{13,5},{2,10},{6,14},... | collective-permute-start | bytes 258056 | tf_op jit(solution)/shard_map/ppermute | solution.py:355
  33.2 4.4 %collective-permute-start.6 = (bf16[256,128]{1,0:T(8,128)(2,1)S(1)}, bf16[256,128]{1,0:T(8,128)(2,1)S(1)}, u32[]{:S(2)}, u32[]{:S(2)}) collective-permute-start(bf16[256,128]{1,0:T(8,128)(2,1)S(1)} %get-tuple-element.34), channel_id=1, source_target_pairs={{0,4},{4,0},{8,12},{12,8},{1,5},{5,1},{9,13},{13,9},{2,6},{6,2},{1... | collective-permute-start | bytes 196616 | tf_op jit(solution)/shard_map/ppermute | solution.py:355
  37.9 6.9 %copy-start.3 = (f32[512]{0:T(512)S(1)}, f32[512]{0:T(512)}, u32[]{:S(2)}) copy-start(f32[512]{0:T(512)} %param.6) | copy-start | bytes 6148
  37.9 5.3 %collective-permute-start.10 = (bf16[256,128]{1,0:T(8,128)(2,1)S(1)}, bf16[256,128]{1,0:T(8,128)(2,1)S(1)}, u32[]{:S(2)}, u32[]{:S(2)}) collective-permute-start(bf16[256,128]{1,0:T(8,128)(2,1)S(1)} %get-tuple-element.40.refs_1_), channel_id=1, source_target_pairs={{0,8},{4,12},{8,0},{12,4},{1,9},{5,13},{9,1},{13,5},{2,10},{6,14},... | collective-permute-start | bytes 196616 | tf_op jit(solution)/shard_map/ppermute | solution.py:355
  40.1 5.0 %collective-permute-start.9 = (bf16[256,128]{1,0:T(8,128)(2,1)S(1)}, bf16[256,128]{1,0:T(8,128)(2,1)S(1)}, u32[]{:S(2)}, u32[]{:S(2)}) collective-permute-start(bf16[256,128]{1,0:T(8,128)(2,1)S(1)} %get-tuple-element.40.refs_1_), channel_id=1, source_target_pairs={{0,4},{4,0},{8,12},{12,8},{1,5},{5,1},{9,13},{13,9},{2,6},{6,2},{1... | collective-permute-start | bytes 196616 | tf_op jit(solution)/shard_map/ppermute | solution.py:355
  43.2 4.3 %collective-permute-start.11 = (bf16[256,128]{1,0:T(8,128)(2,1)S(1)}, bf16[256,128]{1,0:T(8,128)(2,1)S(1)}, u32[]{:S(2)}, u32[]{:S(2)}) collective-permute-start(bf16[256,128]{1,0:T(8,128)(2,1)S(1)} %collective-permute-done.10.refs_3_), channel_id=1, source_target_pairs={{0,4},{4,0},{8,12},{12,8},{1,5},{5,1},{9,13},{13,9},{2,6},{6,2},{1... | collective-permute-start | bytes 196616 | tf_op jit(solution)/shard_map/ppermute | solution.py:355
  48.8 1.7 %collective-permute-start.12 = (f32[608,128]{1,0:T(8,128)S(1)}, f32[608,128]{1,0:T(8,128)S(1)}, u32[]{:S(2)}, u32[]{:S(2)}) collective-permute-start(f32[608,128]{1,0:T(8,128)S(1)} %get-tuple-element.44), channel_id=1, source_target_pairs={{0,1},{1,0},{2,3},{3,2},{4,5},{5,4},{6,7},{7,6},{8,9},{9,8},{10,11... | collective-permute-start | bytes 933896 | tf_op jit(solution)/shard_map/ppermute | solution.py:355
  50.5 6.0 %collective-permute-start.13 = (bf16[576,128]{1,0:T(8,128)(2,1)S(1)}, bf16[576,128]{1,0:T(8,128)(2,1)S(1)}, u32[]{:S(2)}, u32[]{:S(2)}) collective-permute-start(bf16[576,128]{1,0:T(8,128)(2,1)S(1)} %get-tuple-element.45.refs_0_), channel_id=1, source_target_pairs={{0,2},{1,3},{2,0},{3,1},{4,6},{5,7},{6,4},{7,5},{8,10},{9,11},{10,... | collective-permute-start | bytes 442376 | tf_op jit(solution)/shard_map/ppermute | solution.py:355
  56.5 1.4 %collective-permute-start.14 = (bf16[576,128]{1,0:T(8,128)(2,1)S(1)}, bf16[576,128]{1,0:T(8,128)(2,1)S(1)}, u32[]{:S(2)}, u32[]{:S(2)}) collective-permute-start(bf16[576,128]{1,0:T(8,128)(2,1)S(1)} %shard_map.81.refs_1_), channel_id=1, source_target_pairs={{0,1},{1,0},{2,3},{3,2},{4,5},{5,4},{6,7},{7,6},{8,9},{9,8},{10,11... | collective-permute-start | bytes 442376 | tf_op jit(solution)/shard_map/ppermute | solution.py:355
  59.5 5.1 %collective-permute-start.16 = (bf16[320,128]{1,0:T(8,128)(2,1)S(1)}, bf16[320,128]{1,0:T(8,128)(2,1)S(1)}, u32[]{:S(2)}, u32[]{:S(2)}) collective-permute-start(bf16[320,128]{1,0:T(8,128)(2,1)S(1)} %get-tuple-element.48.refs_0_), channel_id=1, source_target_pairs={{0,4},{4,0},{8,12},{12,8},{1,5},{5,1},{9,13},{13,9},{2,6},{6,2},{1... | collective-permute-start | bytes 245768 | tf_op jit(solution)/shard_map/ppermute | solution.py:355
  61.0 8.4 %collective-permute-start.15 = (bf16[256,128]{1,0:T(8,128)(2,1)S(1)}, bf16[256,128]{1,0:T(8,128)(2,1)S(1)}, u32[]{:S(2)}, u32[]{:S(2)}) collective-permute-start(bf16[256,128]{1,0:T(8,128)(2,1)S(1)} %get-tuple-element.47), channel_id=1, source_target_pairs={{0,4},{4,0},{8,12},{12,8},{1,5},{5,1},{9,13},{13,9},{2,6},{6,2},{1... | collective-permute-start | bytes 196616 | tf_op jit(solution)/shard_map/ppermute | solution.py:355
  64.8 5.3 %collective-permute-start.17 = (bf16[320,128]{1,0:T(8,128)(2,1)S(1)}, bf16[320,128]{1,0:T(8,128)(2,1)S(1)}, u32[]{:S(2)}, u32[]{:S(2)}) collective-permute-start(bf16[320,128]{1,0:T(8,128)(2,1)S(1)} %get-tuple-element.50), channel_id=1, source_target_pairs={{0,8},{4,12},{8,0},{12,4},{1,9},{5,13},{9,1},{13,5},{2,10},{6,14},... | collective-permute-start | bytes 245768 | tf_op jit(solution)/shard_map/ppermute | solution.py:355

commit v6 on v5

v6 whole, which is shorter than its diff:
```python
import jax
import jax.numpy as jnp
from jax import lax
from jax.experimental import pallas as pl
from jax.experimental.pallas import tpu as pltpu
from jax.sharding import PartitionSpec as P

BLOCK = 128
TILE = 8
AHEAD = 4
DIAG = 16
F32, BF16 = jnp.float32, jnp.bfloat16
FP32 = lax.Precision.HIGHEST
VMEM = pl.BlockSpec(memory_space=pltpu.VMEM)
SMEM = pl.BlockSpec(memory_space=pltpu.SMEM)
ANY = pl.BlockSpec(memory_space=pl.ANY)


def nt_dot(a, b, precision=None):
    return lax.dot_general(
        a, b, (((1,), (1,)), ((), ())), precision=precision, preferred_element_type=F32
    )


def tn_dot(a, b):
    return lax.dot_general(
        a, b, (((0,), (0,)), ((), ())), precision=FP32, preferred_element_type=F32
    )


def nn_dot(a, b):
    return lax.dot_general(
        a, b, (((1,), (0,)), ((), ())), precision=FP32, preferred_element_type=F32
    )


def call(kernel, outs, ins, scratch=(), specs=None, cost=None):
    flat_ins, ins_tree = jax.tree.flatten(tuple(ins))
    flat_outs, outs_tree = jax.tree.flatten(tuple(outs))

    def body(*refs):
        middle, last = len(flat_ins), len(flat_ins) + len(flat_outs)
        kernel(
            *jax.tree.unflatten(ins_tree, refs[:middle]),
            *jax.tree.unflatten(outs_tree, refs[middle:last]),
            *refs[last:],
        )

    def space(x):
        return SMEM if x.dtype == jnp.int32 else VMEM

    results = pl.pallas_call(
        body,
        out_shape=flat_outs,
        in_specs=specs or [space(x) for x in flat_ins],
        out_specs=[space(x) for x in flat_outs],
        scratch_shapes=list(scratch),
        compiler_params=pltpu.CompilerParams(vmem_limit_bytes=48 * 1024 * 1024),
        cost_estimate=cost,
    )(*flat_ins)
    return jax.tree.unflatten(outs_tree, results)


def lanes(j):
    return slice(j * BLOCK, (j + 1) * BLOCK)


def rows(j, count):
    return slice(j * count, (j + 1) * count)


def split(value):
    high = value.astype(BF16)
    return high, (value - high.astype(F32)).astype(BF16)


def sum_rows(refs, at):
    total = refs[0][at, :].astype(F32)
    for ref in refs[1:]:
        total += ref[at, :].astype(F32)
    return total


def eye(n):
    return lax.broadcasted_iota(jnp.int32, (n, n), 0) == lax.broadcasted_iota(jnp.int32, (n, n), 1)


def cast_kernel(v_ref, out_ref):
    frames = v_ref.shape[0]
    for j in range(v_ref.shape[1] // BLOCK):
        out_ref[rows(j, frames), :] = v_ref[:, lanes(j)].astype(BF16)


def stage_kernel(row_span, stretch, brow, bcol, blocks, index_ref, out_ref, sem):
    copy = pltpu.make_async_copy(blocks, out_ref, sem)
    copy.start()
    for k in range(brow.shape[0]):
        index_ref[0, k] = lax.rem(brow[k], row_span)
        index_ref[1, k] = lax.div(bcol[k], row_span) * stretch + lax.rem(bcol[k], stretch)
    copy.wait()


def turn_kernel(blocks, out_ref):
    for k in range(blocks.shape[0]):
        out_ref[k] = blocks[k].T


def as_row(column):
    n = column.shape[0]
    return jnp.sum(jnp.where(eye(n), column, 0.0), axis=0, keepdims=True)


def as_tile(row):
    at = lax.broadcasted_iota(jnp.int32, (DIAG, row.shape[1]), 0)
    return jnp.where(at == 0, row, 0.0)


def split_tile(row):
    high, low = split(row)
    at = lax.broadcasted_iota(jnp.int32, (DIAG, row.shape[1]), 0)
    return jnp.where(at == 0, high.astype(F32), jnp.where(at == 1, low.astype(F32), 0.0)).astype(BF16)


def tile_row(tile):
    return tile[0:1, :] + tile[1:2, :]


def energy_kernel(v_ref, prior, out_ref):
    value = v_ref[...]
    plain = jnp.sum(value * value, axis=1, keepdims=True)
    weighted = jnp.sum(value * value * prior[...], axis=1, keepdims=True)
    out_ref[...] = as_tile(jnp.concatenate([as_row(plain), as_row(weighted)], axis=1))


def grams_kernel(v_ref, next_ref, prior, out_ref):
    n = v_ref.shape[0]
    for at, ref in ((slice(0, n), v_ref), (slice(n, 2 * n), next_ref)):
        value = ref[...]
        both = jnp.concatenate([value, value * prior[...]], axis=0)
        out_ref[at, :] = nt_dot(value, both, FP32)


def add_kernel(parts, out_ref):
    total = parts[0][...]
    for part in parts[1:]:
        total += part[...]
    out_ref[...] = total


def fill(panel, ref, at, stretch):
    frames = panel.shape[1]
    for j in range(stretch):
        panel[at * stretch + j] = ref[rows(j, frames), :]


def fill_foot(panel, own, received, stretch, cols):
    core = lax.rem(lax.axis_index("col"), 2)
    frames = panel.shape[1]
    for ref, side in ((own, core), (received, 1 - core)):
        for x in range(cols // 2):
            for j in range(stretch):
                panel[(2 * x + side) * stretch + j] = ref[rows(x * stretch + j, frames), :]


def foot_gram(own, received, data, frames):
    whole = jnp.concatenate(
        [ref[rows(j, frames), :] for ref in (own, received) for j in range(data // frames)], axis=1
    )
    return whole, jnp.concatenate([jnp.zeros_like(whole), whole], axis=0)


def first_grams_kernel(data, parts, own, received, out_ref):
    n = parts[0].shape[0] // 2
    total = parts[0][...]
    for part in parts[1:]:
        total += part[...]
    out_ref[...] = total
    out_ref[:n, :] += nt_dot(*foot_gram(own, received, data, n))


def second_gram_kernel(data, own, received, out_ref):
    n = out_ref.shape[0]
    whole, padded = foot_gram(own, received, data, n)
    gram = nt_dot(whole, whole)
    out_ref[...] = jnp.concatenate(split(gram), axis=1)


def second_pair_kernel(own, received, gram_ref, out_ref):
    n = own.shape[0]
    both = own[...].astype(F32) + received[...].astype(F32)
    value = both[:, :n] + both[:, n:]
    gram_ref[...] = value
    out_ref[...] = jnp.concatenate(split(value), axis=1)


def forward_kernel(stretch, cols, index, search, blocks, tile, keep_ref, send_ref, acc, panel):
    frames = panel.shape[1]
    me = lax.axis_index("row")
    for flip, ref in enumerate(search):
        fill(panel, ref, lax.bitwise_xor(me, flip), stretch)
    acc[...] = jnp.zeros_like(acc)
    for k in range(blocks.shape[0]):
        acc[index[0, k]] += jnp.dot(panel[index[1, k]], blocks[k], preferred_element_type=F32)
    core = lax.rem(lax.axis_index("col"), 2)
    for x in range(cols // 2):
        for j in range(stretch):
            at = rows(x * stretch + j, frames)
            keep_ref[at, :] = acc[(2 * x + core) * stretch + j]
            send_ref[at, :] = acc[(2 * x + 1 - core) * stretch + j]
    if tile:
        at = cols // 2 * stretch * frames
        keep_ref[at:, :] = tile[0][...]
        send_ref[at:, :] = tile[0][...]


def pair_kernel(data, frames, keep, received, out_ref):
    for j in range(data // frames):
        at = rows(j, frames)
        out_ref[at, :] = (keep[at, :] + received[at, :]).astype(BF16)
    if out_ref.shape[0] > data:
        out_ref[data:, :] = split_tile(keep[data : data + 1, :] + received[data : data + 1, :])


def chips_kernel(data, frames, parts, out_ref):
    for j in range(data // frames):
        at = rows(j, frames)
        out_ref[at, :] = sum_rows(parts, at).astype(BF16)
    if out_ref.shape[0] > data:
        out_ref[data:, :] = split_tile(tile_row(sum_rows(parts, slice(data, data + DIAG))))


def backward_kernel(
    stretch, cols, last, index, own, received, blocks,
    far_refs, near_ref, keep_refs, keep_ref, acc, panel,
):
    frames = panel.shape[1]
    data = cols // 2 * stretch * frames
    fill_foot(panel, own, received, stretch, cols)
    acc[...] = jnp.zeros_like(acc)
    for k in range(blocks.shape[0]):
        acc[index[1, k]] += jnp.dot(panel[index[0, k]], blocks[k], preferred_element_type=F32)
    me = lax.axis_index("row")
    for far, (far_ref, kept_ref) in enumerate(zip(far_refs, keep_refs)):
        shard = lax.bitwise_xor(me, 2 * (far + 1))
        other = lax.bitwise_xor(shard, 1)
        for j in range(stretch):
            kept_ref[rows(j, frames), :] = acc[shard * stretch + j]
            far_ref[rows(j, frames), :] = acc[other * stretch + j].astype(BF16)
    other = lax.bitwise_xor(me, 1)
    for j in range(stretch):
        keep_ref[rows(j, frames), :] = acc[me * stretch + j]
        near_ref[rows(j, frames), :] = acc[other * stretch + j].astype(BF16)
    if not last:
        squares = jnp.zeros((frames, BLOCK), F32)
        for b in range(panel.shape[0]):
            part = panel[b].astype(F32)
            squares += part * part
        energy = as_row(jnp.sum(squares, axis=1, keepdims=True))
        row = tile_row(own[data:, :].astype(F32))
        row += jnp.concatenate([jnp.zeros_like(energy), energy], axis=1)
        far_refs[0][stretch * frames :, :] = split_tile(row)


def rows_kernel(data, frames, sent, received, kept, out_refs):
    for out_ref, kept_ref, received_ref in zip(out_refs, kept, received):
        for j in range(data // frames):
            at = rows(j, frames)
            out_ref[at, :] = (kept_ref[at, :] + received_ref[at, :].astype(F32)).astype(BF16)
    if out_refs[0].shape[0] > data:
        tile = split_tile(tile_row(sum_rows((sent, received[0]), slice(data, data + DIAG))))
        for out_ref in out_refs:
            out_ref[data:, :] = tile


def own_sum(keep, near, far, j, frames):
    at = rows(j, frames)
    return keep[at, :] + sum_rows((near, *far), at)


def frame_shift(diagonal, frames):
    row = 1.25 * diagonal[:, frames:] / diagonal[:, :frames]
    return jnp.sum(jnp.where(eye(frames), row, 0.0), axis=1, keepdims=True), row


def image_kernel(
    keep, near, far, sent, v_ref, prior, image_ref, next_ref, cast_ref, diag_ref
):
    frames = v_ref.shape[0]
    data = cast_ref.shape[0]
    diagonal = tile_row(sum_rows((sent, *far), slice(data, data + DIAG)))
    diag_ref[...] = as_tile(diagonal)
    shift, _ = frame_shift(diagonal, frames)
    for j in range(data // frames):
        value = v_ref[:, lanes(j)]
        image = own_sum(keep, near, far, j, frames) + prior[:, lanes(j)] * value
        following = image - shift * value
        image_ref[:, lanes(j)] = image
        next_ref[:, lanes(j)] = following
        cast_ref[rows(j, frames), :] = following.astype(BF16)


def eliminate(matrix, right, n):
    width = matrix.shape[1] + right.shape[1]
    work = jnp.concatenate([matrix, right], axis=1)
    work = [work[rows(i, TILE), :] for i in range(n // TILE)]
    at = lax.broadcasted_iota(jnp.int32, (TILE, width), 0)

    def column(k):
        return [jnp.broadcast_to(t[:, k : k + 1], (TILE, width)) for t in work]

    def step(tiles, spread, k, pivot):
        i, s = divmod(k, TILE)
        row = tiles[i][s : s + 1, :] * pivot
        done = [t - c * row for t, c in zip(tiles, spread)]
        done[i] = jnp.where(at == s, row, done[i])
        return done

    ahead = [column(k) for k in range(AHEAD)]
    for k in range(n):
        i, s = divmod(k, TILE)
        spread = ahead.pop(0)
        pivot = 1.0 / spread[i][s : s + 1, :]
        ahead = [step(later, spread, k, pivot) for later in ahead]
        work = step(work, spread, k, pivot)
        if k + AHEAD < n:
            ahead.append(column(k + AHEAD))
    return jnp.concatenate(work, axis=0)[:, n:]


def middle_kernel(grams, diag_ref, out_ref):
    n = grams.shape[0] // 2
    norm, energy = grams[:n, :n], grams[:n, n:]
    shift, shift_row = frame_shift(diag_ref[0:1, :], n)
    inverse = eliminate(energy, jnp.where(eye(n), 1.0, 0.0), n)
    next_rhs = energy - shift * norm
    cross = grams[n:, :n] + next_rhs * shift_row
    alpha = nn_dot(inverse, norm)
    conj = nn_dot(inverse, cross.T)
    out_ref[0] = alpha
    out_ref[1] = conj
    out_ref[2] = grams[n:, n:] - nn_dot(cross, conj)
    out_ref[3] = next_rhs - nn_dot(cross, alpha)


def solve_kernel(gram, parts, middle, out_ref):
    n = gram.shape[0]
    schur = gram[...] + middle[2]
    for part in parts:
        both = part[...].astype(F32)
        schur += both[:, :n] + both[:, n:]
    gamma = eliminate(schur, middle[3], n)
    out_ref[:n, :] = middle[0] - nn_dot(middle[1], gamma)
    out_ref[n:, :] = gamma


def final_kernel(keep, near, far, v_ref, image_ref, next_ref, prior, coeffs_ref, x_ref, r_ref):
    n = v_ref.shape[0]
    coeffs = coeffs_ref[...]
    for j in range(keep.shape[0] // n):
        value = v_ref[:, lanes(j)]
        following = next_ref[:, lanes(j)]
        second_image = own_sum(keep, near, far, j, n) + prior[:, lanes(j)] * following
        x_ref[:, lanes(j)] = tn_dot(coeffs, jnp.concatenate([value, following], axis=0))
        r_ref[:, lanes(j)] = value - tn_dot(
            coeffs, jnp.concatenate([image_ref[:, lanes(j)], second_image], axis=0)
        )


def swapped(x, axis, flip):
    return lax.ppermute(x, axis, [(i, i ^ flip) for i in range(lax.axis_size(axis))])


def others(x, axis):
    return (x, *(swapped(x, axis, flip) for flip in range(2, lax.axis_size(axis), 2)))


def gather(x, axis):
    return tuple(part for own in others(x, axis) for part in (own, swapped(own, axis, 1)))


def shards(right_side, prior, blocks, block_row, block_col):
    frames, pix = right_side.shape
    stretch = pix // BLOCK
    n_rows, n_cols = lax.axis_size("row"), lax.axis_size("col")
    row_span, col_span = stretch * n_cols, stretch * n_rows
    prior = prior.reshape(1, pix)
    stored = blocks.shape[0]
    half_cols = n_cols // 2 * stretch * frames

    def shape(dims, dtype=F32):
        return jax.ShapeDtypeStruct(dims, dtype)

    own = shape((frames, pix))
    cast_type = shape((stretch * frames, BLOCK), BF16)
    aside = pl.CostEstimate(flops=2 * 10**9, bytes_accessed=8 * 10**6, transcendentals=0)
    pairs = n_rows // 2 - 1

    def forward(search, tile):
        size = half_cols + (DIAG if tile else 0)
        keep, send = call(
            lambda *refs: forward_kernel(stretch, n_cols, *refs),
            (shape((size, BLOCK)),) * 2,
            (index, search, turned, tile),
            [
                pltpu.VMEM((row_span, frames, BLOCK), F32),
                pltpu.VMEM((col_span, frames, BLOCK), BF16),
            ],
        )
        received = swapped(send, "col", 1)
        (pair,) = call(
            lambda *refs: pair_kernel(half_cols, frames, *refs),
            (shape((size, BLOCK), BF16),),
            (keep, received),
        )
        (foot,) = call(
            lambda *refs: chips_kernel(half_cols, frames, *refs),
            (shape((size, BLOCK), BF16),),
            (others(pair, "col"),),
        )
        return foot, swapped(foot, "col", 1)

    def backward(foot, last):
        size = stretch * frames
        extra = 0 if last else DIAG
        far, near, kept, keep = call(
            lambda *refs: backward_kernel(stretch, n_cols, last, *refs),
            (
                tuple(shape((size + (0 if p else extra), BLOCK), BF16) for p in range(pairs)),
                shape((size, BLOCK), BF16),
                (shape((size, BLOCK)),) * pairs,
                shape((size, BLOCK)),
            ),
            (index, *foot, staged),
            [
                pltpu.VMEM((col_span, frames, BLOCK), F32),
                pltpu.VMEM((row_span, frames, BLOCK), BF16),
            ],
        )
        received = tuple(swapped(x, "row", 1) for x in far)
        near = swapped(near, "row", 1)
        (sums,) = call(
            lambda *refs: rows_kernel(size, frames, *refs),
            ((shape((size + extra, BLOCK), BF16),) * pairs,),
            (far[0], received, kept),
        )
        far = tuple(swapped(x, "row", 2 * (p + 1)) for p, x in enumerate(sums))
        return keep, near, far, sums[0]

    def add(parts):
        return call(add_kernel, (shape(parts[0].shape),), (parts,))[0]

    (cast,) = call(cast_kernel, (cast_type,), (right_side,))
    search = gather(cast, "row")
    index, staged = call(
        lambda *refs: stage_kernel(row_span, stretch, *refs),
        (shape((2, stored), jnp.int32), shape(blocks.shape, BF16)),
        (block_row, block_col, blocks),
        [pltpu.SemaphoreType.DMA],
        specs=[SMEM, SMEM, ANY],
        cost=aside,
    )
    (turned,) = call(turn_kernel, (shape(blocks.shape, BF16),), (staged,), cost=aside)
    (tile,) = call(energy_kernel, (shape((DIAG, 2 * frames)),), (right_side, prior), cost=aside)
    foot = forward(search, (tile,))
    keep, near, far, sent = backward(foot, False)
    image, following, cast, diagonal = call(
        image_kernel,
        (own, own, cast_type, shape((DIAG, 2 * frames))),
        (keep, near, far, sent, right_side, prior),
    )
    search = gather(cast, "row")
    (grams,) = call(
        grams_kernel, (shape((2 * frames,) * 2),), (right_side, following, prior), cost=aside
    )
    grams = add((grams, swapped(grams, "col", 1)))
    (grams,) = call(
        lambda *refs: first_grams_kernel(half_cols, *refs),
        (shape(grams.shape),),
        (others(grams, "col"), *foot),
        cost=aside,
    )
    foot = forward(search, ())
    grams = add((grams, swapped(grams, "row", 1)))
    grams = add(others(grams, "row"))
    (second,) = call(
        lambda *refs: second_gram_kernel(half_cols, *refs),
        (shape((frames, 2 * frames), BF16),),
        foot,
    )
    gram, second = call(
        second_pair_kernel,
        (shape((frames, frames)), shape((frames, 2 * frames), BF16)),
        (second, swapped(second, "row", 1)),
    )
    second = others(second, "row")[1:]
    keep, near, far, _ = backward(foot, True)
    (middle,) = call(middle_kernel, (shape((4, frames, frames)),), (grams, diagonal), cost=aside)
    (coeffs,) = call(
        solve_kernel, (shape((2 * frames, frames)),), (gram, second, middle), cost=aside
    )
    return tuple(
        call(
            final_kernel,
            (own, own),
            (keep, near, far, right_side, image, following, prior, coeffs),
        )
    )


def solution(mesh):
    return jax.shard_map(
        shards,
        mesh=mesh,
        in_specs=(
            P("groups", ("row", "col")),
            P(("row", "col")),
            P(("row", "col"), None, None),
            P(("row", "col")),
            P(("row", "col")),
        ),
        out_specs=(P("groups", ("row", "col")), P("groups", ("row", "col"))),
        check_vma=False,
    )
```

time: 73.7 us -> 82 us (1.11)
  waiting for transfers between devices: 28.9 us -> 39.5 us
  starting transfers between devices: 25.9 us -> 22.8 us
  local copies, waits for them, and re-layouts: 1.6 us -> 3.02 us
    ppermute x18 -> x24, waiting for transfers between devices: 28.9 us -> 39.5 us  [swapped(): lax.ppermute(x, axis, [(i, i ^ flip) for i in range(lax.axis_size(axis))])]
    ppermute x18 -> x24, starting transfers between devices: 25.9 us -> 22.8 us  [swapped(): lax.ppermute(x, axis, [(i, i ^ flip) for i in range(lax.axis_size(axis))])]
    unnamed x14, local copies, waits for them, and re-layouts: 1.6 us -> 3.02 us
    pallas_call x18 -> x25, Pallas kernels: 16.3 us -> 15.7 us  [call(): pl.pallas_call(body, out_shape=flat_outs, in_specs=specs or [space(x) for...]
  transfers between devices with their start and end apart: 18 -> 24, of which waited for: 14 -> 17; matrix products, arithmetic and copies ran while one was open for 0% -> 0% of each run, Pallas kernels for 8% -> 12%
where the time goes in v6:
time: 82 us; the launch traced here: 81.9 us
  waiting for transfers between devices  39.5 us (48%)
  starting transfers between devices  22.8 us (28%)
  Pallas kernels  15.7 us (19%)
  local copies, waits for them, and re-layouts  3.02 us (4%)
  between operations  0.85 us (1%)
    ppermute x24, waiting for transfers between devices, swapped(): lax.ppermute(x, axis, [(i, i ^ flip) for i in range(lax.axis_size(axis))])  39.5 us
    ppermute x24, starting transfers between devices, swapped(): lax.ppermute(x, axis, [(i, i ^ flip) for i in range(lax.axis_size(axis))])  22.8 us
    pallas_call x25, Pallas kernels, call(): pl.pallas_call(body, out_shape=flat_outs, in_specs=specs or [space(x) for...  15.7 us
    unnamed x14, local copies, waits for them, and re-layouts  3.02 us
  transfers between devices with their start and end apart: 24, of which 17 were waited for; matrix products, arithmetic and copies ran while one was open for 0% of the time, Pallas kernels for 12%

profile of v6, /device:TPU:0, one launch (start us, length us, event | category | flops | bytes accessed | tf_op | source)
XLA Modules:
  0.0 81.9 jit_solution(4579225437812171534)
XLA Ops:
  1.5 4.1 %collective-permute-start.1 = (bf16[256,128]{1,0:T(8,128)(2,1)S(1)}, bf16[256,128]{1,0:T(8,128)(2,1)S(1)}, u32[]{:S(2)}, u32[]{:S(2)}) collective-permute-start(bf16[256,128]{1,0:T(8,128)(2,1)S(1)} %shard_map.69.refs_1_), channel_id=1, source_target_pairs={{0,8},{4,12},{8,0},{12,4},{1,9},{5,13},{9,1},{13,5},{2,10},{6,14},... | collective-permute-start | bytes 196616 | tf_op jit(solution)/shard_map/ppermute | solution.py:370
  5.7 1.6 %collective-permute-start = (bf16[256,128]{1,0:T(8,128)(2,1)S(1)}, bf16[256,128]{1,0:T(8,128)(2,1)S(1)}, u32[]{:S(2)}, u32[]{:S(2)}) collective-permute-start(bf16[256,128]{1,0:T(8,128)(2,1)S(1)} %shard_map.69.refs_1_), channel_id=1, source_target_pairs={{0,4},{4,0},{8,12},{12,8},{1,5},{5,1},{9,13},{13,9},{2,6},{6,2},{1... | collective-permute-start | bytes 196616 | tf_op jit(solution)/shard_map/ppermute | solution.py:370
  8.1 1.4 %copy-done.4 = bf16[64,128,128]{2,1,0:T(8,128)(2,1)S(1)} copy-done((bf16[64,128,128]{2,1,0:T(8,128)(2,1)S(1)}, bf16[64,128,128]{2,1,0:T(8,128)(2,1)}, u32[]{:S(2)}) %copy-start.4) | copy-done | bytes 2097176
  9.5 1.6 %shard_map.68 = (s32[2,64]{1,0:T(2,128)S(1)}, bf16[64,128,128]{2,1,0:T(8,128)(2,1)S(1)}) custom-call(s32[64]{0:T(128)S(1)} %copy-done.5, s32[64]{0:T(128)S(1)} %copy-done.6, bf16[64,128,128]{2,1,0:T(8,128)(2,1)S(1)} %copy-done.4), custom_call_target="tpu_custom_call" | custom-call | flops 2000000000 | bytes 8000000 | tf_op jit(solution)/shard_map/pallas_call | solution.py:52
  12.3 3.2 %collective-permute-done.2.refs_4_ = bf16[256,128]{1,0:T(8,128)(2,1)S(1)} collective-permute-done((bf16[256,128]{1,0:T(8,128)(2,1)S(1)}, bf16[256,128]{1,0:T(8,128)(2,1)S(1)}, u32[]{:S(2)}, u32[]{:S(2)}) %collective-permute-start.2) | collective-permute-done | bytes 65568 | tf_op jit(solution)/shard_map/ppermute | solution.py:370
  15.5 1.3 %shard_map.72 = (f32[528,128]{1,0:T(8,128)S(1)}, f32[528,128]{1,0:T(8,128)S(1)}) custom-call(s32[2,64]{1,0:T(2,128)S(1)} %get-tuple-element.22.refs_0_, bf16[256,128]{1,0:T(8,128)(2,1)S(1)} %shard_map.69.refs_1_, bf16[256,128]{1,0:T(8,128)(2,1)S(1)} %collective-permute-done.refs_2_, bf16[256,128]{1,0:T(8,128)(2,1)S(1)} %collective-permute-done.1.refs_3_, ...), custom_call_target="tpu_custom_call" | custom-call | tf_op jit(solution)/shard_map/pallas_call | solution.py:52
  16.9 1.5 %collective-permute-done.3.refs_1_ = f32[528,128]{1,0:T(8,128)S(1)} collective-permute-done((f32[528,128]{1,0:T(8,128)S(1)}, f32[528,128]{1,0:T(8,128)S(1)}, u32[]{:S(2)}, u32[]{:S(2)}) %collective-permute-start.3) | collective-permute-done | bytes 270368 | tf_op jit(solution)/shard_map/ppermute | solution.py:370
  18.5 1.6 %collective-permute-start.4 = (bf16[528,128]{1,0:T(8,128)(2,1)S(1)}, bf16[528,128]{1,0:T(8,128)(2,1)S(1)}, u32[]{:S(2)}, u32[]{:S(2)}) collective-permute-start(bf16[528,128]{1,0:T(8,128)(2,1)S(1)} %shard_map.73.refs_0_), channel_id=1, source_target_pairs={{0,2},{1,3},{2,0},{3,1},{4,6},{5,7},{6,4},{7,5},{8,10},{9,11},{10,... | collective-permute-start | bytes 405512 | tf_op jit(solution)/shard_map/ppermute | solution.py:370
  20.0 4.1 %collective-permute-done.4.refs_1_ = bf16[528,128]{1,0:T(8,128)(2,1)S(1)} collective-permute-done((bf16[528,128]{1,0:T(8,128)(2,1)S(1)}, bf16[528,128]{1,0:T(8,128)(2,1)S(1)}, u32[]{:S(2)}, u32[]{:S(2)}) %collective-permute-start.4) | collective-permute-done | bytes 135200 | tf_op jit(solution)/shard_map/ppermute | solution.py:370
  24.3 1.3 %collective-permute-done.5.refs_2_.refs_3_ = bf16[528,128]{1,0:T(8,128)(2,1)S(1)} collective-permute-done((bf16[528,128]{1,0:T(8,128)(2,1)S(1)}, bf16[528,128]{1,0:T(8,128)(2,1)S(1)}, u32[]{:S(2)}, u32[]{:S(2)}) %collective-permute-start.5) | collective-permute-done | bytes 135200 | tf_op jit(solution)/shard_map/ppermute | solution.py:370
  25.6 1.3 %shard_map.75 = (bf16[272,128]{1,0:T(8,128)(2,1)S(1)}, bf16[256,128]{1,0:T(8,128)(2,1)S(1)}, f32[256,128]{1,0:T(8,128)S(1)}, f32[256,128]{1,0:T(8,128)S(1)}) custom-call(s32[2,64]{1,0:T(2,128)S(1)} %get-tuple-element.22.refs_0_, bf16[528,128]{1,0:T(8,128)(2,1)S(1)} %shard_map.74.refs_1_.refs_2_, bf16[528,128]{1,0:T(8,128)(2,1)S(1)} %collective-permute-done.5.refs_2_.refs_3_, ...), custom_call_target="tpu_custom_call" | custom-call | tf_op jit(solution)/shard_map/pallas_call | solution.py:52
  27.4 3.9 %collective-permute-done.7.refs_1_ = bf16[272,128]{1,0:T(8,128)(2,1)S(1)} collective-permute-done((bf16[272,128]{1,0:T(8,128)(2,1)S(1)}, bf16[272,128]{1,0:T(8,128)(2,1)S(1)}, u32[]{:S(2)}, u32[]{:S(2)}) %collective-permute-start.7) | collective-permute-done | bytes 69664 | tf_op jit(solution)/shard_map/ppermute | solution.py:370
  31.7 1.7 %collective-permute-start.6 = (bf16[256,128]{1,0:T(8,128)(2,1)S(1)}, bf16[256,128]{1,0:T(8,128)(2,1)S(1)}, u32[]{:S(2)}, u32[]{:S(2)}) collective-permute-start(bf16[256,128]{1,0:T(8,128)(2,1)S(1)} %get-tuple-element.27), channel_id=1, source_target_pairs={{0,4},{4,0},{8,12},{12,8},{1,5},{5,1},{9,13},{13,9},{2,6},{6,2},{1... | collective-permute-start | bytes 196616 | tf_op jit(solution)/shard_map/ppermute | solution.py:370
  33.4 2.6 %collective-permute-done.6.refs_1_ = bf16[256,128]{1,0:T(8,128)(2,1)S(1)} collective-permute-done((bf16[256,128]{1,0:T(8,128)(2,1)S(1)}, bf16[256,128]{1,0:T(8,128)(2,1)S(1)}, u32[]{:S(2)}, u32[]{:S(2)}) %collective-permute-start.6) | collective-permute-done | bytes 65568 | tf_op jit(solution)/shard_map/ppermute | solution.py:370
  36.0 1.3 %collective-permute-done.8.refs_2_ = bf16[272,128]{1,0:T(8,128)(2,1)S(1)} collective-permute-done((bf16[272,128]{1,0:T(8,128)(2,1)S(1)}, bf16[272,128]{1,0:T(8,128)(2,1)S(1)}, u32[]{:S(2)}, u32[]{:S(2)}) %collective-permute-start.8) | collective-permute-done | bytes 69664 | tf_op jit(solution)/shard_map/ppermute | solution.py:370
  37.5 1.4 %collective-permute-start.10 = (bf16[256,128]{1,0:T(8,128)(2,1)S(1)}, bf16[256,128]{1,0:T(8,128)(2,1)S(1)}, u32[]{:S(2)}, u32[]{:S(2)}) collective-permute-start(bf16[256,128]{1,0:T(8,128)(2,1)S(1)} %get-tuple-element.30.refs_1_), channel_id=1, source_target_pairs={{0,8},{4,12},{8,0},{12,4},{1,9},{5,13},{9,1},{13,5},{2,10},{6,14},... | collective-permute-start | bytes 196616 | tf_op jit(solution)/shard_map/ppermute | solution.py:370
  40.0 3.5 %collective-permute-done.10.refs_3_ = bf16[256,128]{1,0:T(8,128)(2,1)S(1)} collective-permute-done((bf16[256,128]{1,0:T(8,128)(2,1)S(1)}, bf16[256,128]{1,0:T(8,128)(2,1)S(1)}, u32[]{:S(2)}, u32[]{:S(2)}) %collective-permute-start.10) | collective-permute-done | bytes 65568 | tf_op jit(solution)/shard_map/ppermute | solution.py:370
  44.4 3.3 %collective-permute-done.11.refs_4_ = bf16[256,128]{1,0:T(8,128)(2,1)S(1)} collective-permute-done((bf16[256,128]{1,0:T(8,128)(2,1)S(1)}, bf16[256,128]{1,0:T(8,128)(2,1)S(1)}, u32[]{:S(2)}, u32[]{:S(2)}) %collective-permute-start.11) | collective-permute-done | bytes 65568 | tf_op jit(solution)/shard_map/ppermute | solution.py:370
  47.7 1.3 %shard_map.78 = (f32[512,128]{1,0:T(8,128)S(1)}, f32[512,128]{1,0:T(8,128)S(1)}) custom-call(s32[2,64]{1,0:T(2,128)S(1)} %get-tuple-element.22.refs_0_, bf16[256,128]{1,0:T(8,128)(2,1)S(1)} %get-tuple-element.30.refs_1_, bf16[256,128]{1,0:T(8,128)(2,1)S(1)} %collective-permute-done.9.refs_2_, bf16[256,128]{1,0:T(8,128)(2,1)S(1)} %collective-permute-done.10.refs_3_, ...), custom_call_target="tpu_custom_call" | custom-call | tf_op jit(solution)/shard_map/pallas_call | solution.py:52
  50.6 1.6 %collective-permute-start.13 = (bf16[512,128]{1,0:T(8,128)(2,1)S(1)}, bf16[512,128]{1,0:T(8,128)(2,1)S(1)}, u32[]{:S(2)}, u32[]{:S(2)}) collective-permute-start(bf16[512,128]{1,0:T(8,128)(2,1)S(1)} %shard_map.79.refs_0_), channel_id=1, source_target_pairs={{0,2},{1,3},{2,0},{3,1},{4,6},{5,7},{6,4},{7,5},{8,10},{9,11},{10,... | collective-permute-start | bytes 393224 | tf_op jit(solution)/shard_map/ppermute | solution.py:370
  52.2 1.3 %collective-permute-done.20.refs_1_ = f32[128,128]{1,0:T(8,128)S(1)} collective-permute-done((f32[128,128]{1,0:T(8,128)S(1)}, f32[128,128]{1,0:T(8,128)S(1)}, u32[]{:S(2)}, u32[]{:S(2)}) %collective-permute-start.20) | collective-permute-done | bytes 65568 | tf_op jit(solution)/shard_map/ppermute | solution.py:370
  54.0 2.2 %collective-permute-done.13.refs_1_ = bf16[512,128]{1,0:T(8,128)(2,1)S(1)} collective-permute-done((bf16[512,128]{1,0:T(8,128)(2,1)S(1)}, bf16[512,128]{1,0:T(8,128)(2,1)S(1)}, u32[]{:S(2)}, u32[]{:S(2)}) %collective-permute-start.13) | collective-permute-done | bytes 131104 | tf_op jit(solution)/shard_map/ppermute | solution.py:370
  56.3 1.4 %collective-permute-done.21.refs_1_ = f32[128,128]{1,0:T(8,128)S(1)} collective-permute-done((f32[128,128]{1,0:T(8,128)S(1)}, f32[128,128]{1,0:T(8,128)S(1)}, u32[]{:S(2)}, u32[]{:S(2)}) %collective-permute-start.21) | collective-permute-done | bytes 65568 | tf_op jit(solution)/shard_map/ppermute | solution.py:370
  58.1 4.3 %collective-permute-done.22.refs_1_ = f32[128,128]{1,0:T(8,128)S(1)} collective-permute-done((f32[128,128]{1,0:T(8,128)S(1)}, f32[128,128]{1,0:T(8,128)S(1)}, u32[]{:S(2)}, u32[]{:S(2)}) %collective-permute-start.22) | collective-permute-done | bytes 65568 | tf_op jit(solution)/shard_map/ppermute | solution.py:370
  63.8 1.3 %collective-permute-start.18 = (bf16[64,128]{1,0:T(8,128)(2,1)S(1)}, bf16[64,128]{1,0:T(8,128)(2,1)S(1)}, u32[]{:S(2)}, u32[]{:S(2)}) collective-permute-start(bf16[64,128]{1,0:T(8,128)(2,1)S(1)} %shard_map.83.refs_0_), channel_id=1, source_target_pairs={{0,4},{4,0},{8,12},{12,8},{1,5},{5,1},{9,13},{13,9},{2,6},{6,2},{1... | collective-permute-start | bytes 49160 | tf_op jit(solution)/shard_map/ppermute | solution.py:370
  65.1 2.7 %collective-permute-done.23.refs_1_ = f32[128,128]{1,0:T(8,128)S(1)} collective-permute-done((f32[128,128]{1,0:T(8,128)S(1)}, f32[128,128]{1,0:T(8,128)S(1)}, u32[]{:S(2)}, u32[]{:S(2)}) %collective-permute-start.23) | collective-permute-done | bytes 65568 | tf_op jit(solution)/shard_map/ppermute | solution.py:370
  67.8 1.3 %shard_map.81 = (bf16[256,128]{1,0:T(8,128)(2,1)S(1)}, bf16[256,128]{1,0:T(8,128)(2,1)S(1)}, f32[256,128]{1,0:T(8,128)S(1)}, f32[256,128]{1,0:T(8,128)S(1)}) custom-call(s32[2,64]{1,0:T(2,128)S(1)} %get-tuple-element.22.refs_0_, bf16[512,128]{1,0:T(8,128)(2,1)S(1)} %shard_map.80.refs_1_.refs_0_, ...), custom_call_target="tpu_custom_call" | custom-call | tf_op jit(solution)/shard_map/pallas_call | solution.py:52
  69.4 2.8 %collective-permute-start.19 = (bf16[64,128]{1,0:T(8,128)(2,1)S(1)}, bf16[64,128]{1,0:T(8,128)(2,1)S(1)}, u32[]{:S(2)}, u32[]{:S(2)}) collective-permute-start(bf16[64,128]{1,0:T(8,128)(2,1)S(1)} %get-tuple-element.40), channel_id=1, source_target_pairs={{0,8},{4,12},{8,0},{12,4},{1,9},{5,13},{9,1},{13,5},{2,10},{6,14},... | collective-permute-start | bytes 49160 | tf_op jit(solution)/shard_map/ppermute | solution.py:370
  72.2 2.9 %shard_map.90.refs_2_ = f32[4,64,64]{2,1,0:T(8,128)S(1)} custom-call(f32[128,128]{1,0:T(8,128)S(1)} %shard_map.89.refs_0_, f32[16,128]{1,0:T(8,128)S(1)} %get-tuple-element.41.refs_1_), custom_call_target="tpu_custom_call" | custom-call | flops 2000000000 | bytes 8000000 | tf_op jit(solution)/shard_map/pallas_call | solution.py:52
  75.3 2.0 %collective-permute-start.17 = (bf16[256,128]{1,0:T(8,128)(2,1)S(1)}, bf16[256,128]{1,0:T(8,128)(2,1)S(1)}, u32[]{:S(2)}, u32[]{:S(2)}) collective-permute-start(bf16[256,128]{1,0:T(8,128)(2,1)S(1)} %shard_map.82), channel_id=1, source_target_pairs={{0,8},{4,12},{8,0},{12,4},{1,9},{5,13},{9,1},{13,5},{2,10},{6,14},... | collective-permute-start | bytes 196616 | tf_op jit(solution)/shard_map/ppermute | solution.py:370
  77.3 2.1 %shard_map.91.refs_7_ = f32[128,64]{1,0:T(8,128)S(1)} custom-call(f32[64,64]{1,0:T(8,128)S(1)} %get-tuple-element.39.refs_0_, bf16[64,128]{1,0:T(8,128)(2,1)S(1)} %collective-permute-done.19.refs_1_, f32[4,64,64]{2,1,0:T(8,128)S(1)} %shard_map.90.refs_2_), custom_call_target="tpu_custom_call" | custom-call | flops 2000000000 | bytes 8000000 | tf_op jit(solution)/shard_map/pallas_call | solution.py:52
  80.5 1.3 %shard_map.92 = (f32[64,512]{1,0:T(8,128)}, f32[64,512]{1,0:T(8,128)}) custom-call(f32[256,128]{1,0:T(8,128)S(1)} %get-tuple-element.33.refs_0_, bf16[256,128]{1,0:T(8,128)(2,1)S(1)} %collective-permute-done.15.refs_1_, bf16[256,128]{1,0:T(8,128)(2,1)S(1)} %collective-permute-done.17.refs_2_, f32[64,512]{1,0:T(8,128)S(1)} %copy-done.1, ...), custom_call_target="tpu_custom_call" | custom-call | tf_op jit(solution)/shard_map/pallas_call | solution.py:52
  (55 shorter events, 12.1 us)
Async XLA Ops:
  0.6 0.9 %copy-start = (f32[64,512]{1,0:T(8,128)S(1)}, f32[64,512]{1,0:T(8,128)}, u32[]{:S(2)}) copy-start(f32[64,512]{1,0:T(8,128)} %refs_3_.1) | copy-start | bytes 393220
  1.5 9.6 %collective-permute-start.1 = (bf16[256,128]{1,0:T(8,128)(2,1)S(1)}, bf16[256,128]{1,0:T(8,128)(2,1)S(1)}, u32[]{:S(2)}, u32[]{:S(2)}) collective-permute-start(bf16[256,128]{1,0:T(8,128)(2,1)S(1)} %shard_map.69.refs_1_), channel_id=1, source_target_pairs={{0,8},{4,12},{8,0},{12,4},{1,9},{5,13},{9,1},{13,5},{2,10},{6,14},... | collective-permute-start | bytes 196616 | tf_op jit(solution)/shard_map/ppermute | solution.py:370
  5.7 6.6 %collective-permute-start = (bf16[256,128]{1,0:T(8,128)(2,1)S(1)}, bf16[256,128]{1,0:T(8,128)(2,1)S(1)}, u32[]{:S(2)}, u32[]{:S(2)}) collective-permute-start(bf16[256,128]{1,0:T(8,128)(2,1)S(1)} %shard_map.69.refs_1_), channel_id=1, source_target_pairs={{0,4},{4,0},{8,12},{12,8},{1,5},{5,1},{9,13},{13,9},{2,6},{6,2},{1... | collective-permute-start | bytes 196616 | tf_op jit(solution)/shard_map/ppermute | solution.py:370
  7.2 0.7 copy-start.2
  7.9 1.6 %copy-start.4 = (bf16[64,128,128]{2,1,0:T(8,128)(2,1)S(1)}, bf16[64,128,128]{2,1,0:T(8,128)(2,1)}, u32[]{:S(2)}) copy-start(bf16[64,128,128]{2,1,0:T(8,128)(2,1)} %refs_2_.1) | copy-start | bytes 6291460
  7.9 1.6 %copy-start.5 = (s32[64]{0:T(128)S(1)}, s32[64]{0:T(128)}, u32[]{:S(2)}) copy-start(s32[64]{0:T(128)} %refs_0_.4) | copy-start | bytes 772
  7.9 1.6 %copy-start.6 = (s32[64]{0:T(128)S(1)}, s32[64]{0:T(128)}, u32[]{:S(2)}) copy-start(s32[64]{0:T(128)} %refs_1_.1) | copy-start | bytes 772
  11.2 4.3 %collective-permute-start.2 = (bf16[256,128]{1,0:T(8,128)(2,1)S(1)}, bf16[256,128]{1,0:T(8,128)(2,1)S(1)}, u32[]{:S(2)}, u32[]{:S(2)}) collective-permute-start(bf16[256,128]{1,0:T(8,128)(2,1)S(1)} %collective-permute-done.1.refs_3_), channel_id=1, source_target_pairs={{0,4},{4,0},{8,12},{12,8},{1,5},{5,1},{9,13},{13,9},{2,6},{6,2},{1... | collective-permute-start | bytes 196616 | tf_op jit(solution)/shard_map/ppermute | solution.py:370
  16.8 20.5 %copy-start.1 = (f32[64,512]{1,0:T(8,128)S(1)}, f32[64,512]{1,0:T(8,128)}, u32[]{:S(2)}) copy-start(f32[64,512]{1,0:T(8,128)} %refs_3_.1) | copy-start | bytes 393220
  16.8 20.5 %copy-start.3 = (f32[512]{0:T(512)S(1)}, f32[512]{0:T(512)}, u32[]{:S(2)}) copy-start(f32[512]{0:T(512)} %param.6) | copy-start | bytes 6148
  16.8 1.6 %collective-permute-start.3 = (f32[528,128]{1,0:T(8,128)S(1)}, f32[528,128]{1,0:T(8,128)S(1)}, u32[]{:S(2)}, u32[]{:S(2)}) collective-permute-start(f32[528,128]{1,0:T(8,128)S(1)} %get-tuple-element.25), channel_id=1, source_target_pairs={{0,1},{1,0},{2,3},{3,2},{4,5},{5,4},{6,7},{7,6},{8,9},{9,8},{10,11... | collective-permute-start | bytes 811016 | tf_op jit(solution)/shard_map/ppermute | solution.py:370
  18.5 5.7 %collective-permute-start.4 = (bf16[528,128]{1,0:T(8,128)(2,1)S(1)}, bf16[528,128]{1,0:T(8,128)(2,1)S(1)}, u32[]{:S(2)}, u32[]{:S(2)}) collective-permute-start(bf16[528,128]{1,0:T(8,128)(2,1)S(1)} %shard_map.73.refs_0_), channel_id=1, source_target_pairs={{0,2},{1,3},{2,0},{3,1},{4,6},{5,7},{6,4},{7,5},{8,10},{9,11},{10,... | collective-permute-start | bytes 405512 | tf_op jit(solution)/shard_map/ppermute | solution.py:370
  24.2 1.4 %collective-permute-start.5 = (bf16[528,128]{1,0:T(8,128)(2,1)S(1)}, bf16[528,128]{1,0:T(8,128)(2,1)S(1)}, u32[]{:S(2)}, u32[]{:S(2)}) collective-permute-start(bf16[528,128]{1,0:T(8,128)(2,1)S(1)} %shard_map.74.refs_1_.refs_2_), channel_id=1, source_target_pairs={{0,1},{1,0},{2,3},{3,2},{4,5},{5,4},{6,7},{7,6},{8,9},{9,8},{10,11... | collective-permute-start | bytes 405512 | tf_op jit(solution)/shard_map/ppermute | solution.py:370
  26.9 4.4 %collective-permute-start.7 = (bf16[272,128]{1,0:T(8,128)(2,1)S(1)}, bf16[272,128]{1,0:T(8,128)(2,1)S(1)}, u32[]{:S(2)}, u32[]{:S(2)}) collective-permute-start(bf16[272,128]{1,0:T(8,128)(2,1)S(1)} %get-tuple-element.28.refs_0_), channel_id=1, source_target_pairs={{0,4},{4,0},{8,12},{12,8},{1,5},{5,1},{9,13},{13,9},{2,6},{6,2},{1... | collective-permute-start | bytes 208904 | tf_op jit(solution)/shard_map/ppermute | solution.py:370
  31.3 5.9 %collective-permute-start.8 = (bf16[272,128]{1,0:T(8,128)(2,1)S(1)}, bf16[272,128]{1,0:T(8,128)(2,1)S(1)}, u32[]{:S(2)}, u32[]{:S(2)}) collective-permute-start(bf16[272,128]{1,0:T(8,128)(2,1)S(1)} %shard_map.76.refs_3_), channel_id=1, source_target_pairs={{0,8},{4,12},{8,0},{12,4},{1,9},{5,13},{9,1},{13,5},{2,10},{6,14},... | collective-permute-start | bytes 208904 | tf_op jit(solution)/shard_map/ppermute | solution.py:370
  31.7 4.3 %collective-permute-start.6 = (bf16[256,128]{1,0:T(8,128)(2,1)S(1)}, bf16[256,128]{1,0:T(8,128)(2,1)S(1)}, u32[]{:S(2)}, u32[]{:S(2)}) collective-permute-start(bf16[256,128]{1,0:T(8,128)(2,1)S(1)} %get-tuple-element.27), channel_id=1, source_target_pairs={{0,4},{4,0},{8,12},{12,8},{1,5},{5,1},{9,13},{13,9},{2,6},{6,2},{1... | collective-permute-start | bytes 196616 | tf_op jit(solution)/shard_map/ppermute | solution.py:370
  37.5 5.9 %collective-permute-start.10 = (bf16[256,128]{1,0:T(8,128)(2,1)S(1)}, bf16[256,128]{1,0:T(8,128)(2,1)S(1)}, u32[]{:S(2)}, u32[]{:S(2)}) collective-permute-start(bf16[256,128]{1,0:T(8,128)(2,1)S(1)} %get-tuple-element.30.refs_1_), channel_id=1, source_target_pairs={{0,8},{4,12},{8,0},{12,4},{1,9},{5,13},{9,1},{13,5},{2,10},{6,14},... | collective-permute-start | bytes 196616 | tf_op jit(solution)/shard_map/ppermute | solution.py:370
  38.9 5.5 %collective-permute-start.9 = (bf16[256,128]{1,0:T(8,128)(2,1)S(1)}, bf16[256,128]{1,0:T(8,128)(2,1)S(1)}, u32[]{:S(2)}, u32[]{:S(2)}) collective-permute-start(bf16[256,128]{1,0:T(8,128)(2,1)S(1)} %get-tuple-element.30.refs_1_), channel_id=1, source_target_pairs={{0,4},{4,0},{8,12},{12,8},{1,5},{5,1},{9,13},{13,9},{2,6},{6,2},{1... | collective-permute-start | bytes 196616 | tf_op jit(solution)/shard_map/ppermute | solution.py:370
  43.4 4.3 %collective-permute-start.11 = (bf16[256,128]{1,0:T(8,128)(2,1)S(1)}, bf16[256,128]{1,0:T(8,128)(2,1)S(1)}, u32[]{:S(2)}, u32[]{:S(2)}) collective-permute-start(bf16[256,128]{1,0:T(8,128)(2,1)S(1)} %collective-permute-done.10.refs_3_), channel_id=1, source_target_pairs={{0,4},{4,0},{8,12},{12,8},{1,5},{5,1},{9,13},{13,9},{2,6},{6,2},{1... | collective-permute-start | bytes 196616 | tf_op jit(solution)/shard_map/ppermute | solution.py:370
  49.0 1.6 %collective-permute-start.12 = (f32[512,128]{1,0:T(8,128)S(1)}, f32[512,128]{1,0:T(8,128)S(1)}, u32[]{:S(2)}, u32[]{:S(2)}) collective-permute-start(f32[512,128]{1,0:T(8,128)S(1)} %get-tuple-element.32), channel_id=1, source_target_pairs={{0,1},{1,0},{2,3},{3,2},{4,5},{5,4},{6,7},{7,6},{8,9},{9,8},{10,11... | collective-permute-start | bytes 786440 | tf_op jit(solution)/shard_map/ppermute | solution.py:370
  50.6 5.6 %collective-permute-start.13 = (bf16[512,128]{1,0:T(8,128)(2,1)S(1)}, bf16[512,128]{1,0:T(8,128)(2,1)S(1)}, u32[]{:S(2)}, u32[]{:S(2)}) collective-permute-start(bf16[512,128]{1,0:T(8,128)(2,1)S(1)} %shard_map.79.refs_0_), channel_id=1, source_target_pairs={{0,2},{1,3},{2,0},{3,1},{4,6},{5,7},{6,4},{7,5},{8,10},{9,11},{10,... | collective-permute-start | bytes 393224 | tf_op jit(solution)/shard_map/ppermute | solution.py:370
  52.2 1.3 %collective-permute-start.20 = (f32[128,128]{1,0:T(8,128)S(1)}, f32[128,128]{1,0:T(8,128)S(1)}, u32[]{:S(2)}, u32[]{:S(2)}) collective-permute-start(f32[128,128]{1,0:T(8,128)S(1)} %shard_map.85.refs_0_), channel_id=1, source_target_pairs={{0,1},{1,0},{2,3},{3,2},{4,5},{5,4},{6,7},{7,6},{8,9},{9,8},{10,11... | collective-permute-start | bytes 196616 | tf_op jit(solution)/shard_map/ppermute | solution.py:370
  53.4 4.3 %collective-permute-start.21 = (f32[128,128]{1,0:T(8,128)S(1)}, f32[128,128]{1,0:T(8,128)S(1)}, u32[]{:S(2)}, u32[]{:S(2)}) collective-permute-start(f32[128,128]{1,0:T(8,128)S(1)} %shard_map.86.refs_0_), channel_id=1, source_target_pairs={{0,2},{1,3},{2,0},{3,1},{4,6},{5,7},{6,4},{7,5},{8,10},{9,11},{10,... | collective-permute-start | bytes 196616 | tf_op jit(solution)/shard_map/ppermute | solution.py:370
  56.2 7.3 %collective-permute-start.14 = (bf16[512,128]{1,0:T(8,128)(2,1)S(1)}, bf16[512,128]{1,0:T(8,128)(2,1)S(1)}, u32[]{:S(2)}, u32[]{:S(2)}) collective-permute-start(bf16[512,128]{1,0:T(8,128)(2,1)S(1)} %shard_map.80.refs_1_.refs_0_), channel_id=1, source_target_pairs={{0,1},{1,0},{2,3},{3,2},{4,5},{5,4},{6,7},{7,6},{8,9},{9,8},{10,11... | collective-permute-start | bytes 393224 | tf_op jit(solution)/shard_map/ppermute | solution.py:370
  58.1 4.3 %collective-permute-start.22 = (f32[128,128]{1,0:T(8,128)S(1)}, f32[128,128]{1,0:T(8,128)S(1)}, u32[]{:S(2)}, u32[]{:S(2)}) collective-permute-start(f32[128,128]{1,0:T(8,128)S(1)} %shard_map.87.refs_0_), channel_id=1, source_target_pairs={{0,4},{4,0},{8,12},{12,8},{1,5},{5,1},{9,13},{13,9},{2,6},{6,2},{1... | collective-permute-start | bytes 196616 | tf_op jit(solution)/shard_map/ppermute | solution.py:370
  62.4 5.4 %collective-permute-start.23 = (f32[128,128]{1,0:T(8,128)S(1)}, f32[128,128]{1,0:T(8,128)S(1)}, u32[]{:S(2)}, u32[]{:S(2)}) collective-permute-start(f32[128,128]{1,0:T(8,128)S(1)} %shard_map.88.refs_0_), channel_id=1, source_target_pairs={{0,8},{4,12},{8,0},{12,4},{1,9},{5,13},{9,1},{13,5},{2,10},{6,14},... | collective-permute-start | bytes 196616 | tf_op jit(solution)/shard_map/ppermute | solution.py:370
  63.8 5.4 %collective-permute-start.18 = (bf16[64,128]{1,0:T(8,128)(2,1)S(1)}, bf16[64,128]{1,0:T(8,128)(2,1)S(1)}, u32[]{:S(2)}, u32[]{:S(2)}) collective-permute-start(bf16[64,128]{1,0:T(8,128)(2,1)S(1)} %shard_map.83.refs_0_), channel_id=1, source_target_pairs={{0,4},{4,0},{8,12},{12,8},{1,5},{5,1},{9,13},{13,9},{2,6},{6,2},{1... | collective-permute-start | bytes 49160 | tf_op jit(solution)/shard_map/ppermute | solution.py:370
  69.1 6.2 %collective-permute-start.16 = (bf16[256,128]{1,0:T(8,128)(2,1)S(1)}, bf16[256,128]{1,0:T(8,128)(2,1)S(1)}, u32[]{:S(2)}, u32[]{:S(2)}) collective-permute-start(bf16[256,128]{1,0:T(8,128)(2,1)S(1)} %get-tuple-element.35.refs_0_), channel_id=1, source_target_pairs={{0,4},{4,0},{8,12},{12,8},{1,5},{5,1},{9,13},{13,9},{2,6},{6,2},{1... | collective-permute-start | bytes 196616 | tf_op jit(solution)/shard_map/ppermute | solution.py:370
  69.4 8.0 %collective-permute-start.19 = (bf16[64,128]{1,0:T(8,128)(2,1)S(1)}, bf16[64,128]{1,0:T(8,128)(2,1)S(1)}, u32[]{:S(2)}, u32[]{:S(2)}) collective-permute-start(bf16[64,128]{1,0:T(8,128)(2,1)S(1)} %get-tuple-element.40), channel_id=1, source_target_pairs={{0,8},{4,12},{8,0},{12,4},{1,9},{5,13},{9,1},{13,5},{2,10},{6,14},... | collective-permute-start | bytes 49160 | tf_op jit(solution)/shard_map/ppermute | solution.py:370
  75.1 4.4 %collective-permute-start.15 = (bf16[256,128]{1,0:T(8,128)(2,1)S(1)}, bf16[256,128]{1,0:T(8,128)(2,1)S(1)}, u32[]{:S(2)}, u32[]{:S(2)}) collective-permute-start(bf16[256,128]{1,0:T(8,128)(2,1)S(1)} %get-tuple-element.34), channel_id=1, source_target_pairs={{0,4},{4,0},{8,12},{12,8},{1,5},{5,1},{9,13},{13,9},{2,6},{6,2},{1... | collective-permute-start | bytes 196616 | tf_op jit(solution)/shard_map/ppermute | solution.py:370
  75.3 5.2 %collective-permute-start.17 = (bf16[256,128]{1,0:T(8,128)(2,1)S(1)}, bf16[256,128]{1,0:T(8,128)(2,1)S(1)}, u32[]{:S(2)}, u32[]{:S(2)}) collective-permute-start(bf16[256,128]{1,0:T(8,128)(2,1)S(1)} %shard_map.82), channel_id=1, source_target_pairs={{0,8},{4,12},{8,0},{12,4},{1,9},{5,13},{9,1},{13,5},{2,10},{6,14},... | collective-permute-start | bytes 196616 | tf_op jit(solution)/shard_map/ppermute | solution.py:370

commit v7 on v5

--- a/solution.py
+++ b/solution.py
@@ -13,7 +13,6 @@
 FP32 = lax.Precision.HIGHEST
 VMEM = pl.BlockSpec(memory_space=pltpu.VMEM)
 SMEM = pl.BlockSpec(memory_space=pltpu.SMEM)
-ANY = pl.BlockSpec(memory_space=pl.ANY)
 
 
 def nt_dot(a, b, precision=None):
@@ -34,7 +33,7 @@
     )
 
 
-def call(kernel, outs, ins, scratch=(), specs=None, cost=None):
+def call(kernel, outs, ins, scratch=(), cost=None):
     flat_ins, ins_tree = jax.tree.flatten(tuple(ins))
     flat_outs, outs_tree = jax.tree.flatten(tuple(outs))
 
@@ -52,7 +51,7 @@
     results = pl.pallas_call(
         body,
         out_shape=flat_outs,
-        in_specs=specs or [space(x) for x in flat_ins],
+        in_specs=[space(x) for x in flat_ins],
         out_specs=[space(x) for x in flat_outs],
         scratch_shapes=list(scratch),
         compiler_params=pltpu.CompilerParams(vmem_limit_bytes=48 * 1024 * 1024),
@@ -91,17 +90,10 @@
         out_ref[rows(j, frames), :] = v_ref[:, lanes(j)].astype(BF16)
 
 
-def stage_kernel(row_span, stretch, brow, bcol, blocks, index_ref, out_ref, sem):
-    copy = pltpu.make_async_copy(blocks, out_ref, sem)
-    copy.start()
-    for k in range(brow.shape[0]):
+def turn_kernel(row_span, stretch, brow, bcol, blocks, index_ref, out_ref):
+    for k in range(blocks.shape[0]):
         index_ref[0, k] = lax.rem(brow[k], row_span)
         index_ref[1, k] = lax.div(bcol[k], row_span) * stretch + lax.rem(bcol[k], stretch)
-    copy.wait()
-
-
-def turn_kernel(blocks, out_ref):
-    for k in range(blocks.shape[0]):
         out_ref[k] = blocks[k].T
 
 
@@ -127,11 +119,7 @@
         fill(panel, ref, lax.bitwise_xor(me, flip), stretch)
     acc[...] = jnp.zeros_like(acc)
     for k in range(blocks.shape[0]):
-        if half:
-            part = jnp.dot(panel[index[1, k]], blocks[k], preferred_element_type=F32)
-        else:
-            part = nt_dot(panel[index[1, k]], blocks[k])
-        acc[index[0, k]] += part
+        acc[index[0, k]] += jnp.dot(panel[index[1, k]], blocks[k], preferred_element_type=F32)
     core = lax.rem(lax.axis_index("col"), 2)
     for x in range(cols // 2):
         for j in range(stretch):
@@ -169,7 +157,7 @@
         first_refs[0][at, :] = received[data + frames :, :]
 
 
-def chips_kernel(frames, parts, out_ref):
+def chips_kernel(frames, parts, before, out_ref):
     split_at = frames // 2
     data = out_ref.shape[0] - frames
     for j in range(data // frames):
@@ -191,10 +179,7 @@
         for x in range(cols // 2):
             for j in range(stretch):
                 panel[(2 * x + side) * stretch + j] = ref[rows(x * stretch + j, frames), :]
-        at = pl.ds(pl.multiple_of(side * split_at, split_at), split_at)
-        gram[at, :] = ref[data : data + split_at, :].astype(F32) + ref[data + split_at :, :].astype(
-            F32
-        )
+    fill_gram(gram, own, received, data, frames)
     acc[...] = jnp.zeros_like(acc)
     for k in range(blocks.shape[0]):
         acc[index[1, k]] += jnp.dot(panel[index[0, k]], blocks[k], preferred_element_type=F32)
@@ -209,51 +194,71 @@
     for j in range(stretch):
         keep_ref[rows(j, frames), :] = acc[me * stretch + j]
         near_ref[rows(j, frames), :] = acc[other * stretch + j].astype(BF16)
+    if last:
+        norm_refs[0][...] = gram[:, :frames]
+        return
     whole = whole_of(panel)
     total = gram[...] + nt_dot(whole, jnp.concatenate([jnp.zeros_like(whole), whole], axis=0))
     at = stretch * frames
     out_ref = far_refs[0]
-    if last:
-        high, low = split(total[:, frames:])
-        out_ref[at:, :] = jnp.concatenate([high, low], axis=1)
-        norm_refs[0][...] = total[:, :frames]
-    else:
-        gram[...] = total
-        out_ref[at : at + split_at, :], out_ref[at + split_at : at + frames, :] = split(
-            gram[pl.ds(pl.multiple_of(core * split_at, split_at), split_at), :]
-        )
-        lane = lax.broadcasted_iota(jnp.int32, total.shape, 1)
-        row = lax.broadcasted_iota(jnp.int32, total.shape, 0)
-        on_diagonal = jnp.logical_or(lane == row, lane == row + frames)
-        diagonal = jnp.sum(jnp.where(on_diagonal, total, 0.0), axis=0, keepdims=True)
-        row = lax.broadcasted_iota(jnp.int32, (DIAG, 2 * frames), 0)
-        out_ref[at + frames :, :] = jnp.where(row == 0, diagonal, 0.0).astype(BF16)
-
-
-def rows_kernel(last, frames, sent, received, kept, out_refs, gram_ref, diag_ref):
+    gram[...] = total
+    out_ref[at : at + split_at, :], out_ref[at + split_at : at + frames, :] = split(
+        gram[pl.ds(pl.multiple_of(core * split_at, split_at), split_at), :]
+    )
+    lane = lax.broadcasted_iota(jnp.int32, total.shape, 1)
+    row = lax.broadcasted_iota(jnp.int32, total.shape, 0)
+    on_diagonal = jnp.logical_or(lane == row, lane == row + frames)
+    diagonal = jnp.sum(jnp.where(on_diagonal, total, 0.0), axis=0, keepdims=True)
+    row = lax.broadcasted_iota(jnp.int32, (DIAG, 2 * frames), 0)
+    out_ref[at + frames :, :] = jnp.where(row == 0, diagonal, 0.0).astype(BF16)
+
+
+def rows_kernel(frames, sent, received, kept, before, out_refs, gram_refs):
     split_at = frames // 2
     data = kept[0].shape[0]
     for out_ref, kept_ref, received_ref in zip(out_refs, kept, received):
         for j in range(data // frames):
             at = rows(j, frames)
             out_ref[at, :] = (kept_ref[at, :] + received_ref[at, :].astype(F32)).astype(BF16)
-    pair = (sent, received[0])
-    if last:
-        both = sum_rows(pair, slice(data, data + frames))
-        value = both[:, :frames] + both[:, frames:]
-        block = jnp.concatenate(split(value), axis=1)
-        gram_ref[...] = value
-    else:
+    if gram_refs:
+        pair = (sent, received[0])
         high, low = slice(data, data + split_at), slice(data + split_at, data + frames)
         value = sum_rows(pair, high) + sum_rows(pair, low)
-        gram_ref[...] = value
         block = jnp.concatenate(split(value), axis=0)
         tile = sum_rows(pair, slice(data + frames, data + frames + DIAG)).astype(BF16)
-        diag_ref[0][...] = tile
-    for out_ref in out_refs:
-        out_ref[data : data + frames, :] = block
-        if not last:
+        gram_refs[0][...] = value
+        gram_refs[1][...] = tile
+        for out_ref in out_refs:
+            out_ref[data : data + frames, :] = block
             out_ref[data + frames :, :] = tile
+
+
+def fill_gram(gram, own, received, data, frames):
+    split_at = frames // 2
+    core = lax.rem(lax.axis_index("col"), 2)
+    for ref, side in ((own, core), (received, 1 - core)):
+        at = pl.ds(pl.multiple_of(side * split_at, split_at), split_at)
+        gram[at, :] = ref[data : data + split_at, :].astype(F32) + ref[data + split_at :, :].astype(
+            F32
+        )
+
+
+def second_gram_kernel(data, own, received, out_ref, gram):
+    frames = out_ref.shape[0]
+    fill_gram(gram, own, received, data, frames)
+    whole = jnp.concatenate(
+        [ref[rows(j, frames), :] for ref in (own, received) for j in range(data // frames)], axis=1
+    )
+    value = gram[:, frames:] + nt_dot(whole, whole)
+    out_ref[...] = jnp.concatenate(split(value), axis=1)
+
+
+def second_pair_kernel(own, received, gram_ref, out_ref):
+    n = own.shape[0]
+    both = own[...].astype(F32) + received[...].astype(F32)
+    value = both[:, :n] + both[:, n:]
+    gram_ref[...] = value
+    out_ref[...] = jnp.concatenate(split(value), axis=1)
 
 
 def own_sum(keep, near, far, j, frames):
@@ -317,11 +322,16 @@
     return jnp.concatenate(work, axis=0)[:, n:]
 
 
-def middle_kernel(first, norm_ref, diag_ref, out_ref):
+def inverse_kernel(first, out_ref):
+    n = first.shape[0]
+    out_ref[...] = eliminate(first[:, n:], jnp.where(eye(n), 1.0, 0.0), n)
+
+
+def middle_kernel(first, inverse_ref, norm_ref, diag_ref, out_ref):
     n = first.shape[0]
     norm, energy = first[:, :n], first[:, n:]
     shift, shift_row = frame_shift(diag_ref[0:1, :], n)
-    inverse = eliminate(energy, jnp.where(eye(n), 1.0, 0.0), n)
+    inverse = inverse_ref[...]
     next_rhs = energy - shift * norm
     cross = norm_ref[...] + next_rhs * shift_row
     alpha = nn_dot(inverse, norm)
@@ -332,16 +342,21 @@
     out_ref[3] = next_rhs - nn_dot(cross, alpha)
 
 
-def final_kernel(
-    keep, near, far, gram, v_ref, image_ref, next_ref, prior, middle, x_ref, r_ref
-):
+def solve_kernel(gram, parts, middle, out_ref):
+    n = gram.shape[0]
+    schur = gram[...] - middle[2]
+    for part in parts:
+        both = part[...].astype(F32)
+        schur += both[:, :n] + both[:, n:]
+    gamma = eliminate(schur, middle[3], n)
+    out_ref[:n, :] = middle[0] - nn_dot(middle[1], gamma)
+    out_ref[n:, :] = gamma
+
+
+def final_kernel(keep, near, far, v_ref, image_ref, next_ref, prior, coeffs_ref, x_ref, r_ref):
     n = v_ref.shape[0]
-    data = keep.shape[0]
-    second = sum_rows(far, slice(data, data + n))
-    schur = gram[...] + second[:, :n] + second[:, n:] - middle[2]
-    gamma = eliminate(schur, middle[3], n)
-    coeffs = jnp.concatenate([middle[0] - nn_dot(middle[1], gamma), gamma], axis=0)
-    for j in range(data // n):
+    coeffs = coeffs_ref[...]
+    for j in range(keep.shape[0] // n):
         value = v_ref[:, lanes(j)]
         following = next_ref[:, lanes(j)]
         second_image = own_sum(keep, near, far, j, n) + prior[:, lanes(j)] * following
@@ -355,9 +370,12 @@
     return lax.ppermute(x, axis, [(i, i ^ flip) for i in range(lax.axis_size(axis))])
 
 
+def others(x, axis):
+    return (x, *(swapped(x, axis, flip) for flip in range(2, lax.axis_size(axis), 2)))
+
+
 def gather(x, axis):
-    even = [x] + [swapped(x, axis, flip) for flip in range(2, lax.axis_size(axis), 2)]
-    return tuple(part for own in even for part in (own, swapped(own, axis, 1)))
+    return tuple(part for own in others(x, axis) for part in (own, swapped(own, axis, 1)))
 
 
 def shards(right_side, prior, blocks, block_row, block_col):
@@ -377,12 +395,14 @@
     cast_type = shape((stretch * frames, BLOCK), BF16)
     aside = pl.CostEstimate(flops=2 * 10**9, bytes_accessed=8 * 10**6, transcendentals=0)
 
+    pairs = n_rows // 2 - 1
+
     def forward(search, gram, half):
         size = half_cols + frames + (frames // 2 if half else 0)
         keep, send = call(
             lambda *refs: forward_kernel(stretch, n_cols, *refs),
             (shape((size, BLOCK)),) * 2,
-            (index, search, turned if half else staged, gram, half),
+            (index, search, turned, gram, half),
             [
                 pltpu.VMEM((row_span, frames, BLOCK), F32),
                 pltpu.VMEM((col_span, frames, BLOCK), BF16),
@@ -394,18 +414,17 @@
             (shape((half_cols + frames, BLOCK), BF16), (gram_type,) if half else ()),
             (keep, received),
         )
-        parts = tuple([pair] + [swapped(pair, "col", flip) for flip in range(2, n_cols, 2)])
+        inverse = call(inverse_kernel, (shape((frames, frames)),), first, cost=aside) if half else ()
         (foot,) = call(
             lambda *refs: chips_kernel(frames, *refs),
             (shape((half_cols + frames, BLOCK), BF16),),
-            (parts,),
-        )
-        return foot, swapped(foot, "col", 1), first
-
-    def backward(own_foot, other_foot, last):
+            (others(pair, "col"), inverse),
+        )
+        return (foot, swapped(foot, "col", 1)), (*first, *inverse)
+
+    def backward(foot, last):
         size = stretch * frames
-        extra = frames + (0 if last else DIAG)
-        pairs = n_rows // 2 - 1
+        extra = 0 if last else frames + DIAG
         far, near, kept, keep, norm = call(
             lambda *refs: backward_kernel(stretch, n_cols, last, *refs),
             (
@@ -415,7 +434,7 @@
                 shape((size, BLOCK)),
                 (shape((frames, frames)),) if last else (),
             ),
-            (index, own_foot, other_foot, staged),
+            (index, *foot, blocks),
             [
                 pltpu.VMEM((col_span, frames, BLOCK), F32),
                 pltpu.VMEM((row_span, frames, BLOCK), BF16),
@@ -424,32 +443,38 @@
         )
         received = tuple(swapped(x, "row", 1) for x in far)
         near = swapped(near, "row", 1)
-        sums, gram, tile = call(
-            lambda *refs: rows_kernel(last, frames, *refs),
+        middle = ()
+        if last:
+            middle = call(
+                middle_kernel,
+                (shape((4, frames, frames)),),
+                (first, inverse, *norm, diagonal),
+                cost=aside,
+            )
+        sums, gram = call(
+            lambda *refs: rows_kernel(frames, *refs),
             (
                 (shape((size + extra, BLOCK), BF16),) * pairs,
-                shape((frames, frames) if last else (frames // 2, 2 * frames)),
-                () if last else (shape((DIAG, 2 * frames), BF16),),
+                ()
+                if last
+                else (shape((frames // 2, 2 * frames)), shape((DIAG, 2 * frames), BF16)),
             ),
-            (far[0], received, kept),
+            (far[0], received, kept, middle),
         )
         far = tuple(swapped(x, "row", 2 * (p + 1)) for p, x in enumerate(sums))
-        return (keep, near, far, gram, *tile), norm
+        return (keep, near, far, *gram), middle
 
     (cast,) = call(cast_kernel, (cast_type,), (right_side,))
     search = gather(cast, "row")
-    index, staged = call(
-        lambda *refs: stage_kernel(row_span, stretch, *refs),
+    index, turned = call(
+        lambda *refs: turn_kernel(row_span, stretch, *refs),
         (shape((2, stored), jnp.int32), shape(blocks.shape, BF16)),
         (block_row, block_col, blocks),
-        [pltpu.SemaphoreType.DMA],
-        specs=[SMEM, SMEM, ANY],
         cost=aside,
     )
     (gram,) = call(gram_kernel, (gram_type,), (right_side, prior), cost=aside)
-    own_foot, other_foot, _ = forward(search, gram, ())
-    (turned,) = call(turn_kernel, (shape(blocks.shape, BF16),), (staged,), cost=aside)
-    parts, _ = backward(own_foot, other_foot, False)
+    foot, _ = forward(search, gram, ())
+    parts, _ = backward(foot, False)
     image, following, cast, half, diagonal = call(
         image_kernel,
         (own, own, cast_type, shape((frames // 2, 2 * frames)), shape((DIAG, 2 * frames))),
@@ -457,16 +482,28 @@
     )
     search = gather(cast, "row")
     (gram,) = call(gram_kernel, (gram_type,), (following, prior), cost=aside)
-    own_foot, other_foot, (first,) = forward(search, gram, (half,))
-    parts, (norm,) = backward(own_foot, other_foot, True)
-    (middle,) = call(
-        middle_kernel, (shape((4, frames, frames)),), (first, norm, diagonal), cost=aside
+    foot, (first, inverse) = forward(search, gram, (half,))
+    (second,) = call(
+        lambda *refs: second_gram_kernel(half_cols, *refs),
+        (shape((frames, 2 * frames), BF16),),
+        foot,
+        [pltpu.VMEM((frames, 2 * frames), F32)],
+    )
+    gram, second = call(
+        second_pair_kernel,
+        (shape((frames, frames)), shape((frames, 2 * frames), BF16)),
+        (second, swapped(second, "row", 1)),
+    )
+    second = others(second, "row")[1:]
+    parts, middle = backward(foot, True)
+    (coeffs,) = call(
+        solve_kernel, (shape((2 * frames, frames)),), (gram, second, *middle), cost=aside
     )
     return tuple(
         call(
             final_kernel,
             (own, own),
-            (*parts, right_side, image, following, prior, middle),
+            (*parts, right_side, image, following, prior, coeffs),
         )
     )
 

time: 73.7 us -> 73.6 us (level)
  starting transfers between devices: 25.9 us -> 30.7 us
  waiting for transfers between devices: 28.9 us -> 25.1 us
  Pallas kernels: 16.3 us -> 15.2 us
    ppermute x18 -> x20, starting transfers between devices: 25.9 us -> 30.7 us  [swapped(): lax.ppermute(x, axis, [(i, i ^ flip) for i in range(lax.axis_size(axis))])]
    ppermute x18 -> x20, waiting for transfers between devices: 28.9 us -> 25.1 us  [swapped(): lax.ppermute(x, axis, [(i, i ^ flip) for i in range(lax.axis_size(axis))])]
    pallas_call x18 -> x21, Pallas kernels: 16.3 us -> 15.2 us  [call(): pl.pallas_call(body, out_shape=flat_outs, in_specs=[space(x) for x in fla...]
  transfers between devices with their start and end apart: 18 -> 20, of which waited for: 14 -> 13; matrix products, arithmetic and copies ran while one was open for 0% -> 0% of each run, Pallas kernels for 8% -> 12%
where the time goes in v7:
time: 73.6 us; the launch traced here: 73.4 us
  starting transfers between devices  30.7 us (42%)
  waiting for transfers between devices  25.1 us (34%)
  Pallas kernels  15.2 us (21%)
  local copies, waits for them, and re-layouts  1.6 us (2%)
  between operations  0.84 us (1%)
    ppermute x20, starting transfers between devices, swapped(): lax.ppermute(x, axis, [(i, i ^ flip) for i in range(lax.axis_size(axis))])  30.7 us
    ppermute x20, waiting for transfers between devices, swapped(): lax.ppermute(x, axis, [(i, i ^ flip) for i in range(lax.axis_size(axis))])  25.1 us
    pallas_call x21, Pallas kernels, call(): pl.pallas_call(body, out_shape=flat_outs, in_specs=[space(x) for x in fla...  15.2 us
    unnamed x14, local copies, waits for them, and re-layouts  1.6 us
  transfers between devices with their start and end apart: 20, of which 13 were waited for; matrix products, arithmetic and copies ran while one was open for 0% of the time, Pallas kernels for 12%

profile of v7, /device:TPU:0, one launch (start us, length us, event | category | flops | bytes accessed | tf_op | source)
XLA Modules:
  0.0 73.4 jit_solution(10934203696256991672)
XLA Ops:
  1.5 4.1 %collective-permute-start.1 = (bf16[256,128]{1,0:T(8,128)(2,1)S(1)}, bf16[256,128]{1,0:T(8,128)(2,1)S(1)}, u32[]{:S(2)}, u32[]{:S(2)}) collective-permute-start(bf16[256,128]{1,0:T(8,128)(2,1)S(1)} %shard_map.69.refs_1_), channel_id=1, source_target_pairs={{0,8},{4,12},{8,0},{12,4},{1,9},{5,13},{9,1},{13,5},{2,10},{6,14},... | collective-permute-start | bytes 196616 | tf_op jit(solution)/shard_map/ppermute | solution.py:370
  5.7 1.6 %collective-permute-start = (bf16[256,128]{1,0:T(8,128)(2,1)S(1)}, bf16[256,128]{1,0:T(8,128)(2,1)S(1)}, u32[]{:S(2)}, u32[]{:S(2)}) collective-permute-start(bf16[256,128]{1,0:T(8,128)(2,1)S(1)} %shard_map.69.refs_1_), channel_id=1, source_target_pairs={{0,4},{4,0},{8,12},{12,8},{1,5},{5,1},{9,13},{13,9},{2,6},{6,2},{1... | collective-permute-start | bytes 196616 | tf_op jit(solution)/shard_map/ppermute | solution.py:370
  8.7 1.4 %collective-permute-start.2 = (bf16[256,128]{1,0:T(8,128)(2,1)S(1)}, bf16[256,128]{1,0:T(8,128)(2,1)S(1)}, u32[]{:S(2)}, u32[]{:S(2)}) collective-permute-start(bf16[256,128]{1,0:T(8,128)(2,1)S(1)} %collective-permute-done.1.refs_3_), channel_id=1, source_target_pairs={{0,4},{4,0},{8,12},{12,8},{1,5},{5,1},{9,13},{13,9},{2,6},{6,2},{1... | collective-permute-start | bytes 196616 | tf_op jit(solution)/shard_map/ppermute | solution.py:370
  10.1 2.0 %shard_map.68 = (s32[2,64]{1,0:T(2,128)S(1)}, bf16[64,128,128]{2,1,0:T(8,128)(2,1)S(1)}) custom-call(s32[64]{0:T(128)S(1)} %copy-done.5, s32[64]{0:T(128)S(1)} %copy-done.6, bf16[64,128,128]{2,1,0:T(8,128)(2,1)S(1)} %copy-done), custom_call_target="tpu_custom_call" | custom-call | flops 2000000000 | bytes 8000000 | tf_op jit(solution)/shard_map/pallas_call | solution.py:51
  14.4 1.6 %collective-permute-done.3.refs_1_ = f32[576,128]{1,0:T(8,128)S(1)} collective-permute-done((f32[576,128]{1,0:T(8,128)S(1)}, f32[576,128]{1,0:T(8,128)S(1)}, u32[]{:S(2)}, u32[]{:S(2)}) %collective-permute-start.3) | collective-permute-done | bytes 294944 | tf_op jit(solution)/shard_map/ppermute | solution.py:370
  16.0 1.9 %collective-permute-start.4 = (bf16[576,128]{1,0:T(8,128)(2,1)S(1)}, bf16[576,128]{1,0:T(8,128)(2,1)S(1)}, u32[]{:S(2)}, u32[]{:S(2)}) collective-permute-start(bf16[576,128]{1,0:T(8,128)(2,1)S(1)} %shard_map.72.refs_0_), channel_id=1, source_target_pairs={{0,2},{1,3},{2,0},{3,1},{4,6},{5,7},{6,4},{7,5},{8,10},{9,11},{10,... | collective-permute-start | bytes 442376 | tf_op jit(solution)/shard_map/ppermute | solution.py:370
  17.9 4.1 %collective-permute-done.4.refs_1_ = bf16[576,128]{1,0:T(8,128)(2,1)S(1)} collective-permute-done((bf16[576,128]{1,0:T(8,128)(2,1)S(1)}, bf16[576,128]{1,0:T(8,128)(2,1)S(1)}, u32[]{:S(2)}, u32[]{:S(2)}) %collective-permute-start.4) | collective-permute-done | bytes 147488 | tf_op jit(solution)/shard_map/ppermute | solution.py:370
  22.2 1.4 %collective-permute-done.5.refs_2_ = bf16[576,128]{1,0:T(8,128)(2,1)S(1)} collective-permute-done((bf16[576,128]{1,0:T(8,128)(2,1)S(1)}, bf16[576,128]{1,0:T(8,128)(2,1)S(1)}, u32[]{:S(2)}, u32[]{:S(2)}) %collective-permute-start.5) | collective-permute-done | bytes 147488 | tf_op jit(solution)/shard_map/ppermute | solution.py:370
  23.5 1.5 %shard_map.74 = (bf16[336,128]{1,0:T(8,128)(2,1)S(1)}, bf16[256,128]{1,0:T(8,128)(2,1)S(1)}, f32[256,128]{1,0:T(8,128)S(1)}, f32[256,128]{1,0:T(8,128)S(1)}) custom-call(s32[2,64]{1,0:T(2,128)S(1)} %get-tuple-element.29.refs_0_, bf16[576,128]{1,0:T(8,128)(2,1)S(1)} %shard_map.73.refs_1_, bf16[576,128]{1,0:T(8,128)(2,1)S(1)} %collective-permute-done.5.refs_2_, ...), custom_call_target="tpu_custom_call" | custom-call | tf_op jit(solution)/shard_map/pallas_call | solution.py:51
  25.0 1.3 %collective-permute-start.7 = (bf16[336,128]{1,0:T(8,128)(2,1)S(1)}, bf16[336,128]{1,0:T(8,128)(2,1)S(1)}, u32[]{:S(2)}, u32[]{:S(2)}) collective-permute-start(bf16[336,128]{1,0:T(8,128)(2,1)S(1)} %get-tuple-element.35.refs_0_), channel_id=1, source_target_pairs={{0,4},{4,0},{8,12},{12,8},{1,5},{5,1},{9,13},{13,9},{2,6},{6,2},{1... | collective-permute-start | bytes 258056 | tf_op jit(solution)/shard_map/ppermute | solution.py:370
  26.3 3.3 %collective-permute-done.7.refs_1_ = bf16[336,128]{1,0:T(8,128)(2,1)S(1)} collective-permute-done((bf16[336,128]{1,0:T(8,128)(2,1)S(1)}, bf16[336,128]{1,0:T(8,128)(2,1)S(1)}, u32[]{:S(2)}, u32[]{:S(2)}) %collective-permute-start.7) | collective-permute-done | bytes 86048 | tf_op jit(solution)/shard_map/ppermute | solution.py:370
  29.7 2.8 %collective-permute-start.8 = (bf16[336,128]{1,0:T(8,128)(2,1)S(1)}, bf16[336,128]{1,0:T(8,128)(2,1)S(1)}, u32[]{:S(2)}, u32[]{:S(2)}) collective-permute-start(bf16[336,128]{1,0:T(8,128)(2,1)S(1)} %get-tuple-element.37), channel_id=1, source_target_pairs={{0,8},{4,12},{8,0},{12,4},{1,9},{5,13},{9,1},{13,5},{2,10},{6,14},... | collective-permute-start | bytes 258056 | tf_op jit(solution)/shard_map/ppermute | solution.py:370
  32.4 1.7 %collective-permute-start.6 = (bf16[256,128]{1,0:T(8,128)(2,1)S(1)}, bf16[256,128]{1,0:T(8,128)(2,1)S(1)}, u32[]{:S(2)}, u32[]{:S(2)}) collective-permute-start(bf16[256,128]{1,0:T(8,128)(2,1)S(1)} %get-tuple-element.34), channel_id=1, source_target_pairs={{0,4},{4,0},{8,12},{12,8},{1,5},{5,1},{9,13},{13,9},{2,6},{6,2},{1... | collective-permute-start | bytes 196616 | tf_op jit(solution)/shard_map/ppermute | solution.py:370
  34.2 2.6 %collective-permute-done.6.refs_1_ = bf16[256,128]{1,0:T(8,128)(2,1)S(1)} collective-permute-done((bf16[256,128]{1,0:T(8,128)(2,1)S(1)}, bf16[256,128]{1,0:T(8,128)(2,1)S(1)}, u32[]{:S(2)}, u32[]{:S(2)}) %collective-permute-start.6) | collective-permute-done | bytes 65568 | tf_op jit(solution)/shard_map/ppermute | solution.py:370
  37.1 1.7 %collective-permute-start.10 = (bf16[256,128]{1,0:T(8,128)(2,1)S(1)}, bf16[256,128]{1,0:T(8,128)(2,1)S(1)}, u32[]{:S(2)}, u32[]{:S(2)}) collective-permute-start(bf16[256,128]{1,0:T(8,128)(2,1)S(1)} %get-tuple-element.40.refs_1_), channel_id=1, source_target_pairs={{0,8},{4,12},{8,0},{12,4},{1,9},{5,13},{9,1},{13,5},{2,10},{6,14},... | collective-permute-start | bytes 196616 | tf_op jit(solution)/shard_map/ppermute | solution.py:370
  38.8 2.1 %collective-permute-start.9 = (bf16[256,128]{1,0:T(8,128)(2,1)S(1)}, bf16[256,128]{1,0:T(8,128)(2,1)S(1)}, u32[]{:S(2)}, u32[]{:S(2)}) collective-permute-start(bf16[256,128]{1,0:T(8,128)(2,1)S(1)} %get-tuple-element.40.refs_1_), channel_id=1, source_target_pairs={{0,4},{4,0},{8,12},{12,8},{1,5},{5,1},{9,13},{13,9},{2,6},{6,2},{1... | collective-permute-start | bytes 196616 | tf_op jit(solution)/shard_map/ppermute | solution.py:370
  40.9 1.4 %collective-permute-done.10.refs_3_ = bf16[256,128]{1,0:T(8,128)(2,1)S(1)} collective-permute-done((bf16[256,128]{1,0:T(8,128)(2,1)S(1)}, bf16[256,128]{1,0:T(8,128)(2,1)S(1)}, u32[]{:S(2)}, u32[]{:S(2)}) %collective-permute-start.10) | collective-permute-done | bytes 65568 | tf_op jit(solution)/shard_map/ppermute | solution.py:370
  42.3 1.6 %collective-permute-start.11 = (bf16[256,128]{1,0:T(8,128)(2,1)S(1)}, bf16[256,128]{1,0:T(8,128)(2,1)S(1)}, u32[]{:S(2)}, u32[]{:S(2)}) collective-permute-start(bf16[256,128]{1,0:T(8,128)(2,1)S(1)} %collective-permute-done.10.refs_3_), channel_id=1, source_target_pairs={{0,4},{4,0},{8,12},{12,8},{1,5},{5,1},{9,13},{13,9},{2,6},{6,2},{1... | collective-permute-start | bytes 196616 | tf_op jit(solution)/shard_map/ppermute | solution.py:370
  44.3 2.2 %collective-permute-done.11.refs_4_ = bf16[256,128]{1,0:T(8,128)(2,1)S(1)} collective-permute-done((bf16[256,128]{1,0:T(8,128)(2,1)S(1)}, bf16[256,128]{1,0:T(8,128)(2,1)S(1)}, u32[]{:S(2)}, u32[]{:S(2)}) %collective-permute-start.11) | collective-permute-done | bytes 65568 | tf_op jit(solution)/shard_map/ppermute | solution.py:370
  46.6 1.4 %shard_map.78 = (f32[608,128]{1,0:T(8,128)S(1)}, f32[608,128]{1,0:T(8,128)S(1)}) custom-call(s32[2,64]{1,0:T(2,128)S(1)} %get-tuple-element.29.refs_0_, bf16[256,128]{1,0:T(8,128)(2,1)S(1)} %get-tuple-element.40.refs_1_, bf16[256,128]{1,0:T(8,128)(2,1)S(1)} %collective-permute-done.9.refs_2_, bf16[256,128]{1,0:T(8,128)(2,1)S(1)} %collective-permute-done.10.refs_3_, ...), custom_call_target="tpu_custom_call" | custom-call | tf_op jit(solution)/shard_map/pallas_call | solution.py:51
  48.0 1.6 %collective-permute-done.12.refs_1_ = f32[608,128]{1,0:T(8,128)S(1)} collective-permute-done((f32[608,128]{1,0:T(8,128)S(1)}, f32[608,128]{1,0:T(8,128)S(1)}, u32[]{:S(2)}, u32[]{:S(2)}) %collective-permute-start.12) | collective-permute-done | bytes 311328 | tf_op jit(solution)/shard_map/ppermute | solution.py:370
  49.7 1.6 %collective-permute-start.13 = (bf16[576,128]{1,0:T(8,128)(2,1)S(1)}, bf16[576,128]{1,0:T(8,128)(2,1)S(1)}, u32[]{:S(2)}, u32[]{:S(2)}) collective-permute-start(bf16[576,128]{1,0:T(8,128)(2,1)S(1)} %get-tuple-element.45.refs_0_), channel_id=1, source_target_pairs={{0,2},{1,3},{2,0},{3,1},{4,6},{5,7},{6,4},{7,5},{8,10},{9,11},{10,... | collective-permute-start | bytes 442376 | tf_op jit(solution)/shard_map/ppermute | solution.py:370
  51.2 1.7 %shard_map.80.refs_2_.refs_1_ = f32[64,64]{1,0:T(8,128)S(1)} custom-call(f32[64,128]{1,0:T(8,128)S(1)} %get-tuple-element.46.refs_0_), custom_call_target="tpu_custom_call" | custom-call | flops 2000000000 | bytes 8000000 | tf_op jit(solution)/shard_map/pallas_call | solution.py:51
  53.0 2.7 %collective-permute-done.13.refs_1_ = bf16[576,128]{1,0:T(8,128)(2,1)S(1)} collective-permute-done((bf16[576,128]{1,0:T(8,128)(2,1)S(1)}, bf16[576,128]{1,0:T(8,128)(2,1)S(1)}, u32[]{:S(2)}, u32[]{:S(2)}) %collective-permute-start.13) | collective-permute-done | bytes 147488 | tf_op jit(solution)/shard_map/ppermute | solution.py:370
  55.7 1.4 %collective-permute-done.14.refs_2_.refs_1_ = bf16[576,128]{1,0:T(8,128)(2,1)S(1)} collective-permute-done((bf16[576,128]{1,0:T(8,128)(2,1)S(1)}, bf16[576,128]{1,0:T(8,128)(2,1)S(1)}, u32[]{:S(2)}, u32[]{:S(2)}) %collective-permute-start.14) | collective-permute-done | bytes 147488 | tf_op jit(solution)/shard_map/ppermute | solution.py:370
  57.5 1.7 %collective-permute-start.18 = (bf16[64,128]{1,0:T(8,128)(2,1)S(1)}, bf16[64,128]{1,0:T(8,128)(2,1)S(1)}, u32[]{:S(2)}, u32[]{:S(2)}) collective-permute-start(bf16[64,128]{1,0:T(8,128)(2,1)S(1)} %shard_map.85.refs_0_), channel_id=1, source_target_pairs={{0,4},{4,0},{8,12},{12,8},{1,5},{5,1},{9,13},{13,9},{2,6},{6,2},{1... | collective-permute-start | bytes 49160 | tf_op jit(solution)/shard_map/ppermute | solution.py:370
  59.1 1.3 %shard_map.82 = (bf16[256,128]{1,0:T(8,128)(2,1)S(1)}, bf16[256,128]{1,0:T(8,128)(2,1)S(1)}, f32[256,128]{1,0:T(8,128)S(1)}, f32[256,128]{1,0:T(8,128)S(1)}, f32[64,64]{1,0:T(8,128)S(1)}) custom-call(s32[2,64]{1,0:T(2,128)S(1)} %get-tuple-element.29.refs_0_, bf16[576,128]{1,0:T(8,128)(2,1)S(1)} %shard_map.81.refs_1_.refs_0_, ...), custom_call_target="tpu_custom_call" | custom-call | tf_op jit(solution)/shard_map/pallas_call | solution.py:51
  60.9 1.6 %collective-permute-start.16 = (bf16[256,128]{1,0:T(8,128)(2,1)S(1)}, bf16[256,128]{1,0:T(8,128)(2,1)S(1)}, u32[]{:S(2)}, u32[]{:S(2)}) collective-permute-start(bf16[256,128]{1,0:T(8,128)(2,1)S(1)} %get-tuple-element.49.refs_0_), channel_id=1, source_target_pairs={{0,4},{4,0},{8,12},{12,8},{1,5},{5,1},{9,13},{13,9},{2,6},{6,2},{1... | collective-permute-start | bytes 196616 | tf_op jit(solution)/shard_map/ppermute | solution.py:370
  62.7 2.5 %collective-permute-start.19 = (bf16[64,128]{1,0:T(8,128)(2,1)S(1)}, bf16[64,128]{1,0:T(8,128)(2,1)S(1)}, u32[]{:S(2)}, u32[]{:S(2)}) collective-permute-start(bf16[64,128]{1,0:T(8,128)(2,1)S(1)} %get-tuple-element.55), channel_id=1, source_target_pairs={{0,8},{4,12},{8,0},{12,4},{1,9},{5,13},{9,1},{13,5},{2,10},{6,14},... | collective-permute-start | bytes 49160 | tf_op jit(solution)/shard_map/ppermute | solution.py:370
  66.2 2.4 %collective-permute-start.17 = (bf16[256,128]{1,0:T(8,128)(2,1)S(1)}, bf16[256,128]{1,0:T(8,128)(2,1)S(1)}, u32[]{:S(2)}, u32[]{:S(2)}) collective-permute-start(bf16[256,128]{1,0:T(8,128)(2,1)S(1)} %shard_map.84), channel_id=1, source_target_pairs={{0,8},{4,12},{8,0},{12,4},{1,9},{5,13},{9,1},{13,5},{2,10},{6,14},... | collective-permute-start | bytes 196616 | tf_op jit(solution)/shard_map/ppermute | solution.py:370
  68.6 2.1 %shard_map.87.refs_7_ = f32[128,64]{1,0:T(8,128)S(1)} custom-call(f32[64,64]{1,0:T(8,128)S(1)} %get-tuple-element.54.refs_0_, bf16[64,128]{1,0:T(8,128)(2,1)S(1)} %collective-permute-done.19.refs_1_, f32[4,64,64]{2,1,0:T(8,128)S(1)} %shard_map.83.refs_3_.refs_2_), custom_call_target="tpu_custom_call" | custom-call | flops 2000000000 | bytes 8000000 | tf_op jit(solution)/shard_map/pallas_call | solution.py:51
  70.7 1.4 %collective-permute-done.17.refs_2_ = bf16[256,128]{1,0:T(8,128)(2,1)S(1)} collective-permute-done((bf16[256,128]{1,0:T(8,128)(2,1)S(1)}, bf16[256,128]{1,0:T(8,128)(2,1)S(1)}, u32[]{:S(2)}, u32[]{:S(2)}) %collective-permute-start.17) | collective-permute-done | bytes 65568 | tf_op jit(solution)/shard_map/ppermute | solution.py:370
  (43 shorter events, 8.9 us)
Async XLA Ops:
  0.6 0.9 %copy-start.1 = (f32[64,512]{1,0:T(8,128)S(1)}, f32[64,512]{1,0:T(8,128)}, u32[]{:S(2)}) copy-start(f32[64,512]{1,0:T(8,128)} %refs_3_.5) | copy-start | bytes 393220
  1.5 7.2 %collective-permute-start.1 = (bf16[256,128]{1,0:T(8,128)(2,1)S(1)}, bf16[256,128]{1,0:T(8,128)(2,1)S(1)}, u32[]{:S(2)}, u32[]{:S(2)}) collective-permute-start(bf16[256,128]{1,0:T(8,128)(2,1)S(1)} %shard_map.69.refs_1_), channel_id=1, source_target_pairs={{0,8},{4,12},{8,0},{12,4},{1,9},{5,13},{9,1},{13,5},{2,10},{6,14},... | collective-permute-start | bytes 196616 | tf_op jit(solution)/shard_map/ppermute | solution.py:370
  5.7 6.4 %collective-permute-start = (bf16[256,128]{1,0:T(8,128)(2,1)S(1)}, bf16[256,128]{1,0:T(8,128)(2,1)S(1)}, u32[]{:S(2)}, u32[]{:S(2)}) collective-permute-start(bf16[256,128]{1,0:T(8,128)(2,1)S(1)} %shard_map.69.refs_1_), channel_id=1, source_target_pairs={{0,4},{4,0},{8,12},{12,8},{1,5},{5,1},{9,13},{13,9},{2,6},{6,2},{1... | collective-permute-start | bytes 196616 | tf_op jit(solution)/shard_map/ppermute | solution.py:370
  7.2 0.7 copy-start.3
  7.9 2.2 %copy-start = (bf16[64,128,128]{2,1,0:T(8,128)(2,1)S(1)}, bf16[64,128,128]{2,1,0:T(8,128)(2,1)}, u32[]{:S(2)}) copy-start(bf16[64,128,128]{2,1,0:T(8,128)(2,1)} %refs_3_.4) | copy-start | bytes 6291460
  7.9 2.2 %copy-start.5 = (s32[64]{0:T(128)S(1)}, s32[64]{0:T(128)}, u32[]{:S(2)}) copy-start(s32[64]{0:T(128)} %refs_0_.3) | copy-start | bytes 772
  7.9 2.2 %copy-start.6 = (s32[64]{0:T(128)S(1)}, s32[64]{0:T(128)}, u32[]{:S(2)}) copy-start(s32[64]{0:T(128)} %refs_1_.1) | copy-start | bytes 772
  8.7 4.3 %collective-permute-start.2 = (bf16[256,128]{1,0:T(8,128)(2,1)S(1)}, bf16[256,128]{1,0:T(8,128)(2,1)S(1)}, u32[]{:S(2)}, u32[]{:S(2)}) collective-permute-start(bf16[256,128]{1,0:T(8,128)(2,1)S(1)} %collective-permute-done.1.refs_3_), channel_id=1, source_target_pairs={{0,4},{4,0},{8,12},{12,8},{1,5},{5,1},{9,13},{13,9},{2,6},{6,2},{1... | collective-permute-start | bytes 196616 | tf_op jit(solution)/shard_map/ppermute | solution.py:370
  14.3 22.6 %copy-start.2 = (f32[64,512]{1,0:T(8,128)S(1)}, f32[64,512]{1,0:T(8,128)}, u32[]{:S(2)}) copy-start(f32[64,512]{1,0:T(8,128)} %refs_3_.5) | copy-start | bytes 393220
  14.3 22.5 %copy-start.4 = (f32[512]{0:T(512)S(1)}, f32[512]{0:T(512)}, u32[]{:S(2)}) copy-start(f32[512]{0:T(512)} %param.6) | copy-start | bytes 6148
  14.3 1.6 %collective-permute-start.3 = (f32[576,128]{1,0:T(8,128)S(1)}, f32[576,128]{1,0:T(8,128)S(1)}, u32[]{:S(2)}, u32[]{:S(2)}) collective-permute-start(f32[576,128]{1,0:T(8,128)S(1)} %get-tuple-element.32), channel_id=1, source_target_pairs={{0,1},{1,0},{2,3},{3,2},{4,5},{5,4},{6,7},{7,6},{8,9},{9,8},{10,11... | collective-permute-start | bytes 884744 | tf_op jit(solution)/shard_map/ppermute | solution.py:370
  16.0 6.1 %collective-permute-start.4 = (bf16[576,128]{1,0:T(8,128)(2,1)S(1)}, bf16[576,128]{1,0:T(8,128)(2,1)S(1)}, u32[]{:S(2)}, u32[]{:S(2)}) collective-permute-start(bf16[576,128]{1,0:T(8,128)(2,1)S(1)} %shard_map.72.refs_0_), channel_id=1, source_target_pairs={{0,2},{1,3},{2,0},{3,1},{4,6},{5,7},{6,4},{7,5},{8,10},{9,11},{10,... | collective-permute-start | bytes 442376 | tf_op jit(solution)/shard_map/ppermute | solution.py:370
  22.1 1.4 %collective-permute-start.5 = (bf16[576,128]{1,0:T(8,128)(2,1)S(1)}, bf16[576,128]{1,0:T(8,128)(2,1)S(1)}, u32[]{:S(2)}, u32[]{:S(2)}) collective-permute-start(bf16[576,128]{1,0:T(8,128)(2,1)S(1)} %shard_map.73.refs_1_), channel_id=1, source_target_pairs={{0,1},{1,0},{2,3},{3,2},{4,5},{5,4},{6,7},{7,6},{8,9},{9,8},{10,11... | collective-permute-start | bytes 442376 | tf_op jit(solution)/shard_map/ppermute | solution.py:370
  25.0 4.6 %collective-permute-start.7 = (bf16[336,128]{1,0:T(8,128)(2,1)S(1)}, bf16[336,128]{1,0:T(8,128)(2,1)S(1)}, u32[]{:S(2)}, u32[]{:S(2)}) collective-permute-start(bf16[336,128]{1,0:T(8,128)(2,1)S(1)} %get-tuple-element.35.refs_0_), channel_id=1, source_target_pairs={{0,4},{4,0},{8,12},{12,8},{1,5},{5,1},{9,13},{13,9},{2,6},{6,2},{1... | collective-permute-start | bytes 258056 | tf_op jit(solution)/shard_map/ppermute | solution.py:370
  29.7 7.2 %collective-permute-start.8 = (bf16[336,128]{1,0:T(8,128)(2,1)S(1)}, bf16[336,128]{1,0:T(8,128)(2,1)S(1)}, u32[]{:S(2)}, u32[]{:S(2)}) collective-permute-start(bf16[336,128]{1,0:T(8,128)(2,1)S(1)} %get-tuple-element.37), channel_id=1, source_target_pairs={{0,8},{4,12},{8,0},{12,4},{1,9},{5,13},{9,1},{13,5},{2,10},{6,14},... | collective-permute-start | bytes 258056 | tf_op jit(solution)/shard_map/ppermute | solution.py:370
  32.4 4.4 %collective-permute-start.6 = (bf16[256,128]{1,0:T(8,128)(2,1)S(1)}, bf16[256,128]{1,0:T(8,128)(2,1)S(1)}, u32[]{:S(2)}, u32[]{:S(2)}) collective-permute-start(bf16[256,128]{1,0:T(8,128)(2,1)S(1)} %get-tuple-element.34), channel_id=1, source_target_pairs={{0,4},{4,0},{8,12},{12,8},{1,5},{5,1},{9,13},{13,9},{2,6},{6,2},{1... | collective-permute-start | bytes 196616 | tf_op jit(solution)/shard_map/ppermute | solution.py:370
  37.1 5.2 %collective-permute-start.10 = (bf16[256,128]{1,0:T(8,128)(2,1)S(1)}, bf16[256,128]{1,0:T(8,128)(2,1)S(1)}, u32[]{:S(2)}, u32[]{:S(2)}) collective-permute-start(bf16[256,128]{1,0:T(8,128)(2,1)S(1)} %get-tuple-element.40.refs_1_), channel_id=1, source_target_pairs={{0,8},{4,12},{8,0},{12,4},{1,9},{5,13},{9,1},{13,5},{2,10},{6,14},... | collective-permute-start | bytes 196616 | tf_op jit(solution)/shard_map/ppermute | solution.py:370
  38.8 5.6 %collective-permute-start.9 = (bf16[256,128]{1,0:T(8,128)(2,1)S(1)}, bf16[256,128]{1,0:T(8,128)(2,1)S(1)}, u32[]{:S(2)}, u32[]{:S(2)}) collective-permute-start(bf16[256,128]{1,0:T(8,128)(2,1)S(1)} %get-tuple-element.40.refs_1_), channel_id=1, source_target_pairs={{0,4},{4,0},{8,12},{12,8},{1,5},{5,1},{9,13},{13,9},{2,6},{6,2},{1... | collective-permute-start | bytes 196616 | tf_op jit(solution)/shard_map/ppermute | solution.py:370
  42.3 4.3 %collective-permute-start.11 = (bf16[256,128]{1,0:T(8,128)(2,1)S(1)}, bf16[256,128]{1,0:T(8,128)(2,1)S(1)}, u32[]{:S(2)}, u32[]{:S(2)}) collective-permute-start(bf16[256,128]{1,0:T(8,128)(2,1)S(1)} %collective-permute-done.10.refs_3_), channel_id=1, source_target_pairs={{0,4},{4,0},{8,12},{12,8},{1,5},{5,1},{9,13},{13,9},{2,6},{6,2},{1... | collective-permute-start | bytes 196616 | tf_op jit(solution)/shard_map/ppermute | solution.py:370
  48.0 1.7 %collective-permute-start.12 = (f32[608,128]{1,0:T(8,128)S(1)}, f32[608,128]{1,0:T(8,128)S(1)}, u32[]{:S(2)}, u32[]{:S(2)}) collective-permute-start(f32[608,128]{1,0:T(8,128)S(1)} %get-tuple-element.44), channel_id=1, source_target_pairs={{0,1},{1,0},{2,3},{3,2},{4,5},{5,4},{6,7},{7,6},{8,9},{9,8},{10,11... | collective-permute-start | bytes 933896 | tf_op jit(solution)/shard_map/ppermute | solution.py:370
  49.7 6.0 %collective-permute-start.13 = (bf16[576,128]{1,0:T(8,128)(2,1)S(1)}, bf16[576,128]{1,0:T(8,128)(2,1)S(1)}, u32[]{:S(2)}, u32[]{:S(2)}) collective-permute-start(bf16[576,128]{1,0:T(8,128)(2,1)S(1)} %get-tuple-element.45.refs_0_), channel_id=1, source_target_pairs={{0,2},{1,3},{2,0},{3,1},{4,6},{5,7},{6,4},{7,5},{8,10},{9,11},{10,... | collective-permute-start | bytes 442376 | tf_op jit(solution)/shard_map/ppermute | solution.py:370
  55.7 1.4 %collective-permute-start.14 = (bf16[576,128]{1,0:T(8,128)(2,1)S(1)}, bf16[576,128]{1,0:T(8,128)(2,1)S(1)}, u32[]{:S(2)}, u32[]{:S(2)}) collective-permute-start(bf16[576,128]{1,0:T(8,128)(2,1)S(1)} %shard_map.81.refs_1_.refs_0_), channel_id=1, source_target_pairs={{0,1},{1,0},{2,3},{3,2},{4,5},{5,4},{6,7},{7,6},{8,9},{9,8},{10,11... | collective-permute-start | bytes 442376 | tf_op jit(solution)/shard_map/ppermute | solution.py:370
  57.5 5.1 %collective-permute-start.18 = (bf16[64,128]{1,0:T(8,128)(2,1)S(1)}, bf16[64,128]{1,0:T(8,128)(2,1)S(1)}, u32[]{:S(2)}, u32[]{:S(2)}) collective-permute-start(bf16[64,128]{1,0:T(8,128)(2,1)S(1)} %shard_map.85.refs_0_), channel_id=1, source_target_pairs={{0,4},{4,0},{8,12},{12,8},{1,5},{5,1},{9,13},{13,9},{2,6},{6,2},{1... | collective-permute-start | bytes 49160 | tf_op jit(solution)/shard_map/ppermute | solution.py:370
  60.4 10.2 %collective-permute-start.15 = (bf16[256,128]{1,0:T(8,128)(2,1)S(1)}, bf16[256,128]{1,0:T(8,128)(2,1)S(1)}, u32[]{:S(2)}, u32[]{:S(2)}) collective-permute-start(bf16[256,128]{1,0:T(8,128)(2,1)S(1)} %get-tuple-element.48), channel_id=1, source_target_pairs={{0,4},{4,0},{8,12},{12,8},{1,5},{5,1},{9,13},{13,9},{2,6},{6,2},{1... | collective-permute-start | bytes 196616 | tf_op jit(solution)/shard_map/ppermute | solution.py:370
  60.9 5.2 %collective-permute-start.16 = (bf16[256,128]{1,0:T(8,128)(2,1)S(1)}, bf16[256,128]{1,0:T(8,128)(2,1)S(1)}, u32[]{:S(2)}, u32[]{:S(2)}) collective-permute-start(bf16[256,128]{1,0:T(8,128)(2,1)S(1)} %get-tuple-element.49.refs_0_), channel_id=1, source_target_pairs={{0,4},{4,0},{8,12},{12,8},{1,5},{5,1},{9,13},{13,9},{2,6},{6,2},{1... | collective-permute-start | bytes 196616 | tf_op jit(solution)/shard_map/ppermute | solution.py:370
  62.7 5.9 %collective-permute-start.19 = (bf16[64,128]{1,0:T(8,128)(2,1)S(1)}, bf16[64,128]{1,0:T(8,128)(2,1)S(1)}, u32[]{:S(2)}, u32[]{:S(2)}) collective-permute-start(bf16[64,128]{1,0:T(8,128)(2,1)S(1)} %get-tuple-element.55), channel_id=1, source_target_pairs={{0,8},{4,12},{8,0},{12,4},{1,9},{5,13},{9,1},{13,5},{2,10},{6,14},... | collective-permute-start | bytes 49160 | tf_op jit(solution)/shard_map/ppermute | solution.py:370
  66.2 5.9 %collective-permute-start.17 = (bf16[256,128]{1,0:T(8,128)(2,1)S(1)}, bf16[256,128]{1,0:T(8,128)(2,1)S(1)}, u32[]{:S(2)}, u32[]{:S(2)}) collective-permute-start(bf16[256,128]{1,0:T(8,128)(2,1)S(1)} %shard_map.84), channel_id=1, source_target_pairs={{0,8},{4,12},{8,0},{12,4},{1,9},{5,13},{9,1},{13,5},{2,10},{6,14},... | collective-permute-start | bytes 196616 | tf_op jit(solution)/shard_map/ppermute | solution.py:370

commit v8 on v7

--- a/solution.py
+++ b/solution.py
@@ -169,7 +169,7 @@
 
 def backward_kernel(
     stretch, cols, last, index, own, received, blocks,
-    far_refs, near_ref, keep_refs, keep_ref, norm_refs, acc, panel, gram,
+    far_refs, keep_ref, last_refs, acc, panel, gram,
 ):
     frames = panel.shape[1]
     split_at = frames // 2
@@ -184,6 +184,16 @@
     for k in range(blocks.shape[0]):
         acc[index[1, k]] += jnp.dot(panel[index[0, k]], blocks[k], preferred_element_type=F32)
     me = lax.axis_index("row")
+    for j in range(stretch):
+        keep_ref[rows(j, frames), :] = acc[me * stretch + j]
+    if last:
+        for at, far_ref in enumerate(far_refs):
+            shard = lax.bitwise_xor(me, len(far_refs) - at)
+            for j in range(stretch):
+                far_ref[rows(j, frames), :] = acc[shard * stretch + j].astype(BF16)
+        last_refs[0][...] = gram[:, :frames]
+        return
+    near_ref, keep_refs = last_refs
     for far, (far_ref, kept_ref) in enumerate(zip(far_refs, keep_refs)):
         shard = lax.bitwise_xor(me, 2 * (far + 1))
         other = lax.bitwise_xor(shard, 1)
@@ -192,11 +202,7 @@
             far_ref[rows(j, frames), :] = acc[other * stretch + j].astype(BF16)
     other = lax.bitwise_xor(me, 1)
     for j in range(stretch):
-        keep_ref[rows(j, frames), :] = acc[me * stretch + j]
         near_ref[rows(j, frames), :] = acc[other * stretch + j].astype(BF16)
-    if last:
-        norm_refs[0][...] = gram[:, :frames]
-        return
     whole = whole_of(panel)
     total = gram[...] + nt_dot(whole, jnp.concatenate([jnp.zeros_like(whole), whole], axis=0))
     at = stretch * frames
@@ -213,24 +219,23 @@
     out_ref[at + frames :, :] = jnp.where(row == 0, diagonal, 0.0).astype(BF16)
 
 
-def rows_kernel(frames, sent, received, kept, before, out_refs, gram_refs):
+def rows_kernel(frames, sent, received, kept, out_refs, gram_ref, tile_ref):
     split_at = frames // 2
     data = kept[0].shape[0]
     for out_ref, kept_ref, received_ref in zip(out_refs, kept, received):
         for j in range(data // frames):
             at = rows(j, frames)
             out_ref[at, :] = (kept_ref[at, :] + received_ref[at, :].astype(F32)).astype(BF16)
-    if gram_refs:
-        pair = (sent, received[0])
-        high, low = slice(data, data + split_at), slice(data + split_at, data + frames)
-        value = sum_rows(pair, high) + sum_rows(pair, low)
-        block = jnp.concatenate(split(value), axis=0)
-        tile = sum_rows(pair, slice(data + frames, data + frames + DIAG)).astype(BF16)
-        gram_refs[0][...] = value
-        gram_refs[1][...] = tile
-        for out_ref in out_refs:
-            out_ref[data : data + frames, :] = block
-            out_ref[data + frames :, :] = tile
+    pair = (sent, received[0])
+    high, low = slice(data, data + split_at), slice(data + split_at, data + frames)
+    value = sum_rows(pair, high) + sum_rows(pair, low)
+    block = jnp.concatenate(split(value), axis=0)
+    tile = sum_rows(pair, slice(data + frames, data + frames + DIAG)).astype(BF16)
+    gram_ref[...] = value
+    tile_ref[...] = tile
+    for out_ref in out_refs:
+        out_ref[data : data + frames, :] = block
+        out_ref[data + frames :, :] = tile
 
 
 def fill_gram(gram, own, received, data, frames):
@@ -261,9 +266,9 @@
     out_ref[...] = jnp.concatenate(split(value), axis=1)
 
 
-def own_sum(keep, near, far, j, frames):
+def own_sum(keep, parts, j, frames):
     at = rows(j, frames)
-    return keep[at, :] + sum_rows((near, *far), at)
+    return keep[at, :] + sum_rows(parts, at)
 
 
 def frame_shift(diagonal, frames):
@@ -282,7 +287,7 @@
     shift, _ = frame_shift(diagonal[0:1, :], frames)
     for j in range(data // frames):
         value = v_ref[:, lanes(j)]
-        image = own_sum(keep, near, far, j, frames) + prior[:, lanes(j)] * value
+        image = own_sum(keep, (near, *far), j, frames) + prior[:, lanes(j)] * value
         following = image - shift * value
         image_ref[:, lanes(j)] = image
         next_ref[:, lanes(j)] = following
@@ -353,13 +358,13 @@
     out_ref[n:, :] = gamma
 
 
-def final_kernel(keep, near, far, v_ref, image_ref, next_ref, prior, coeffs_ref, x_ref, r_ref):
+def final_kernel(keep, parts, v_ref, image_ref, next_ref, prior, coeffs_ref, x_ref, r_ref):
     n = v_ref.shape[0]
     coeffs = coeffs_ref[...]
     for j in range(keep.shape[0] // n):
         value = v_ref[:, lanes(j)]
         following = next_ref[:, lanes(j)]
-        second_image = own_sum(keep, near, far, j, n) + prior[:, lanes(j)] * following
+        second_image = own_sum(keep, parts, j, n) + prior[:, lanes(j)] * following
         x_ref[:, lanes(j)] = tn_dot(coeffs, jnp.concatenate([value, following], axis=0))
         r_ref[:, lanes(j)] = value - tn_dot(
             coeffs, jnp.concatenate([image_ref[:, lanes(j)], second_image], axis=0)
@@ -422,18 +427,13 @@
         )
         return (foot, swapped(foot, "col", 1)), (*first, *inverse)
 
-    def backward(foot, last):
-        size = stretch * frames
-        extra = 0 if last else frames + DIAG
-        far, near, kept, keep, norm = call(
-            lambda *refs: backward_kernel(stretch, n_cols, last, *refs),
-            (
-                tuple(shape((size + (0 if p else extra), BLOCK), BF16) for p in range(pairs)),
-                shape((size, BLOCK), BF16),
-                (shape((size, BLOCK)),) * pairs,
-                shape((size, BLOCK)),
-                (shape((frames, frames)),) if last else (),
-            ),
+    size = stretch * frames
+    small = frames + DIAG
+
+    def backward(foot, outs):
+        return call(
+            lambda *refs: backward_kernel(stretch, n_cols, len(outs[2]) == 1, *refs),
+            outs,
             (index, *foot, blocks),
             [
                 pltpu.VMEM((col_span, frames, BLOCK), F32),
@@ -441,28 +441,6 @@
                 pltpu.VMEM((frames, 2 * frames), F32),
             ],
         )
-        received = tuple(swapped(x, "row", 1) for x in far)
-        near = swapped(near, "row", 1)
-        middle = ()
-        if last:
-            middle = call(
-                middle_kernel,
-                (shape((4, frames, frames)),),
-                (first, inverse, *norm, diagonal),
-                cost=aside,
-            )
-        sums, gram = call(
-            lambda *refs: rows_kernel(frames, *refs),
-            (
-                (shape((size + extra, BLOCK), BF16),) * pairs,
-                ()
-                if last
-                else (shape((frames // 2, 2 * frames)), shape((DIAG, 2 * frames), BF16)),
-            ),
-            (far[0], received, kept, middle),
-        )
-        far = tuple(swapped(x, "row", 2 * (p + 1)) for p, x in enumerate(sums))
-        return (keep, near, far, *gram), middle
 
     (cast,) = call(cast_kernel, (cast_type,), (right_side,))
     search = gather(cast, "row")
@@ -474,11 +452,30 @@
     )
     (gram,) = call(gram_kernel, (gram_type,), (right_side, prior), cost=aside)
     foot, _ = forward(search, gram, ())
-    parts, _ = backward(foot, False)
+    far, keep, (near, kept) = backward(
+        foot,
+        (
+            tuple(shape((size + (0 if p else small), BLOCK), BF16) for p in range(pairs)),
+            shape((size, BLOCK)),
+            (shape((size, BLOCK), BF16), (shape((size, BLOCK)),) * pairs),
+        ),
+    )
+    received = tuple(swapped(x, "row", 1) for x in far)
+    near = swapped(near, "row", 1)
+    sums, gram, tile = call(
+        lambda *refs: rows_kernel(frames, *refs),
+        (
+            (shape((size + small, BLOCK), BF16),) * pairs,
+            shape((frames // 2, 2 * frames)),
+            shape((DIAG, 2 * frames), BF16),
+        ),
+        (far[0], received, kept),
+    )
+    far = tuple(swapped(x, "row", 2 * (p + 1)) for p, x in enumerate(sums))
     image, following, cast, half, diagonal = call(
         image_kernel,
         (own, own, cast_type, shape((frames // 2, 2 * frames)), shape((DIAG, 2 * frames))),
-        (*parts, right_side, prior),
+        (keep, near, far, gram, tile, right_side, prior),
     )
     search = gather(cast, "row")
     (gram,) = call(gram_kernel, (gram_type,), (following, prior), cost=aside)
@@ -495,15 +492,29 @@
         (second, swapped(second, "row", 1)),
     )
     second = others(second, "row")[1:]
-    parts, middle = backward(foot, True)
+    parts, keep, (norm,) = backward(
+        foot,
+        (
+            (shape((size, BLOCK), BF16),) * (n_rows - 1),
+            shape((size, BLOCK)),
+            (shape((frames, frames)),),
+        ),
+    )
+    parts = tuple(swapped(x, "row", n_rows - 1 - at) for at, x in enumerate(parts))
+    (middle,) = call(
+        middle_kernel,
+        (shape((4, frames, frames)),),
+        (first, inverse, norm, diagonal),
+        cost=aside,
+    )
     (coeffs,) = call(
-        solve_kernel, (shape((2 * frames, frames)),), (gram, second, *middle), cost=aside
+        solve_kernel, (shape((2 * frames, frames)),), (gram, second, middle), cost=aside
     )
     return tuple(
         call(
             final_kernel,
             (own, own),
-            (*parts, right_side, image, following, prior, coeffs),
+            (keep, parts, right_side, image, following, prior, coeffs),
         )
     )
 

time: 73.6 us -> 73.8 us (level)
  waiting for transfers between devices: 25.1 us -> 26.2 us
  starting transfers between devices: 30.7 us -> 29.8 us
    ppermute x20, waiting for transfers between devices: 25.1 us -> 26.2 us  [swapped(): lax.ppermute(x, axis, [(i, i ^ flip) for i in range(lax.axis_size(axis))])]
    ppermute x20, starting transfers between devices: 30.7 us -> 29.8 us  [swapped(): lax.ppermute(x, axis, [(i, i ^ flip) for i in range(lax.axis_size(axis))])]
    pallas_call x21 -> x20, Pallas kernels: 15.2 us -> 15.2 us  [call(): pl.pallas_call(body, out_shape=flat_outs, in_specs=[space(x) for x in fla...]
where the time goes in v8:
time: 73.8 us; the launch traced here: 73.6 us
  starting transfers between devices  29.8 us (40%)
  waiting for transfers between devices  26.2 us (36%)
  Pallas kernels  15.2 us (21%)
  local copies, waits for them, and re-layouts  1.6 us (2%)
  between operations  0.84 us (1%)
    ppermute x20, starting transfers between devices, swapped(): lax.ppermute(x, axis, [(i, i ^ flip) for i in range(lax.axis_size(axis))])  29.8 us
    ppermute x20, waiting for transfers between devices, swapped(): lax.ppermute(x, axis, [(i, i ^ flip) for i in range(lax.axis_size(axis))])  26.2 us
    pallas_call x20, Pallas kernels, call(): pl.pallas_call(body, out_shape=flat_outs, in_specs=[space(x) for x in fla...  15.2 us
    unnamed x14, local copies, waits for them, and re-layouts  1.6 us
  transfers between devices with their start and end apart: 20, of which 13 were waited for; matrix products, arithmetic and copies ran while one was open for 0% of the time, Pallas kernels for 12%

profile of v8, /device:TPU:0, one launch (start us, length us, event | category | flops | bytes accessed | tf_op | source)
XLA Modules:
  0.0 73.6 jit_solution(2859330423942694226)
XLA Ops:
  1.5 4.1 %collective-permute-start.1 = (bf16[256,128]{1,0:T(8,128)(2,1)S(1)}, bf16[256,128]{1,0:T(8,128)(2,1)S(1)}, u32[]{:S(2)}, u32[]{:S(2)}) collective-permute-start(bf16[256,128]{1,0:T(8,128)(2,1)S(1)} %shard_map.69.refs_1_), channel_id=1, source_target_pairs={{0,8},{4,12},{8,0},{12,4},{1,9},{5,13},{9,1},{13,5},{2,10},{6,14},... | collective-permute-start | bytes 196616 | tf_op jit(solution)/shard_map/ppermute | solution.py:375
  5.7 1.6 %collective-permute-start = (bf16[256,128]{1,0:T(8,128)(2,1)S(1)}, bf16[256,128]{1,0:T(8,128)(2,1)S(1)}, u32[]{:S(2)}, u32[]{:S(2)}) collective-permute-start(bf16[256,128]{1,0:T(8,128)(2,1)S(1)} %shard_map.69.refs_1_), channel_id=1, source_target_pairs={{0,4},{4,0},{8,12},{12,8},{1,5},{5,1},{9,13},{13,9},{2,6},{6,2},{1... | collective-permute-start | bytes 196616 | tf_op jit(solution)/shard_map/ppermute | solution.py:375
  8.7 1.4 %collective-permute-start.2 = (bf16[256,128]{1,0:T(8,128)(2,1)S(1)}, bf16[256,128]{1,0:T(8,128)(2,1)S(1)}, u32[]{:S(2)}, u32[]{:S(2)}) collective-permute-start(bf16[256,128]{1,0:T(8,128)(2,1)S(1)} %collective-permute-done.1.refs_3_), channel_id=1, source_target_pairs={{0,4},{4,0},{8,12},{12,8},{1,5},{5,1},{9,13},{13,9},{2,6},{6,2},{1... | collective-permute-start | bytes 196616 | tf_op jit(solution)/shard_map/ppermute | solution.py:375
  10.1 2.0 %shard_map.68 = (s32[2,64]{1,0:T(2,128)S(1)}, bf16[64,128,128]{2,1,0:T(8,128)(2,1)S(1)}) custom-call(s32[64]{0:T(128)S(1)} %copy-done.5, s32[64]{0:T(128)S(1)} %copy-done.6, bf16[64,128,128]{2,1,0:T(8,128)(2,1)S(1)} %copy-done), custom_call_target="tpu_custom_call" | custom-call | flops 2000000000 | bytes 8000000 | tf_op jit(solution)/shard_map/pallas_call | solution.py:51
  14.4 1.6 %collective-permute-done.3.refs_1_ = f32[576,128]{1,0:T(8,128)S(1)} collective-permute-done((f32[576,128]{1,0:T(8,128)S(1)}, f32[576,128]{1,0:T(8,128)S(1)}, u32[]{:S(2)}, u32[]{:S(2)}) %collective-permute-start.3) | collective-permute-done | bytes 294944 | tf_op jit(solution)/shard_map/ppermute | solution.py:375
  16.0 1.9 %collective-permute-start.4 = (bf16[576,128]{1,0:T(8,128)(2,1)S(1)}, bf16[576,128]{1,0:T(8,128)(2,1)S(1)}, u32[]{:S(2)}, u32[]{:S(2)}) collective-permute-start(bf16[576,128]{1,0:T(8,128)(2,1)S(1)} %shard_map.72.refs_0_), channel_id=1, source_target_pairs={{0,2},{1,3},{2,0},{3,1},{4,6},{5,7},{6,4},{7,5},{8,10},{9,11},{10,... | collective-permute-start | bytes 442376 | tf_op jit(solution)/shard_map/ppermute | solution.py:375
  17.9 4.1 %collective-permute-done.4.refs_1_ = bf16[576,128]{1,0:T(8,128)(2,1)S(1)} collective-permute-done((bf16[576,128]{1,0:T(8,128)(2,1)S(1)}, bf16[576,128]{1,0:T(8,128)(2,1)S(1)}, u32[]{:S(2)}, u32[]{:S(2)}) %collective-permute-start.4) | collective-permute-done | bytes 147488 | tf_op jit(solution)/shard_map/ppermute | solution.py:375
  22.2 1.4 %collective-permute-done.5.refs_2_ = bf16[576,128]{1,0:T(8,128)(2,1)S(1)} collective-permute-done((bf16[576,128]{1,0:T(8,128)(2,1)S(1)}, bf16[576,128]{1,0:T(8,128)(2,1)S(1)}, u32[]{:S(2)}, u32[]{:S(2)}) %collective-permute-start.5) | collective-permute-done | bytes 147488 | tf_op jit(solution)/shard_map/ppermute | solution.py:375
  23.5 1.5 %shard_map.74 = (bf16[336,128]{1,0:T(8,128)(2,1)S(1)}, f32[256,128]{1,0:T(8,128)S(1)}, bf16[256,128]{1,0:T(8,128)(2,1)S(1)}, f32[256,128]{1,0:T(8,128)S(1)}) custom-call(s32[2,64]{1,0:T(2,128)S(1)} %get-tuple-element.29.refs_0_, bf16[576,128]{1,0:T(8,128)(2,1)S(1)} %shard_map.73.refs_1_, bf16[576,128]{1,0:T(8,128)(2,1)S(1)} %collective-permute-done.5.refs_2_, ...), custom_call_target="tpu_custom_call" | custom-call | tf_op jit(solution)/shard_map/pallas_call | solution.py:51
  25.0 1.3 %collective-permute-start.7 = (bf16[336,128]{1,0:T(8,128)(2,1)S(1)}, bf16[336,128]{1,0:T(8,128)(2,1)S(1)}, u32[]{:S(2)}, u32[]{:S(2)}) collective-permute-start(bf16[336,128]{1,0:T(8,128)(2,1)S(1)} %get-tuple-element.35.refs_0_), channel_id=1, source_target_pairs={{0,4},{4,0},{8,12},{12,8},{1,5},{5,1},{9,13},{13,9},{2,6},{6,2},{1... | collective-permute-start | bytes 258056 | tf_op jit(solution)/shard_map/ppermute | solution.py:375
  26.3 3.3 %collective-permute-done.7.refs_1_ = bf16[336,128]{1,0:T(8,128)(2,1)S(1)} collective-permute-done((bf16[336,128]{1,0:T(8,128)(2,1)S(1)}, bf16[336,128]{1,0:T(8,128)(2,1)S(1)}, u32[]{:S(2)}, u32[]{:S(2)}) %collective-permute-start.7) | collective-permute-done | bytes 86048 | tf_op jit(solution)/shard_map/ppermute | solution.py:375
  29.7 2.8 %collective-permute-start.8 = (bf16[336,128]{1,0:T(8,128)(2,1)S(1)}, bf16[336,128]{1,0:T(8,128)(2,1)S(1)}, u32[]{:S(2)}, u32[]{:S(2)}) collective-permute-start(bf16[336,128]{1,0:T(8,128)(2,1)S(1)} %get-tuple-element.37), channel_id=1, source_target_pairs={{0,8},{4,12},{8,0},{12,4},{1,9},{5,13},{9,1},{13,5},{2,10},{6,14},... | collective-permute-start | bytes 258056 | tf_op jit(solution)/shard_map/ppermute | solution.py:375
  32.4 1.7 %collective-permute-start.6 = (bf16[256,128]{1,0:T(8,128)(2,1)S(1)}, bf16[256,128]{1,0:T(8,128)(2,1)S(1)}, u32[]{:S(2)}, u32[]{:S(2)}) collective-permute-start(bf16[256,128]{1,0:T(8,128)(2,1)S(1)} %get-tuple-element.34), channel_id=1, source_target_pairs={{0,4},{4,0},{8,12},{12,8},{1,5},{5,1},{9,13},{13,9},{2,6},{6,2},{1... | collective-permute-start | bytes 196616 | tf_op jit(solution)/shard_map/ppermute | solution.py:375
  34.2 2.6 %collective-permute-done.6.refs_1_ = bf16[256,128]{1,0:T(8,128)(2,1)S(1)} collective-permute-done((bf16[256,128]{1,0:T(8,128)(2,1)S(1)}, bf16[256,128]{1,0:T(8,128)(2,1)S(1)}, u32[]{:S(2)}, u32[]{:S(2)}) %collective-permute-start.6) | collective-permute-done | bytes 65568 | tf_op jit(solution)/shard_map/ppermute | solution.py:375
  37.1 1.7 %collective-permute-start.10 = (bf16[256,128]{1,0:T(8,128)(2,1)S(1)}, bf16[256,128]{1,0:T(8,128)(2,1)S(1)}, u32[]{:S(2)}, u32[]{:S(2)}) collective-permute-start(bf16[256,128]{1,0:T(8,128)(2,1)S(1)} %get-tuple-element.40.refs_1_), channel_id=1, source_target_pairs={{0,8},{4,12},{8,0},{12,4},{1,9},{5,13},{9,1},{13,5},{2,10},{6,14},... | collective-permute-start | bytes 196616 | tf_op jit(solution)/shard_map/ppermute | solution.py:375
  38.8 2.1 %collective-permute-start.9 = (bf16[256,128]{1,0:T(8,128)(2,1)S(1)}, bf16[256,128]{1,0:T(8,128)(2,1)S(1)}, u32[]{:S(2)}, u32[]{:S(2)}) collective-permute-start(bf16[256,128]{1,0:T(8,128)(2,1)S(1)} %get-tuple-element.40.refs_1_), channel_id=1, source_target_pairs={{0,4},{4,0},{8,12},{12,8},{1,5},{5,1},{9,13},{13,9},{2,6},{6,2},{1... | collective-permute-start | bytes 196616 | tf_op jit(solution)/shard_map/ppermute | solution.py:375
  40.9 1.4 %collective-permute-done.10.refs_3_ = bf16[256,128]{1,0:T(8,128)(2,1)S(1)} collective-permute-done((bf16[256,128]{1,0:T(8,128)(2,1)S(1)}, bf16[256,128]{1,0:T(8,128)(2,1)S(1)}, u32[]{:S(2)}, u32[]{:S(2)}) %collective-permute-start.10) | collective-permute-done | bytes 65568 | tf_op jit(solution)/shard_map/ppermute | solution.py:375
  42.3 1.6 %collective-permute-start.11 = (bf16[256,128]{1,0:T(8,128)(2,1)S(1)}, bf16[256,128]{1,0:T(8,128)(2,1)S(1)}, u32[]{:S(2)}, u32[]{:S(2)}) collective-permute-start(bf16[256,128]{1,0:T(8,128)(2,1)S(1)} %collective-permute-done.10.refs_3_), channel_id=1, source_target_pairs={{0,4},{4,0},{8,12},{12,8},{1,5},{5,1},{9,13},{13,9},{2,6},{6,2},{1... | collective-permute-start | bytes 196616 | tf_op jit(solution)/shard_map/ppermute | solution.py:375
  44.3 2.2 %collective-permute-done.11.refs_4_ = bf16[256,128]{1,0:T(8,128)(2,1)S(1)} collective-permute-done((bf16[256,128]{1,0:T(8,128)(2,1)S(1)}, bf16[256,128]{1,0:T(8,128)(2,1)S(1)}, u32[]{:S(2)}, u32[]{:S(2)}) %collective-permute-start.11) | collective-permute-done | bytes 65568 | tf_op jit(solution)/shard_map/ppermute | solution.py:375
  46.6 1.4 %shard_map.78 = (f32[608,128]{1,0:T(8,128)S(1)}, f32[608,128]{1,0:T(8,128)S(1)}) custom-call(s32[2,64]{1,0:T(2,128)S(1)} %get-tuple-element.29.refs_0_, bf16[256,128]{1,0:T(8,128)(2,1)S(1)} %get-tuple-element.40.refs_1_, bf16[256,128]{1,0:T(8,128)(2,1)S(1)} %collective-permute-done.9.refs_2_, bf16[256,128]{1,0:T(8,128)(2,1)S(1)} %collective-permute-done.10.refs_3_, ...), custom_call_target="tpu_custom_call" | custom-call | tf_op jit(solution)/shard_map/pallas_call | solution.py:51
  48.0 1.6 %collective-permute-done.12.refs_1_ = f32[608,128]{1,0:T(8,128)S(1)} collective-permute-done((f32[608,128]{1,0:T(8,128)S(1)}, f32[608,128]{1,0:T(8,128)S(1)}, u32[]{:S(2)}, u32[]{:S(2)}) %collective-permute-start.12) | collective-permute-done | bytes 311328 | tf_op jit(solution)/shard_map/ppermute | solution.py:375
  49.7 1.6 %collective-permute-start.13 = (bf16[576,128]{1,0:T(8,128)(2,1)S(1)}, bf16[576,128]{1,0:T(8,128)(2,1)S(1)}, u32[]{:S(2)}, u32[]{:S(2)}) collective-permute-start(bf16[576,128]{1,0:T(8,128)(2,1)S(1)} %get-tuple-element.45.refs_0_), channel_id=1, source_target_pairs={{0,2},{1,3},{2,0},{3,1},{4,6},{5,7},{6,4},{7,5},{8,10},{9,11},{10,... | collective-permute-start | bytes 442376 | tf_op jit(solution)/shard_map/ppermute | solution.py:375
  51.2 1.7 %shard_map.80.refs_2_.refs_1_ = f32[64,64]{1,0:T(8,128)S(1)} custom-call(f32[64,128]{1,0:T(8,128)S(1)} %get-tuple-element.46.refs_0_), custom_call_target="tpu_custom_call" | custom-call | flops 2000000000 | bytes 8000000 | tf_op jit(solution)/shard_map/pallas_call | solution.py:51
  53.0 2.7 %collective-permute-done.13.refs_1_ = bf16[576,128]{1,0:T(8,128)(2,1)S(1)} collective-permute-done((bf16[576,128]{1,0:T(8,128)(2,1)S(1)}, bf16[576,128]{1,0:T(8,128)(2,1)S(1)}, u32[]{:S(2)}, u32[]{:S(2)}) %collective-permute-start.13) | collective-permute-done | bytes 147488 | tf_op jit(solution)/shard_map/ppermute | solution.py:375
  55.8 1.4 %collective-permute-done.14.refs_2_.refs_1_ = bf16[576,128]{1,0:T(8,128)(2,1)S(1)} collective-permute-done((bf16[576,128]{1,0:T(8,128)(2,1)S(1)}, bf16[576,128]{1,0:T(8,128)(2,1)S(1)}, u32[]{:S(2)}, u32[]{:S(2)}) %collective-permute-start.14) | collective-permute-done | bytes 147488 | tf_op jit(solution)/shard_map/ppermute | solution.py:375
  57.5 1.7 %collective-permute-start.18 = (bf16[64,128]{1,0:T(8,128)(2,1)S(1)}, bf16[64,128]{1,0:T(8,128)(2,1)S(1)}, u32[]{:S(2)}, u32[]{:S(2)}) collective-permute-start(bf16[64,128]{1,0:T(8,128)(2,1)S(1)} %shard_map.83.refs_0_), channel_id=1, source_target_pairs={{0,4},{4,0},{8,12},{12,8},{1,5},{5,1},{9,13},{13,9},{2,6},{6,2},{1... | collective-permute-start | bytes 49160 | tf_op jit(solution)/shard_map/ppermute | solution.py:375
  60.4 2.2 %collective-permute-start.15 = (bf16[256,128]{1,0:T(8,128)(2,1)S(1)}, bf16[256,128]{1,0:T(8,128)(2,1)S(1)}, u32[]{:S(2)}, u32[]{:S(2)}) collective-permute-start(bf16[256,128]{1,0:T(8,128)(2,1)S(1)} %get-tuple-element.48), channel_id=1, source_target_pairs={{0,12},{4,8},{8,4},{12,0},{1,13},{5,9},{9,5},{13,1},{2,14},{6,10},... | collective-permute-start | bytes 196616 | tf_op jit(solution)/shard_map/ppermute | solution.py:375
  63.1 1.8 %collective-permute-start.17 = (bf16[256,128]{1,0:T(8,128)(2,1)S(1)}, bf16[256,128]{1,0:T(8,128)(2,1)S(1)}, u32[]{:S(2)}, u32[]{:S(2)}) collective-permute-start(bf16[256,128]{1,0:T(8,128)(2,1)S(1)} %get-tuple-element.50), channel_id=1, source_target_pairs={{0,4},{4,0},{8,12},{12,8},{1,5},{5,1},{9,13},{13,9},{2,6},{6,2},{1... | collective-permute-start | bytes 196616 | tf_op jit(solution)/shard_map/ppermute | solution.py:375
  65.0 1.6 %collective-permute-start.19 = (bf16[64,128]{1,0:T(8,128)(2,1)S(1)}, bf16[64,128]{1,0:T(8,128)(2,1)S(1)}, u32[]{:S(2)}, u32[]{:S(2)}) collective-permute-start(bf16[64,128]{1,0:T(8,128)(2,1)S(1)} %get-tuple-element.53), channel_id=1, source_target_pairs={{0,8},{4,12},{8,0},{12,4},{1,9},{5,13},{9,1},{13,5},{2,10},{6,14},... | collective-permute-start | bytes 49160 | tf_op jit(solution)/shard_map/ppermute | solution.py:375
  67.6 2.6 %collective-permute-done.19.refs_1_ = bf16[64,128]{1,0:T(8,128)(2,1)S(1)} collective-permute-done((bf16[64,128]{1,0:T(8,128)(2,1)S(1)}, bf16[64,128]{1,0:T(8,128)(2,1)S(1)}, u32[]{:S(2)}, u32[]{:S(2)}) %collective-permute-start.19) | collective-permute-done | bytes 16416 | tf_op jit(solution)/shard_map/ppermute | solution.py:375
  70.2 2.1 %shard_map.86.refs_8_ = f32[128,64]{1,0:T(8,128)S(1)} custom-call(f32[64,64]{1,0:T(8,128)S(1)} %get-tuple-element.52.refs_0_, bf16[64,128]{1,0:T(8,128)(2,1)S(1)} %collective-permute-done.19.refs_1_, f32[4,64,64]{2,1,0:T(8,128)S(1)} %shard_map.85.refs_2_), custom_call_target="tpu_custom_call" | custom-call | flops 2000000000 | bytes 8000000 | tf_op jit(solution)/shard_map/pallas_call | solution.py:51
  72.3 1.3 %shard_map.87 = (f32[64,512]{1,0:T(8,128)}, f32[64,512]{1,0:T(8,128)}) custom-call(f32[256,128]{1,0:T(8,128)S(1)} %get-tuple-element.47.refs_0_, bf16[256,128]{1,0:T(8,128)(2,1)S(1)} %collective-permute-done.15.refs_1_, bf16[256,128]{1,0:T(8,128)(2,1)S(1)} %collective-permute-done.16.refs_2_, bf16[256,128]{1,0:T(8,128)(2,1)S(1)} %collective-permute-done.17.refs_3_, ...), custom_call_target="tpu_custom_call" | custom-call | tf_op jit(solution)/shard_map/pallas_call | solution.py:51
  (42 shorter events, 8.9 us)
Async XLA Ops:
  0.6 0.9 %copy-start.1 = (f32[64,512]{1,0:T(8,128)S(1)}, f32[64,512]{1,0:T(8,128)}, u32[]{:S(2)}) copy-start(f32[64,512]{1,0:T(8,128)} %refs_4_.1) | copy-start | bytes 393220
  1.5 7.2 %collective-permute-start.1 = (bf16[256,128]{1,0:T(8,128)(2,1)S(1)}, bf16[256,128]{1,0:T(8,128)(2,1)S(1)}, u32[]{:S(2)}, u32[]{:S(2)}) collective-permute-start(bf16[256,128]{1,0:T(8,128)(2,1)S(1)} %shard_map.69.refs_1_), channel_id=1, source_target_pairs={{0,8},{4,12},{8,0},{12,4},{1,9},{5,13},{9,1},{13,5},{2,10},{6,14},... | collective-permute-start | bytes 196616 | tf_op jit(solution)/shard_map/ppermute | solution.py:375
  5.7 6.4 %collective-permute-start = (bf16[256,128]{1,0:T(8,128)(2,1)S(1)}, bf16[256,128]{1,0:T(8,128)(2,1)S(1)}, u32[]{:S(2)}, u32[]{:S(2)}) collective-permute-start(bf16[256,128]{1,0:T(8,128)(2,1)S(1)} %shard_map.69.refs_1_), channel_id=1, source_target_pairs={{0,4},{4,0},{8,12},{12,8},{1,5},{5,1},{9,13},{13,9},{2,6},{6,2},{1... | collective-permute-start | bytes 196616 | tf_op jit(solution)/shard_map/ppermute | solution.py:375
  7.2 0.7 copy-start.3
  7.9 2.2 %copy-start = (bf16[64,128,128]{2,1,0:T(8,128)(2,1)S(1)}, bf16[64,128,128]{2,1,0:T(8,128)(2,1)}, u32[]{:S(2)}) copy-start(bf16[64,128,128]{2,1,0:T(8,128)(2,1)} %refs_3_.3) | copy-start | bytes 6291460
  7.9 2.2 %copy-start.5 = (s32[64]{0:T(128)S(1)}, s32[64]{0:T(128)}, u32[]{:S(2)}) copy-start(s32[64]{0:T(128)} %refs_0_.3) | copy-start | bytes 772
  7.9 2.2 %copy-start.6 = (s32[64]{0:T(128)S(1)}, s32[64]{0:T(128)}, u32[]{:S(2)}) copy-start(s32[64]{0:T(128)} %refs_1_.1) | copy-start | bytes 772
  8.7 4.3 %collective-permute-start.2 = (bf16[256,128]{1,0:T(8,128)(2,1)S(1)}, bf16[256,128]{1,0:T(8,128)(2,1)S(1)}, u32[]{:S(2)}, u32[]{:S(2)}) collective-permute-start(bf16[256,128]{1,0:T(8,128)(2,1)S(1)} %collective-permute-done.1.refs_3_), channel_id=1, source_target_pairs={{0,4},{4,0},{8,12},{12,8},{1,5},{5,1},{9,13},{13,9},{2,6},{6,2},{1... | collective-permute-start | bytes 196616 | tf_op jit(solution)/shard_map/ppermute | solution.py:375
  14.3 22.6 %copy-start.2 = (f32[64,512]{1,0:T(8,128)S(1)}, f32[64,512]{1,0:T(8,128)}, u32[]{:S(2)}) copy-start(f32[64,512]{1,0:T(8,128)} %refs_4_.1) | copy-start | bytes 393220
  14.3 22.5 %copy-start.4 = (f32[512]{0:T(512)S(1)}, f32[512]{0:T(512)}, u32[]{:S(2)}) copy-start(f32[512]{0:T(512)} %param.6) | copy-start | bytes 6148
  14.3 1.6 %collective-permute-start.3 = (f32[576,128]{1,0:T(8,128)S(1)}, f32[576,128]{1,0:T(8,128)S(1)}, u32[]{:S(2)}, u32[]{:S(2)}) collective-permute-start(f32[576,128]{1,0:T(8,128)S(1)} %get-tuple-element.32), channel_id=1, source_target_pairs={{0,1},{1,0},{2,3},{3,2},{4,5},{5,4},{6,7},{7,6},{8,9},{9,8},{10,11... | collective-permute-start | bytes 884744 | tf_op jit(solution)/shard_map/ppermute | solution.py:375
  16.0 6.1 %collective-permute-start.4 = (bf16[576,128]{1,0:T(8,128)(2,1)S(1)}, bf16[576,128]{1,0:T(8,128)(2,1)S(1)}, u32[]{:S(2)}, u32[]{:S(2)}) collective-permute-start(bf16[576,128]{1,0:T(8,128)(2,1)S(1)} %shard_map.72.refs_0_), channel_id=1, source_target_pairs={{0,2},{1,3},{2,0},{3,1},{4,6},{5,7},{6,4},{7,5},{8,10},{9,11},{10,... | collective-permute-start | bytes 442376 | tf_op jit(solution)/shard_map/ppermute | solution.py:375
  22.1 1.4 %collective-permute-start.5 = (bf16[576,128]{1,0:T(8,128)(2,1)S(1)}, bf16[576,128]{1,0:T(8,128)(2,1)S(1)}, u32[]{:S(2)}, u32[]{:S(2)}) collective-permute-start(bf16[576,128]{1,0:T(8,128)(2,1)S(1)} %shard_map.73.refs_1_), channel_id=1, source_target_pairs={{0,1},{1,0},{2,3},{3,2},{4,5},{5,4},{6,7},{7,6},{8,9},{9,8},{10,11... | collective-permute-start | bytes 442376 | tf_op jit(solution)/shard_map/ppermute | solution.py:375
  25.0 4.6 %collective-permute-start.7 = (bf16[336,128]{1,0:T(8,128)(2,1)S(1)}, bf16[336,128]{1,0:T(8,128)(2,1)S(1)}, u32[]{:S(2)}, u32[]{:S(2)}) collective-permute-start(bf16[336,128]{1,0:T(8,128)(2,1)S(1)} %get-tuple-element.35.refs_0_), channel_id=1, source_target_pairs={{0,4},{4,0},{8,12},{12,8},{1,5},{5,1},{9,13},{13,9},{2,6},{6,2},{1... | collective-permute-start | bytes 258056 | tf_op jit(solution)/shard_map/ppermute | solution.py:375
  29.7 7.2 %collective-permute-start.8 = (bf16[336,128]{1,0:T(8,128)(2,1)S(1)}, bf16[336,128]{1,0:T(8,128)(2,1)S(1)}, u32[]{:S(2)}, u32[]{:S(2)}) collective-permute-start(bf16[336,128]{1,0:T(8,128)(2,1)S(1)} %get-tuple-element.37), channel_id=1, source_target_pairs={{0,8},{4,12},{8,0},{12,4},{1,9},{5,13},{9,1},{13,5},{2,10},{6,14},... | collective-permute-start | bytes 258056 | tf_op jit(solution)/shard_map/ppermute | solution.py:375
  32.4 4.4 %collective-permute-start.6 = (bf16[256,128]{1,0:T(8,128)(2,1)S(1)}, bf16[256,128]{1,0:T(8,128)(2,1)S(1)}, u32[]{:S(2)}, u32[]{:S(2)}) collective-permute-start(bf16[256,128]{1,0:T(8,128)(2,1)S(1)} %get-tuple-element.34), channel_id=1, source_target_pairs={{0,4},{4,0},{8,12},{12,8},{1,5},{5,1},{9,13},{13,9},{2,6},{6,2},{1... | collective-permute-start | bytes 196616 | tf_op jit(solution)/shard_map/ppermute | solution.py:375
  37.1 5.2 %collective-permute-start.10 = (bf16[256,128]{1,0:T(8,128)(2,1)S(1)}, bf16[256,128]{1,0:T(8,128)(2,1)S(1)}, u32[]{:S(2)}, u32[]{:S(2)}) collective-permute-start(bf16[256,128]{1,0:T(8,128)(2,1)S(1)} %get-tuple-element.40.refs_1_), channel_id=1, source_target_pairs={{0,8},{4,12},{8,0},{12,4},{1,9},{5,13},{9,1},{13,5},{2,10},{6,14},... | collective-permute-start | bytes 196616 | tf_op jit(solution)/shard_map/ppermute | solution.py:375
  38.8 5.6 %collective-permute-start.9 = (bf16[256,128]{1,0:T(8,128)(2,1)S(1)}, bf16[256,128]{1,0:T(8,128)(2,1)S(1)}, u32[]{:S(2)}, u32[]{:S(2)}) collective-permute-start(bf16[256,128]{1,0:T(8,128)(2,1)S(1)} %get-tuple-element.40.refs_1_), channel_id=1, source_target_pairs={{0,4},{4,0},{8,12},{12,8},{1,5},{5,1},{9,13},{13,9},{2,6},{6,2},{1... | collective-permute-start | bytes 196616 | tf_op jit(solution)/shard_map/ppermute | solution.py:375
  42.3 4.3 %collective-permute-start.11 = (bf16[256,128]{1,0:T(8,128)(2,1)S(1)}, bf16[256,128]{1,0:T(8,128)(2,1)S(1)}, u32[]{:S(2)}, u32[]{:S(2)}) collective-permute-start(bf16[256,128]{1,0:T(8,128)(2,1)S(1)} %collective-permute-done.10.refs_3_), channel_id=1, source_target_pairs={{0,4},{4,0},{8,12},{12,8},{1,5},{5,1},{9,13},{13,9},{2,6},{6,2},{1... | collective-permute-start | bytes 196616 | tf_op jit(solution)/shard_map/ppermute | solution.py:375
  48.0 1.7 %collective-permute-start.12 = (f32[608,128]{1,0:T(8,128)S(1)}, f32[608,128]{1,0:T(8,128)S(1)}, u32[]{:S(2)}, u32[]{:S(2)}) collective-permute-start(f32[608,128]{1,0:T(8,128)S(1)} %get-tuple-element.44), channel_id=1, source_target_pairs={{0,1},{1,0},{2,3},{3,2},{4,5},{5,4},{6,7},{7,6},{8,9},{9,8},{10,11... | collective-permute-start | bytes 933896 | tf_op jit(solution)/shard_map/ppermute | solution.py:375
  49.7 6.0 %collective-permute-start.13 = (bf16[576,128]{1,0:T(8,128)(2,1)S(1)}, bf16[576,128]{1,0:T(8,128)(2,1)S(1)}, u32[]{:S(2)}, u32[]{:S(2)}) collective-permute-start(bf16[576,128]{1,0:T(8,128)(2,1)S(1)} %get-tuple-element.45.refs_0_), channel_id=1, source_target_pairs={{0,2},{1,3},{2,0},{3,1},{4,6},{5,7},{6,4},{7,5},{8,10},{9,11},{10,... | collective-permute-start | bytes 442376 | tf_op jit(solution)/shard_map/ppermute | solution.py:375
  55.7 1.4 %collective-permute-start.14 = (bf16[576,128]{1,0:T(8,128)(2,1)S(1)}, bf16[576,128]{1,0:T(8,128)(2,1)S(1)}, u32[]{:S(2)}, u32[]{:S(2)}) collective-permute-start(bf16[576,128]{1,0:T(8,128)(2,1)S(1)} %shard_map.81.refs_1_.refs_0_), channel_id=1, source_target_pairs={{0,1},{1,0},{2,3},{3,2},{4,5},{5,4},{6,7},{7,6},{8,9},{9,8},{10,11... | collective-permute-start | bytes 442376 | tf_op jit(solution)/shard_map/ppermute | solution.py:375
  57.5 7.4 %collective-permute-start.18 = (bf16[64,128]{1,0:T(8,128)(2,1)S(1)}, bf16[64,128]{1,0:T(8,128)(2,1)S(1)}, u32[]{:S(2)}, u32[]{:S(2)}) collective-permute-start(bf16[64,128]{1,0:T(8,128)(2,1)S(1)} %shard_map.83.refs_0_), channel_id=1, source_target_pairs={{0,4},{4,0},{8,12},{12,8},{1,5},{5,1},{9,13},{13,9},{2,6},{6,2},{1... | collective-permute-start | bytes 49160 | tf_op jit(solution)/shard_map/ppermute | solution.py:375
  60.4 11.9 %collective-permute-start.15 = (bf16[256,128]{1,0:T(8,128)(2,1)S(1)}, bf16[256,128]{1,0:T(8,128)(2,1)S(1)}, u32[]{:S(2)}, u32[]{:S(2)}) collective-permute-start(bf16[256,128]{1,0:T(8,128)(2,1)S(1)} %get-tuple-element.48), channel_id=1, source_target_pairs={{0,12},{4,8},{8,4},{12,0},{1,13},{5,9},{9,5},{13,1},{2,14},{6,10},... | collective-permute-start | bytes 196616 | tf_op jit(solution)/shard_map/ppermute | solution.py:375
  62.6 9.7 %collective-permute-start.16 = (bf16[256,128]{1,0:T(8,128)(2,1)S(1)}, bf16[256,128]{1,0:T(8,128)(2,1)S(1)}, u32[]{:S(2)}, u32[]{:S(2)}) collective-permute-start(bf16[256,128]{1,0:T(8,128)(2,1)S(1)} %get-tuple-element.49), channel_id=1, source_target_pairs={{0,8},{4,12},{8,0},{12,4},{1,9},{5,13},{9,1},{13,5},{2,10},{6,14},... | collective-permute-start | bytes 196616 | tf_op jit(solution)/shard_map/ppermute | solution.py:375
  63.1 9.2 %collective-permute-start.17 = (bf16[256,128]{1,0:T(8,128)(2,1)S(1)}, bf16[256,128]{1,0:T(8,128)(2,1)S(1)}, u32[]{:S(2)}, u32[]{:S(2)}) collective-permute-start(bf16[256,128]{1,0:T(8,128)(2,1)S(1)} %get-tuple-element.50), channel_id=1, source_target_pairs={{0,4},{4,0},{8,12},{12,8},{1,5},{5,1},{9,13},{13,9},{2,6},{6,2},{1... | collective-permute-start | bytes 196616 | tf_op jit(solution)/shard_map/ppermute | solution.py:375
  65.0 5.2 %collective-permute-start.19 = (bf16[64,128]{1,0:T(8,128)(2,1)S(1)}, bf16[64,128]{1,0:T(8,128)(2,1)S(1)}, u32[]{:S(2)}, u32[]{:S(2)}) collective-permute-start(bf16[64,128]{1,0:T(8,128)(2,1)S(1)} %get-tuple-element.53), channel_id=1, source_target_pairs={{0,8},{4,12},{8,0},{12,4},{1,9},{5,13},{9,1},{13,5},{2,10},{6,14},... | collective-permute-start | bytes 49160 | tf_op jit(solution)/shard_map/ppermute | solution.py:375

commit v9 on v7

--- a/solution.py
+++ b/solution.py
@@ -261,9 +261,15 @@
     out_ref[...] = jnp.concatenate(split(value), axis=1)
 
 
-def own_sum(keep, near, far, j, frames):
+def near_kernel(keep, near, sum_ref, cast_ref):
+    total = keep[...] + near[...].astype(F32)
+    sum_ref[...] = total
+    cast_ref[...] = total.astype(BF16)
+
+
+def own_sum(keep, parts, j, frames):
     at = rows(j, frames)
-    return keep[at, :] + sum_rows((near, *far), at)
+    return keep[at, :] + sum_rows(parts, at)
 
 
 def frame_shift(diagonal, frames):
@@ -272,7 +278,7 @@
 
 
 def image_kernel(
-    keep, near, far, gram, tile, v_ref, prior, image_ref, next_ref, cast_ref, half_ref, diag_ref
+    pair_sum, far, gram, tile, v_ref, prior, image_ref, next_ref, cast_ref, half_ref, diag_ref
 ):
     frames = v_ref.shape[0]
     split_at = frames // 2
@@ -282,7 +288,7 @@
     shift, _ = frame_shift(diagonal[0:1, :], frames)
     for j in range(data // frames):
         value = v_ref[:, lanes(j)]
-        image = own_sum(keep, near, far, j, frames) + prior[:, lanes(j)] * value
+        image = own_sum(pair_sum, far, j, frames) + prior[:, lanes(j)] * value
         following = image - shift * value
         image_ref[:, lanes(j)] = image
         next_ref[:, lanes(j)] = following
@@ -292,6 +298,28 @@
         + sum_rows(far, slice(data, data + split_at))
         + sum_rows(far, slice(data + split_at, data + frames))
     )
+
+
+def remainder_kernel(v_ref, prior, before, out_ref):
+    frames = v_ref.shape[0]
+    stretch = v_ref.shape[1] // BLOCK
+    for j in range(stretch):
+        out_ref[rows(j, frames), :] = split(v_ref[:, lanes(j)])[1]
+    terms = [part.astype(F32) for part in split(prior[...])]
+    lines = [part[:, lanes(j)] for part in terms for j in range(stretch)]
+    lines.append(jnp.zeros((DIAG - len(lines), BLOCK), F32))
+    out_ref[stretch * frames :, :] = jnp.concatenate(lines, axis=0).astype(BF16)
+
+
+def cross_kernel(frames, own, received, high, low, diag_ref, cast_ref):
+    stretch = cast_ref.shape[0] // frames
+    shift, _ = frame_shift(diag_ref[0:1, :], frames)
+    tile = low[stretch * frames :, :].astype(F32)
+    for j in range(stretch):
+        at = rows(j, frames)
+        weight = tile[j : j + 1, :] + tile[stretch + j : stretch + j + 1, :]
+        value = sum_rows((high, low), at)
+        cast_ref[at, :] = (sum_rows((own, received), at) + (weight - shift) * value).astype(BF16)
 
 
 def eliminate(matrix, right, n):
@@ -359,7 +387,7 @@
     for j in range(keep.shape[0] // n):
         value = v_ref[:, lanes(j)]
         following = next_ref[:, lanes(j)]
-        second_image = own_sum(keep, near, far, j, n) + prior[:, lanes(j)] * following
+        second_image = own_sum(keep, (near, *far), j, n) + prior[:, lanes(j)] * following
         x_ref[:, lanes(j)] = tn_dot(coeffs, jnp.concatenate([value, following], axis=0))
         r_ref[:, lanes(j)] = value - tn_dot(
             coeffs, jnp.concatenate([image_ref[:, lanes(j)], second_image], axis=0)
@@ -414,13 +442,23 @@
             (shape((half_cols + frames, BLOCK), BF16), (gram_type,) if half else ()),
             (keep, received),
         )
-        inverse = call(inverse_kernel, (shape((frames, frames)),), first, cost=aside) if half else ()
+        if half:
+            aside_of_chips = call(inverse_kernel, (shape((frames, frames)),), first, cost=aside)
+        elif n_rows == 4:
+            (remainder,) = call(
+                remainder_kernel,
+                (shape((stretch * frames + DIAG, BLOCK), BF16),),
+                (right_side, prior, pair),
+            )
+            aside_of_chips = [swapped(remainder, "row", 2)]
+        else:
+            aside_of_chips = []
         (foot,) = call(
             lambda *refs: chips_kernel(frames, *refs),
             (shape((half_cols + frames, BLOCK), BF16),),
-            (others(pair, "col"), inverse),
-        )
-        return (foot, swapped(foot, "col", 1)), (*first, *inverse)
+            (others(pair, "col"), aside_of_chips),
+        )
+        return (foot, swapped(foot, "col", 1)), (*first, *aside_of_chips)
 
     def backward(foot, last):
         size = stretch * frames
@@ -462,7 +500,7 @@
             (far[0], received, kept, middle),
         )
         far = tuple(swapped(x, "row", 2 * (p + 1)) for p, x in enumerate(sums))
-        return (keep, near, far, *gram), middle
+        return (keep, near, far, *gram), (middle if last else sums)
 
     (cast,) = call(cast_kernel, (cast_type,), (right_side,))
     search = gather(cast, "row")
@@ -473,14 +511,31 @@
         cost=aside,
     )
     (gram,) = call(gram_kernel, (gram_type,), (right_side, prior), cost=aside)
-    foot, _ = forward(search, gram, ())
-    parts, _ = backward(foot, False)
+    foot, remainder = forward(search, gram, ())
+    (keep, near, far, gram, tile), sums = backward(foot, False)
+    pair_sum, pair_cast = call(
+        near_kernel, (shape((stretch * frames, BLOCK)), cast_type), (keep, near)
+    )
     image, following, cast, half, diagonal = call(
         image_kernel,
         (own, own, cast_type, shape((frames // 2, 2 * frames)), shape((DIAG, 2 * frames))),
-        (*parts, right_side, prior),
-    )
-    search = gather(cast, "row")
+        (pair_sum, far, gram, tile, right_side, prior),
+    )
+    if n_rows == 4:
+        (cross,) = call(
+            lambda *refs: cross_kernel(frames, *refs),
+            (cast_type,),
+            (
+                sums[0],
+                swapped(pair_cast, "row", 2),
+                search[2],
+                *remainder,
+                diagonal,
+            ),
+        )
+        search = (cast, swapped(cast, "row", 1), cross, swapped(cross, "row", 1))
+    else:
+        search = gather(cast, "row")
     (gram,) = call(gram_kernel, (gram_type,), (following, prior), cost=aside)
     foot, (first, inverse) = forward(search, gram, (half,))
     (second,) = call(

time: 73.6 us -> 73 us (level)
  starting transfers between devices: 30.7 us -> 25.2 us
  waiting for transfers between devices: 25.1 us -> 29.7 us
    ppermute x20 -> x21, starting transfers between devices: 30.7 us -> 25.2 us  [swapped(): lax.ppermute(x, axis, [(i, i ^ flip) for i in range(lax.axis_size(axis))])]
    ppermute x20 -> x21, waiting for transfers between devices: 25.1 us -> 29.7 us  [swapped(): lax.ppermute(x, axis, [(i, i ^ flip) for i in range(lax.axis_size(axis))])]
    pallas_call x21 -> x24, Pallas kernels: 15.2 us -> 15.5 us  [call(): pl.pallas_call(body, out_shape=flat_outs, in_specs=[space(x) for x in fla...]
  transfers between devices with their start and end apart: 20 -> 21, of which waited for: 13 -> 16; matrix products, arithmetic and copies ran while one was open for 0% -> 0% of each run, Pallas kernels for 12% -> 13%
where the time goes in v9:
time: 73 us; the launch traced here: 72.8 us
  waiting for transfers between devices  29.7 us (41%)
  starting transfers between devices  25.2 us (35%)
  Pallas kernels  15.5 us (21%)
  local copies, waits for them, and re-layouts  1.6 us (2%)
  between operations  0.82 us (1%)
    ppermute x21, waiting for transfers between devices, swapped(): lax.ppermute(x, axis, [(i, i ^ flip) for i in range(lax.axis_size(axis))])  29.7 us
    ppermute x21, starting transfers between devices, swapped(): lax.ppermute(x, axis, [(i, i ^ flip) for i in range(lax.axis_size(axis))])  25.2 us
    pallas_call x24, Pallas kernels, call(): pl.pallas_call(body, out_shape=flat_outs, in_specs=[space(x) for x in fla...  15.5 us
    unnamed x14, local copies, waits for them, and re-layouts  1.6 us
  transfers between devices with their start and end apart: 21, of which 16 were waited for; matrix products, arithmetic and copies ran while one was open for 0% of the time, Pallas kernels for 13%

profile of v9, /device:TPU:0, one launch (start us, length us, event | category | flops | bytes accessed | tf_op | source)
XLA Modules:
  0.0 72.8 jit_solution(10648719840713278719)
XLA Ops:
  1.5 4.1 %collective-permute-start.1 = (bf16[256,128]{1,0:T(8,128)(2,1)S(1)}, bf16[256,128]{1,0:T(8,128)(2,1)S(1)}, u32[]{:S(2)}, u32[]{:S(2)}) collective-permute-start(bf16[256,128]{1,0:T(8,128)(2,1)S(1)} %shard_map.69.refs_1_), channel_id=1, source_target_pairs={{0,8},{4,12},{8,0},{12,4},{1,9},{5,13},{9,1},{13,5},{2,10},{6,14},... | collective-permute-start | bytes 196616 | tf_op jit(solution)/shard_map/ppermute | solution.py:398
  5.7 1.6 %collective-permute-start = (bf16[256,128]{1,0:T(8,128)(2,1)S(1)}, bf16[256,128]{1,0:T(8,128)(2,1)S(1)}, u32[]{:S(2)}, u32[]{:S(2)}) collective-permute-start(bf16[256,128]{1,0:T(8,128)(2,1)S(1)} %shard_map.69.refs_1_), channel_id=1, source_target_pairs={{0,4},{4,0},{8,12},{12,8},{1,5},{5,1},{9,13},{13,9},{2,6},{6,2},{1... | collective-permute-start | bytes 196616 | tf_op jit(solution)/shard_map/ppermute | solution.py:398
  8.7 1.4 %collective-permute-start.2 = (bf16[256,128]{1,0:T(8,128)(2,1)S(1)}, bf16[256,128]{1,0:T(8,128)(2,1)S(1)}, u32[]{:S(2)}, u32[]{:S(2)}) collective-permute-start(bf16[256,128]{1,0:T(8,128)(2,1)S(1)} %collective-permute-done.1.refs_3_.refs_2_), channel_id=1, source_target_pairs={{0,4},{4,0},{8,12},{12,8},{1,5},{5,1},{9,13},{13,9},{2,6},{6,2},{1... | collective-permute-start | bytes 196616 | tf_op jit(solution)/shard_map/ppermute | solution.py:398
  10.1 2.0 %shard_map.68 = (s32[2,64]{1,0:T(2,128)S(1)}, bf16[64,128,128]{2,1,0:T(8,128)(2,1)S(1)}) custom-call(s32[64]{0:T(128)S(1)} %copy-done.5, s32[64]{0:T(128)S(1)} %copy-done.6, bf16[64,128,128]{2,1,0:T(8,128)(2,1)S(1)} %copy-done), custom_call_target="tpu_custom_call" | custom-call | flops 2000000000 | bytes 8000000 | tf_op jit(solution)/shard_map/pallas_call | solution.py:51
  13.0 1.3 %shard_map.71 = (f32[576,128]{1,0:T(8,128)S(1)}, f32[576,128]{1,0:T(8,128)S(1)}) custom-call(s32[2,64]{1,0:T(2,128)S(1)} %get-tuple-element.31.refs_0_, bf16[256,128]{1,0:T(8,128)(2,1)S(1)} %shard_map.69.refs_1_, bf16[256,128]{1,0:T(8,128)(2,1)S(1)} %collective-permute-done.refs_2_, bf16[256,128]{1,0:T(8,128)(2,1)S(1)} %collective-permute-done.1.refs_3_.refs_2_, ...), custom_call_target="tpu_custom_call" | custom-call | tf_op jit(solution)/shard_map/pallas_call | solution.py:51
  14.4 1.6 %collective-permute-done.3.refs_1_ = f32[576,128]{1,0:T(8,128)S(1)} collective-permute-done((f32[576,128]{1,0:T(8,128)S(1)}, f32[576,128]{1,0:T(8,128)S(1)}, u32[]{:S(2)}, u32[]{:S(2)}) %collective-permute-start.3) | collective-permute-done | bytes 294944 | tf_op jit(solution)/shard_map/ppermute | solution.py:398
  16.0 1.9 %collective-permute-start.4 = (bf16[576,128]{1,0:T(8,128)(2,1)S(1)}, bf16[576,128]{1,0:T(8,128)(2,1)S(1)}, u32[]{:S(2)}, u32[]{:S(2)}) collective-permute-start(bf16[576,128]{1,0:T(8,128)(2,1)S(1)} %shard_map.72.refs_2_.refs_0_), channel_id=1, source_target_pairs={{0,2},{1,3},{2,0},{3,1},{4,6},{5,7},{6,4},{7,5},{8,10},{9,11},{10,... | collective-permute-start | bytes 442376 | tf_op jit(solution)/shard_map/ppermute | solution.py:398
  17.9 2.4 %collective-permute-start.5 = (bf16[272,128]{1,0:T(8,128)(2,1)S(1)}, bf16[272,128]{1,0:T(8,128)(2,1)S(1)}, u32[]{:S(2)}, u32[]{:S(2)}) collective-permute-start(bf16[272,128]{1,0:T(8,128)(2,1)S(1)} %shard_map.73), channel_id=1, source_target_pairs={{0,8},{4,12},{8,0},{12,4},{1,9},{5,13},{9,1},{13,5},{2,10},{6,14},... | collective-permute-start | bytes 208904 | tf_op jit(solution)/shard_map/ppermute | solution.py:398
  20.3 4.3 %collective-permute-done.5.refs_2_.refs_3_ = bf16[272,128]{1,0:T(8,128)(2,1)S(1)} collective-permute-done((bf16[272,128]{1,0:T(8,128)(2,1)S(1)}, bf16[272,128]{1,0:T(8,128)(2,1)S(1)}, u32[]{:S(2)}, u32[]{:S(2)}) %collective-permute-start.5) | collective-permute-done | bytes 69664 | tf_op jit(solution)/shard_map/ppermute | solution.py:398
  24.7 1.4 %collective-permute-done.6.refs_2_ = bf16[576,128]{1,0:T(8,128)(2,1)S(1)} collective-permute-done((bf16[576,128]{1,0:T(8,128)(2,1)S(1)}, bf16[576,128]{1,0:T(8,128)(2,1)S(1)}, u32[]{:S(2)}, u32[]{:S(2)}) %collective-permute-start.6) | collective-permute-done | bytes 147488 | tf_op jit(solution)/shard_map/ppermute | solution.py:398
  26.0 1.5 %shard_map.75 = (bf16[336,128]{1,0:T(8,128)(2,1)S(1)}, bf16[256,128]{1,0:T(8,128)(2,1)S(1)}, f32[256,128]{1,0:T(8,128)S(1)}, f32[256,128]{1,0:T(8,128)S(1)}) custom-call(s32[2,64]{1,0:T(2,128)S(1)} %get-tuple-element.31.refs_0_, bf16[576,128]{1,0:T(8,128)(2,1)S(1)} %shard_map.74.refs_1_, bf16[576,128]{1,0:T(8,128)(2,1)S(1)} %collective-permute-done.6.refs_2_, ...), custom_call_target="tpu_custom_call" | custom-call | tf_op jit(solution)/shard_map/pallas_call | solution.py:51
  27.7 1.9 %collective-permute-start.7 = (bf16[256,128]{1,0:T(8,128)(2,1)S(1)}, bf16[256,128]{1,0:T(8,128)(2,1)S(1)}, u32[]{:S(2)}, u32[]{:S(2)}) collective-permute-start(bf16[256,128]{1,0:T(8,128)(2,1)S(1)} %get-tuple-element.36), channel_id=1, source_target_pairs={{0,4},{4,0},{8,12},{12,8},{1,5},{5,1},{9,13},{13,9},{2,6},{6,2},{1... | collective-permute-start | bytes 196616 | tf_op jit(solution)/shard_map/ppermute | solution.py:398
  29.6 3.3 %collective-permute-done.8.refs_1_ = bf16[336,128]{1,0:T(8,128)(2,1)S(1)} collective-permute-done((bf16[336,128]{1,0:T(8,128)(2,1)S(1)}, bf16[336,128]{1,0:T(8,128)(2,1)S(1)}, u32[]{:S(2)}, u32[]{:S(2)}) %collective-permute-start.8) | collective-permute-done | bytes 86048 | tf_op jit(solution)/shard_map/ppermute | solution.py:398
  32.9 1.5 %collective-permute-start.9 = (bf16[336,128]{1,0:T(8,128)(2,1)S(1)}, bf16[336,128]{1,0:T(8,128)(2,1)S(1)}, u32[]{:S(2)}, u32[]{:S(2)}) collective-permute-start(bf16[336,128]{1,0:T(8,128)(2,1)S(1)} %get-tuple-element.40.refs_0_), channel_id=1, source_target_pairs={{0,8},{4,12},{8,0},{12,4},{1,9},{5,13},{9,1},{13,5},{2,10},{6,14},... | collective-permute-start | bytes 258056 | tf_op jit(solution)/shard_map/ppermute | solution.py:398
  34.4 1.5 %collective-permute-start.11 = (bf16[256,128]{1,0:T(8,128)(2,1)S(1)}, bf16[256,128]{1,0:T(8,128)(2,1)S(1)}, u32[]{:S(2)}, u32[]{:S(2)}) collective-permute-start(bf16[256,128]{1,0:T(8,128)(2,1)S(1)} %get-tuple-element.44), channel_id=1, source_target_pairs={{0,8},{4,12},{8,0},{12,4},{1,9},{5,13},{9,1},{13,5},{2,10},{6,14},... | collective-permute-start | bytes 196616 | tf_op jit(solution)/shard_map/ppermute | solution.py:398
  36.0 4.2 %collective-permute-done.9.refs_1_ = bf16[336,128]{1,0:T(8,128)(2,1)S(1)} collective-permute-done((bf16[336,128]{1,0:T(8,128)(2,1)S(1)}, bf16[336,128]{1,0:T(8,128)(2,1)S(1)}, u32[]{:S(2)}, u32[]{:S(2)}) %collective-permute-start.9) | collective-permute-done | bytes 86048 | tf_op jit(solution)/shard_map/ppermute | solution.py:398
  41.9 1.0 %collective-permute-start.12 = (bf16[256,128]{1,0:T(8,128)(2,1)S(1)}, bf16[256,128]{1,0:T(8,128)(2,1)S(1)}, u32[]{:S(2)}, u32[]{:S(2)}) collective-permute-start(bf16[256,128]{1,0:T(8,128)(2,1)S(1)} %shard_map.79.refs_3_), channel_id=1, source_target_pairs={{0,4},{4,0},{8,12},{12,8},{1,5},{5,1},{9,13},{13,9},{2,6},{6,2},{1... | collective-permute-start | bytes 196616 | tf_op jit(solution)/shard_map/ppermute | solution.py:398
  43.3 1.5 %collective-permute-done.10.refs_2_ = bf16[256,128]{1,0:T(8,128)(2,1)S(1)} collective-permute-done((bf16[256,128]{1,0:T(8,128)(2,1)S(1)}, bf16[256,128]{1,0:T(8,128)(2,1)S(1)}, u32[]{:S(2)}, u32[]{:S(2)}) %collective-permute-start.10) | collective-permute-done | bytes 65568 | tf_op jit(solution)/shard_map/ppermute | solution.py:398
  44.8 1.4 %collective-permute-done.12.refs_4_ = bf16[256,128]{1,0:T(8,128)(2,1)S(1)} collective-permute-done((bf16[256,128]{1,0:T(8,128)(2,1)S(1)}, bf16[256,128]{1,0:T(8,128)(2,1)S(1)}, u32[]{:S(2)}, u32[]{:S(2)}) %collective-permute-start.12) | collective-permute-done | bytes 65568 | tf_op jit(solution)/shard_map/ppermute | solution.py:398
  46.2 1.4 %shard_map.81 = (f32[608,128]{1,0:T(8,128)S(1)}, f32[608,128]{1,0:T(8,128)S(1)}) custom-call(s32[2,64]{1,0:T(2,128)S(1)} %get-tuple-element.31.refs_0_, bf16[256,128]{1,0:T(8,128)(2,1)S(1)} %get-tuple-element.43.refs_1_, bf16[256,128]{1,0:T(8,128)(2,1)S(1)} %collective-permute-done.10.refs_2_, bf16[256,128]{1,0:T(8,128)(2,1)S(1)} %shard_map.79.refs_3_, ...), custom_call_target="tpu_custom_call" | custom-call | tf_op jit(solution)/shard_map/pallas_call | solution.py:51
  47.7 1.6 %collective-permute-done.13.refs_1_ = f32[608,128]{1,0:T(8,128)S(1)} collective-permute-done((f32[608,128]{1,0:T(8,128)S(1)}, f32[608,128]{1,0:T(8,128)S(1)}, u32[]{:S(2)}, u32[]{:S(2)}) %collective-permute-start.13) | collective-permute-done | bytes 311328 | tf_op jit(solution)/shard_map/ppermute | solution.py:398
  49.9 1.7 %shard_map.83.refs_2_.refs_1_ = f32[64,64]{1,0:T(8,128)S(1)} custom-call(f32[64,128]{1,0:T(8,128)S(1)} %get-tuple-element.51.refs_0_), custom_call_target="tpu_custom_call" | custom-call | flops 2000000000 | bytes 8000000 | tf_op jit(solution)/shard_map/pallas_call | solution.py:51
  51.6 3.6 %collective-permute-done.14.refs_1_ = bf16[576,128]{1,0:T(8,128)(2,1)S(1)} collective-permute-done((bf16[576,128]{1,0:T(8,128)(2,1)S(1)}, bf16[576,128]{1,0:T(8,128)(2,1)S(1)}, u32[]{:S(2)}, u32[]{:S(2)}) %collective-permute-start.14) | collective-permute-done | bytes 147488 | tf_op jit(solution)/shard_map/ppermute | solution.py:398
  55.4 1.4 %collective-permute-done.15.refs_2_.refs_1_ = bf16[576,128]{1,0:T(8,128)(2,1)S(1)} collective-permute-done((bf16[576,128]{1,0:T(8,128)(2,1)S(1)}, bf16[576,128]{1,0:T(8,128)(2,1)S(1)}, u32[]{:S(2)}, u32[]{:S(2)}) %collective-permute-start.15) | collective-permute-done | bytes 147488 | tf_op jit(solution)/shard_map/ppermute | solution.py:398
  57.1 1.0 %collective-permute-start.19 = (bf16[64,128]{1,0:T(8,128)(2,1)S(1)}, bf16[64,128]{1,0:T(8,128)(2,1)S(1)}, u32[]{:S(2)}, u32[]{:S(2)}) collective-permute-start(bf16[64,128]{1,0:T(8,128)(2,1)S(1)} %shard_map.88.refs_0_), channel_id=1, source_target_pairs={{0,4},{4,0},{8,12},{12,8},{1,5},{5,1},{9,13},{13,9},{2,6},{6,2},{1... | collective-permute-start | bytes 49160 | tf_op jit(solution)/shard_map/ppermute | solution.py:398
  58.0 1.3 %shard_map.85 = (bf16[256,128]{1,0:T(8,128)(2,1)S(1)}, bf16[256,128]{1,0:T(8,128)(2,1)S(1)}, f32[256,128]{1,0:T(8,128)S(1)}, f32[256,128]{1,0:T(8,128)S(1)}, f32[64,64]{1,0:T(8,128)S(1)}) custom-call(s32[2,64]{1,0:T(2,128)S(1)} %get-tuple-element.31.refs_0_, bf16[576,128]{1,0:T(8,128)(2,1)S(1)} %shard_map.84.refs_1_.refs_0_, ...), custom_call_target="tpu_custom_call" | custom-call | tf_op jit(solution)/shard_map/pallas_call | solution.py:51
  59.3 1.2 %collective-permute-start.17 = (bf16[256,128]{1,0:T(8,128)(2,1)S(1)}, bf16[256,128]{1,0:T(8,128)(2,1)S(1)}, u32[]{:S(2)}, u32[]{:S(2)}) collective-permute-start(bf16[256,128]{1,0:T(8,128)(2,1)S(1)} %get-tuple-element.54.refs_0_), channel_id=1, source_target_pairs={{0,4},{4,0},{8,12},{12,8},{1,5},{5,1},{9,13},{13,9},{2,6},{6,2},{1... | collective-permute-start | bytes 196616 | tf_op jit(solution)/shard_map/ppermute | solution.py:398
  61.0 2.5 %collective-permute-start.20 = (bf16[64,128]{1,0:T(8,128)(2,1)S(1)}, bf16[64,128]{1,0:T(8,128)(2,1)S(1)}, u32[]{:S(2)}, u32[]{:S(2)}) collective-permute-start(bf16[64,128]{1,0:T(8,128)(2,1)S(1)} %get-tuple-element.59), channel_id=1, source_target_pairs={{0,8},{4,12},{8,0},{12,4},{1,9},{5,13},{9,1},{13,5},{2,10},{6,14},... | collective-permute-start | bytes 49160 | tf_op jit(solution)/shard_map/ppermute | solution.py:398
  64.4 1.1 %collective-permute-start.16 = (bf16[256,128]{1,0:T(8,128)(2,1)S(1)}, bf16[256,128]{1,0:T(8,128)(2,1)S(1)}, u32[]{:S(2)}, u32[]{:S(2)}) collective-permute-start(bf16[256,128]{1,0:T(8,128)(2,1)S(1)} %get-tuple-element.53), channel_id=1, source_target_pairs={{0,4},{4,0},{8,12},{12,8},{1,5},{5,1},{9,13},{13,9},{2,6},{6,2},{1... | collective-permute-start | bytes 196616 | tf_op jit(solution)/shard_map/ppermute | solution.py:398
  66.4 2.1 %shard_map.90.refs_7_ = f32[128,64]{1,0:T(8,128)S(1)} custom-call(f32[64,64]{1,0:T(8,128)S(1)} %get-tuple-element.58.refs_0_, bf16[64,128]{1,0:T(8,128)(2,1)S(1)} %collective-permute-done.20.refs_1_, f32[4,64,64]{2,1,0:T(8,128)S(1)} %shard_map.86.refs_3_.refs_2_), custom_call_target="tpu_custom_call" | custom-call | flops 2000000000 | bytes 8000000 | tf_op jit(solution)/shard_map/pallas_call | solution.py:51
  69.2 2.3 %collective-permute-done.18.refs_2_ = bf16[256,128]{1,0:T(8,128)(2,1)S(1)} collective-permute-done((bf16[256,128]{1,0:T(8,128)(2,1)S(1)}, bf16[256,128]{1,0:T(8,128)(2,1)S(1)}, u32[]{:S(2)}, u32[]{:S(2)}) %collective-permute-start.18) | collective-permute-done | bytes 65568 | tf_op jit(solution)/shard_map/ppermute | solution.py:398
  71.5 1.3 %shard_map.91 = (f32[64,512]{1,0:T(8,128)}, f32[64,512]{1,0:T(8,128)}) custom-call(f32[256,128]{1,0:T(8,128)S(1)} %get-tuple-element.52.refs_0_, bf16[256,128]{1,0:T(8,128)(2,1)S(1)} %collective-permute-done.16.refs_1_, bf16[256,128]{1,0:T(8,128)(2,1)S(1)} %collective-permute-done.18.refs_2_, f32[64,512]{1,0:T(8,128)S(1)} %copy-done.2, ...), custom_call_target="tpu_custom_call" | custom-call | tf_op jit(solution)/shard_map/pallas_call | solution.py:51
  (48 shorter events, 9.9 us)
Async XLA Ops:
  0.6 0.9 %copy-start.1 = (f32[64,512]{1,0:T(8,128)S(1)}, f32[64,512]{1,0:T(8,128)}, u32[]{:S(2)}) copy-start(f32[64,512]{1,0:T(8,128)} %refs_3_.5) | copy-start | bytes 393220
  1.5 7.2 %collective-permute-start.1 = (bf16[256,128]{1,0:T(8,128)(2,1)S(1)}, bf16[256,128]{1,0:T(8,128)(2,1)S(1)}, u32[]{:S(2)}, u32[]{:S(2)}) collective-permute-start(bf16[256,128]{1,0:T(8,128)(2,1)S(1)} %shard_map.69.refs_1_), channel_id=1, source_target_pairs={{0,8},{4,12},{8,0},{12,4},{1,9},{5,13},{9,1},{13,5},{2,10},{6,14},... | collective-permute-start | bytes 196616 | tf_op jit(solution)/shard_map/ppermute | solution.py:398
  5.7 6.5 %collective-permute-start = (bf16[256,128]{1,0:T(8,128)(2,1)S(1)}, bf16[256,128]{1,0:T(8,128)(2,1)S(1)}, u32[]{:S(2)}, u32[]{:S(2)}) collective-permute-start(bf16[256,128]{1,0:T(8,128)(2,1)S(1)} %shard_map.69.refs_1_), channel_id=1, source_target_pairs={{0,4},{4,0},{8,12},{12,8},{1,5},{5,1},{9,13},{13,9},{2,6},{6,2},{1... | collective-permute-start | bytes 196616 | tf_op jit(solution)/shard_map/ppermute | solution.py:398
  7.2 0.7 copy-start.3
  7.9 2.2 %copy-start = (bf16[64,128,128]{2,1,0:T(8,128)(2,1)S(1)}, bf16[64,128,128]{2,1,0:T(8,128)(2,1)}, u32[]{:S(2)}) copy-start(bf16[64,128,128]{2,1,0:T(8,128)(2,1)} %refs_3_.4) | copy-start | bytes 6291460
  7.9 2.2 %copy-start.5 = (s32[64]{0:T(128)S(1)}, s32[64]{0:T(128)}, u32[]{:S(2)}) copy-start(s32[64]{0:T(128)} %refs_0_.4) | copy-start | bytes 772
  7.9 2.2 %copy-start.6 = (s32[64]{0:T(128)S(1)}, s32[64]{0:T(128)}, u32[]{:S(2)}) copy-start(s32[64]{0:T(128)} %refs_1_.1) | copy-start | bytes 772
  8.7 4.3 %collective-permute-start.2 = (bf16[256,128]{1,0:T(8,128)(2,1)S(1)}, bf16[256,128]{1,0:T(8,128)(2,1)S(1)}, u32[]{:S(2)}, u32[]{:S(2)}) collective-permute-start(bf16[256,128]{1,0:T(8,128)(2,1)S(1)} %collective-permute-done.1.refs_3_.refs_2_), channel_id=1, source_target_pairs={{0,4},{4,0},{8,12},{12,8},{1,5},{5,1},{9,13},{13,9},{2,6},{6,2},{1... | collective-permute-start | bytes 196616 | tf_op jit(solution)/shard_map/ppermute | solution.py:398
  12.1 5.8 %copy-start.2 = (f32[64,512]{1,0:T(8,128)S(1)}, f32[64,512]{1,0:T(8,128)}, u32[]{:S(2)}) copy-start(f32[64,512]{1,0:T(8,128)} %refs_3_.5) | copy-start | bytes 393220
  12.1 5.8 %copy-start.4 = (f32[512]{0:T(512)S(1)}, f32[512]{0:T(512)}, u32[]{:S(2)}) copy-start(f32[512]{0:T(512)} %param.6) | copy-start | bytes 6148
  14.3 1.6 %collective-permute-start.3 = (f32[576,128]{1,0:T(8,128)S(1)}, f32[576,128]{1,0:T(8,128)S(1)}, u32[]{:S(2)}, u32[]{:S(2)}) collective-permute-start(f32[576,128]{1,0:T(8,128)S(1)} %get-tuple-element.34), channel_id=1, source_target_pairs={{0,1},{1,0},{2,3},{3,2},{4,5},{5,4},{6,7},{7,6},{8,9},{9,8},{10,11... | collective-permute-start | bytes 884744 | tf_op jit(solution)/shard_map/ppermute | solution.py:398
  16.0 8.6 %collective-permute-start.4 = (bf16[576,128]{1,0:T(8,128)(2,1)S(1)}, bf16[576,128]{1,0:T(8,128)(2,1)S(1)}, u32[]{:S(2)}, u32[]{:S(2)}) collective-permute-start(bf16[576,128]{1,0:T(8,128)(2,1)S(1)} %shard_map.72.refs_2_.refs_0_), channel_id=1, source_target_pairs={{0,2},{1,3},{2,0},{3,1},{4,6},{5,7},{6,4},{7,5},{8,10},{9,11},{10,... | collective-permute-start | bytes 442376 | tf_op jit(solution)/shard_map/ppermute | solution.py:398
  17.9 6.6 %collective-permute-start.5 = (bf16[272,128]{1,0:T(8,128)(2,1)S(1)}, bf16[272,128]{1,0:T(8,128)(2,1)S(1)}, u32[]{:S(2)}, u32[]{:S(2)}) collective-permute-start(bf16[272,128]{1,0:T(8,128)(2,1)S(1)} %shard_map.73), channel_id=1, source_target_pairs={{0,8},{4,12},{8,0},{12,4},{1,9},{5,13},{9,1},{13,5},{2,10},{6,14},... | collective-permute-start | bytes 208904 | tf_op jit(solution)/shard_map/ppermute | solution.py:398
  24.6 1.4 %collective-permute-start.6 = (bf16[576,128]{1,0:T(8,128)(2,1)S(1)}, bf16[576,128]{1,0:T(8,128)(2,1)S(1)}, u32[]{:S(2)}, u32[]{:S(2)}) collective-permute-start(bf16[576,128]{1,0:T(8,128)(2,1)S(1)} %shard_map.74.refs_1_), channel_id=1, source_target_pairs={{0,1},{1,0},{2,3},{3,2},{4,5},{5,4},{6,7},{7,6},{8,9},{9,8},{10,11... | collective-permute-start | bytes 442376 | tf_op jit(solution)/shard_map/ppermute | solution.py:398
  27.5 5.3 %collective-permute-start.8 = (bf16[336,128]{1,0:T(8,128)(2,1)S(1)}, bf16[336,128]{1,0:T(8,128)(2,1)S(1)}, u32[]{:S(2)}, u32[]{:S(2)}) collective-permute-start(bf16[336,128]{1,0:T(8,128)(2,1)S(1)} %get-tuple-element.38.refs_0_), channel_id=1, source_target_pairs={{0,4},{4,0},{8,12},{12,8},{1,5},{5,1},{9,13},{13,9},{2,6},{6,2},{1... | collective-permute-start | bytes 258056 | tf_op jit(solution)/shard_map/ppermute | solution.py:398
  27.7 6.7 %collective-permute-start.7 = (bf16[256,128]{1,0:T(8,128)(2,1)S(1)}, bf16[256,128]{1,0:T(8,128)(2,1)S(1)}, u32[]{:S(2)}, u32[]{:S(2)}) collective-permute-start(bf16[256,128]{1,0:T(8,128)(2,1)S(1)} %get-tuple-element.36), channel_id=1, source_target_pairs={{0,4},{4,0},{8,12},{12,8},{1,5},{5,1},{9,13},{13,9},{2,6},{6,2},{1... | collective-permute-start | bytes 196616 | tf_op jit(solution)/shard_map/ppermute | solution.py:398
  32.9 7.3 %collective-permute-start.9 = (bf16[336,128]{1,0:T(8,128)(2,1)S(1)}, bf16[336,128]{1,0:T(8,128)(2,1)S(1)}, u32[]{:S(2)}, u32[]{:S(2)}) collective-permute-start(bf16[336,128]{1,0:T(8,128)(2,1)S(1)} %get-tuple-element.40.refs_0_), channel_id=1, source_target_pairs={{0,8},{4,12},{8,0},{12,4},{1,9},{5,13},{9,1},{13,5},{2,10},{6,14},... | collective-permute-start | bytes 258056 | tf_op jit(solution)/shard_map/ppermute | solution.py:398
  34.4 7.2 %collective-permute-start.11 = (bf16[256,128]{1,0:T(8,128)(2,1)S(1)}, bf16[256,128]{1,0:T(8,128)(2,1)S(1)}, u32[]{:S(2)}, u32[]{:S(2)}) collective-permute-start(bf16[256,128]{1,0:T(8,128)(2,1)S(1)} %get-tuple-element.44), channel_id=1, source_target_pairs={{0,8},{4,12},{8,0},{12,4},{1,9},{5,13},{9,1},{13,5},{2,10},{6,14},... | collective-permute-start | bytes 196616 | tf_op jit(solution)/shard_map/ppermute | solution.py:398
  40.5 4.3 %collective-permute-start.10 = (bf16[256,128]{1,0:T(8,128)(2,1)S(1)}, bf16[256,128]{1,0:T(8,128)(2,1)S(1)}, u32[]{:S(2)}, u32[]{:S(2)}) collective-permute-start(bf16[256,128]{1,0:T(8,128)(2,1)S(1)} %get-tuple-element.43.refs_1_), channel_id=1, source_target_pairs={{0,4},{4,0},{8,12},{12,8},{1,5},{5,1},{9,13},{13,9},{2,6},{6,2},{1... | collective-permute-start | bytes 196616 | tf_op jit(solution)/shard_map/ppermute | solution.py:398
  41.9 4.3 %collective-permute-start.12 = (bf16[256,128]{1,0:T(8,128)(2,1)S(1)}, bf16[256,128]{1,0:T(8,128)(2,1)S(1)}, u32[]{:S(2)}, u32[]{:S(2)}) collective-permute-start(bf16[256,128]{1,0:T(8,128)(2,1)S(1)} %shard_map.79.refs_3_), channel_id=1, source_target_pairs={{0,4},{4,0},{8,12},{12,8},{1,5},{5,1},{9,13},{13,9},{2,6},{6,2},{1... | collective-permute-start | bytes 196616 | tf_op jit(solution)/shard_map/ppermute | solution.py:398
  47.6 1.7 %collective-permute-start.13 = (f32[608,128]{1,0:T(8,128)S(1)}, f32[608,128]{1,0:T(8,128)S(1)}, u32[]{:S(2)}, u32[]{:S(2)}) collective-permute-start(f32[608,128]{1,0:T(8,128)S(1)} %get-tuple-element.49), channel_id=1, source_target_pairs={{0,1},{1,0},{2,3},{3,2},{4,5},{5,4},{6,7},{7,6},{8,9},{9,8},{10,11... | collective-permute-start | bytes 933896 | tf_op jit(solution)/shard_map/ppermute | solution.py:398
  49.3 6.0 %collective-permute-start.14 = (bf16[576,128]{1,0:T(8,128)(2,1)S(1)}, bf16[576,128]{1,0:T(8,128)(2,1)S(1)}, u32[]{:S(2)}, u32[]{:S(2)}) collective-permute-start(bf16[576,128]{1,0:T(8,128)(2,1)S(1)} %get-tuple-element.50.refs_0_), channel_id=1, source_target_pairs={{0,2},{1,3},{2,0},{3,1},{4,6},{5,7},{6,4},{7,5},{8,10},{9,11},{10,... | collective-permute-start | bytes 442376 | tf_op jit(solution)/shard_map/ppermute | solution.py:398
  55.3 1.4 %collective-permute-start.15 = (bf16[576,128]{1,0:T(8,128)(2,1)S(1)}, bf16[576,128]{1,0:T(8,128)(2,1)S(1)}, u32[]{:S(2)}, u32[]{:S(2)}) collective-permute-start(bf16[576,128]{1,0:T(8,128)(2,1)S(1)} %shard_map.84.refs_1_.refs_0_), channel_id=1, source_target_pairs={{0,1},{1,0},{2,3},{3,2},{4,5},{5,4},{6,7},{7,6},{8,9},{9,8},{10,11... | collective-permute-start | bytes 442376 | tf_op jit(solution)/shard_map/ppermute | solution.py:398
  57.1 3.8 %collective-permute-start.19 = (bf16[64,128]{1,0:T(8,128)(2,1)S(1)}, bf16[64,128]{1,0:T(8,128)(2,1)S(1)}, u32[]{:S(2)}, u32[]{:S(2)}) collective-permute-start(bf16[64,128]{1,0:T(8,128)(2,1)S(1)} %shard_map.88.refs_0_), channel_id=1, source_target_pairs={{0,4},{4,0},{8,12},{12,8},{1,5},{5,1},{9,13},{13,9},{2,6},{6,2},{1... | collective-permute-start | bytes 49160 | tf_op jit(solution)/shard_map/ppermute | solution.py:398
  59.3 6.2 %collective-permute-start.17 = (bf16[256,128]{1,0:T(8,128)(2,1)S(1)}, bf16[256,128]{1,0:T(8,128)(2,1)S(1)}, u32[]{:S(2)}, u32[]{:S(2)}) collective-permute-start(bf16[256,128]{1,0:T(8,128)(2,1)S(1)} %get-tuple-element.54.refs_0_), channel_id=1, source_target_pairs={{0,4},{4,0},{8,12},{12,8},{1,5},{5,1},{9,13},{13,9},{2,6},{6,2},{1... | collective-permute-start | bytes 196616 | tf_op jit(solution)/shard_map/ppermute | solution.py:398
  61.0 5.4 %collective-permute-start.20 = (bf16[64,128]{1,0:T(8,128)(2,1)S(1)}, bf16[64,128]{1,0:T(8,128)(2,1)S(1)}, u32[]{:S(2)}, u32[]{:S(2)}) collective-permute-start(bf16[64,128]{1,0:T(8,128)(2,1)S(1)} %get-tuple-element.59), channel_id=1, source_target_pairs={{0,8},{4,12},{8,0},{12,4},{1,9},{5,13},{9,1},{13,5},{2,10},{6,14},... | collective-permute-start | bytes 49160 | tf_op jit(solution)/shard_map/ppermute | solution.py:398
  64.4 4.8 %collective-permute-start.16 = (bf16[256,128]{1,0:T(8,128)(2,1)S(1)}, bf16[256,128]{1,0:T(8,128)(2,1)S(1)}, u32[]{:S(2)}, u32[]{:S(2)}) collective-permute-start(bf16[256,128]{1,0:T(8,128)(2,1)S(1)} %get-tuple-element.53), channel_id=1, source_target_pairs={{0,4},{4,0},{8,12},{12,8},{1,5},{5,1},{9,13},{13,9},{2,6},{6,2},{1... | collective-permute-start | bytes 196616 | tf_op jit(solution)/shard_map/ppermute | solution.py:398
  65.6 5.9 %collective-permute-start.18 = (bf16[256,128]{1,0:T(8,128)(2,1)S(1)}, bf16[256,128]{1,0:T(8,128)(2,1)S(1)}, u32[]{:S(2)}, u32[]{:S(2)}) collective-permute-start(bf16[256,128]{1,0:T(8,128)(2,1)S(1)} %shard_map.87), channel_id=1, source_target_pairs={{0,8},{4,12},{8,0},{12,4},{1,9},{5,13},{9,1},{13,5},{2,10},{6,14},... | collective-permute-start | bytes 196616 | tf_op jit(solution)/shard_map/ppermute | solution.py:398

commit v10 on v9

--- a/solution.py
+++ b/solution.py
@@ -213,7 +213,7 @@
     out_ref[at + frames :, :] = jnp.where(row == 0, diagonal, 0.0).astype(BF16)
 
 
-def rows_kernel(frames, sent, received, kept, before, out_refs, gram_refs):
+def rows_kernel(frames, sent, received, kept, out_refs, gram_refs):
     split_at = frames // 2
     data = kept[0].shape[0]
     for out_ref, kept_ref, received_ref in zip(out_refs, kept, received):
@@ -355,8 +355,8 @@
     out_ref[...] = eliminate(first[:, n:], jnp.where(eye(n), 1.0, 0.0), n)
 
 
-def middle_kernel(first, inverse_ref, norm_ref, diag_ref, out_ref):
-    n = first.shape[0]
+def solve_kernel(gram, parts, first, inverse_ref, norm_ref, diag_ref, out_ref):
+    n = gram.shape[0]
     norm, energy = first[:, :n], first[:, n:]
     shift, shift_row = frame_shift(diag_ref[0:1, :], n)
     inverse = inverse_ref[...]
@@ -364,20 +364,12 @@
     cross = norm_ref[...] + next_rhs * shift_row
     alpha = nn_dot(inverse, norm)
     conj = nn_dot(inverse, cross.T)
-    out_ref[0] = alpha
-    out_ref[1] = conj
-    out_ref[2] = nn_dot(cross, conj)
-    out_ref[3] = next_rhs - nn_dot(cross, alpha)
-
-
-def solve_kernel(gram, parts, middle, out_ref):
-    n = gram.shape[0]
-    schur = gram[...] - middle[2]
+    schur = gram[...] - nn_dot(cross, conj)
     for part in parts:
         both = part[...].astype(F32)
         schur += both[:, :n] + both[:, n:]
-    gamma = eliminate(schur, middle[3], n)
-    out_ref[:n, :] = middle[0] - nn_dot(middle[1], gamma)
+    gamma = eliminate(schur, next_rhs - nn_dot(cross, alpha), n)
+    out_ref[:n, :] = alpha - nn_dot(conj, gamma)
     out_ref[n:, :] = gamma
 
 
@@ -481,14 +473,6 @@
         )
         received = tuple(swapped(x, "row", 1) for x in far)
         near = swapped(near, "row", 1)
-        middle = ()
-        if last:
-            middle = call(
-                middle_kernel,
-                (shape((4, frames, frames)),),
-                (first, inverse, *norm, diagonal),
-                cost=aside,
-            )
         sums, gram = call(
             lambda *refs: rows_kernel(frames, *refs),
             (
@@ -497,10 +481,10 @@
                 if last
                 else (shape((frames // 2, 2 * frames)), shape((DIAG, 2 * frames), BF16)),
             ),
-            (far[0], received, kept, middle),
+            (far[0], received, kept),
         )
         far = tuple(swapped(x, "row", 2 * (p + 1)) for p, x in enumerate(sums))
-        return (keep, near, far, *gram), (middle if last else sums)
+        return (keep, near, far, *gram), (norm if last else sums)
 
     (cast,) = call(cast_kernel, (cast_type,), (right_side,))
     search = gather(cast, "row")
@@ -550,9 +534,12 @@
         (second, swapped(second, "row", 1)),
     )
     second = others(second, "row")[1:]
-    parts, middle = backward(foot, True)
+    parts, norm = backward(foot, True)
     (coeffs,) = call(
-        solve_kernel, (shape((2 * frames, frames)),), (gram, second, *middle), cost=aside
+        solve_kernel,
+        (shape((2 * frames, frames)),),
+        (gram, second, first, inverse, *norm, diagonal),
+        cost=aside,
     )
     return tuple(
         call(

time: 73 us -> 74.3 us (1.018)
  waiting for transfers between devices: 29.7 us -> 31.5 us
    ppermute x21, waiting for transfers between devices: 29.7 us -> 31.5 us  [swapped(): lax.ppermute(x, axis, [(i, i ^ flip) for i in range(lax.axis_size(axis))])]
    pallas_call x24 -> x23, Pallas kernels: 15.5 us -> 15.4 us  [call(): pl.pallas_call(body, out_shape=flat_outs, in_specs=[space(x) for x in fla...]
  transfers between devices with their start and end apart: 21 -> 21, of which waited for: 16 -> 16; matrix products, arithmetic and copies ran while one was open for 0% -> 0% of each run, Pallas kernels for 13% -> 11%
where the time goes in v10:
time: 74.3 us; the launch traced here: 74.2 us
  waiting for transfers between devices  31.5 us (42%)
  starting transfers between devices  24.8 us (33%)
  Pallas kernels  15.4 us (21%)
  local copies, waits for them, and re-layouts  1.6 us (2%)
  between operations  0.82 us (1%)
    ppermute x21, waiting for transfers between devices, swapped(): lax.ppermute(x, axis, [(i, i ^ flip) for i in range(lax.axis_size(axis))])  31.5 us
    ppermute x21, starting transfers between devices, swapped(): lax.ppermute(x, axis, [(i, i ^ flip) for i in range(lax.axis_size(axis))])  24.8 us
    pallas_call x23, Pallas kernels, call(): pl.pallas_call(body, out_shape=flat_outs, in_specs=[space(x) for x in fla...  15.4 us
    unnamed x14, local copies, waits for them, and re-layouts  1.6 us
  transfers between devices with their start and end apart: 21, of which 16 were waited for; matrix products, arithmetic and copies ran while one was open for 0% of the time, Pallas kernels for 11%

profile of v10, /device:TPU:0, one launch (start us, length us, event | category | flops | bytes accessed | tf_op | source)
XLA Modules:
  0.0 74.2 jit_solution(8670481182803425324)
XLA Ops:
  1.5 4.1 %collective-permute-start.1 = (bf16[256,128]{1,0:T(8,128)(2,1)S(1)}, bf16[256,128]{1,0:T(8,128)(2,1)S(1)}, u32[]{:S(2)}, u32[]{:S(2)}) collective-permute-start(bf16[256,128]{1,0:T(8,128)(2,1)S(1)} %shard_map.69.refs_1_), channel_id=1, source_target_pairs={{0,8},{4,12},{8,0},{12,4},{1,9},{5,13},{9,1},{13,5},{2,10},{6,14},... | collective-permute-start | bytes 196616 | tf_op jit(solution)/shard_map/ppermute | solution.py:390
  5.7 1.6 %collective-permute-start = (bf16[256,128]{1,0:T(8,128)(2,1)S(1)}, bf16[256,128]{1,0:T(8,128)(2,1)S(1)}, u32[]{:S(2)}, u32[]{:S(2)}) collective-permute-start(bf16[256,128]{1,0:T(8,128)(2,1)S(1)} %shard_map.69.refs_1_), channel_id=1, source_target_pairs={{0,4},{4,0},{8,12},{12,8},{1,5},{5,1},{9,13},{13,9},{2,6},{6,2},{1... | collective-permute-start | bytes 196616 | tf_op jit(solution)/shard_map/ppermute | solution.py:390
  8.7 1.4 %collective-permute-start.2 = (bf16[256,128]{1,0:T(8,128)(2,1)S(1)}, bf16[256,128]{1,0:T(8,128)(2,1)S(1)}, u32[]{:S(2)}, u32[]{:S(2)}) collective-permute-start(bf16[256,128]{1,0:T(8,128)(2,1)S(1)} %collective-permute-done.1.refs_3_.refs_2_), channel_id=1, source_target_pairs={{0,4},{4,0},{8,12},{12,8},{1,5},{5,1},{9,13},{13,9},{2,6},{6,2},{1... | collective-permute-start | bytes 196616 | tf_op jit(solution)/shard_map/ppermute | solution.py:390
  10.1 2.0 %shard_map.68 = (s32[2,64]{1,0:T(2,128)S(1)}, bf16[64,128,128]{2,1,0:T(8,128)(2,1)S(1)}) custom-call(s32[64]{0:T(128)S(1)} %copy-done.5, s32[64]{0:T(128)S(1)} %copy-done.6, bf16[64,128,128]{2,1,0:T(8,128)(2,1)S(1)} %copy-done), custom_call_target="tpu_custom_call" | custom-call | flops 2000000000 | bytes 8000000 | tf_op jit(solution)/shard_map/pallas_call | solution.py:51
  13.0 1.3 %shard_map.71 = (f32[576,128]{1,0:T(8,128)S(1)}, f32[576,128]{1,0:T(8,128)S(1)}) custom-call(s32[2,64]{1,0:T(2,128)S(1)} %get-tuple-element.31.refs_0_, bf16[256,128]{1,0:T(8,128)(2,1)S(1)} %shard_map.69.refs_1_, bf16[256,128]{1,0:T(8,128)(2,1)S(1)} %collective-permute-done.refs_2_, bf16[256,128]{1,0:T(8,128)(2,1)S(1)} %collective-permute-done.1.refs_3_.refs_2_, ...), custom_call_target="tpu_custom_call" | custom-call | tf_op jit(solution)/shard_map/pallas_call | solution.py:51
  14.4 1.6 %collective-permute-done.3.refs_1_ = f32[576,128]{1,0:T(8,128)S(1)} collective-permute-done((f32[576,128]{1,0:T(8,128)S(1)}, f32[576,128]{1,0:T(8,128)S(1)}, u32[]{:S(2)}, u32[]{:S(2)}) %collective-permute-start.3) | collective-permute-done | bytes 294944 | tf_op jit(solution)/shard_map/ppermute | solution.py:390
  16.0 1.9 %collective-permute-start.4 = (bf16[576,128]{1,0:T(8,128)(2,1)S(1)}, bf16[576,128]{1,0:T(8,128)(2,1)S(1)}, u32[]{:S(2)}, u32[]{:S(2)}) collective-permute-start(bf16[576,128]{1,0:T(8,128)(2,1)S(1)} %shard_map.72.refs_2_.refs_0_), channel_id=1, source_target_pairs={{0,2},{1,3},{2,0},{3,1},{4,6},{5,7},{6,4},{7,5},{8,10},{9,11},{10,... | collective-permute-start | bytes 442376 | tf_op jit(solution)/shard_map/ppermute | solution.py:390
  17.9 2.4 %collective-permute-start.5 = (bf16[272,128]{1,0:T(8,128)(2,1)S(1)}, bf16[272,128]{1,0:T(8,128)(2,1)S(1)}, u32[]{:S(2)}, u32[]{:S(2)}) collective-permute-start(bf16[272,128]{1,0:T(8,128)(2,1)S(1)} %shard_map.73), channel_id=1, source_target_pairs={{0,8},{4,12},{8,0},{12,4},{1,9},{5,13},{9,1},{13,5},{2,10},{6,14},... | collective-permute-start | bytes 208904 | tf_op jit(solution)/shard_map/ppermute | solution.py:390
  20.3 4.3 %collective-permute-done.5.refs_2_.refs_3_ = bf16[272,128]{1,0:T(8,128)(2,1)S(1)} collective-permute-done((bf16[272,128]{1,0:T(8,128)(2,1)S(1)}, bf16[272,128]{1,0:T(8,128)(2,1)S(1)}, u32[]{:S(2)}, u32[]{:S(2)}) %collective-permute-start.5) | collective-permute-done | bytes 69664 | tf_op jit(solution)/shard_map/ppermute | solution.py:390
  24.7 1.4 %collective-permute-done.6.refs_2_ = bf16[576,128]{1,0:T(8,128)(2,1)S(1)} collective-permute-done((bf16[576,128]{1,0:T(8,128)(2,1)S(1)}, bf16[576,128]{1,0:T(8,128)(2,1)S(1)}, u32[]{:S(2)}, u32[]{:S(2)}) %collective-permute-start.6) | collective-permute-done | bytes 147488 | tf_op jit(solution)/shard_map/ppermute | solution.py:390
  26.0 1.5 %shard_map.75 = (bf16[336,128]{1,0:T(8,128)(2,1)S(1)}, bf16[256,128]{1,0:T(8,128)(2,1)S(1)}, f32[256,128]{1,0:T(8,128)S(1)}, f32[256,128]{1,0:T(8,128)S(1)}) custom-call(s32[2,64]{1,0:T(2,128)S(1)} %get-tuple-element.31.refs_0_, bf16[576,128]{1,0:T(8,128)(2,1)S(1)} %shard_map.74.refs_1_, bf16[576,128]{1,0:T(8,128)(2,1)S(1)} %collective-permute-done.6.refs_2_, ...), custom_call_target="tpu_custom_call" | custom-call | tf_op jit(solution)/shard_map/pallas_call | solution.py:51
  27.7 1.9 %collective-permute-start.7 = (bf16[256,128]{1,0:T(8,128)(2,1)S(1)}, bf16[256,128]{1,0:T(8,128)(2,1)S(1)}, u32[]{:S(2)}, u32[]{:S(2)}) collective-permute-start(bf16[256,128]{1,0:T(8,128)(2,1)S(1)} %get-tuple-element.36), channel_id=1, source_target_pairs={{0,4},{4,0},{8,12},{12,8},{1,5},{5,1},{9,13},{13,9},{2,6},{6,2},{1... | collective-permute-start | bytes 196616 | tf_op jit(solution)/shard_map/ppermute | solution.py:390
  29.6 3.3 %collective-permute-done.8.refs_1_ = bf16[336,128]{1,0:T(8,128)(2,1)S(1)} collective-permute-done((bf16[336,128]{1,0:T(8,128)(2,1)S(1)}, bf16[336,128]{1,0:T(8,128)(2,1)S(1)}, u32[]{:S(2)}, u32[]{:S(2)}) %collective-permute-start.8) | collective-permute-done | bytes 86048 | tf_op jit(solution)/shard_map/ppermute | solution.py:390
  32.9 1.5 %collective-permute-start.9 = (bf16[336,128]{1,0:T(8,128)(2,1)S(1)}, bf16[336,128]{1,0:T(8,128)(2,1)S(1)}, u32[]{:S(2)}, u32[]{:S(2)}) collective-permute-start(bf16[336,128]{1,0:T(8,128)(2,1)S(1)} %get-tuple-element.40.refs_0_), channel_id=1, source_target_pairs={{0,8},{4,12},{8,0},{12,4},{1,9},{5,13},{9,1},{13,5},{2,10},{6,14},... | collective-permute-start | bytes 258056 | tf_op jit(solution)/shard_map/ppermute | solution.py:390
  34.4 1.5 %collective-permute-start.11 = (bf16[256,128]{1,0:T(8,128)(2,1)S(1)}, bf16[256,128]{1,0:T(8,128)(2,1)S(1)}, u32[]{:S(2)}, u32[]{:S(2)}) collective-permute-start(bf16[256,128]{1,0:T(8,128)(2,1)S(1)} %get-tuple-element.44), channel_id=1, source_target_pairs={{0,8},{4,12},{8,0},{12,4},{1,9},{5,13},{9,1},{13,5},{2,10},{6,14},... | collective-permute-start | bytes 196616 | tf_op jit(solution)/shard_map/ppermute | solution.py:390
  36.0 4.2 %collective-permute-done.9.refs_1_ = bf16[336,128]{1,0:T(8,128)(2,1)S(1)} collective-permute-done((bf16[336,128]{1,0:T(8,128)(2,1)S(1)}, bf16[336,128]{1,0:T(8,128)(2,1)S(1)}, u32[]{:S(2)}, u32[]{:S(2)}) %collective-permute-start.9) | collective-permute-done | bytes 86048 | tf_op jit(solution)/shard_map/ppermute | solution.py:390
  41.9 1.0 %collective-permute-start.12 = (bf16[256,128]{1,0:T(8,128)(2,1)S(1)}, bf16[256,128]{1,0:T(8,128)(2,1)S(1)}, u32[]{:S(2)}, u32[]{:S(2)}) collective-permute-start(bf16[256,128]{1,0:T(8,128)(2,1)S(1)} %shard_map.79.refs_3_), channel_id=1, source_target_pairs={{0,4},{4,0},{8,12},{12,8},{1,5},{5,1},{9,13},{13,9},{2,6},{6,2},{1... | collective-permute-start | bytes 196616 | tf_op jit(solution)/shard_map/ppermute | solution.py:390
  43.2 1.5 %collective-permute-done.10.refs_2_ = bf16[256,128]{1,0:T(8,128)(2,1)S(1)} collective-permute-done((bf16[256,128]{1,0:T(8,128)(2,1)S(1)}, bf16[256,128]{1,0:T(8,128)(2,1)S(1)}, u32[]{:S(2)}, u32[]{:S(2)}) %collective-permute-start.10) | collective-permute-done | bytes 65568 | tf_op jit(solution)/shard_map/ppermute | solution.py:390
  44.8 1.4 %collective-permute-done.12.refs_4_ = bf16[256,128]{1,0:T(8,128)(2,1)S(1)} collective-permute-done((bf16[256,128]{1,0:T(8,128)(2,1)S(1)}, bf16[256,128]{1,0:T(8,128)(2,1)S(1)}, u32[]{:S(2)}, u32[]{:S(2)}) %collective-permute-start.12) | collective-permute-done | bytes 65568 | tf_op jit(solution)/shard_map/ppermute | solution.py:390
  46.2 1.4 %shard_map.81 = (f32[608,128]{1,0:T(8,128)S(1)}, f32[608,128]{1,0:T(8,128)S(1)}) custom-call(s32[2,64]{1,0:T(2,128)S(1)} %get-tuple-element.31.refs_0_, bf16[256,128]{1,0:T(8,128)(2,1)S(1)} %get-tuple-element.43.refs_1_, bf16[256,128]{1,0:T(8,128)(2,1)S(1)} %collective-permute-done.10.refs_2_, bf16[256,128]{1,0:T(8,128)(2,1)S(1)} %shard_map.79.refs_3_, ...), custom_call_target="tpu_custom_call" | custom-call | tf_op jit(solution)/shard_map/pallas_call | solution.py:51
  47.7 1.6 %collective-permute-done.13.refs_1_ = f32[608,128]{1,0:T(8,128)S(1)} collective-permute-done((f32[608,128]{1,0:T(8,128)S(1)}, f32[608,128]{1,0:T(8,128)S(1)}, u32[]{:S(2)}, u32[]{:S(2)}) %collective-permute-start.13) | collective-permute-done | bytes 311328 | tf_op jit(solution)/shard_map/ppermute | solution.py:390
  49.9 1.7 %shard_map.83.refs_2_.refs_3_ = f32[64,64]{1,0:T(8,128)S(1)} custom-call(f32[64,128]{1,0:T(8,128)S(1)} %get-tuple-element.51.refs_0_.refs_2_), custom_call_target="tpu_custom_call" | custom-call | flops 2000000000 | bytes 8000000 | tf_op jit(solution)/shard_map/pallas_call | solution.py:51
  51.6 3.6 %collective-permute-done.14.refs_1_ = bf16[576,128]{1,0:T(8,128)(2,1)S(1)} collective-permute-done((bf16[576,128]{1,0:T(8,128)(2,1)S(1)}, bf16[576,128]{1,0:T(8,128)(2,1)S(1)}, u32[]{:S(2)}, u32[]{:S(2)}) %collective-permute-start.14) | collective-permute-done | bytes 147488 | tf_op jit(solution)/shard_map/ppermute | solution.py:390
  55.4 1.4 %collective-permute-done.15.refs_2_.refs_1_ = bf16[576,128]{1,0:T(8,128)(2,1)S(1)} collective-permute-done((bf16[576,128]{1,0:T(8,128)(2,1)S(1)}, bf16[576,128]{1,0:T(8,128)(2,1)S(1)}, u32[]{:S(2)}, u32[]{:S(2)}) %collective-permute-start.15) | collective-permute-done | bytes 147488 | tf_op jit(solution)/shard_map/ppermute | solution.py:390
  56.7 1.3 %shard_map.85 = (bf16[256,128]{1,0:T(8,128)(2,1)S(1)}, bf16[256,128]{1,0:T(8,128)(2,1)S(1)}, f32[256,128]{1,0:T(8,128)S(1)}, f32[256,128]{1,0:T(8,128)S(1)}, f32[64,64]{1,0:T(8,128)S(1)}) custom-call(s32[2,64]{1,0:T(2,128)S(1)} %get-tuple-element.31.refs_0_, bf16[576,128]{1,0:T(8,128)(2,1)S(1)} %shard_map.84.refs_1_.refs_0_, ...), custom_call_target="tpu_custom_call" | custom-call | tf_op jit(solution)/shard_map/pallas_call | solution.py:51
  58.0 1.0 %collective-permute-start.17 = (bf16[256,128]{1,0:T(8,128)(2,1)S(1)}, bf16[256,128]{1,0:T(8,128)(2,1)S(1)}, u32[]{:S(2)}, u32[]{:S(2)}) collective-permute-start(bf16[256,128]{1,0:T(8,128)(2,1)S(1)} %get-tuple-element.54.refs_0_), channel_id=1, source_target_pairs={{0,4},{4,0},{8,12},{12,8},{1,5},{5,1},{9,13},{13,9},{2,6},{6,2},{1... | collective-permute-start | bytes 196616 | tf_op jit(solution)/shard_map/ppermute | solution.py:390
  59.4 1.1 %collective-permute-start.19 = (bf16[64,128]{1,0:T(8,128)(2,1)S(1)}, bf16[64,128]{1,0:T(8,128)(2,1)S(1)}, u32[]{:S(2)}, u32[]{:S(2)}) collective-permute-start(bf16[64,128]{1,0:T(8,128)(2,1)S(1)} %shard_map.87.refs_0_), channel_id=1, source_target_pairs={{0,4},{4,0},{8,12},{12,8},{1,5},{5,1},{9,13},{13,9},{2,6},{6,2},{1... | collective-permute-start | bytes 49160 | tf_op jit(solution)/shard_map/ppermute | solution.py:390
  60.5 2.6 %collective-permute-done.19.refs_1_ = bf16[64,128]{1,0:T(8,128)(2,1)S(1)} collective-permute-done((bf16[64,128]{1,0:T(8,128)(2,1)S(1)}, bf16[64,128]{1,0:T(8,128)(2,1)S(1)}, u32[]{:S(2)}, u32[]{:S(2)}) %collective-permute-start.19) | collective-permute-done | bytes 16416 | tf_op jit(solution)/shard_map/ppermute | solution.py:390
  63.3 2.7 %collective-permute-start.20 = (bf16[64,128]{1,0:T(8,128)(2,1)S(1)}, bf16[64,128]{1,0:T(8,128)(2,1)S(1)}, u32[]{:S(2)}, u32[]{:S(2)}) collective-permute-start(bf16[64,128]{1,0:T(8,128)(2,1)S(1)} %get-tuple-element.58), channel_id=1, source_target_pairs={{0,8},{4,12},{8,0},{12,4},{1,9},{5,13},{9,1},{13,5},{2,10},{6,14},... | collective-permute-start | bytes 49160 | tf_op jit(solution)/shard_map/ppermute | solution.py:390
  68.1 2.9 %shard_map.89.refs_7_ = f32[128,64]{1,0:T(8,128)S(1)} custom-call(f32[64,64]{1,0:T(8,128)S(1)} %get-tuple-element.57.refs_0_, bf16[64,128]{1,0:T(8,128)(2,1)S(1)} %collective-permute-done.20.refs_1_, f32[64,128]{1,0:T(8,128)S(1)} %get-tuple-element.51.refs_0_.refs_2_, f32[64,64]{1,0:T(8,128)S(1)} %shard_map.83.refs_2_.refs_3_, ...), custom_call_target="tpu_custom_call" | custom-call | flops 2000000000 | bytes 8000000 | tf_op jit(solution)/shard_map/pallas_call | solution.py:51
  71.0 1.9 %collective-permute-done.18.refs_2_ = bf16[256,128]{1,0:T(8,128)(2,1)S(1)} collective-permute-done((bf16[256,128]{1,0:T(8,128)(2,1)S(1)}, bf16[256,128]{1,0:T(8,128)(2,1)S(1)}, u32[]{:S(2)}, u32[]{:S(2)}) %collective-permute-start.18) | collective-permute-done | bytes 65568 | tf_op jit(solution)/shard_map/ppermute | solution.py:390
  72.9 1.3 %shard_map.90 = (f32[64,512]{1,0:T(8,128)}, f32[64,512]{1,0:T(8,128)}) custom-call(f32[256,128]{1,0:T(8,128)S(1)} %get-tuple-element.52.refs_0_, bf16[256,128]{1,0:T(8,128)(2,1)S(1)} %collective-permute-done.16.refs_1_, bf16[256,128]{1,0:T(8,128)(2,1)S(1)} %collective-permute-done.18.refs_2_, f32[64,512]{1,0:T(8,128)S(1)} %copy-done.2, ...), custom_call_target="tpu_custom_call" | custom-call | tf_op jit(solution)/shard_map/pallas_call | solution.py:51
  (47 shorter events, 9.2 us)
Async XLA Ops:
  0.6 0.9 %copy-start.1 = (f32[64,512]{1,0:T(8,128)S(1)}, f32[64,512]{1,0:T(8,128)}, u32[]{:S(2)}) copy-start(f32[64,512]{1,0:T(8,128)} %refs_3_.5) | copy-start | bytes 393220
  1.5 7.2 %collective-permute-start.1 = (bf16[256,128]{1,0:T(8,128)(2,1)S(1)}, bf16[256,128]{1,0:T(8,128)(2,1)S(1)}, u32[]{:S(2)}, u32[]{:S(2)}) collective-permute-start(bf16[256,128]{1,0:T(8,128)(2,1)S(1)} %shard_map.69.refs_1_), channel_id=1, source_target_pairs={{0,8},{4,12},{8,0},{12,4},{1,9},{5,13},{9,1},{13,5},{2,10},{6,14},... | collective-permute-start | bytes 196616 | tf_op jit(solution)/shard_map/ppermute | solution.py:390
  5.7 6.5 %collective-permute-start = (bf16[256,128]{1,0:T(8,128)(2,1)S(1)}, bf16[256,128]{1,0:T(8,128)(2,1)S(1)}, u32[]{:S(2)}, u32[]{:S(2)}) collective-permute-start(bf16[256,128]{1,0:T(8,128)(2,1)S(1)} %shard_map.69.refs_1_), channel_id=1, source_target_pairs={{0,4},{4,0},{8,12},{12,8},{1,5},{5,1},{9,13},{13,9},{2,6},{6,2},{1... | collective-permute-start | bytes 196616 | tf_op jit(solution)/shard_map/ppermute | solution.py:390
  7.2 0.7 copy-start.3
  7.9 2.2 %copy-start = (bf16[64,128,128]{2,1,0:T(8,128)(2,1)S(1)}, bf16[64,128,128]{2,1,0:T(8,128)(2,1)}, u32[]{:S(2)}) copy-start(bf16[64,128,128]{2,1,0:T(8,128)(2,1)} %refs_3_.4) | copy-start | bytes 6291460
  7.9 2.2 %copy-start.5 = (s32[64]{0:T(128)S(1)}, s32[64]{0:T(128)}, u32[]{:S(2)}) copy-start(s32[64]{0:T(128)} %refs_0_.4) | copy-start | bytes 772
  7.9 2.2 %copy-start.6 = (s32[64]{0:T(128)S(1)}, s32[64]{0:T(128)}, u32[]{:S(2)}) copy-start(s32[64]{0:T(128)} %refs_1_.1) | copy-start | bytes 772
  8.7 4.3 %collective-permute-start.2 = (bf16[256,128]{1,0:T(8,128)(2,1)S(1)}, bf16[256,128]{1,0:T(8,128)(2,1)S(1)}, u32[]{:S(2)}, u32[]{:S(2)}) collective-permute-start(bf16[256,128]{1,0:T(8,128)(2,1)S(1)} %collective-permute-done.1.refs_3_.refs_2_), channel_id=1, source_target_pairs={{0,4},{4,0},{8,12},{12,8},{1,5},{5,1},{9,13},{13,9},{2,6},{6,2},{1... | collective-permute-start | bytes 196616 | tf_op jit(solution)/shard_map/ppermute | solution.py:390
  12.1 5.8 %copy-start.2 = (f32[64,512]{1,0:T(8,128)S(1)}, f32[64,512]{1,0:T(8,128)}, u32[]{:S(2)}) copy-start(f32[64,512]{1,0:T(8,128)} %refs_3_.5) | copy-start | bytes 393220
  12.1 5.8 %copy-start.4 = (f32[512]{0:T(512)S(1)}, f32[512]{0:T(512)}, u32[]{:S(2)}) copy-start(f32[512]{0:T(512)} %param.6) | copy-start | bytes 6148
  14.3 1.6 %collective-permute-start.3 = (f32[576,128]{1,0:T(8,128)S(1)}, f32[576,128]{1,0:T(8,128)S(1)}, u32[]{:S(2)}, u32[]{:S(2)}) collective-permute-start(f32[576,128]{1,0:T(8,128)S(1)} %get-tuple-element.34), channel_id=1, source_target_pairs={{0,1},{1,0},{2,3},{3,2},{4,5},{5,4},{6,7},{7,6},{8,9},{9,8},{10,11... | collective-permute-start | bytes 884744 | tf_op jit(solution)/shard_map/ppermute | solution.py:390
  16.0 8.6 %collective-permute-start.4 = (bf16[576,128]{1,0:T(8,128)(2,1)S(1)}, bf16[576,128]{1,0:T(8,128)(2,1)S(1)}, u32[]{:S(2)}, u32[]{:S(2)}) collective-permute-start(bf16[576,128]{1,0:T(8,128)(2,1)S(1)} %shard_map.72.refs_2_.refs_0_), channel_id=1, source_target_pairs={{0,2},{1,3},{2,0},{3,1},{4,6},{5,7},{6,4},{7,5},{8,10},{9,11},{10,... | collective-permute-start | bytes 442376 | tf_op jit(solution)/shard_map/ppermute | solution.py:390
  17.9 6.6 %collective-permute-start.5 = (bf16[272,128]{1,0:T(8,128)(2,1)S(1)}, bf16[272,128]{1,0:T(8,128)(2,1)S(1)}, u32[]{:S(2)}, u32[]{:S(2)}) collective-permute-start(bf16[272,128]{1,0:T(8,128)(2,1)S(1)} %shard_map.73), channel_id=1, source_target_pairs={{0,8},{4,12},{8,0},{12,4},{1,9},{5,13},{9,1},{13,5},{2,10},{6,14},... | collective-permute-start | bytes 208904 | tf_op jit(solution)/shard_map/ppermute | solution.py:390
  24.6 1.4 %collective-permute-start.6 = (bf16[576,128]{1,0:T(8,128)(2,1)S(1)}, bf16[576,128]{1,0:T(8,128)(2,1)S(1)}, u32[]{:S(2)}, u32[]{:S(2)}) collective-permute-start(bf16[576,128]{1,0:T(8,128)(2,1)S(1)} %shard_map.74.refs_1_), channel_id=1, source_target_pairs={{0,1},{1,0},{2,3},{3,2},{4,5},{5,4},{6,7},{7,6},{8,9},{9,8},{10,11... | collective-permute-start | bytes 442376 | tf_op jit(solution)/shard_map/ppermute | solution.py:390
  27.5 5.3 %collective-permute-start.8 = (bf16[336,128]{1,0:T(8,128)(2,1)S(1)}, bf16[336,128]{1,0:T(8,128)(2,1)S(1)}, u32[]{:S(2)}, u32[]{:S(2)}) collective-permute-start(bf16[336,128]{1,0:T(8,128)(2,1)S(1)} %get-tuple-element.38.refs_0_), channel_id=1, source_target_pairs={{0,4},{4,0},{8,12},{12,8},{1,5},{5,1},{9,13},{13,9},{2,6},{6,2},{1... | collective-permute-start | bytes 258056 | tf_op jit(solution)/shard_map/ppermute | solution.py:390
  27.7 6.7 %collective-permute-start.7 = (bf16[256,128]{1,0:T(8,128)(2,1)S(1)}, bf16[256,128]{1,0:T(8,128)(2,1)S(1)}, u32[]{:S(2)}, u32[]{:S(2)}) collective-permute-start(bf16[256,128]{1,0:T(8,128)(2,1)S(1)} %get-tuple-element.36), channel_id=1, source_target_pairs={{0,4},{4,0},{8,12},{12,8},{1,5},{5,1},{9,13},{13,9},{2,6},{6,2},{1... | collective-permute-start | bytes 196616 | tf_op jit(solution)/shard_map/ppermute | solution.py:390
  32.9 7.3 %collective-permute-start.9 = (bf16[336,128]{1,0:T(8,128)(2,1)S(1)}, bf16[336,128]{1,0:T(8,128)(2,1)S(1)}, u32[]{:S(2)}, u32[]{:S(2)}) collective-permute-start(bf16[336,128]{1,0:T(8,128)(2,1)S(1)} %get-tuple-element.40.refs_0_), channel_id=1, source_target_pairs={{0,8},{4,12},{8,0},{12,4},{1,9},{5,13},{9,1},{13,5},{2,10},{6,14},... | collective-permute-start | bytes 258056 | tf_op jit(solution)/shard_map/ppermute | solution.py:390
  34.4 7.2 %collective-permute-start.11 = (bf16[256,128]{1,0:T(8,128)(2,1)S(1)}, bf16[256,128]{1,0:T(8,128)(2,1)S(1)}, u32[]{:S(2)}, u32[]{:S(2)}) collective-permute-start(bf16[256,128]{1,0:T(8,128)(2,1)S(1)} %get-tuple-element.44), channel_id=1, source_target_pairs={{0,8},{4,12},{8,0},{12,4},{1,9},{5,13},{9,1},{13,5},{2,10},{6,14},... | collective-permute-start | bytes 196616 | tf_op jit(solution)/shard_map/ppermute | solution.py:390
  40.5 4.3 %collective-permute-start.10 = (bf16[256,128]{1,0:T(8,128)(2,1)S(1)}, bf16[256,128]{1,0:T(8,128)(2,1)S(1)}, u32[]{:S(2)}, u32[]{:S(2)}) collective-permute-start(bf16[256,128]{1,0:T(8,128)(2,1)S(1)} %get-tuple-element.43.refs_1_), channel_id=1, source_target_pairs={{0,4},{4,0},{8,12},{12,8},{1,5},{5,1},{9,13},{13,9},{2,6},{6,2},{1... | collective-permute-start | bytes 196616 | tf_op jit(solution)/shard_map/ppermute | solution.py:390
  41.9 4.3 %collective-permute-start.12 = (bf16[256,128]{1,0:T(8,128)(2,1)S(1)}, bf16[256,128]{1,0:T(8,128)(2,1)S(1)}, u32[]{:S(2)}, u32[]{:S(2)}) collective-permute-start(bf16[256,128]{1,0:T(8,128)(2,1)S(1)} %shard_map.79.refs_3_), channel_id=1, source_target_pairs={{0,4},{4,0},{8,12},{12,8},{1,5},{5,1},{9,13},{13,9},{2,6},{6,2},{1... | collective-permute-start | bytes 196616 | tf_op jit(solution)/shard_map/ppermute | solution.py:390
  47.6 1.7 %collective-permute-start.13 = (f32[608,128]{1,0:T(8,128)S(1)}, f32[608,128]{1,0:T(8,128)S(1)}, u32[]{:S(2)}, u32[]{:S(2)}) collective-permute-start(f32[608,128]{1,0:T(8,128)S(1)} %get-tuple-element.49), channel_id=1, source_target_pairs={{0,1},{1,0},{2,3},{3,2},{4,5},{5,4},{6,7},{7,6},{8,9},{9,8},{10,11... | collective-permute-start | bytes 933896 | tf_op jit(solution)/shard_map/ppermute | solution.py:390
  49.3 6.0 %collective-permute-start.14 = (bf16[576,128]{1,0:T(8,128)(2,1)S(1)}, bf16[576,128]{1,0:T(8,128)(2,1)S(1)}, u32[]{:S(2)}, u32[]{:S(2)}) collective-permute-start(bf16[576,128]{1,0:T(8,128)(2,1)S(1)} %get-tuple-element.50.refs_0_), channel_id=1, source_target_pairs={{0,2},{1,3},{2,0},{3,1},{4,6},{5,7},{6,4},{7,5},{8,10},{9,11},{10,... | collective-permute-start | bytes 442376 | tf_op jit(solution)/shard_map/ppermute | solution.py:390
  55.3 1.4 %collective-permute-start.15 = (bf16[576,128]{1,0:T(8,128)(2,1)S(1)}, bf16[576,128]{1,0:T(8,128)(2,1)S(1)}, u32[]{:S(2)}, u32[]{:S(2)}) collective-permute-start(bf16[576,128]{1,0:T(8,128)(2,1)S(1)} %shard_map.84.refs_1_.refs_0_), channel_id=1, source_target_pairs={{0,1},{1,0},{2,3},{3,2},{4,5},{5,4},{6,7},{7,6},{8,9},{9,8},{10,11... | collective-permute-start | bytes 442376 | tf_op jit(solution)/shard_map/ppermute | solution.py:390
  58.0 8.9 %collective-permute-start.17 = (bf16[256,128]{1,0:T(8,128)(2,1)S(1)}, bf16[256,128]{1,0:T(8,128)(2,1)S(1)}, u32[]{:S(2)}, u32[]{:S(2)}) collective-permute-start(bf16[256,128]{1,0:T(8,128)(2,1)S(1)} %get-tuple-element.54.refs_0_), channel_id=1, source_target_pairs={{0,4},{4,0},{8,12},{12,8},{1,5},{5,1},{9,13},{13,9},{2,6},{6,2},{1... | collective-permute-start | bytes 196616 | tf_op jit(solution)/shard_map/ppermute | solution.py:390
  59.4 3.8 %collective-permute-start.19 = (bf16[64,128]{1,0:T(8,128)(2,1)S(1)}, bf16[64,128]{1,0:T(8,128)(2,1)S(1)}, u32[]{:S(2)}, u32[]{:S(2)}) collective-permute-start(bf16[64,128]{1,0:T(8,128)(2,1)S(1)} %shard_map.87.refs_0_), channel_id=1, source_target_pairs={{0,4},{4,0},{8,12},{12,8},{1,5},{5,1},{9,13},{13,9},{2,6},{6,2},{1... | collective-permute-start | bytes 49160 | tf_op jit(solution)/shard_map/ppermute | solution.py:390
  63.3 4.8 %collective-permute-start.20 = (bf16[64,128]{1,0:T(8,128)(2,1)S(1)}, bf16[64,128]{1,0:T(8,128)(2,1)S(1)}, u32[]{:S(2)}, u32[]{:S(2)}) collective-permute-start(bf16[64,128]{1,0:T(8,128)(2,1)S(1)} %get-tuple-element.58), channel_id=1, source_target_pairs={{0,8},{4,12},{8,0},{12,4},{1,9},{5,13},{9,1},{13,5},{2,10},{6,14},... | collective-permute-start | bytes 49160 | tf_op jit(solution)/shard_map/ppermute | solution.py:390
  66.0 5.0 %collective-permute-start.16 = (bf16[256,128]{1,0:T(8,128)(2,1)S(1)}, bf16[256,128]{1,0:T(8,128)(2,1)S(1)}, u32[]{:S(2)}, u32[]{:S(2)}) collective-permute-start(bf16[256,128]{1,0:T(8,128)(2,1)S(1)} %get-tuple-element.53), channel_id=1, source_target_pairs={{0,4},{4,0},{8,12},{12,8},{1,5},{5,1},{9,13},{13,9},{2,6},{6,2},{1... | collective-permute-start | bytes 196616 | tf_op jit(solution)/shard_map/ppermute | solution.py:390
  66.9 5.9 %collective-permute-start.18 = (bf16[256,128]{1,0:T(8,128)(2,1)S(1)}, bf16[256,128]{1,0:T(8,128)(2,1)S(1)}, u32[]{:S(2)}, u32[]{:S(2)}) collective-permute-start(bf16[256,128]{1,0:T(8,128)(2,1)S(1)} %shard_map.86), channel_id=1, source_target_pairs={{0,8},{4,12},{8,0},{12,4},{1,9},{5,13},{9,1},{13,5},{2,10},{6,14},... | collective-permute-start | bytes 196616 | tf_op jit(solution)/shard_map/ppermute | solution.py:390

commit v11 on v10

--- a/solution.py
+++ b/solution.py
@@ -168,8 +168,8 @@
 
 
 def backward_kernel(
-    stretch, cols, last, index, own, received, blocks,
-    far_refs, near_ref, keep_refs, keep_ref, norm_refs, acc, panel, gram,
+    stretch, cols, last, index, own, received, blocks, before,
+    far_refs, near_ref, keep_refs, keep_ref, acc, panel, gram,
 ):
     frames = panel.shape[1]
     split_at = frames // 2
@@ -179,7 +179,8 @@
         for x in range(cols // 2):
             for j in range(stretch):
                 panel[(2 * x + side) * stretch + j] = ref[rows(x * stretch + j, frames), :]
-    fill_gram(gram, own, received, data, frames)
+    if not last:
+        fill_gram(gram, own, received, data, frames)
     acc[...] = jnp.zeros_like(acc)
     for k in range(blocks.shape[0]):
         acc[index[1, k]] += jnp.dot(panel[index[0, k]], blocks[k], preferred_element_type=F32)
@@ -195,7 +196,6 @@
         keep_ref[rows(j, frames), :] = acc[me * stretch + j]
         near_ref[rows(j, frames), :] = acc[other * stretch + j].astype(BF16)
     if last:
-        norm_refs[0][...] = gram[:, :frames]
         return
     whole = whole_of(panel)
     total = gram[...] + nt_dot(whole, jnp.concatenate([jnp.zeros_like(whole), whole], axis=0))
@@ -243,12 +243,13 @@
         )
 
 
-def second_gram_kernel(data, own, received, out_ref, gram):
+def second_gram_kernel(data, own, received, out_ref, norm_ref, gram):
     frames = out_ref.shape[0]
     fill_gram(gram, own, received, data, frames)
     whole = jnp.concatenate(
         [ref[rows(j, frames), :] for ref in (own, received) for j in range(data // frames)], axis=1
     )
+    norm_ref[...] = gram[:, :frames]
     value = gram[:, frames:] + nt_dot(whole, whole)
     out_ref[...] = jnp.concatenate(split(value), axis=1)
 
@@ -452,19 +453,18 @@
         )
         return (foot, swapped(foot, "col", 1)), (*first, *aside_of_chips)
 
-    def backward(foot, last):
+    def backward(foot, before, last):
         size = stretch * frames
         extra = 0 if last else frames + DIAG
-        far, near, kept, keep, norm = call(
+        far, near, kept, keep = call(
             lambda *refs: backward_kernel(stretch, n_cols, last, *refs),
             (
                 tuple(shape((size + (0 if p else extra), BLOCK), BF16) for p in range(pairs)),
                 shape((size, BLOCK), BF16),
                 (shape((size, BLOCK)),) * pairs,
                 shape((size, BLOCK)),
-                (shape((frames, frames)),) if last else (),
             ),
-            (index, *foot, blocks),
+            (index, *foot, blocks, before),
             [
                 pltpu.VMEM((col_span, frames, BLOCK), F32),
                 pltpu.VMEM((row_span, frames, BLOCK), BF16),
@@ -484,7 +484,7 @@
             (far[0], received, kept),
         )
         far = tuple(swapped(x, "row", 2 * (p + 1)) for p, x in enumerate(sums))
-        return (keep, near, far, *gram), (norm if last else sums)
+        return (keep, near, far, *gram), sums
 
     (cast,) = call(cast_kernel, (cast_type,), (right_side,))
     search = gather(cast, "row")
@@ -496,7 +496,7 @@
     )
     (gram,) = call(gram_kernel, (gram_type,), (right_side, prior), cost=aside)
     foot, remainder = forward(search, gram, ())
-    (keep, near, far, gram, tile), sums = backward(foot, False)
+    (keep, near, far, gram, tile), sums = backward(foot, (), False)
     pair_sum, pair_cast = call(
         near_kernel, (shape((stretch * frames, BLOCK)), cast_type), (keep, near)
     )
@@ -522,9 +522,9 @@
         search = gather(cast, "row")
     (gram,) = call(gram_kernel, (gram_type,), (following, prior), cost=aside)
     foot, (first, inverse) = forward(search, gram, (half,))
-    (second,) = call(
+    second, norm = call(
         lambda *refs: second_gram_kernel(half_cols, *refs),
-        (shape((frames, 2 * frames), BF16),),
+        (shape((frames, 2 * frames), BF16), shape((frames, frames))),
         foot,
         [pltpu.VMEM((frames, 2 * frames), F32)],
     )
@@ -534,11 +534,11 @@
         (second, swapped(second, "row", 1)),
     )
     second = others(second, "row")[1:]
-    parts, norm = backward(foot, True)
+    parts, _ = backward(foot, (norm,), True)
     (coeffs,) = call(
         solve_kernel,
         (shape((2 * frames, frames)),),
-        (gram, second, first, inverse, *norm, diagonal),
+        (gram, second, first, inverse, norm, diagonal),
         cost=aside,
     )
     return tuple(

time: 74.3 us -> 74.3 us (level)
  no operation moved by 1% of the time
where the time goes in v11:
time: 74.3 us; the launch traced here: 74.1 us
  waiting for transfers between devices  31.5 us (42%)
  starting transfers between devices  24.8 us (33%)
  Pallas kernels  15.3 us (21%)
  local copies, waits for them, and re-layouts  1.6 us (2%)
  between operations  0.82 us (1%)
    ppermute x21, waiting for transfers between devices, swapped(): lax.ppermute(x, axis, [(i, i ^ flip) for i in range(lax.axis_size(axis))])  31.5 us
    ppermute x21, starting transfers between devices, swapped(): lax.ppermute(x, axis, [(i, i ^ flip) for i in range(lax.axis_size(axis))])  24.8 us
    pallas_call x23, Pallas kernels, call(): pl.pallas_call(body, out_shape=flat_outs, in_specs=[space(x) for x in fla...  15.3 us
    unnamed x14, local copies, waits for them, and re-layouts  1.6 us
  transfers between devices with their start and end apart: 21, of which 16 were waited for; matrix products, arithmetic and copies ran while one was open for 0% of the time, Pallas kernels for 11%

profile of v11, /device:TPU:0, one launch (start us, length us, event | category | flops | bytes accessed | tf_op | source)
XLA Modules:
  0.0 74.1 jit_solution(308340742791048063)
XLA Ops:
  1.5 4.1 %collective-permute-start.1 = (bf16[256,128]{1,0:T(8,128)(2,1)S(1)}, bf16[256,128]{1,0:T(8,128)(2,1)S(1)}, u32[]{:S(2)}, u32[]{:S(2)}) collective-permute-start(bf16[256,128]{1,0:T(8,128)(2,1)S(1)} %shard_map.69.refs_1_), channel_id=1, source_target_pairs={{0,8},{4,12},{8,0},{12,4},{1,9},{5,13},{9,1},{13,5},{2,10},{6,14},... | collective-permute-start | bytes 196616 | tf_op jit(solution)/shard_map/ppermute | solution.py:391
  5.7 1.6 %collective-permute-start = (bf16[256,128]{1,0:T(8,128)(2,1)S(1)}, bf16[256,128]{1,0:T(8,128)(2,1)S(1)}, u32[]{:S(2)}, u32[]{:S(2)}) collective-permute-start(bf16[256,128]{1,0:T(8,128)(2,1)S(1)} %shard_map.69.refs_1_), channel_id=1, source_target_pairs={{0,4},{4,0},{8,12},{12,8},{1,5},{5,1},{9,13},{13,9},{2,6},{6,2},{1... | collective-permute-start | bytes 196616 | tf_op jit(solution)/shard_map/ppermute | solution.py:391
  8.7 1.4 %collective-permute-start.2 = (bf16[256,128]{1,0:T(8,128)(2,1)S(1)}, bf16[256,128]{1,0:T(8,128)(2,1)S(1)}, u32[]{:S(2)}, u32[]{:S(2)}) collective-permute-start(bf16[256,128]{1,0:T(8,128)(2,1)S(1)} %collective-permute-done.1.refs_3_.refs_2_), channel_id=1, source_target_pairs={{0,4},{4,0},{8,12},{12,8},{1,5},{5,1},{9,13},{13,9},{2,6},{6,2},{1... | collective-permute-start | bytes 196616 | tf_op jit(solution)/shard_map/ppermute | solution.py:391
  10.1 2.0 %shard_map.68 = (s32[2,64]{1,0:T(2,128)S(1)}, bf16[64,128,128]{2,1,0:T(8,128)(2,1)S(1)}) custom-call(s32[64]{0:T(128)S(1)} %copy-done.5, s32[64]{0:T(128)S(1)} %copy-done.6, bf16[64,128,128]{2,1,0:T(8,128)(2,1)S(1)} %copy-done), custom_call_target="tpu_custom_call" | custom-call | flops 2000000000 | bytes 8000000 | tf_op jit(solution)/shard_map/pallas_call | solution.py:51
  13.0 1.3 %shard_map.71 = (f32[576,128]{1,0:T(8,128)S(1)}, f32[576,128]{1,0:T(8,128)S(1)}) custom-call(s32[2,64]{1,0:T(2,128)S(1)} %get-tuple-element.32.refs_0_, bf16[256,128]{1,0:T(8,128)(2,1)S(1)} %shard_map.69.refs_1_, bf16[256,128]{1,0:T(8,128)(2,1)S(1)} %collective-permute-done.refs_2_, bf16[256,128]{1,0:T(8,128)(2,1)S(1)} %collective-permute-done.1.refs_3_.refs_2_, ...), custom_call_target="tpu_custom_call" | custom-call | tf_op jit(solution)/shard_map/pallas_call | solution.py:51
  14.4 1.6 %collective-permute-done.3.refs_1_ = f32[576,128]{1,0:T(8,128)S(1)} collective-permute-done((f32[576,128]{1,0:T(8,128)S(1)}, f32[576,128]{1,0:T(8,128)S(1)}, u32[]{:S(2)}, u32[]{:S(2)}) %collective-permute-start.3) | collective-permute-done | bytes 294944 | tf_op jit(solution)/shard_map/ppermute | solution.py:391
  16.0 1.9 %collective-permute-start.4 = (bf16[576,128]{1,0:T(8,128)(2,1)S(1)}, bf16[576,128]{1,0:T(8,128)(2,1)S(1)}, u32[]{:S(2)}, u32[]{:S(2)}) collective-permute-start(bf16[576,128]{1,0:T(8,128)(2,1)S(1)} %shard_map.72.refs_2_.refs_0_), channel_id=1, source_target_pairs={{0,2},{1,3},{2,0},{3,1},{4,6},{5,7},{6,4},{7,5},{8,10},{9,11},{10,... | collective-permute-start | bytes 442376 | tf_op jit(solution)/shard_map/ppermute | solution.py:391
  17.9 2.4 %collective-permute-start.5 = (bf16[272,128]{1,0:T(8,128)(2,1)S(1)}, bf16[272,128]{1,0:T(8,128)(2,1)S(1)}, u32[]{:S(2)}, u32[]{:S(2)}) collective-permute-start(bf16[272,128]{1,0:T(8,128)(2,1)S(1)} %shard_map.73), channel_id=1, source_target_pairs={{0,8},{4,12},{8,0},{12,4},{1,9},{5,13},{9,1},{13,5},{2,10},{6,14},... | collective-permute-start | bytes 208904 | tf_op jit(solution)/shard_map/ppermute | solution.py:391
  20.3 4.3 %collective-permute-done.5.refs_2_.refs_3_ = bf16[272,128]{1,0:T(8,128)(2,1)S(1)} collective-permute-done((bf16[272,128]{1,0:T(8,128)(2,1)S(1)}, bf16[272,128]{1,0:T(8,128)(2,1)S(1)}, u32[]{:S(2)}, u32[]{:S(2)}) %collective-permute-start.5) | collective-permute-done | bytes 69664 | tf_op jit(solution)/shard_map/ppermute | solution.py:391
  24.7 1.4 %collective-permute-done.6.refs_2_ = bf16[576,128]{1,0:T(8,128)(2,1)S(1)} collective-permute-done((bf16[576,128]{1,0:T(8,128)(2,1)S(1)}, bf16[576,128]{1,0:T(8,128)(2,1)S(1)}, u32[]{:S(2)}, u32[]{:S(2)}) %collective-permute-start.6) | collective-permute-done | bytes 147488 | tf_op jit(solution)/shard_map/ppermute | solution.py:391
  26.0 1.5 %shard_map.75 = (bf16[336,128]{1,0:T(8,128)(2,1)S(1)}, bf16[256,128]{1,0:T(8,128)(2,1)S(1)}, f32[256,128]{1,0:T(8,128)S(1)}, f32[256,128]{1,0:T(8,128)S(1)}) custom-call(s32[2,64]{1,0:T(2,128)S(1)} %get-tuple-element.32.refs_0_, bf16[576,128]{1,0:T(8,128)(2,1)S(1)} %shard_map.74.refs_1_, bf16[576,128]{1,0:T(8,128)(2,1)S(1)} %collective-permute-done.6.refs_2_, ...), custom_call_target="tpu_custom_call" | custom-call | tf_op jit(solution)/shard_map/pallas_call | solution.py:51
  27.7 1.9 %collective-permute-start.7 = (bf16[256,128]{1,0:T(8,128)(2,1)S(1)}, bf16[256,128]{1,0:T(8,128)(2,1)S(1)}, u32[]{:S(2)}, u32[]{:S(2)}) collective-permute-start(bf16[256,128]{1,0:T(8,128)(2,1)S(1)} %get-tuple-element.37), channel_id=1, source_target_pairs={{0,4},{4,0},{8,12},{12,8},{1,5},{5,1},{9,13},{13,9},{2,6},{6,2},{1... | collective-permute-start | bytes 196616 | tf_op jit(solution)/shard_map/ppermute | solution.py:391
  29.6 3.3 %collective-permute-done.8.refs_1_ = bf16[336,128]{1,0:T(8,128)(2,1)S(1)} collective-permute-done((bf16[336,128]{1,0:T(8,128)(2,1)S(1)}, bf16[336,128]{1,0:T(8,128)(2,1)S(1)}, u32[]{:S(2)}, u32[]{:S(2)}) %collective-permute-start.8) | collective-permute-done | bytes 86048 | tf_op jit(solution)/shard_map/ppermute | solution.py:391
  32.9 1.5 %collective-permute-start.9 = (bf16[336,128]{1,0:T(8,128)(2,1)S(1)}, bf16[336,128]{1,0:T(8,128)(2,1)S(1)}, u32[]{:S(2)}, u32[]{:S(2)}) collective-permute-start(bf16[336,128]{1,0:T(8,128)(2,1)S(1)} %get-tuple-element.41.refs_0_), channel_id=1, source_target_pairs={{0,8},{4,12},{8,0},{12,4},{1,9},{5,13},{9,1},{13,5},{2,10},{6,14},... | collective-permute-start | bytes 258056 | tf_op jit(solution)/shard_map/ppermute | solution.py:391
  34.4 1.5 %collective-permute-start.11 = (bf16[256,128]{1,0:T(8,128)(2,1)S(1)}, bf16[256,128]{1,0:T(8,128)(2,1)S(1)}, u32[]{:S(2)}, u32[]{:S(2)}) collective-permute-start(bf16[256,128]{1,0:T(8,128)(2,1)S(1)} %get-tuple-element.45), channel_id=1, source_target_pairs={{0,8},{4,12},{8,0},{12,4},{1,9},{5,13},{9,1},{13,5},{2,10},{6,14},... | collective-permute-start | bytes 196616 | tf_op jit(solution)/shard_map/ppermute | solution.py:391
  36.0 4.2 %collective-permute-done.9.refs_1_ = bf16[336,128]{1,0:T(8,128)(2,1)S(1)} collective-permute-done((bf16[336,128]{1,0:T(8,128)(2,1)S(1)}, bf16[336,128]{1,0:T(8,128)(2,1)S(1)}, u32[]{:S(2)}, u32[]{:S(2)}) %collective-permute-start.9) | collective-permute-done | bytes 86048 | tf_op jit(solution)/shard_map/ppermute | solution.py:391
  41.9 1.0 %collective-permute-start.12 = (bf16[256,128]{1,0:T(8,128)(2,1)S(1)}, bf16[256,128]{1,0:T(8,128)(2,1)S(1)}, u32[]{:S(2)}, u32[]{:S(2)}) collective-permute-start(bf16[256,128]{1,0:T(8,128)(2,1)S(1)} %shard_map.79.refs_3_), channel_id=1, source_target_pairs={{0,4},{4,0},{8,12},{12,8},{1,5},{5,1},{9,13},{13,9},{2,6},{6,2},{1... | collective-permute-start | bytes 196616 | tf_op jit(solution)/shard_map/ppermute | solution.py:391
  43.2 1.5 %collective-permute-done.10.refs_2_ = bf16[256,128]{1,0:T(8,128)(2,1)S(1)} collective-permute-done((bf16[256,128]{1,0:T(8,128)(2,1)S(1)}, bf16[256,128]{1,0:T(8,128)(2,1)S(1)}, u32[]{:S(2)}, u32[]{:S(2)}) %collective-permute-start.10) | collective-permute-done | bytes 65568 | tf_op jit(solution)/shard_map/ppermute | solution.py:391
  44.8 1.4 %collective-permute-done.12.refs_4_ = bf16[256,128]{1,0:T(8,128)(2,1)S(1)} collective-permute-done((bf16[256,128]{1,0:T(8,128)(2,1)S(1)}, bf16[256,128]{1,0:T(8,128)(2,1)S(1)}, u32[]{:S(2)}, u32[]{:S(2)}) %collective-permute-start.12) | collective-permute-done | bytes 65568 | tf_op jit(solution)/shard_map/ppermute | solution.py:391
  46.2 1.4 %shard_map.81 = (f32[608,128]{1,0:T(8,128)S(1)}, f32[608,128]{1,0:T(8,128)S(1)}) custom-call(s32[2,64]{1,0:T(2,128)S(1)} %get-tuple-element.32.refs_0_, bf16[256,128]{1,0:T(8,128)(2,1)S(1)} %get-tuple-element.44.refs_1_, bf16[256,128]{1,0:T(8,128)(2,1)S(1)} %collective-permute-done.10.refs_2_, bf16[256,128]{1,0:T(8,128)(2,1)S(1)} %shard_map.79.refs_3_, ...), custom_call_target="tpu_custom_call" | custom-call | tf_op jit(solution)/shard_map/pallas_call | solution.py:51
  47.7 1.6 %collective-permute-done.13.refs_1_ = f32[608,128]{1,0:T(8,128)S(1)} collective-permute-done((f32[608,128]{1,0:T(8,128)S(1)}, f32[608,128]{1,0:T(8,128)S(1)}, u32[]{:S(2)}, u32[]{:S(2)}) %collective-permute-start.13) | collective-permute-done | bytes 311328 | tf_op jit(solution)/shard_map/ppermute | solution.py:391
  49.9 1.7 %shard_map.83.refs_2_.refs_3_ = f32[64,64]{1,0:T(8,128)S(1)} custom-call(f32[64,128]{1,0:T(8,128)S(1)} %get-tuple-element.52.refs_0_.refs_2_), custom_call_target="tpu_custom_call" | custom-call | flops 2000000000 | bytes 8000000 | tf_op jit(solution)/shard_map/pallas_call | solution.py:51
  51.6 3.6 %collective-permute-done.14.refs_1_ = bf16[576,128]{1,0:T(8,128)(2,1)S(1)} collective-permute-done((bf16[576,128]{1,0:T(8,128)(2,1)S(1)}, bf16[576,128]{1,0:T(8,128)(2,1)S(1)}, u32[]{:S(2)}, u32[]{:S(2)}) %collective-permute-start.14) | collective-permute-done | bytes 147488 | tf_op jit(solution)/shard_map/ppermute | solution.py:391
  55.4 1.4 %collective-permute-done.15.refs_1_.refs_2_ = bf16[576,128]{1,0:T(8,128)(2,1)S(1)} collective-permute-done((bf16[576,128]{1,0:T(8,128)(2,1)S(1)}, bf16[576,128]{1,0:T(8,128)(2,1)S(1)}, u32[]{:S(2)}, u32[]{:S(2)}) %collective-permute-start.15) | collective-permute-done | bytes 147488 | tf_op jit(solution)/shard_map/ppermute | solution.py:391
  57.1 1.3 %shard_map.86 = (bf16[256,128]{1,0:T(8,128)(2,1)S(1)}, bf16[256,128]{1,0:T(8,128)(2,1)S(1)}, f32[256,128]{1,0:T(8,128)S(1)}, f32[256,128]{1,0:T(8,128)S(1)}) custom-call(s32[2,64]{1,0:T(2,128)S(1)} %get-tuple-element.32.refs_0_, bf16[576,128]{1,0:T(8,128)(2,1)S(1)} %shard_map.84.refs_0_.refs_1_, ...), custom_call_target="tpu_custom_call" | custom-call | tf_op jit(solution)/shard_map/pallas_call | solution.py:51
  58.4 1.0 %collective-permute-start.17 = (bf16[256,128]{1,0:T(8,128)(2,1)S(1)}, bf16[256,128]{1,0:T(8,128)(2,1)S(1)}, u32[]{:S(2)}, u32[]{:S(2)}) collective-permute-start(bf16[256,128]{1,0:T(8,128)(2,1)S(1)} %get-tuple-element.56.refs_0_), channel_id=1, source_target_pairs={{0,4},{4,0},{8,12},{12,8},{1,5},{5,1},{9,13},{13,9},{2,6},{6,2},{1... | collective-permute-start | bytes 196616 | tf_op jit(solution)/shard_map/ppermute | solution.py:391
  59.4 1.1 %collective-permute-start.19 = (bf16[64,128]{1,0:T(8,128)(2,1)S(1)}, bf16[64,128]{1,0:T(8,128)(2,1)S(1)}, u32[]{:S(2)}, u32[]{:S(2)}) collective-permute-start(bf16[64,128]{1,0:T(8,128)(2,1)S(1)} %get-tuple-element.59.refs_0_), channel_id=1, source_target_pairs={{0,4},{4,0},{8,12},{12,8},{1,5},{5,1},{9,13},{13,9},{2,6},{6,2},{1... | collective-permute-start | bytes 49160 | tf_op jit(solution)/shard_map/ppermute | solution.py:391
  60.5 2.6 %collective-permute-done.19.refs_1_ = bf16[64,128]{1,0:T(8,128)(2,1)S(1)} collective-permute-done((bf16[64,128]{1,0:T(8,128)(2,1)S(1)}, bf16[64,128]{1,0:T(8,128)(2,1)S(1)}, u32[]{:S(2)}, u32[]{:S(2)}) %collective-permute-start.19) | collective-permute-done | bytes 16416 | tf_op jit(solution)/shard_map/ppermute | solution.py:391
  63.3 2.7 %collective-permute-start.20 = (bf16[64,128]{1,0:T(8,128)(2,1)S(1)}, bf16[64,128]{1,0:T(8,128)(2,1)S(1)}, u32[]{:S(2)}, u32[]{:S(2)}) collective-permute-start(bf16[64,128]{1,0:T(8,128)(2,1)S(1)} %get-tuple-element.61), channel_id=1, source_target_pairs={{0,8},{4,12},{8,0},{12,4},{1,9},{5,13},{9,1},{13,5},{2,10},{6,14},... | collective-permute-start | bytes 49160 | tf_op jit(solution)/shard_map/ppermute | solution.py:391
  68.0 2.9 %shard_map.89.refs_7_ = f32[128,64]{1,0:T(8,128)S(1)} custom-call(f32[64,64]{1,0:T(8,128)S(1)} %get-tuple-element.60.refs_0_, bf16[64,128]{1,0:T(8,128)(2,1)S(1)} %collective-permute-done.20.refs_1_, f32[64,128]{1,0:T(8,128)S(1)} %get-tuple-element.52.refs_0_.refs_2_, f32[64,64]{1,0:T(8,128)S(1)} %shard_map.83.refs_2_.refs_3_, ...), custom_call_target="tpu_custom_call" | custom-call | flops 2000000000 | bytes 8000000 | tf_op jit(solution)/shard_map/pallas_call | solution.py:51
  70.9 1.9 %collective-permute-done.18.refs_2_ = bf16[256,128]{1,0:T(8,128)(2,1)S(1)} collective-permute-done((bf16[256,128]{1,0:T(8,128)(2,1)S(1)}, bf16[256,128]{1,0:T(8,128)(2,1)S(1)}, u32[]{:S(2)}, u32[]{:S(2)}) %collective-permute-start.18) | collective-permute-done | bytes 65568 | tf_op jit(solution)/shard_map/ppermute | solution.py:391
  72.8 1.3 %shard_map.90 = (f32[64,512]{1,0:T(8,128)}, f32[64,512]{1,0:T(8,128)}) custom-call(f32[256,128]{1,0:T(8,128)S(1)} %get-tuple-element.54.refs_0_, bf16[256,128]{1,0:T(8,128)(2,1)S(1)} %collective-permute-done.16.refs_1_, bf16[256,128]{1,0:T(8,128)(2,1)S(1)} %collective-permute-done.18.refs_2_, f32[64,512]{1,0:T(8,128)S(1)} %copy-done.2, ...), custom_call_target="tpu_custom_call" | custom-call | tf_op jit(solution)/shard_map/pallas_call | solution.py:51
  (47 shorter events, 9.2 us)
Async XLA Ops:
  0.6 0.9 %copy-start.1 = (f32[64,512]{1,0:T(8,128)S(1)}, f32[64,512]{1,0:T(8,128)}, u32[]{:S(2)}) copy-start(f32[64,512]{1,0:T(8,128)} %refs_3_.5) | copy-start | bytes 393220
  1.5 7.2 %collective-permute-start.1 = (bf16[256,128]{1,0:T(8,128)(2,1)S(1)}, bf16[256,128]{1,0:T(8,128)(2,1)S(1)}, u32[]{:S(2)}, u32[]{:S(2)}) collective-permute-start(bf16[256,128]{1,0:T(8,128)(2,1)S(1)} %shard_map.69.refs_1_), channel_id=1, source_target_pairs={{0,8},{4,12},{8,0},{12,4},{1,9},{5,13},{9,1},{13,5},{2,10},{6,14},... | collective-permute-start | bytes 196616 | tf_op jit(solution)/shard_map/ppermute | solution.py:391
  5.7 6.5 %collective-permute-start = (bf16[256,128]{1,0:T(8,128)(2,1)S(1)}, bf16[256,128]{1,0:T(8,128)(2,1)S(1)}, u32[]{:S(2)}, u32[]{:S(2)}) collective-permute-start(bf16[256,128]{1,0:T(8,128)(2,1)S(1)} %shard_map.69.refs_1_), channel_id=1, source_target_pairs={{0,4},{4,0},{8,12},{12,8},{1,5},{5,1},{9,13},{13,9},{2,6},{6,2},{1... | collective-permute-start | bytes 196616 | tf_op jit(solution)/shard_map/ppermute | solution.py:391
  7.2 0.7 copy-start.3
  7.9 2.2 %copy-start = (bf16[64,128,128]{2,1,0:T(8,128)(2,1)S(1)}, bf16[64,128,128]{2,1,0:T(8,128)(2,1)}, u32[]{:S(2)}) copy-start(bf16[64,128,128]{2,1,0:T(8,128)(2,1)} %refs_3_.4) | copy-start | bytes 6291460
  7.9 2.2 %copy-start.5 = (s32[64]{0:T(128)S(1)}, s32[64]{0:T(128)}, u32[]{:S(2)}) copy-start(s32[64]{0:T(128)} %refs_0_.4) | copy-start | bytes 772
  7.9 2.2 %copy-start.6 = (s32[64]{0:T(128)S(1)}, s32[64]{0:T(128)}, u32[]{:S(2)}) copy-start(s32[64]{0:T(128)} %refs_1_.1) | copy-start | bytes 772
  8.7 4.3 %collective-permute-start.2 = (bf16[256,128]{1,0:T(8,128)(2,1)S(1)}, bf16[256,128]{1,0:T(8,128)(2,1)S(1)}, u32[]{:S(2)}, u32[]{:S(2)}) collective-permute-start(bf16[256,128]{1,0:T(8,128)(2,1)S(1)} %collective-permute-done.1.refs_3_.refs_2_), channel_id=1, source_target_pairs={{0,4},{4,0},{8,12},{12,8},{1,5},{5,1},{9,13},{13,9},{2,6},{6,2},{1... | collective-permute-start | bytes 196616 | tf_op jit(solution)/shard_map/ppermute | solution.py:391
  12.1 5.8 %copy-start.2 = (f32[64,512]{1,0:T(8,128)S(1)}, f32[64,512]{1,0:T(8,128)}, u32[]{:S(2)}) copy-start(f32[64,512]{1,0:T(8,128)} %refs_3_.5) | copy-start | bytes 393220
  12.1 5.8 %copy-start.4 = (f32[512]{0:T(512)S(1)}, f32[512]{0:T(512)}, u32[]{:S(2)}) copy-start(f32[512]{0:T(512)} %param.6) | copy-start | bytes 6148
  14.3 1.6 %collective-permute-start.3 = (f32[576,128]{1,0:T(8,128)S(1)}, f32[576,128]{1,0:T(8,128)S(1)}, u32[]{:S(2)}, u32[]{:S(2)}) collective-permute-start(f32[576,128]{1,0:T(8,128)S(1)} %get-tuple-element.35), channel_id=1, source_target_pairs={{0,1},{1,0},{2,3},{3,2},{4,5},{5,4},{6,7},{7,6},{8,9},{9,8},{10,11... | collective-permute-start | bytes 884744 | tf_op jit(solution)/shard_map/ppermute | solution.py:391
  16.0 8.6 %collective-permute-start.4 = (bf16[576,128]{1,0:T(8,128)(2,1)S(1)}, bf16[576,128]{1,0:T(8,128)(2,1)S(1)}, u32[]{:S(2)}, u32[]{:S(2)}) collective-permute-start(bf16[576,128]{1,0:T(8,128)(2,1)S(1)} %shard_map.72.refs_2_.refs_0_), channel_id=1, source_target_pairs={{0,2},{1,3},{2,0},{3,1},{4,6},{5,7},{6,4},{7,5},{8,10},{9,11},{10,... | collective-permute-start | bytes 442376 | tf_op jit(solution)/shard_map/ppermute | solution.py:391
  17.9 6.6 %collective-permute-start.5 = (bf16[272,128]{1,0:T(8,128)(2,1)S(1)}, bf16[272,128]{1,0:T(8,128)(2,1)S(1)}, u32[]{:S(2)}, u32[]{:S(2)}) collective-permute-start(bf16[272,128]{1,0:T(8,128)(2,1)S(1)} %shard_map.73), channel_id=1, source_target_pairs={{0,8},{4,12},{8,0},{12,4},{1,9},{5,13},{9,1},{13,5},{2,10},{6,14},... | collective-permute-start | bytes 208904 | tf_op jit(solution)/shard_map/ppermute | solution.py:391
  24.6 1.4 %collective-permute-start.6 = (bf16[576,128]{1,0:T(8,128)(2,1)S(1)}, bf16[576,128]{1,0:T(8,128)(2,1)S(1)}, u32[]{:S(2)}, u32[]{:S(2)}) collective-permute-start(bf16[576,128]{1,0:T(8,128)(2,1)S(1)} %shard_map.74.refs_1_), channel_id=1, source_target_pairs={{0,1},{1,0},{2,3},{3,2},{4,5},{5,4},{6,7},{7,6},{8,9},{9,8},{10,11... | collective-permute-start | bytes 442376 | tf_op jit(solution)/shard_map/ppermute | solution.py:391
  27.5 5.4 %collective-permute-start.8 = (bf16[336,128]{1,0:T(8,128)(2,1)S(1)}, bf16[336,128]{1,0:T(8,128)(2,1)S(1)}, u32[]{:S(2)}, u32[]{:S(2)}) collective-permute-start(bf16[336,128]{1,0:T(8,128)(2,1)S(1)} %get-tuple-element.39.refs_0_), channel_id=1, source_target_pairs={{0,4},{4,0},{8,12},{12,8},{1,5},{5,1},{9,13},{13,9},{2,6},{6,2},{1... | collective-permute-start | bytes 258056 | tf_op jit(solution)/shard_map/ppermute | solution.py:391
  27.7 6.7 %collective-permute-start.7 = (bf16[256,128]{1,0:T(8,128)(2,1)S(1)}, bf16[256,128]{1,0:T(8,128)(2,1)S(1)}, u32[]{:S(2)}, u32[]{:S(2)}) collective-permute-start(bf16[256,128]{1,0:T(8,128)(2,1)S(1)} %get-tuple-element.37), channel_id=1, source_target_pairs={{0,4},{4,0},{8,12},{12,8},{1,5},{5,1},{9,13},{13,9},{2,6},{6,2},{1... | collective-permute-start | bytes 196616 | tf_op jit(solution)/shard_map/ppermute | solution.py:391
  32.9 7.3 %collective-permute-start.9 = (bf16[336,128]{1,0:T(8,128)(2,1)S(1)}, bf16[336,128]{1,0:T(8,128)(2,1)S(1)}, u32[]{:S(2)}, u32[]{:S(2)}) collective-permute-start(bf16[336,128]{1,0:T(8,128)(2,1)S(1)} %get-tuple-element.41.refs_0_), channel_id=1, source_target_pairs={{0,8},{4,12},{8,0},{12,4},{1,9},{5,13},{9,1},{13,5},{2,10},{6,14},... | collective-permute-start | bytes 258056 | tf_op jit(solution)/shard_map/ppermute | solution.py:391
  34.4 7.2 %collective-permute-start.11 = (bf16[256,128]{1,0:T(8,128)(2,1)S(1)}, bf16[256,128]{1,0:T(8,128)(2,1)S(1)}, u32[]{:S(2)}, u32[]{:S(2)}) collective-permute-start(bf16[256,128]{1,0:T(8,128)(2,1)S(1)} %get-tuple-element.45), channel_id=1, source_target_pairs={{0,8},{4,12},{8,0},{12,4},{1,9},{5,13},{9,1},{13,5},{2,10},{6,14},... | collective-permute-start | bytes 196616 | tf_op jit(solution)/shard_map/ppermute | solution.py:391
  40.5 4.3 %collective-permute-start.10 = (bf16[256,128]{1,0:T(8,128)(2,1)S(1)}, bf16[256,128]{1,0:T(8,128)(2,1)S(1)}, u32[]{:S(2)}, u32[]{:S(2)}) collective-permute-start(bf16[256,128]{1,0:T(8,128)(2,1)S(1)} %get-tuple-element.44.refs_1_), channel_id=1, source_target_pairs={{0,4},{4,0},{8,12},{12,8},{1,5},{5,1},{9,13},{13,9},{2,6},{6,2},{1... | collective-permute-start | bytes 196616 | tf_op jit(solution)/shard_map/ppermute | solution.py:391
  41.9 4.3 %collective-permute-start.12 = (bf16[256,128]{1,0:T(8,128)(2,1)S(1)}, bf16[256,128]{1,0:T(8,128)(2,1)S(1)}, u32[]{:S(2)}, u32[]{:S(2)}) collective-permute-start(bf16[256,128]{1,0:T(8,128)(2,1)S(1)} %shard_map.79.refs_3_), channel_id=1, source_target_pairs={{0,4},{4,0},{8,12},{12,8},{1,5},{5,1},{9,13},{13,9},{2,6},{6,2},{1... | collective-permute-start | bytes 196616 | tf_op jit(solution)/shard_map/ppermute | solution.py:391
  47.6 1.7 %collective-permute-start.13 = (f32[608,128]{1,0:T(8,128)S(1)}, f32[608,128]{1,0:T(8,128)S(1)}, u32[]{:S(2)}, u32[]{:S(2)}) collective-permute-start(f32[608,128]{1,0:T(8,128)S(1)} %get-tuple-element.50), channel_id=1, source_target_pairs={{0,1},{1,0},{2,3},{3,2},{4,5},{5,4},{6,7},{7,6},{8,9},{9,8},{10,11... | collective-permute-start | bytes 933896 | tf_op jit(solution)/shard_map/ppermute | solution.py:391
  49.3 6.0 %collective-permute-start.14 = (bf16[576,128]{1,0:T(8,128)(2,1)S(1)}, bf16[576,128]{1,0:T(8,128)(2,1)S(1)}, u32[]{:S(2)}, u32[]{:S(2)}) collective-permute-start(bf16[576,128]{1,0:T(8,128)(2,1)S(1)} %get-tuple-element.51.refs_0_), channel_id=1, source_target_pairs={{0,2},{1,3},{2,0},{3,1},{4,6},{5,7},{6,4},{7,5},{8,10},{9,11},{10,... | collective-permute-start | bytes 442376 | tf_op jit(solution)/shard_map/ppermute | solution.py:391
  55.3 1.4 %collective-permute-start.15 = (bf16[576,128]{1,0:T(8,128)(2,1)S(1)}, bf16[576,128]{1,0:T(8,128)(2,1)S(1)}, u32[]{:S(2)}, u32[]{:S(2)}) collective-permute-start(bf16[576,128]{1,0:T(8,128)(2,1)S(1)} %shard_map.84.refs_0_.refs_1_), channel_id=1, source_target_pairs={{0,1},{1,0},{2,3},{3,2},{4,5},{5,4},{6,7},{7,6},{8,9},{9,8},{10,11... | collective-permute-start | bytes 442376 | tf_op jit(solution)/shard_map/ppermute | solution.py:391
  58.4 8.5 %collective-permute-start.17 = (bf16[256,128]{1,0:T(8,128)(2,1)S(1)}, bf16[256,128]{1,0:T(8,128)(2,1)S(1)}, u32[]{:S(2)}, u32[]{:S(2)}) collective-permute-start(bf16[256,128]{1,0:T(8,128)(2,1)S(1)} %get-tuple-element.56.refs_0_), channel_id=1, source_target_pairs={{0,4},{4,0},{8,12},{12,8},{1,5},{5,1},{9,13},{13,9},{2,6},{6,2},{1... | collective-permute-start | bytes 196616 | tf_op jit(solution)/shard_map/ppermute | solution.py:391
  59.4 3.7 %collective-permute-start.19 = (bf16[64,128]{1,0:T(8,128)(2,1)S(1)}, bf16[64,128]{1,0:T(8,128)(2,1)S(1)}, u32[]{:S(2)}, u32[]{:S(2)}) collective-permute-start(bf16[64,128]{1,0:T(8,128)(2,1)S(1)} %get-tuple-element.59.refs_0_), channel_id=1, source_target_pairs={{0,4},{4,0},{8,12},{12,8},{1,5},{5,1},{9,13},{13,9},{2,6},{6,2},{1... | collective-permute-start | bytes 49160 | tf_op jit(solution)/shard_map/ppermute | solution.py:391
  63.3 4.8 %collective-permute-start.20 = (bf16[64,128]{1,0:T(8,128)(2,1)S(1)}, bf16[64,128]{1,0:T(8,128)(2,1)S(1)}, u32[]{:S(2)}, u32[]{:S(2)}) collective-permute-start(bf16[64,128]{1,0:T(8,128)(2,1)S(1)} %get-tuple-element.61), channel_id=1, source_target_pairs={{0,8},{4,12},{8,0},{12,4},{1,9},{5,13},{9,1},{13,5},{2,10},{6,14},... | collective-permute-start | bytes 49160 | tf_op jit(solution)/shard_map/ppermute | solution.py:391
  65.9 5.0 %collective-permute-start.16 = (bf16[256,128]{1,0:T(8,128)(2,1)S(1)}, bf16[256,128]{1,0:T(8,128)(2,1)S(1)}, u32[]{:S(2)}, u32[]{:S(2)}) collective-permute-start(bf16[256,128]{1,0:T(8,128)(2,1)S(1)} %get-tuple-element.55), channel_id=1, source_target_pairs={{0,4},{4,0},{8,12},{12,8},{1,5},{5,1},{9,13},{13,9},{2,6},{6,2},{1... | collective-permute-start | bytes 196616 | tf_op jit(solution)/shard_map/ppermute | solution.py:391
  66.9 5.9 %collective-permute-start.18 = (bf16[256,128]{1,0:T(8,128)(2,1)S(1)}, bf16[256,128]{1,0:T(8,128)(2,1)S(1)}, u32[]{:S(2)}, u32[]{:S(2)}) collective-permute-start(bf16[256,128]{1,0:T(8,128)(2,1)S(1)} %shard_map.87), channel_id=1, source_target_pairs={{0,8},{4,12},{8,0},{12,4},{1,9},{5,13},{9,1},{13,5},{2,10},{6,14},... | collective-permute-start | bytes 196616 | tf_op jit(solution)/shard_map/ppermute | solution.py:391

commit v12 on v9

--- a/solution.py
+++ b/solution.py
@@ -381,17 +381,24 @@
     out_ref[n:, :] = gamma
 
 
-def final_kernel(keep, near, far, v_ref, image_ref, next_ref, prior, coeffs_ref, x_ref, r_ref):
+def early_kernel(keep, near, v_ref, image_ref, next_ref, prior, coeffs_ref, x_ref, base_ref):
     n = v_ref.shape[0]
     coeffs = coeffs_ref[...]
     for j in range(keep.shape[0] // n):
         value = v_ref[:, lanes(j)]
         following = next_ref[:, lanes(j)]
-        second_image = own_sum(keep, (near, *far), j, n) + prior[:, lanes(j)] * following
+        second_image = own_sum(keep, (near,), j, n) + prior[:, lanes(j)] * following
         x_ref[:, lanes(j)] = tn_dot(coeffs, jnp.concatenate([value, following], axis=0))
-        r_ref[:, lanes(j)] = value - tn_dot(
+        base_ref[:, lanes(j)] = value - tn_dot(
             coeffs, jnp.concatenate([image_ref[:, lanes(j)], second_image], axis=0)
         )
+
+
+def final_kernel(far, base_ref, coeffs_ref, r_ref):
+    n = base_ref.shape[0]
+    gamma = coeffs_ref[n:, :]
+    for j in range(base_ref.shape[1] // BLOCK):
+        r_ref[:, lanes(j)] = base_ref[:, lanes(j)] - tn_dot(gamma, sum_rows(far, rows(j, n)))
 
 
 def swapped(x, axis, flip):
@@ -554,13 +561,15 @@
     (coeffs,) = call(
         solve_kernel, (shape((2 * frames, frames)),), (gram, second, *middle), cost=aside
     )
-    return tuple(
-        call(
-            final_kernel,
-            (own, own),
-            (*parts, right_side, image, following, prior, coeffs),
-        )
-    )
+    keep, near, far = parts
+    x, base = call(
+        early_kernel,
+        (own, own),
+        (keep, near, right_side, image, following, prior, coeffs),
+        cost=aside,
+    )
+    (residual,) = call(final_kernel, (own,), (far, base, coeffs))
+    return x, residual
 
 
 def solution(mesh):

time: 73 us -> 76.9 us (1.053)
  waiting for transfers between devices: 29.7 us -> 33.1 us
  Pallas kernels: 15.5 us -> 16.4 us
    ppermute x21, waiting for transfers between devices: 29.7 us -> 33.1 us  [swapped(): lax.ppermute(x, axis, [(i, i ^ flip) for i in range(lax.axis_size(axis))])]
    pallas_call x24 -> x25, Pallas kernels: 15.5 us -> 16.4 us  [call(): pl.pallas_call(body, out_shape=flat_outs, in_specs=[space(x) for x in fla...]
  transfers between devices with their start and end apart: 21 -> 21, of which waited for: 16 -> 16; matrix products, arithmetic and copies ran while one was open for 0% -> 0% of each run, Pallas kernels for 13% -> 14%
where the time goes in v12:
time: 76.9 us; the launch traced here: 76.7 us
  waiting for transfers between devices  33.1 us (43%)
  starting transfers between devices  24.8 us (32%)
  Pallas kernels  16.4 us (21%)
  local copies, waits for them, and re-layouts  1.6 us (2%)
  between operations  0.81 us (1%)
    ppermute x21, waiting for transfers between devices, swapped(): lax.ppermute(x, axis, [(i, i ^ flip) for i in range(lax.axis_size(axis))])  33.1 us
    ppermute x21, starting transfers between devices, swapped(): lax.ppermute(x, axis, [(i, i ^ flip) for i in range(lax.axis_size(axis))])  24.8 us
    pallas_call x25, Pallas kernels, call(): pl.pallas_call(body, out_shape=flat_outs, in_specs=[space(x) for x in fla...  16.4 us
    unnamed x14, local copies, waits for them, and re-layouts  1.6 us
  transfers between devices with their start and end apart: 21, of which 16 were waited for; matrix products, arithmetic and copies ran while one was open for 0% of the time, Pallas kernels for 14%

profile of v12, /device:TPU:0, one launch (start us, length us, event | category | flops | bytes accessed | tf_op | source)
XLA Modules:
  0.0 76.7 jit_solution(219863550406298048)
XLA Ops:
  1.5 4.1 %collective-permute-start.1 = (bf16[256,128]{1,0:T(8,128)(2,1)S(1)}, bf16[256,128]{1,0:T(8,128)(2,1)S(1)}, u32[]{:S(2)}, u32[]{:S(2)}) collective-permute-start(bf16[256,128]{1,0:T(8,128)(2,1)S(1)} %shard_map.69.refs_1_), channel_id=1, source_target_pairs={{0,8},{4,12},{8,0},{12,4},{1,9},{5,13},{9,1},{13,5},{2,10},{6,14},... | collective-permute-start | bytes 196616 | tf_op jit(solution)/shard_map/ppermute | solution.py:405
  5.7 1.6 %collective-permute-start = (bf16[256,128]{1,0:T(8,128)(2,1)S(1)}, bf16[256,128]{1,0:T(8,128)(2,1)S(1)}, u32[]{:S(2)}, u32[]{:S(2)}) collective-permute-start(bf16[256,128]{1,0:T(8,128)(2,1)S(1)} %shard_map.69.refs_1_), channel_id=1, source_target_pairs={{0,4},{4,0},{8,12},{12,8},{1,5},{5,1},{9,13},{13,9},{2,6},{6,2},{1... | collective-permute-start | bytes 196616 | tf_op jit(solution)/shard_map/ppermute | solution.py:405
  8.7 1.4 %collective-permute-start.2 = (bf16[256,128]{1,0:T(8,128)(2,1)S(1)}, bf16[256,128]{1,0:T(8,128)(2,1)S(1)}, u32[]{:S(2)}, u32[]{:S(2)}) collective-permute-start(bf16[256,128]{1,0:T(8,128)(2,1)S(1)} %collective-permute-done.1.refs_3_.refs_2_), channel_id=1, source_target_pairs={{0,4},{4,0},{8,12},{12,8},{1,5},{5,1},{9,13},{13,9},{2,6},{6,2},{1... | collective-permute-start | bytes 196616 | tf_op jit(solution)/shard_map/ppermute | solution.py:405
  10.1 2.0 %shard_map.68 = (s32[2,64]{1,0:T(2,128)S(1)}, bf16[64,128,128]{2,1,0:T(8,128)(2,1)S(1)}) custom-call(s32[64]{0:T(128)S(1)} %copy-done.5, s32[64]{0:T(128)S(1)} %copy-done.6, bf16[64,128,128]{2,1,0:T(8,128)(2,1)S(1)} %copy-done), custom_call_target="tpu_custom_call" | custom-call | flops 2000000000 | bytes 8000000 | tf_op jit(solution)/shard_map/pallas_call | solution.py:51
  13.0 1.3 %shard_map.71 = (f32[576,128]{1,0:T(8,128)S(1)}, f32[576,128]{1,0:T(8,128)S(1)}) custom-call(s32[2,64]{1,0:T(2,128)S(1)} %get-tuple-element.33.refs_0_, bf16[256,128]{1,0:T(8,128)(2,1)S(1)} %shard_map.69.refs_1_, bf16[256,128]{1,0:T(8,128)(2,1)S(1)} %collective-permute-done.refs_2_, bf16[256,128]{1,0:T(8,128)(2,1)S(1)} %collective-permute-done.1.refs_3_.refs_2_, ...), custom_call_target="tpu_custom_call" | custom-call | tf_op jit(solution)/shard_map/pallas_call | solution.py:51
  14.4 1.6 %collective-permute-done.3.refs_1_ = f32[576,128]{1,0:T(8,128)S(1)} collective-permute-done((f32[576,128]{1,0:T(8,128)S(1)}, f32[576,128]{1,0:T(8,128)S(1)}, u32[]{:S(2)}, u32[]{:S(2)}) %collective-permute-start.3) | collective-permute-done | bytes 294944 | tf_op jit(solution)/shard_map/ppermute | solution.py:405
  16.0 1.9 %collective-permute-start.4 = (bf16[576,128]{1,0:T(8,128)(2,1)S(1)}, bf16[576,128]{1,0:T(8,128)(2,1)S(1)}, u32[]{:S(2)}, u32[]{:S(2)}) collective-permute-start(bf16[576,128]{1,0:T(8,128)(2,1)S(1)} %shard_map.72.refs_2_.refs_0_), channel_id=1, source_target_pairs={{0,2},{1,3},{2,0},{3,1},{4,6},{5,7},{6,4},{7,5},{8,10},{9,11},{10,... | collective-permute-start | bytes 442376 | tf_op jit(solution)/shard_map/ppermute | solution.py:405
  17.9 2.4 %collective-permute-start.5 = (bf16[272,128]{1,0:T(8,128)(2,1)S(1)}, bf16[272,128]{1,0:T(8,128)(2,1)S(1)}, u32[]{:S(2)}, u32[]{:S(2)}) collective-permute-start(bf16[272,128]{1,0:T(8,128)(2,1)S(1)} %shard_map.73), channel_id=1, source_target_pairs={{0,8},{4,12},{8,0},{12,4},{1,9},{5,13},{9,1},{13,5},{2,10},{6,14},... | collective-permute-start | bytes 208904 | tf_op jit(solution)/shard_map/ppermute | solution.py:405
  20.3 4.3 %collective-permute-done.5.refs_2_.refs_3_ = bf16[272,128]{1,0:T(8,128)(2,1)S(1)} collective-permute-done((bf16[272,128]{1,0:T(8,128)(2,1)S(1)}, bf16[272,128]{1,0:T(8,128)(2,1)S(1)}, u32[]{:S(2)}, u32[]{:S(2)}) %collective-permute-start.5) | collective-permute-done | bytes 69664 | tf_op jit(solution)/shard_map/ppermute | solution.py:405
  24.7 1.4 %collective-permute-done.6.refs_2_ = bf16[576,128]{1,0:T(8,128)(2,1)S(1)} collective-permute-done((bf16[576,128]{1,0:T(8,128)(2,1)S(1)}, bf16[576,128]{1,0:T(8,128)(2,1)S(1)}, u32[]{:S(2)}, u32[]{:S(2)}) %collective-permute-start.6) | collective-permute-done | bytes 147488 | tf_op jit(solution)/shard_map/ppermute | solution.py:405
  26.0 1.5 %shard_map.75 = (bf16[336,128]{1,0:T(8,128)(2,1)S(1)}, bf16[256,128]{1,0:T(8,128)(2,1)S(1)}, f32[256,128]{1,0:T(8,128)S(1)}, f32[256,128]{1,0:T(8,128)S(1)}) custom-call(s32[2,64]{1,0:T(2,128)S(1)} %get-tuple-element.33.refs_0_, bf16[576,128]{1,0:T(8,128)(2,1)S(1)} %shard_map.74.refs_1_, bf16[576,128]{1,0:T(8,128)(2,1)S(1)} %collective-permute-done.6.refs_2_, ...), custom_call_target="tpu_custom_call" | custom-call | tf_op jit(solution)/shard_map/pallas_call | solution.py:51
  27.7 1.9 %collective-permute-start.7 = (bf16[256,128]{1,0:T(8,128)(2,1)S(1)}, bf16[256,128]{1,0:T(8,128)(2,1)S(1)}, u32[]{:S(2)}, u32[]{:S(2)}) collective-permute-start(bf16[256,128]{1,0:T(8,128)(2,1)S(1)} %get-tuple-element.38), channel_id=1, source_target_pairs={{0,4},{4,0},{8,12},{12,8},{1,5},{5,1},{9,13},{13,9},{2,6},{6,2},{1... | collective-permute-start | bytes 196616 | tf_op jit(solution)/shard_map/ppermute | solution.py:405
  29.6 3.3 %collective-permute-done.8.refs_1_ = bf16[336,128]{1,0:T(8,128)(2,1)S(1)} collective-permute-done((bf16[336,128]{1,0:T(8,128)(2,1)S(1)}, bf16[336,128]{1,0:T(8,128)(2,1)S(1)}, u32[]{:S(2)}, u32[]{:S(2)}) %collective-permute-start.8) | collective-permute-done | bytes 86048 | tf_op jit(solution)/shard_map/ppermute | solution.py:405
  32.9 1.5 %collective-permute-start.9 = (bf16[336,128]{1,0:T(8,128)(2,1)S(1)}, bf16[336,128]{1,0:T(8,128)(2,1)S(1)}, u32[]{:S(2)}, u32[]{:S(2)}) collective-permute-start(bf16[336,128]{1,0:T(8,128)(2,1)S(1)} %get-tuple-element.42.refs_0_), channel_id=1, source_target_pairs={{0,8},{4,12},{8,0},{12,4},{1,9},{5,13},{9,1},{13,5},{2,10},{6,14},... | collective-permute-start | bytes 258056 | tf_op jit(solution)/shard_map/ppermute | solution.py:405
  34.4 1.5 %collective-permute-start.11 = (bf16[256,128]{1,0:T(8,128)(2,1)S(1)}, bf16[256,128]{1,0:T(8,128)(2,1)S(1)}, u32[]{:S(2)}, u32[]{:S(2)}) collective-permute-start(bf16[256,128]{1,0:T(8,128)(2,1)S(1)} %get-tuple-element.46), channel_id=1, source_target_pairs={{0,8},{4,12},{8,0},{12,4},{1,9},{5,13},{9,1},{13,5},{2,10},{6,14},... | collective-permute-start | bytes 196616 | tf_op jit(solution)/shard_map/ppermute | solution.py:405
  36.0 4.2 %collective-permute-done.9.refs_1_ = bf16[336,128]{1,0:T(8,128)(2,1)S(1)} collective-permute-done((bf16[336,128]{1,0:T(8,128)(2,1)S(1)}, bf16[336,128]{1,0:T(8,128)(2,1)S(1)}, u32[]{:S(2)}, u32[]{:S(2)}) %collective-permute-start.9) | collective-permute-done | bytes 86048 | tf_op jit(solution)/shard_map/ppermute | solution.py:405
  41.9 1.0 %collective-permute-start.12 = (bf16[256,128]{1,0:T(8,128)(2,1)S(1)}, bf16[256,128]{1,0:T(8,128)(2,1)S(1)}, u32[]{:S(2)}, u32[]{:S(2)}) collective-permute-start(bf16[256,128]{1,0:T(8,128)(2,1)S(1)} %shard_map.79.refs_3_), channel_id=1, source_target_pairs={{0,4},{4,0},{8,12},{12,8},{1,5},{5,1},{9,13},{13,9},{2,6},{6,2},{1... | collective-permute-start | bytes 196616 | tf_op jit(solution)/shard_map/ppermute | solution.py:405
  43.2 1.5 %collective-permute-done.10.refs_2_ = bf16[256,128]{1,0:T(8,128)(2,1)S(1)} collective-permute-done((bf16[256,128]{1,0:T(8,128)(2,1)S(1)}, bf16[256,128]{1,0:T(8,128)(2,1)S(1)}, u32[]{:S(2)}, u32[]{:S(2)}) %collective-permute-start.10) | collective-permute-done | bytes 65568 | tf_op jit(solution)/shard_map/ppermute | solution.py:405
  44.8 1.4 %collective-permute-done.12.refs_4_ = bf16[256,128]{1,0:T(8,128)(2,1)S(1)} collective-permute-done((bf16[256,128]{1,0:T(8,128)(2,1)S(1)}, bf16[256,128]{1,0:T(8,128)(2,1)S(1)}, u32[]{:S(2)}, u32[]{:S(2)}) %collective-permute-start.12) | collective-permute-done | bytes 65568 | tf_op jit(solution)/shard_map/ppermute | solution.py:405
  46.2 1.4 %shard_map.81 = (f32[608,128]{1,0:T(8,128)S(1)}, f32[608,128]{1,0:T(8,128)S(1)}) custom-call(s32[2,64]{1,0:T(2,128)S(1)} %get-tuple-element.33.refs_0_, bf16[256,128]{1,0:T(8,128)(2,1)S(1)} %get-tuple-element.45.refs_1_, bf16[256,128]{1,0:T(8,128)(2,1)S(1)} %collective-permute-done.10.refs_2_, bf16[256,128]{1,0:T(8,128)(2,1)S(1)} %shard_map.79.refs_3_, ...), custom_call_target="tpu_custom_call" | custom-call | tf_op jit(solution)/shard_map/pallas_call | solution.py:51
  47.7 1.6 %collective-permute-done.13.refs_1_ = f32[608,128]{1,0:T(8,128)S(1)} collective-permute-done((f32[608,128]{1,0:T(8,128)S(1)}, f32[608,128]{1,0:T(8,128)S(1)}, u32[]{:S(2)}, u32[]{:S(2)}) %collective-permute-start.13) | collective-permute-done | bytes 311328 | tf_op jit(solution)/shard_map/ppermute | solution.py:405
  49.9 1.7 %shard_map.83.refs_2_.refs_1_ = f32[64,64]{1,0:T(8,128)S(1)} custom-call(f32[64,128]{1,0:T(8,128)S(1)} %get-tuple-element.53.refs_0_), custom_call_target="tpu_custom_call" | custom-call | flops 2000000000 | bytes 8000000 | tf_op jit(solution)/shard_map/pallas_call | solution.py:51
  51.6 3.6 %collective-permute-done.14.refs_1_ = bf16[576,128]{1,0:T(8,128)(2,1)S(1)} collective-permute-done((bf16[576,128]{1,0:T(8,128)(2,1)S(1)}, bf16[576,128]{1,0:T(8,128)(2,1)S(1)}, u32[]{:S(2)}, u32[]{:S(2)}) %collective-permute-start.14) | collective-permute-done | bytes 147488 | tf_op jit(solution)/shard_map/ppermute | solution.py:405
  55.4 1.4 %collective-permute-done.15.refs_2_.refs_1_ = bf16[576,128]{1,0:T(8,128)(2,1)S(1)} collective-permute-done((bf16[576,128]{1,0:T(8,128)(2,1)S(1)}, bf16[576,128]{1,0:T(8,128)(2,1)S(1)}, u32[]{:S(2)}, u32[]{:S(2)}) %collective-permute-start.15) | collective-permute-done | bytes 147488 | tf_op jit(solution)/shard_map/ppermute | solution.py:405
  58.0 1.3 %shard_map.85 = (bf16[256,128]{1,0:T(8,128)(2,1)S(1)}, bf16[256,128]{1,0:T(8,128)(2,1)S(1)}, f32[256,128]{1,0:T(8,128)S(1)}, f32[256,128]{1,0:T(8,128)S(1)}, f32[64,64]{1,0:T(8,128)S(1)}) custom-call(s32[2,64]{1,0:T(2,128)S(1)} %get-tuple-element.33.refs_0_, bf16[576,128]{1,0:T(8,128)(2,1)S(1)} %shard_map.84.refs_1_.refs_0_, ...), custom_call_target="tpu_custom_call" | custom-call | tf_op jit(solution)/shard_map/pallas_call | solution.py:51
  59.3 1.5 %collective-permute-done.17.refs_1_ = bf16[64,128]{1,0:T(8,128)(2,1)S(1)} collective-permute-done((bf16[64,128]{1,0:T(8,128)(2,1)S(1)}, bf16[64,128]{1,0:T(8,128)(2,1)S(1)}, u32[]{:S(2)}, u32[]{:S(2)}) %collective-permute-start.17) | collective-permute-done | bytes 16416 | tf_op jit(solution)/shard_map/ppermute | solution.py:405
  61.0 2.5 %collective-permute-start.18 = (bf16[64,128]{1,0:T(8,128)(2,1)S(1)}, bf16[64,128]{1,0:T(8,128)(2,1)S(1)}, u32[]{:S(2)}, u32[]{:S(2)}) collective-permute-start(bf16[64,128]{1,0:T(8,128)(2,1)S(1)} %get-tuple-element.58), channel_id=1, source_target_pairs={{0,8},{4,12},{8,0},{12,4},{1,9},{5,13},{9,1},{13,5},{2,10},{6,14},... | collective-permute-start | bytes 49160 | tf_op jit(solution)/shard_map/ppermute | solution.py:405
  64.4 1.1 %collective-permute-start.16 = (bf16[256,128]{1,0:T(8,128)(2,1)S(1)}, bf16[256,128]{1,0:T(8,128)(2,1)S(1)}, u32[]{:S(2)}, u32[]{:S(2)}) collective-permute-start(bf16[256,128]{1,0:T(8,128)(2,1)S(1)} %get-tuple-element.55), channel_id=1, source_target_pairs={{0,4},{4,0},{8,12},{12,8},{1,5},{5,1},{9,13},{13,9},{2,6},{6,2},{1... | collective-permute-start | bytes 196616 | tf_op jit(solution)/shard_map/ppermute | solution.py:405
  66.5 2.1 %shard_map.89.refs_6_.refs_2_ = f32[128,64]{1,0:T(8,128)S(1)} custom-call(f32[64,64]{1,0:T(8,128)S(1)} %get-tuple-element.57.refs_0_, bf16[64,128]{1,0:T(8,128)(2,1)S(1)} %collective-permute-done.18.refs_1_, f32[4,64,64]{2,1,0:T(8,128)S(1)} %shard_map.88.refs_2_.refs_3_), custom_call_target="tpu_custom_call" | custom-call | flops 2000000000 | bytes 8000000 | tf_op jit(solution)/shard_map/pallas_call | solution.py:51
  68.6 1.2 %collective-permute-done.19.refs_1_ = bf16[256,128]{1,0:T(8,128)(2,1)S(1)} collective-permute-done((bf16[256,128]{1,0:T(8,128)(2,1)S(1)}, bf16[256,128]{1,0:T(8,128)(2,1)S(1)}, u32[]{:S(2)}, u32[]{:S(2)}) %collective-permute-start.19) | collective-permute-done | bytes 65568 | tf_op jit(solution)/shard_map/ppermute | solution.py:405
  70.5 1.3 %shard_map.90 = (f32[64,512]{1,0:T(8,128)}, f32[64,512]{1,0:T(8,128)S(1)}) custom-call(f32[256,128]{1,0:T(8,128)S(1)} %get-tuple-element.54.refs_0_, bf16[256,128]{1,0:T(8,128)(2,1)S(1)} %collective-permute-done.16.refs_1_, f32[64,512]{1,0:T(8,128)S(1)} %copy-done.2, f32[64,512]{1,0:T(8,128)S(1)} %get-tuple-element.56.refs_3_, ...), custom_call_target="tpu_custom_call" | custom-call | flops 2000000000 | bytes 8000000 | tf_op jit(solution)/shard_map/pallas_call | solution.py:51
  71.8 4.0 %collective-permute-done.20.refs_0_ = bf16[256,128]{1,0:T(8,128)(2,1)S(1)} collective-permute-done((bf16[256,128]{1,0:T(8,128)(2,1)S(1)}, bf16[256,128]{1,0:T(8,128)(2,1)S(1)}, u32[]{:S(2)}, u32[]{:S(2)}) %collective-permute-start.20) | collective-permute-done | bytes 65568 | tf_op jit(solution)/shard_map/ppermute | solution.py:405
  (49 shorter events, 11.6 us)
Async XLA Ops:
  0.6 0.9 %copy-start.1 = (f32[64,512]{1,0:T(8,128)S(1)}, f32[64,512]{1,0:T(8,128)}, u32[]{:S(2)}) copy-start(f32[64,512]{1,0:T(8,128)} %refs_2_.3) | copy-start | bytes 393220
  1.5 7.2 %collective-permute-start.1 = (bf16[256,128]{1,0:T(8,128)(2,1)S(1)}, bf16[256,128]{1,0:T(8,128)(2,1)S(1)}, u32[]{:S(2)}, u32[]{:S(2)}) collective-permute-start(bf16[256,128]{1,0:T(8,128)(2,1)S(1)} %shard_map.69.refs_1_), channel_id=1, source_target_pairs={{0,8},{4,12},{8,0},{12,4},{1,9},{5,13},{9,1},{13,5},{2,10},{6,14},... | collective-permute-start | bytes 196616 | tf_op jit(solution)/shard_map/ppermute | solution.py:405
  5.7 6.5 %collective-permute-start = (bf16[256,128]{1,0:T(8,128)(2,1)S(1)}, bf16[256,128]{1,0:T(8,128)(2,1)S(1)}, u32[]{:S(2)}, u32[]{:S(2)}) collective-permute-start(bf16[256,128]{1,0:T(8,128)(2,1)S(1)} %shard_map.69.refs_1_), channel_id=1, source_target_pairs={{0,4},{4,0},{8,12},{12,8},{1,5},{5,1},{9,13},{13,9},{2,6},{6,2},{1... | collective-permute-start | bytes 196616 | tf_op jit(solution)/shard_map/ppermute | solution.py:405
  7.2 0.7 copy-start.3
  7.9 2.2 %copy-start = (bf16[64,128,128]{2,1,0:T(8,128)(2,1)S(1)}, bf16[64,128,128]{2,1,0:T(8,128)(2,1)}, u32[]{:S(2)}) copy-start(bf16[64,128,128]{2,1,0:T(8,128)(2,1)} %refs_3_.3) | copy-start | bytes 6291460
  7.9 2.2 %copy-start.5 = (s32[64]{0:T(128)S(1)}, s32[64]{0:T(128)}, u32[]{:S(2)}) copy-start(s32[64]{0:T(128)} %refs_0_.4) | copy-start | bytes 772
  7.9 2.2 %copy-start.6 = (s32[64]{0:T(128)S(1)}, s32[64]{0:T(128)}, u32[]{:S(2)}) copy-start(s32[64]{0:T(128)} %refs_1_.1) | copy-start | bytes 772
  8.7 4.3 %collective-permute-start.2 = (bf16[256,128]{1,0:T(8,128)(2,1)S(1)}, bf16[256,128]{1,0:T(8,128)(2,1)S(1)}, u32[]{:S(2)}, u32[]{:S(2)}) collective-permute-start(bf16[256,128]{1,0:T(8,128)(2,1)S(1)} %collective-permute-done.1.refs_3_.refs_2_), channel_id=1, source_target_pairs={{0,4},{4,0},{8,12},{12,8},{1,5},{5,1},{9,13},{13,9},{2,6},{6,2},{1... | collective-permute-start | bytes 196616 | tf_op jit(solution)/shard_map/ppermute | solution.py:405
  12.1 5.8 %copy-start.2 = (f32[64,512]{1,0:T(8,128)S(1)}, f32[64,512]{1,0:T(8,128)}, u32[]{:S(2)}) copy-start(f32[64,512]{1,0:T(8,128)} %refs_2_.3) | copy-start | bytes 393220
  14.3 1.6 %collective-permute-start.3 = (f32[576,128]{1,0:T(8,128)S(1)}, f32[576,128]{1,0:T(8,128)S(1)}, u32[]{:S(2)}, u32[]{:S(2)}) collective-permute-start(f32[576,128]{1,0:T(8,128)S(1)} %get-tuple-element.36), channel_id=1, source_target_pairs={{0,1},{1,0},{2,3},{3,2},{4,5},{5,4},{6,7},{7,6},{8,9},{9,8},{10,11... | collective-permute-start | bytes 884744 | tf_op jit(solution)/shard_map/ppermute | solution.py:405
  16.0 8.6 %collective-permute-start.4 = (bf16[576,128]{1,0:T(8,128)(2,1)S(1)}, bf16[576,128]{1,0:T(8,128)(2,1)S(1)}, u32[]{:S(2)}, u32[]{:S(2)}) collective-permute-start(bf16[576,128]{1,0:T(8,128)(2,1)S(1)} %shard_map.72.refs_2_.refs_0_), channel_id=1, source_target_pairs={{0,2},{1,3},{2,0},{3,1},{4,6},{5,7},{6,4},{7,5},{8,10},{9,11},{10,... | collective-permute-start | bytes 442376 | tf_op jit(solution)/shard_map/ppermute | solution.py:405
  17.9 6.6 %collective-permute-start.5 = (bf16[272,128]{1,0:T(8,128)(2,1)S(1)}, bf16[272,128]{1,0:T(8,128)(2,1)S(1)}, u32[]{:S(2)}, u32[]{:S(2)}) collective-permute-start(bf16[272,128]{1,0:T(8,128)(2,1)S(1)} %shard_map.73), channel_id=1, source_target_pairs={{0,8},{4,12},{8,0},{12,4},{1,9},{5,13},{9,1},{13,5},{2,10},{6,14},... | collective-permute-start | bytes 208904 | tf_op jit(solution)/shard_map/ppermute | solution.py:405
  24.6 1.4 %collective-permute-start.6 = (bf16[576,128]{1,0:T(8,128)(2,1)S(1)}, bf16[576,128]{1,0:T(8,128)(2,1)S(1)}, u32[]{:S(2)}, u32[]{:S(2)}) collective-permute-start(bf16[576,128]{1,0:T(8,128)(2,1)S(1)} %shard_map.74.refs_1_), channel_id=1, source_target_pairs={{0,1},{1,0},{2,3},{3,2},{4,5},{5,4},{6,7},{7,6},{8,9},{9,8},{10,11... | collective-permute-start | bytes 442376 | tf_op jit(solution)/shard_map/ppermute | solution.py:405
  27.5 5.3 %collective-permute-start.8 = (bf16[336,128]{1,0:T(8,128)(2,1)S(1)}, bf16[336,128]{1,0:T(8,128)(2,1)S(1)}, u32[]{:S(2)}, u32[]{:S(2)}) collective-permute-start(bf16[336,128]{1,0:T(8,128)(2,1)S(1)} %get-tuple-element.40.refs_0_), channel_id=1, source_target_pairs={{0,4},{4,0},{8,12},{12,8},{1,5},{5,1},{9,13},{13,9},{2,6},{6,2},{1... | collective-permute-start | bytes 258056 | tf_op jit(solution)/shard_map/ppermute | solution.py:405
  27.7 6.7 %collective-permute-start.7 = (bf16[256,128]{1,0:T(8,128)(2,1)S(1)}, bf16[256,128]{1,0:T(8,128)(2,1)S(1)}, u32[]{:S(2)}, u32[]{:S(2)}) collective-permute-start(bf16[256,128]{1,0:T(8,128)(2,1)S(1)} %get-tuple-element.38), channel_id=1, source_target_pairs={{0,4},{4,0},{8,12},{12,8},{1,5},{5,1},{9,13},{13,9},{2,6},{6,2},{1... | collective-permute-start | bytes 196616 | tf_op jit(solution)/shard_map/ppermute | solution.py:405
  32.9 7.3 %collective-permute-start.9 = (bf16[336,128]{1,0:T(8,128)(2,1)S(1)}, bf16[336,128]{1,0:T(8,128)(2,1)S(1)}, u32[]{:S(2)}, u32[]{:S(2)}) collective-permute-start(bf16[336,128]{1,0:T(8,128)(2,1)S(1)} %get-tuple-element.42.refs_0_), channel_id=1, source_target_pairs={{0,8},{4,12},{8,0},{12,4},{1,9},{5,13},{9,1},{13,5},{2,10},{6,14},... | collective-permute-start | bytes 258056 | tf_op jit(solution)/shard_map/ppermute | solution.py:405
  34.4 7.2 %collective-permute-start.11 = (bf16[256,128]{1,0:T(8,128)(2,1)S(1)}, bf16[256,128]{1,0:T(8,128)(2,1)S(1)}, u32[]{:S(2)}, u32[]{:S(2)}) collective-permute-start(bf16[256,128]{1,0:T(8,128)(2,1)S(1)} %get-tuple-element.46), channel_id=1, source_target_pairs={{0,8},{4,12},{8,0},{12,4},{1,9},{5,13},{9,1},{13,5},{2,10},{6,14},... | collective-permute-start | bytes 196616 | tf_op jit(solution)/shard_map/ppermute | solution.py:405
  40.4 4.3 %collective-permute-start.10 = (bf16[256,128]{1,0:T(8,128)(2,1)S(1)}, bf16[256,128]{1,0:T(8,128)(2,1)S(1)}, u32[]{:S(2)}, u32[]{:S(2)}) collective-permute-start(bf16[256,128]{1,0:T(8,128)(2,1)S(1)} %get-tuple-element.45.refs_1_), channel_id=1, source_target_pairs={{0,4},{4,0},{8,12},{12,8},{1,5},{5,1},{9,13},{13,9},{2,6},{6,2},{1... | collective-permute-start | bytes 196616 | tf_op jit(solution)/shard_map/ppermute | solution.py:405
  41.9 4.3 %collective-permute-start.12 = (bf16[256,128]{1,0:T(8,128)(2,1)S(1)}, bf16[256,128]{1,0:T(8,128)(2,1)S(1)}, u32[]{:S(2)}, u32[]{:S(2)}) collective-permute-start(bf16[256,128]{1,0:T(8,128)(2,1)S(1)} %shard_map.79.refs_3_), channel_id=1, source_target_pairs={{0,4},{4,0},{8,12},{12,8},{1,5},{5,1},{9,13},{13,9},{2,6},{6,2},{1... | collective-permute-start | bytes 196616 | tf_op jit(solution)/shard_map/ppermute | solution.py:405
  47.6 1.7 %collective-permute-start.13 = (f32[608,128]{1,0:T(8,128)S(1)}, f32[608,128]{1,0:T(8,128)S(1)}, u32[]{:S(2)}, u32[]{:S(2)}) collective-permute-start(f32[608,128]{1,0:T(8,128)S(1)} %get-tuple-element.51), channel_id=1, source_target_pairs={{0,1},{1,0},{2,3},{3,2},{4,5},{5,4},{6,7},{7,6},{8,9},{9,8},{10,11... | collective-permute-start | bytes 933896 | tf_op jit(solution)/shard_map/ppermute | solution.py:405
  49.3 6.0 %collective-permute-start.14 = (bf16[576,128]{1,0:T(8,128)(2,1)S(1)}, bf16[576,128]{1,0:T(8,128)(2,1)S(1)}, u32[]{:S(2)}, u32[]{:S(2)}) collective-permute-start(bf16[576,128]{1,0:T(8,128)(2,1)S(1)} %get-tuple-element.52.refs_0_), channel_id=1, source_target_pairs={{0,2},{1,3},{2,0},{3,1},{4,6},{5,7},{6,4},{7,5},{8,10},{9,11},{10,... | collective-permute-start | bytes 442376 | tf_op jit(solution)/shard_map/ppermute | solution.py:405
  55.3 1.4 %collective-permute-start.15 = (bf16[576,128]{1,0:T(8,128)(2,1)S(1)}, bf16[576,128]{1,0:T(8,128)(2,1)S(1)}, u32[]{:S(2)}, u32[]{:S(2)}) collective-permute-start(bf16[576,128]{1,0:T(8,128)(2,1)S(1)} %shard_map.84.refs_1_.refs_0_), channel_id=1, source_target_pairs={{0,1},{1,0},{2,3},{3,2},{4,5},{5,4},{6,7},{7,6},{8,9},{9,8},{10,11... | collective-permute-start | bytes 442376 | tf_op jit(solution)/shard_map/ppermute | solution.py:405
  57.1 3.8 %collective-permute-start.17 = (bf16[64,128]{1,0:T(8,128)(2,1)S(1)}, bf16[64,128]{1,0:T(8,128)(2,1)S(1)}, u32[]{:S(2)}, u32[]{:S(2)}) collective-permute-start(bf16[64,128]{1,0:T(8,128)(2,1)S(1)} %shard_map.86.refs_0_), channel_id=1, source_target_pairs={{0,4},{4,0},{8,12},{12,8},{1,5},{5,1},{9,13},{13,9},{2,6},{6,2},{1... | collective-permute-start | bytes 49160 | tf_op jit(solution)/shard_map/ppermute | solution.py:405
  61.0 5.5 %collective-permute-start.18 = (bf16[64,128]{1,0:T(8,128)(2,1)S(1)}, bf16[64,128]{1,0:T(8,128)(2,1)S(1)}, u32[]{:S(2)}, u32[]{:S(2)}) collective-permute-start(bf16[64,128]{1,0:T(8,128)(2,1)S(1)} %get-tuple-element.58), channel_id=1, source_target_pairs={{0,8},{4,12},{8,0},{12,4},{1,9},{5,13},{9,1},{13,5},{2,10},{6,14},... | collective-permute-start | bytes 49160 | tf_op jit(solution)/shard_map/ppermute | solution.py:405
  64.4 6.1 %collective-permute-start.16 = (bf16[256,128]{1,0:T(8,128)(2,1)S(1)}, bf16[256,128]{1,0:T(8,128)(2,1)S(1)}, u32[]{:S(2)}, u32[]{:S(2)}) collective-permute-start(bf16[256,128]{1,0:T(8,128)(2,1)S(1)} %get-tuple-element.55), channel_id=1, source_target_pairs={{0,4},{4,0},{8,12},{12,8},{1,5},{5,1},{9,13},{13,9},{2,6},{6,2},{1... | collective-permute-start | bytes 196616 | tf_op jit(solution)/shard_map/ppermute | solution.py:405
  65.5 4.3 %collective-permute-start.19 = (bf16[256,128]{1,0:T(8,128)(2,1)S(1)}, bf16[256,128]{1,0:T(8,128)(2,1)S(1)}, u32[]{:S(2)}, u32[]{:S(2)}) collective-permute-start(bf16[256,128]{1,0:T(8,128)(2,1)S(1)} %get-tuple-element.61.refs_0_), channel_id=1, source_target_pairs={{0,4},{4,0},{8,12},{12,8},{1,5},{5,1},{9,13},{13,9},{2,6},{6,2},{1... | collective-permute-start | bytes 196616 | tf_op jit(solution)/shard_map/ppermute | solution.py:405
  66.5 4.0 %copy-start.4 = (f32[512]{0:T(512)S(1)}, f32[512]{0:T(512)}, u32[]{:S(2)}) copy-start(f32[512]{0:T(512)} %param.6) | copy-start | bytes 6148
  69.8 5.9 %collective-permute-start.20 = (bf16[256,128]{1,0:T(8,128)(2,1)S(1)}, bf16[256,128]{1,0:T(8,128)(2,1)S(1)}, u32[]{:S(2)}, u32[]{:S(2)}) collective-permute-start(bf16[256,128]{1,0:T(8,128)(2,1)S(1)} %shard_map.91), channel_id=1, source_target_pairs={{0,8},{4,12},{8,0},{12,4},{1,9},{5,13},{9,1},{13,5},{2,10},{6,14},... | collective-permute-start | bytes 196616 | tf_op jit(solution)/shard_map/ppermute | solution.py:405

commit v13 on v10

--- a/solution.py
+++ b/solution.py
@@ -213,21 +213,21 @@
     out_ref[at + frames :, :] = jnp.where(row == 0, diagonal, 0.0).astype(BF16)
 
 
-def rows_kernel(frames, sent, received, kept, out_refs, gram_refs):
+def rows_kernel(frames, sent, received, kept, out_refs, extra_refs):
     split_at = frames // 2
     data = kept[0].shape[0]
     for out_ref, kept_ref, received_ref in zip(out_refs, kept, received):
         for j in range(data // frames):
             at = rows(j, frames)
             out_ref[at, :] = (kept_ref[at, :] + received_ref[at, :].astype(F32)).astype(BF16)
-    if gram_refs:
+    if extra_refs:
         pair = (sent, received[0])
         high, low = slice(data, data + split_at), slice(data + split_at, data + frames)
         value = sum_rows(pair, high) + sum_rows(pair, low)
         block = jnp.concatenate(split(value), axis=0)
         tile = sum_rows(pair, slice(data + frames, data + frames + DIAG)).astype(BF16)
-        gram_refs[0][...] = value
-        gram_refs[1][...] = tile
+        extra_refs[0][...] = value
+        extra_refs[1][...] = tile
         for out_ref in out_refs:
             out_ref[data : data + frames, :] = block
             out_ref[data + frames :, :] = tile
@@ -373,17 +373,24 @@
     out_ref[n:, :] = gamma
 
 
-def final_kernel(keep, near, far, v_ref, image_ref, next_ref, prior, coeffs_ref, x_ref, r_ref):
+def early_kernel(keep, near, v_ref, image_ref, next_ref, prior, coeffs_ref, x_ref, base_ref):
     n = v_ref.shape[0]
     coeffs = coeffs_ref[...]
     for j in range(keep.shape[0] // n):
         value = v_ref[:, lanes(j)]
         following = next_ref[:, lanes(j)]
-        second_image = own_sum(keep, (near, *far), j, n) + prior[:, lanes(j)] * following
+        second_image = own_sum(keep, (near,), j, n) + prior[:, lanes(j)] * following
         x_ref[:, lanes(j)] = tn_dot(coeffs, jnp.concatenate([value, following], axis=0))
-        r_ref[:, lanes(j)] = value - tn_dot(
+        base_ref[:, lanes(j)] = value - tn_dot(
             coeffs, jnp.concatenate([image_ref[:, lanes(j)], second_image], axis=0)
         )
+
+
+def final_kernel(far, base_ref, coeffs_ref, r_ref):
+    n = base_ref.shape[0]
+    gamma = coeffs_ref[n:, :]
+    for j in range(base_ref.shape[1] // BLOCK):
+        r_ref[:, lanes(j)] = base_ref[:, lanes(j)] - tn_dot(gamma, sum_rows(far, rows(j, n)))
 
 
 def swapped(x, axis, flip):
@@ -415,6 +422,7 @@
     cast_type = shape((stretch * frames, BLOCK), BF16)
     aside = pl.CostEstimate(flops=2 * 10**9, bytes_accessed=8 * 10**6, transcendentals=0)
 
+    hidden = pl.CostEstimate(flops=1, bytes_accessed=1, transcendentals=0)
     pairs = n_rows // 2 - 1
 
     def forward(search, gram, half):
@@ -484,7 +492,9 @@
             (far[0], received, kept),
         )
         far = tuple(swapped(x, "row", 2 * (p + 1)) for p, x in enumerate(sums))
-        return (keep, near, far, *gram), (norm if last else sums)
+        if last:
+            return (keep, near, far), norm
+        return (keep, near, far, *gram), sums
 
     (cast,) = call(cast_kernel, (cast_type,), (right_side,))
     search = gather(cast, "row")
@@ -532,22 +542,25 @@
         second_pair_kernel,
         (shape((frames, frames)), shape((frames, 2 * frames), BF16)),
         (second, swapped(second, "row", 1)),
+        cost=aside,
     )
     second = others(second, "row")[1:]
-    parts, norm = backward(foot, True)
+    parts, (norm,) = backward(foot, True)
     (coeffs,) = call(
         solve_kernel,
         (shape((2 * frames, frames)),),
-        (gram, second, first, inverse, *norm, diagonal),
+        (gram, second, first, inverse, norm, diagonal),
         cost=aside,
     )
-    return tuple(
-        call(
-            final_kernel,
-            (own, own),
-            (*parts, right_side, image, following, prior, coeffs),
-        )
-    )
+    keep, near, far = parts
+    x, base = call(
+        early_kernel,
+        (own, own),
+        (keep, near, right_side, image, following, prior, coeffs),
+        cost=hidden,
+    )
+    (residual,) = call(final_kernel, (own,), (far, base, coeffs))
+    return x, residual
 
 
 def solution(mesh):

time: 74.3 us -> 72.3 us (0.973)
  waiting for transfers between devices: 31.5 us -> 26.7 us
  starting transfers between devices: 24.8 us -> 26.7 us
  Pallas kernels: 15.4 us -> 16.3 us
    ppermute x21, waiting for transfers between devices: 31.5 us -> 26.7 us  [swapped(): lax.ppermute(x, axis, [(i, i ^ flip) for i in range(lax.axis_size(axis))])]
    ppermute x21, starting transfers between devices: 24.8 us -> 26.7 us  [swapped(): lax.ppermute(x, axis, [(i, i ^ flip) for i in range(lax.axis_size(axis))])]
    pallas_call x23 -> x24, Pallas kernels: 15.4 us -> 16.3 us  [call(): pl.pallas_call(body, out_shape=flat_outs, in_specs=[space(x) for x in fla...]
  transfers between devices with their start and end apart: 21 -> 21, of which waited for: 16 -> 14; matrix products, arithmetic and copies ran while one was open for 0% -> 0% of each run, Pallas kernels for 11% -> 15%
where the time goes in v13:
time: 72.3 us; the launch traced here: 72.1 us
  starting transfers between devices  26.7 us (37%)
  waiting for transfers between devices  26.7 us (37%)
  Pallas kernels  16.3 us (23%)
  local copies, waits for them, and re-layouts  1.6 us (2%)
  between operations  0.82 us (1%)
    ppermute x21, waiting for transfers between devices, swapped(): lax.ppermute(x, axis, [(i, i ^ flip) for i in range(lax.axis_size(axis))])  26.7 us
    ppermute x21, starting transfers between devices, swapped(): lax.ppermute(x, axis, [(i, i ^ flip) for i in range(lax.axis_size(axis))])  26.7 us
    pallas_call x24, Pallas kernels, call(): pl.pallas_call(body, out_shape=flat_outs, in_specs=[space(x) for x in fla...  16.3 us
    unnamed x14, local copies, waits for them, and re-layouts  1.6 us
  transfers between devices with their start and end apart: 21, of which 14 were waited for; matrix products, arithmetic and copies ran while one was open for 0% of the time, Pallas kernels for 15%

profile of v13, /device:TPU:0, one launch (start us, length us, event | category | flops | bytes accessed | tf_op | source)
XLA Modules:
  0.0 72.1 jit_solution(5475477465520257741)
XLA Ops:
  1.5 4.1 %collective-permute-start.1 = (bf16[256,128]{1,0:T(8,128)(2,1)S(1)}, bf16[256,128]{1,0:T(8,128)(2,1)S(1)}, u32[]{:S(2)}, u32[]{:S(2)}) collective-permute-start(bf16[256,128]{1,0:T(8,128)(2,1)S(1)} %shard_map.69.refs_1_), channel_id=1, source_target_pairs={{0,8},{4,12},{8,0},{12,4},{1,9},{5,13},{9,1},{13,5},{2,10},{6,14},... | collective-permute-start | bytes 196616 | tf_op jit(solution)/shard_map/ppermute | solution.py:397
  5.7 1.6 %collective-permute-start = (bf16[256,128]{1,0:T(8,128)(2,1)S(1)}, bf16[256,128]{1,0:T(8,128)(2,1)S(1)}, u32[]{:S(2)}, u32[]{:S(2)}) collective-permute-start(bf16[256,128]{1,0:T(8,128)(2,1)S(1)} %shard_map.69.refs_1_), channel_id=1, source_target_pairs={{0,4},{4,0},{8,12},{12,8},{1,5},{5,1},{9,13},{13,9},{2,6},{6,2},{1... | collective-permute-start | bytes 196616 | tf_op jit(solution)/shard_map/ppermute | solution.py:397
  8.7 1.4 %collective-permute-start.2 = (bf16[256,128]{1,0:T(8,128)(2,1)S(1)}, bf16[256,128]{1,0:T(8,128)(2,1)S(1)}, u32[]{:S(2)}, u32[]{:S(2)}) collective-permute-start(bf16[256,128]{1,0:T(8,128)(2,1)S(1)} %collective-permute-done.1.refs_3_.refs_2_), channel_id=1, source_target_pairs={{0,4},{4,0},{8,12},{12,8},{1,5},{5,1},{9,13},{13,9},{2,6},{6,2},{1... | collective-permute-start | bytes 196616 | tf_op jit(solution)/shard_map/ppermute | solution.py:397
  10.1 2.0 %shard_map.68 = (s32[2,64]{1,0:T(2,128)S(1)}, bf16[64,128,128]{2,1,0:T(8,128)(2,1)S(1)}) custom-call(s32[64]{0:T(128)S(1)} %copy-done.5, s32[64]{0:T(128)S(1)} %copy-done.6, bf16[64,128,128]{2,1,0:T(8,128)(2,1)S(1)} %copy-done), custom_call_target="tpu_custom_call" | custom-call | flops 2000000000 | bytes 8000000 | tf_op jit(solution)/shard_map/pallas_call | solution.py:51
  13.0 1.3 %shard_map.71 = (f32[576,128]{1,0:T(8,128)S(1)}, f32[576,128]{1,0:T(8,128)S(1)}) custom-call(s32[2,64]{1,0:T(2,128)S(1)} %get-tuple-element.33.refs_0_, bf16[256,128]{1,0:T(8,128)(2,1)S(1)} %shard_map.69.refs_1_, bf16[256,128]{1,0:T(8,128)(2,1)S(1)} %collective-permute-done.refs_2_, bf16[256,128]{1,0:T(8,128)(2,1)S(1)} %collective-permute-done.1.refs_3_.refs_2_, ...), custom_call_target="tpu_custom_call" | custom-call | tf_op jit(solution)/shard_map/pallas_call | solution.py:51
  14.4 1.6 %collective-permute-done.3.refs_1_ = f32[576,128]{1,0:T(8,128)S(1)} collective-permute-done((f32[576,128]{1,0:T(8,128)S(1)}, f32[576,128]{1,0:T(8,128)S(1)}, u32[]{:S(2)}, u32[]{:S(2)}) %collective-permute-start.3) | collective-permute-done | bytes 294944 | tf_op jit(solution)/shard_map/ppermute | solution.py:397
  16.0 1.9 %collective-permute-start.4 = (bf16[576,128]{1,0:T(8,128)(2,1)S(1)}, bf16[576,128]{1,0:T(8,128)(2,1)S(1)}, u32[]{:S(2)}, u32[]{:S(2)}) collective-permute-start(bf16[576,128]{1,0:T(8,128)(2,1)S(1)} %shard_map.72.refs_2_.refs_0_), channel_id=1, source_target_pairs={{0,2},{1,3},{2,0},{3,1},{4,6},{5,7},{6,4},{7,5},{8,10},{9,11},{10,... | collective-permute-start | bytes 442376 | tf_op jit(solution)/shard_map/ppermute | solution.py:397
  17.9 2.4 %collective-permute-start.5 = (bf16[272,128]{1,0:T(8,128)(2,1)S(1)}, bf16[272,128]{1,0:T(8,128)(2,1)S(1)}, u32[]{:S(2)}, u32[]{:S(2)}) collective-permute-start(bf16[272,128]{1,0:T(8,128)(2,1)S(1)} %shard_map.73), channel_id=1, source_target_pairs={{0,8},{4,12},{8,0},{12,4},{1,9},{5,13},{9,1},{13,5},{2,10},{6,14},... | collective-permute-start | bytes 208904 | tf_op jit(solution)/shard_map/ppermute | solution.py:397
  20.3 4.3 %collective-permute-done.5.refs_2_.refs_3_ = bf16[272,128]{1,0:T(8,128)(2,1)S(1)} collective-permute-done((bf16[272,128]{1,0:T(8,128)(2,1)S(1)}, bf16[272,128]{1,0:T(8,128)(2,1)S(1)}, u32[]{:S(2)}, u32[]{:S(2)}) %collective-permute-start.5) | collective-permute-done | bytes 69664 | tf_op jit(solution)/shard_map/ppermute | solution.py:397
  24.7 1.4 %collective-permute-done.6.refs_2_ = bf16[576,128]{1,0:T(8,128)(2,1)S(1)} collective-permute-done((bf16[576,128]{1,0:T(8,128)(2,1)S(1)}, bf16[576,128]{1,0:T(8,128)(2,1)S(1)}, u32[]{:S(2)}, u32[]{:S(2)}) %collective-permute-start.6) | collective-permute-done | bytes 147488 | tf_op jit(solution)/shard_map/ppermute | solution.py:397
  26.0 1.5 %shard_map.75 = (bf16[336,128]{1,0:T(8,128)(2,1)S(1)}, bf16[256,128]{1,0:T(8,128)(2,1)S(1)}, f32[256,128]{1,0:T(8,128)S(1)}, f32[256,128]{1,0:T(8,128)S(1)}) custom-call(s32[2,64]{1,0:T(2,128)S(1)} %get-tuple-element.33.refs_0_, bf16[576,128]{1,0:T(8,128)(2,1)S(1)} %shard_map.74.refs_1_, bf16[576,128]{1,0:T(8,128)(2,1)S(1)} %collective-permute-done.6.refs_2_, ...), custom_call_target="tpu_custom_call" | custom-call | tf_op jit(solution)/shard_map/pallas_call | solution.py:51
  27.7 1.9 %collective-permute-start.7 = (bf16[256,128]{1,0:T(8,128)(2,1)S(1)}, bf16[256,128]{1,0:T(8,128)(2,1)S(1)}, u32[]{:S(2)}, u32[]{:S(2)}) collective-permute-start(bf16[256,128]{1,0:T(8,128)(2,1)S(1)} %get-tuple-element.38), channel_id=1, source_target_pairs={{0,4},{4,0},{8,12},{12,8},{1,5},{5,1},{9,13},{13,9},{2,6},{6,2},{1... | collective-permute-start | bytes 196616 | tf_op jit(solution)/shard_map/ppermute | solution.py:397
  29.6 3.3 %collective-permute-done.8.refs_1_ = bf16[336,128]{1,0:T(8,128)(2,1)S(1)} collective-permute-done((bf16[336,128]{1,0:T(8,128)(2,1)S(1)}, bf16[336,128]{1,0:T(8,128)(2,1)S(1)}, u32[]{:S(2)}, u32[]{:S(2)}) %collective-permute-start.8) | collective-permute-done | bytes 86048 | tf_op jit(solution)/shard_map/ppermute | solution.py:397
  32.9 1.5 %collective-permute-start.9 = (bf16[336,128]{1,0:T(8,128)(2,1)S(1)}, bf16[336,128]{1,0:T(8,128)(2,1)S(1)}, u32[]{:S(2)}, u32[]{:S(2)}) collective-permute-start(bf16[336,128]{1,0:T(8,128)(2,1)S(1)} %get-tuple-element.42.refs_0_), channel_id=1, source_target_pairs={{0,8},{4,12},{8,0},{12,4},{1,9},{5,13},{9,1},{13,5},{2,10},{6,14},... | collective-permute-start | bytes 258056 | tf_op jit(solution)/shard_map/ppermute | solution.py:397
  34.4 1.5 %collective-permute-start.11 = (bf16[256,128]{1,0:T(8,128)(2,1)S(1)}, bf16[256,128]{1,0:T(8,128)(2,1)S(1)}, u32[]{:S(2)}, u32[]{:S(2)}) collective-permute-start(bf16[256,128]{1,0:T(8,128)(2,1)S(1)} %get-tuple-element.46), channel_id=1, source_target_pairs={{0,8},{4,12},{8,0},{12,4},{1,9},{5,13},{9,1},{13,5},{2,10},{6,14},... | collective-permute-start | bytes 196616 | tf_op jit(solution)/shard_map/ppermute | solution.py:397
  36.0 4.2 %collective-permute-done.9.refs_1_ = bf16[336,128]{1,0:T(8,128)(2,1)S(1)} collective-permute-done((bf16[336,128]{1,0:T(8,128)(2,1)S(1)}, bf16[336,128]{1,0:T(8,128)(2,1)S(1)}, u32[]{:S(2)}, u32[]{:S(2)}) %collective-permute-start.9) | collective-permute-done | bytes 86048 | tf_op jit(solution)/shard_map/ppermute | solution.py:397
  41.9 1.0 %collective-permute-start.12 = (bf16[256,128]{1,0:T(8,128)(2,1)S(1)}, bf16[256,128]{1,0:T(8,128)(2,1)S(1)}, u32[]{:S(2)}, u32[]{:S(2)}) collective-permute-start(bf16[256,128]{1,0:T(8,128)(2,1)S(1)} %shard_map.79.refs_3_), channel_id=1, source_target_pairs={{0,4},{4,0},{8,12},{12,8},{1,5},{5,1},{9,13},{13,9},{2,6},{6,2},{1... | collective-permute-start | bytes 196616 | tf_op jit(solution)/shard_map/ppermute | solution.py:397
  43.3 1.5 %collective-permute-done.10.refs_2_ = bf16[256,128]{1,0:T(8,128)(2,1)S(1)} collective-permute-done((bf16[256,128]{1,0:T(8,128)(2,1)S(1)}, bf16[256,128]{1,0:T(8,128)(2,1)S(1)}, u32[]{:S(2)}, u32[]{:S(2)}) %collective-permute-start.10) | collective-permute-done | bytes 65568 | tf_op jit(solution)/shard_map/ppermute | solution.py:397
  44.8 1.4 %collective-permute-done.12.refs_4_ = bf16[256,128]{1,0:T(8,128)(2,1)S(1)} collective-permute-done((bf16[256,128]{1,0:T(8,128)(2,1)S(1)}, bf16[256,128]{1,0:T(8,128)(2,1)S(1)}, u32[]{:S(2)}, u32[]{:S(2)}) %collective-permute-start.12) | collective-permute-done | bytes 65568 | tf_op jit(solution)/shard_map/ppermute | solution.py:397
  46.2 1.4 %shard_map.81 = (f32[608,128]{1,0:T(8,128)S(1)}, f32[608,128]{1,0:T(8,128)S(1)}) custom-call(s32[2,64]{1,0:T(2,128)S(1)} %get-tuple-element.33.refs_0_, bf16[256,128]{1,0:T(8,128)(2,1)S(1)} %get-tuple-element.45.refs_1_, bf16[256,128]{1,0:T(8,128)(2,1)S(1)} %collective-permute-done.10.refs_2_, bf16[256,128]{1,0:T(8,128)(2,1)S(1)} %shard_map.79.refs_3_, ...), custom_call_target="tpu_custom_call" | custom-call | tf_op jit(solution)/shard_map/pallas_call | solution.py:51
  47.7 1.6 %collective-permute-done.13.refs_1_ = f32[608,128]{1,0:T(8,128)S(1)} collective-permute-done((f32[608,128]{1,0:T(8,128)S(1)}, f32[608,128]{1,0:T(8,128)S(1)}, u32[]{:S(2)}, u32[]{:S(2)}) %collective-permute-start.13) | collective-permute-done | bytes 311328 | tf_op jit(solution)/shard_map/ppermute | solution.py:397
  49.9 1.7 %shard_map.83.refs_2_.refs_3_ = f32[64,64]{1,0:T(8,128)S(1)} custom-call(f32[64,128]{1,0:T(8,128)S(1)} %get-tuple-element.53.refs_0_.refs_2_), custom_call_target="tpu_custom_call" | custom-call | flops 2000000000 | bytes 8000000 | tf_op jit(solution)/shard_map/pallas_call | solution.py:51
  51.6 3.6 %collective-permute-done.14.refs_1_ = bf16[576,128]{1,0:T(8,128)(2,1)S(1)} collective-permute-done((bf16[576,128]{1,0:T(8,128)(2,1)S(1)}, bf16[576,128]{1,0:T(8,128)(2,1)S(1)}, u32[]{:S(2)}, u32[]{:S(2)}) %collective-permute-start.14) | collective-permute-done | bytes 147488 | tf_op jit(solution)/shard_map/ppermute | solution.py:397
  55.4 1.4 %collective-permute-done.15.refs_2_.refs_1_ = bf16[576,128]{1,0:T(8,128)(2,1)S(1)} collective-permute-done((bf16[576,128]{1,0:T(8,128)(2,1)S(1)}, bf16[576,128]{1,0:T(8,128)(2,1)S(1)}, u32[]{:S(2)}, u32[]{:S(2)}) %collective-permute-start.15) | collective-permute-done | bytes 147488 | tf_op jit(solution)/shard_map/ppermute | solution.py:397
  58.0 1.3 %shard_map.85 = (bf16[256,128]{1,0:T(8,128)(2,1)S(1)}, bf16[256,128]{1,0:T(8,128)(2,1)S(1)}, f32[256,128]{1,0:T(8,128)S(1)}, f32[256,128]{1,0:T(8,128)S(1)}, f32[64,64]{1,0:T(8,128)S(1)}) custom-call(s32[2,64]{1,0:T(2,128)S(1)} %get-tuple-element.33.refs_0_, bf16[576,128]{1,0:T(8,128)(2,1)S(1)} %shard_map.84.refs_1_.refs_0_, ...), custom_call_target="tpu_custom_call" | custom-call | tf_op jit(solution)/shard_map/pallas_call | solution.py:51
  59.3 1.2 %collective-permute-start.19 = (bf16[256,128]{1,0:T(8,128)(2,1)S(1)}, bf16[256,128]{1,0:T(8,128)(2,1)S(1)}, u32[]{:S(2)}, u32[]{:S(2)}) collective-permute-start(bf16[256,128]{1,0:T(8,128)(2,1)S(1)} %get-tuple-element.61.refs_0_), channel_id=1, source_target_pairs={{0,4},{4,0},{8,12},{12,8},{1,5},{5,1},{9,13},{13,9},{2,6},{6,2},{1... | collective-permute-start | bytes 196616 | tf_op jit(solution)/shard_map/ppermute | solution.py:397
  61.0 2.5 %collective-permute-start.18 = (bf16[64,128]{1,0:T(8,128)(2,1)S(1)}, bf16[64,128]{1,0:T(8,128)(2,1)S(1)}, u32[]{:S(2)}, u32[]{:S(2)}) collective-permute-start(bf16[64,128]{1,0:T(8,128)(2,1)S(1)} %get-tuple-element.58), channel_id=1, source_target_pairs={{0,8},{4,12},{8,0},{12,4},{1,9},{5,13},{9,1},{13,5},{2,10},{6,14},... | collective-permute-start | bytes 49160 | tf_op jit(solution)/shard_map/ppermute | solution.py:397
  63.5 1.1 %collective-permute-start.16 = (bf16[256,128]{1,0:T(8,128)(2,1)S(1)}, bf16[256,128]{1,0:T(8,128)(2,1)S(1)}, u32[]{:S(2)}, u32[]{:S(2)}) collective-permute-start(bf16[256,128]{1,0:T(8,128)(2,1)S(1)} %get-tuple-element.55), channel_id=1, source_target_pairs={{0,4},{4,0},{8,12},{12,8},{1,5},{5,1},{9,13},{13,9},{2,6},{6,2},{1... | collective-permute-start | bytes 196616 | tf_op jit(solution)/shard_map/ppermute | solution.py:397
  64.6 2.4 %collective-permute-start.20 = (bf16[256,128]{1,0:T(8,128)(2,1)S(1)}, bf16[256,128]{1,0:T(8,128)(2,1)S(1)}, u32[]{:S(2)}, u32[]{:S(2)}) collective-permute-start(bf16[256,128]{1,0:T(8,128)(2,1)S(1)} %shard_map.90), channel_id=1, source_target_pairs={{0,8},{4,12},{8,0},{12,4},{1,9},{5,13},{9,1},{13,5},{2,10},{6,14},... | collective-permute-start | bytes 196616 | tf_op jit(solution)/shard_map/ppermute | solution.py:397
  67.0 2.9 %shard_map.88.refs_6_.refs_2_ = f32[128,64]{1,0:T(8,128)S(1)} custom-call(f32[64,64]{1,0:T(8,128)S(1)} %get-tuple-element.57.refs_0_, bf16[64,128]{1,0:T(8,128)(2,1)S(1)} %collective-permute-done.18.refs_1_, f32[64,128]{1,0:T(8,128)S(1)} %get-tuple-element.53.refs_0_.refs_2_, f32[64,64]{1,0:T(8,128)S(1)} %shard_map.83.refs_2_.refs_3_, ...), custom_call_target="tpu_custom_call" | custom-call | flops 2000000000 | bytes 8000000 | tf_op jit(solution)/shard_map/pallas_call | solution.py:51
  69.9 1.3 %shard_map.89 = (f32[64,512]{1,0:T(8,128)}, f32[64,512]{1,0:T(8,128)S(1)}) custom-call(f32[256,128]{1,0:T(8,128)S(1)} %get-tuple-element.54.refs_0_, bf16[256,128]{1,0:T(8,128)(2,1)S(1)} %collective-permute-done.16.refs_1_, f32[64,512]{1,0:T(8,128)S(1)} %copy-done.2, f32[64,512]{1,0:T(8,128)S(1)} %get-tuple-element.56.refs_3_, ...), custom_call_target="tpu_custom_call" | custom-call | flops 1 | bytes 1 | tf_op jit(solution)/shard_map/pallas_call | solution.py:51
  71.2 1.0 %shard_map.91 = f32[64,512]{1,0:T(8,128)} custom-call(bf16[256,128]{1,0:T(8,128)(2,1)S(1)} %collective-permute-done.20.refs_0_, f32[64,512]{1,0:T(8,128)S(1)} %get-tuple-element.63.refs_1_, f32[128,64]{1,0:T(8,128)S(1)} %shard_map.88.refs_6_.refs_2_), custom_call_target="tpu_custom_call" | custom-call | tf_op jit(solution)/shard_map/pallas_call | solution.py:51
  (48 shorter events, 8.4 us)
Async XLA Ops:
  0.6 0.9 %copy-start.1 = (f32[64,512]{1,0:T(8,128)S(1)}, f32[64,512]{1,0:T(8,128)}, u32[]{:S(2)}) copy-start(f32[64,512]{1,0:T(8,128)} %refs_2_.3) | copy-start | bytes 393220
  1.5 7.2 %collective-permute-start.1 = (bf16[256,128]{1,0:T(8,128)(2,1)S(1)}, bf16[256,128]{1,0:T(8,128)(2,1)S(1)}, u32[]{:S(2)}, u32[]{:S(2)}) collective-permute-start(bf16[256,128]{1,0:T(8,128)(2,1)S(1)} %shard_map.69.refs_1_), channel_id=1, source_target_pairs={{0,8},{4,12},{8,0},{12,4},{1,9},{5,13},{9,1},{13,5},{2,10},{6,14},... | collective-permute-start | bytes 196616 | tf_op jit(solution)/shard_map/ppermute | solution.py:397
  5.7 6.5 %collective-permute-start = (bf16[256,128]{1,0:T(8,128)(2,1)S(1)}, bf16[256,128]{1,0:T(8,128)(2,1)S(1)}, u32[]{:S(2)}, u32[]{:S(2)}) collective-permute-start(bf16[256,128]{1,0:T(8,128)(2,1)S(1)} %shard_map.69.refs_1_), channel_id=1, source_target_pairs={{0,4},{4,0},{8,12},{12,8},{1,5},{5,1},{9,13},{13,9},{2,6},{6,2},{1... | collective-permute-start | bytes 196616 | tf_op jit(solution)/shard_map/ppermute | solution.py:397
  7.2 0.7 copy-start.3
  7.9 2.2 %copy-start = (bf16[64,128,128]{2,1,0:T(8,128)(2,1)S(1)}, bf16[64,128,128]{2,1,0:T(8,128)(2,1)}, u32[]{:S(2)}) copy-start(bf16[64,128,128]{2,1,0:T(8,128)(2,1)} %refs_3_.3) | copy-start | bytes 6291460
  7.9 2.2 %copy-start.5 = (s32[64]{0:T(128)S(1)}, s32[64]{0:T(128)}, u32[]{:S(2)}) copy-start(s32[64]{0:T(128)} %refs_0_.4) | copy-start | bytes 772
  7.9 2.2 %copy-start.6 = (s32[64]{0:T(128)S(1)}, s32[64]{0:T(128)}, u32[]{:S(2)}) copy-start(s32[64]{0:T(128)} %refs_1_.1) | copy-start | bytes 772
  8.7 4.3 %collective-permute-start.2 = (bf16[256,128]{1,0:T(8,128)(2,1)S(1)}, bf16[256,128]{1,0:T(8,128)(2,1)S(1)}, u32[]{:S(2)}, u32[]{:S(2)}) collective-permute-start(bf16[256,128]{1,0:T(8,128)(2,1)S(1)} %collective-permute-done.1.refs_3_.refs_2_), channel_id=1, source_target_pairs={{0,4},{4,0},{8,12},{12,8},{1,5},{5,1},{9,13},{13,9},{2,6},{6,2},{1... | collective-permute-start | bytes 196616 | tf_op jit(solution)/shard_map/ppermute | solution.py:397
  12.1 5.8 %copy-start.2 = (f32[64,512]{1,0:T(8,128)S(1)}, f32[64,512]{1,0:T(8,128)}, u32[]{:S(2)}) copy-start(f32[64,512]{1,0:T(8,128)} %refs_2_.3) | copy-start | bytes 393220
  12.1 5.8 %copy-start.4 = (f32[512]{0:T(512)S(1)}, f32[512]{0:T(512)}, u32[]{:S(2)}) copy-start(f32[512]{0:T(512)} %param.6) | copy-start | bytes 6148
  14.3 1.6 %collective-permute-start.3 = (f32[576,128]{1,0:T(8,128)S(1)}, f32[576,128]{1,0:T(8,128)S(1)}, u32[]{:S(2)}, u32[]{:S(2)}) collective-permute-start(f32[576,128]{1,0:T(8,128)S(1)} %get-tuple-element.36), channel_id=1, source_target_pairs={{0,1},{1,0},{2,3},{3,2},{4,5},{5,4},{6,7},{7,6},{8,9},{9,8},{10,11... | collective-permute-start | bytes 884744 | tf_op jit(solution)/shard_map/ppermute | solution.py:397
  16.0 8.6 %collective-permute-start.4 = (bf16[576,128]{1,0:T(8,128)(2,1)S(1)}, bf16[576,128]{1,0:T(8,128)(2,1)S(1)}, u32[]{:S(2)}, u32[]{:S(2)}) collective-permute-start(bf16[576,128]{1,0:T(8,128)(2,1)S(1)} %shard_map.72.refs_2_.refs_0_), channel_id=1, source_target_pairs={{0,2},{1,3},{2,0},{3,1},{4,6},{5,7},{6,4},{7,5},{8,10},{9,11},{10,... | collective-permute-start | bytes 442376 | tf_op jit(solution)/shard_map/ppermute | solution.py:397
  17.9 6.6 %collective-permute-start.5 = (bf16[272,128]{1,0:T(8,128)(2,1)S(1)}, bf16[272,128]{1,0:T(8,128)(2,1)S(1)}, u32[]{:S(2)}, u32[]{:S(2)}) collective-permute-start(bf16[272,128]{1,0:T(8,128)(2,1)S(1)} %shard_map.73), channel_id=1, source_target_pairs={{0,8},{4,12},{8,0},{12,4},{1,9},{5,13},{9,1},{13,5},{2,10},{6,14},... | collective-permute-start | bytes 208904 | tf_op jit(solution)/shard_map/ppermute | solution.py:397
  24.6 1.4 %collective-permute-start.6 = (bf16[576,128]{1,0:T(8,128)(2,1)S(1)}, bf16[576,128]{1,0:T(8,128)(2,1)S(1)}, u32[]{:S(2)}, u32[]{:S(2)}) collective-permute-start(bf16[576,128]{1,0:T(8,128)(2,1)S(1)} %shard_map.74.refs_1_), channel_id=1, source_target_pairs={{0,1},{1,0},{2,3},{3,2},{4,5},{5,4},{6,7},{7,6},{8,9},{9,8},{10,11... | collective-permute-start | bytes 442376 | tf_op jit(solution)/shard_map/ppermute | solution.py:397
  27.5 5.3 %collective-permute-start.8 = (bf16[336,128]{1,0:T(8,128)(2,1)S(1)}, bf16[336,128]{1,0:T(8,128)(2,1)S(1)}, u32[]{:S(2)}, u32[]{:S(2)}) collective-permute-start(bf16[336,128]{1,0:T(8,128)(2,1)S(1)} %get-tuple-element.40.refs_0_), channel_id=1, source_target_pairs={{0,4},{4,0},{8,12},{12,8},{1,5},{5,1},{9,13},{13,9},{2,6},{6,2},{1... | collective-permute-start | bytes 258056 | tf_op jit(solution)/shard_map/ppermute | solution.py:397
  27.7 6.7 %collective-permute-start.7 = (bf16[256,128]{1,0:T(8,128)(2,1)S(1)}, bf16[256,128]{1,0:T(8,128)(2,1)S(1)}, u32[]{:S(2)}, u32[]{:S(2)}) collective-permute-start(bf16[256,128]{1,0:T(8,128)(2,1)S(1)} %get-tuple-element.38), channel_id=1, source_target_pairs={{0,4},{4,0},{8,12},{12,8},{1,5},{5,1},{9,13},{13,9},{2,6},{6,2},{1... | collective-permute-start | bytes 196616 | tf_op jit(solution)/shard_map/ppermute | solution.py:397
  32.9 7.3 %collective-permute-start.9 = (bf16[336,128]{1,0:T(8,128)(2,1)S(1)}, bf16[336,128]{1,0:T(8,128)(2,1)S(1)}, u32[]{:S(2)}, u32[]{:S(2)}) collective-permute-start(bf16[336,128]{1,0:T(8,128)(2,1)S(1)} %get-tuple-element.42.refs_0_), channel_id=1, source_target_pairs={{0,8},{4,12},{8,0},{12,4},{1,9},{5,13},{9,1},{13,5},{2,10},{6,14},... | collective-permute-start | bytes 258056 | tf_op jit(solution)/shard_map/ppermute | solution.py:397
  34.4 7.2 %collective-permute-start.11 = (bf16[256,128]{1,0:T(8,128)(2,1)S(1)}, bf16[256,128]{1,0:T(8,128)(2,1)S(1)}, u32[]{:S(2)}, u32[]{:S(2)}) collective-permute-start(bf16[256,128]{1,0:T(8,128)(2,1)S(1)} %get-tuple-element.46), channel_id=1, source_target_pairs={{0,8},{4,12},{8,0},{12,4},{1,9},{5,13},{9,1},{13,5},{2,10},{6,14},... | collective-permute-start | bytes 196616 | tf_op jit(solution)/shard_map/ppermute | solution.py:397
  40.5 4.3 %collective-permute-start.10 = (bf16[256,128]{1,0:T(8,128)(2,1)S(1)}, bf16[256,128]{1,0:T(8,128)(2,1)S(1)}, u32[]{:S(2)}, u32[]{:S(2)}) collective-permute-start(bf16[256,128]{1,0:T(8,128)(2,1)S(1)} %get-tuple-element.45.refs_1_), channel_id=1, source_target_pairs={{0,4},{4,0},{8,12},{12,8},{1,5},{5,1},{9,13},{13,9},{2,6},{6,2},{1... | collective-permute-start | bytes 196616 | tf_op jit(solution)/shard_map/ppermute | solution.py:397
  41.9 4.3 %collective-permute-start.12 = (bf16[256,128]{1,0:T(8,128)(2,1)S(1)}, bf16[256,128]{1,0:T(8,128)(2,1)S(1)}, u32[]{:S(2)}, u32[]{:S(2)}) collective-permute-start(bf16[256,128]{1,0:T(8,128)(2,1)S(1)} %shard_map.79.refs_3_), channel_id=1, source_target_pairs={{0,4},{4,0},{8,12},{12,8},{1,5},{5,1},{9,13},{13,9},{2,6},{6,2},{1... | collective-permute-start | bytes 196616 | tf_op jit(solution)/shard_map/ppermute | solution.py:397
  47.6 1.7 %collective-permute-start.13 = (f32[608,128]{1,0:T(8,128)S(1)}, f32[608,128]{1,0:T(8,128)S(1)}, u32[]{:S(2)}, u32[]{:S(2)}) collective-permute-start(f32[608,128]{1,0:T(8,128)S(1)} %get-tuple-element.51), channel_id=1, source_target_pairs={{0,1},{1,0},{2,3},{3,2},{4,5},{5,4},{6,7},{7,6},{8,9},{9,8},{10,11... | collective-permute-start | bytes 933896 | tf_op jit(solution)/shard_map/ppermute | solution.py:397
  49.3 6.0 %collective-permute-start.14 = (bf16[576,128]{1,0:T(8,128)(2,1)S(1)}, bf16[576,128]{1,0:T(8,128)(2,1)S(1)}, u32[]{:S(2)}, u32[]{:S(2)}) collective-permute-start(bf16[576,128]{1,0:T(8,128)(2,1)S(1)} %get-tuple-element.52.refs_0_), channel_id=1, source_target_pairs={{0,2},{1,3},{2,0},{3,1},{4,6},{5,7},{6,4},{7,5},{8,10},{9,11},{10,... | collective-permute-start | bytes 442376 | tf_op jit(solution)/shard_map/ppermute | solution.py:397
  55.3 1.4 %collective-permute-start.15 = (bf16[576,128]{1,0:T(8,128)(2,1)S(1)}, bf16[576,128]{1,0:T(8,128)(2,1)S(1)}, u32[]{:S(2)}, u32[]{:S(2)}) collective-permute-start(bf16[576,128]{1,0:T(8,128)(2,1)S(1)} %shard_map.84.refs_1_.refs_0_), channel_id=1, source_target_pairs={{0,1},{1,0},{2,3},{3,2},{4,5},{5,4},{6,7},{7,6},{8,9},{9,8},{10,11... | collective-permute-start | bytes 442376 | tf_op jit(solution)/shard_map/ppermute | solution.py:397
  57.1 3.8 %collective-permute-start.17 = (bf16[64,128]{1,0:T(8,128)(2,1)S(1)}, bf16[64,128]{1,0:T(8,128)(2,1)S(1)}, u32[]{:S(2)}, u32[]{:S(2)}) collective-permute-start(bf16[64,128]{1,0:T(8,128)(2,1)S(1)} %shard_map.86.refs_0_), channel_id=1, source_target_pairs={{0,4},{4,0},{8,12},{12,8},{1,5},{5,1},{9,13},{13,9},{2,6},{6,2},{1... | collective-permute-start | bytes 49160 | tf_op jit(solution)/shard_map/ppermute | solution.py:397
  59.3 5.3 %collective-permute-start.19 = (bf16[256,128]{1,0:T(8,128)(2,1)S(1)}, bf16[256,128]{1,0:T(8,128)(2,1)S(1)}, u32[]{:S(2)}, u32[]{:S(2)}) collective-permute-start(bf16[256,128]{1,0:T(8,128)(2,1)S(1)} %get-tuple-element.61.refs_0_), channel_id=1, source_target_pairs={{0,4},{4,0},{8,12},{12,8},{1,5},{5,1},{9,13},{13,9},{2,6},{6,2},{1... | collective-permute-start | bytes 196616 | tf_op jit(solution)/shard_map/ppermute | solution.py:397
  61.0 6.0 %collective-permute-start.18 = (bf16[64,128]{1,0:T(8,128)(2,1)S(1)}, bf16[64,128]{1,0:T(8,128)(2,1)S(1)}, u32[]{:S(2)}, u32[]{:S(2)}) collective-permute-start(bf16[64,128]{1,0:T(8,128)(2,1)S(1)} %get-tuple-element.58), channel_id=1, source_target_pairs={{0,8},{4,12},{8,0},{12,4},{1,9},{5,13},{9,1},{13,5},{2,10},{6,14},... | collective-permute-start | bytes 49160 | tf_op jit(solution)/shard_map/ppermute | solution.py:397
  63.5 6.4 %collective-permute-start.16 = (bf16[256,128]{1,0:T(8,128)(2,1)S(1)}, bf16[256,128]{1,0:T(8,128)(2,1)S(1)}, u32[]{:S(2)}, u32[]{:S(2)}) collective-permute-start(bf16[256,128]{1,0:T(8,128)(2,1)S(1)} %get-tuple-element.55), channel_id=1, source_target_pairs={{0,4},{4,0},{8,12},{12,8},{1,5},{5,1},{9,13},{13,9},{2,6},{6,2},{1... | collective-permute-start | bytes 196616 | tf_op jit(solution)/shard_map/ppermute | solution.py:397
  64.6 6.6 %collective-permute-start.20 = (bf16[256,128]{1,0:T(8,128)(2,1)S(1)}, bf16[256,128]{1,0:T(8,128)(2,1)S(1)}, u32[]{:S(2)}, u32[]{:S(2)}) collective-permute-start(bf16[256,128]{1,0:T(8,128)(2,1)S(1)} %shard_map.90), channel_id=1, source_target_pairs={{0,8},{4,12},{8,0},{12,4},{1,9},{5,13},{9,1},{13,5},{2,10},{6,14},... | collective-permute-start | bytes 196616 | tf_op jit(solution)/shard_map/ppermute | solution.py:397

commit v14 on v13

--- a/solution.py
+++ b/solution.py
@@ -373,24 +373,21 @@
     out_ref[n:, :] = gamma
 
 
-def early_kernel(keep, near, v_ref, image_ref, next_ref, prior, coeffs_ref, x_ref, base_ref):
+def iterate_kernel(v_ref, next_ref, coeffs_ref, x_ref):
+    coeffs = coeffs_ref[...]
+    for j in range(v_ref.shape[1] // BLOCK):
+        both = jnp.concatenate([v_ref[:, lanes(j)], next_ref[:, lanes(j)]], axis=0)
+        x_ref[:, lanes(j)] = tn_dot(coeffs, both)
+
+
+def residual_kernel(keep, near, far, v_ref, image_ref, next_ref, prior, coeffs_ref, r_ref):
     n = v_ref.shape[0]
     coeffs = coeffs_ref[...]
     for j in range(keep.shape[0] // n):
-        value = v_ref[:, lanes(j)]
-        following = next_ref[:, lanes(j)]
-        second_image = own_sum(keep, (near,), j, n) + prior[:, lanes(j)] * following
-        x_ref[:, lanes(j)] = tn_dot(coeffs, jnp.concatenate([value, following], axis=0))
-        base_ref[:, lanes(j)] = value - tn_dot(
+        second_image = own_sum(keep, (near, *far), j, n) + prior[:, lanes(j)] * next_ref[:, lanes(j)]
+        r_ref[:, lanes(j)] = v_ref[:, lanes(j)] - tn_dot(
             coeffs, jnp.concatenate([image_ref[:, lanes(j)], second_image], axis=0)
         )
-
-
-def final_kernel(far, base_ref, coeffs_ref, r_ref):
-    n = base_ref.shape[0]
-    gamma = coeffs_ref[n:, :]
-    for j in range(base_ref.shape[1] // BLOCK):
-        r_ref[:, lanes(j)] = base_ref[:, lanes(j)] - tn_dot(gamma, sum_rows(far, rows(j, n)))
 
 
 def swapped(x, axis, flip):
@@ -552,15 +549,11 @@
         (gram, second, first, inverse, norm, diagonal),
         cost=aside,
     )
-    keep, near, far = parts
-    x, base = call(
-        early_kernel,
-        (own, own),
-        (keep, near, right_side, image, following, prior, coeffs),
-        cost=hidden,
-    )
-    (residual,) = call(final_kernel, (own,), (far, base, coeffs))
-    return x, residual
+    (iterate,) = call(iterate_kernel, (own,), (right_side, following, coeffs), cost=hidden)
+    (residual,) = call(
+        residual_kernel, (own,), (*parts, right_side, image, following, prior, coeffs)
+    )
+    return iterate, residual
 
 
 def solution(mesh):

time: 72.3 us -> 72.2 us (level)
  no operation moved by 1% of the time
where the time goes in v14:
time: 72.2 us; the launch traced here: 72 us
  starting transfers between devices  26.7 us (37%)
  waiting for transfers between devices  26.7 us (37%)
  Pallas kernels  16.2 us (22%)
  local copies, waits for them, and re-layouts  1.6 us (2%)
  between operations  0.82 us (1%)
    ppermute x21, waiting for transfers between devices, swapped(): lax.ppermute(x, axis, [(i, i ^ flip) for i in range(lax.axis_size(axis))])  26.7 us
    ppermute x21, starting transfers between devices, swapped(): lax.ppermute(x, axis, [(i, i ^ flip) for i in range(lax.axis_size(axis))])  26.7 us
    pallas_call x24, Pallas kernels, call(): pl.pallas_call(body, out_shape=flat_outs, in_specs=[space(x) for x in fla...  16.2 us
    unnamed x14, local copies, waits for them, and re-layouts  1.6 us
  transfers between devices with their start and end apart: 21, of which 14 were waited for; matrix products, arithmetic and copies ran while one was open for 0% of the time, Pallas kernels for 15%

profile of v14, /device:TPU:0, one launch (start us, length us, event | category | flops | bytes accessed | tf_op | source)
XLA Modules:
  0.0 72.0 jit_solution(3831243142675863975)
XLA Ops:
  1.5 4.1 %collective-permute-start.1 = (bf16[256,128]{1,0:T(8,128)(2,1)S(1)}, bf16[256,128]{1,0:T(8,128)(2,1)S(1)}, u32[]{:S(2)}, u32[]{:S(2)}) collective-permute-start(bf16[256,128]{1,0:T(8,128)(2,1)S(1)} %shard_map.69.refs_1_), channel_id=1, source_target_pairs={{0,8},{4,12},{8,0},{12,4},{1,9},{5,13},{9,1},{13,5},{2,10},{6,14},... | collective-permute-start | bytes 196616 | tf_op jit(solution)/shard_map/ppermute | solution.py:394
  5.7 1.6 %collective-permute-start = (bf16[256,128]{1,0:T(8,128)(2,1)S(1)}, bf16[256,128]{1,0:T(8,128)(2,1)S(1)}, u32[]{:S(2)}, u32[]{:S(2)}) collective-permute-start(bf16[256,128]{1,0:T(8,128)(2,1)S(1)} %shard_map.69.refs_1_), channel_id=1, source_target_pairs={{0,4},{4,0},{8,12},{12,8},{1,5},{5,1},{9,13},{13,9},{2,6},{6,2},{1... | collective-permute-start | bytes 196616 | tf_op jit(solution)/shard_map/ppermute | solution.py:394
  8.7 1.4 %collective-permute-start.2 = (bf16[256,128]{1,0:T(8,128)(2,1)S(1)}, bf16[256,128]{1,0:T(8,128)(2,1)S(1)}, u32[]{:S(2)}, u32[]{:S(2)}) collective-permute-start(bf16[256,128]{1,0:T(8,128)(2,1)S(1)} %collective-permute-done.1.refs_3_.refs_2_), channel_id=1, source_target_pairs={{0,4},{4,0},{8,12},{12,8},{1,5},{5,1},{9,13},{13,9},{2,6},{6,2},{1... | collective-permute-start | bytes 196616 | tf_op jit(solution)/shard_map/ppermute | solution.py:394
  10.1 2.0 %shard_map.68 = (s32[2,64]{1,0:T(2,128)S(1)}, bf16[64,128,128]{2,1,0:T(8,128)(2,1)S(1)}) custom-call(s32[64]{0:T(128)S(1)} %copy-done.5, s32[64]{0:T(128)S(1)} %copy-done.6, bf16[64,128,128]{2,1,0:T(8,128)(2,1)S(1)} %copy-done), custom_call_target="tpu_custom_call" | custom-call | flops 2000000000 | bytes 8000000 | tf_op jit(solution)/shard_map/pallas_call | solution.py:51
  13.0 1.3 %shard_map.71 = (f32[576,128]{1,0:T(8,128)S(1)}, f32[576,128]{1,0:T(8,128)S(1)}) custom-call(s32[2,64]{1,0:T(2,128)S(1)} %get-tuple-element.31.refs_0_, bf16[256,128]{1,0:T(8,128)(2,1)S(1)} %shard_map.69.refs_1_, bf16[256,128]{1,0:T(8,128)(2,1)S(1)} %collective-permute-done.refs_2_, bf16[256,128]{1,0:T(8,128)(2,1)S(1)} %collective-permute-done.1.refs_3_.refs_2_, ...), custom_call_target="tpu_custom_call" | custom-call | tf_op jit(solution)/shard_map/pallas_call | solution.py:51
  14.4 1.6 %collective-permute-done.3.refs_1_ = f32[576,128]{1,0:T(8,128)S(1)} collective-permute-done((f32[576,128]{1,0:T(8,128)S(1)}, f32[576,128]{1,0:T(8,128)S(1)}, u32[]{:S(2)}, u32[]{:S(2)}) %collective-permute-start.3) | collective-permute-done | bytes 294944 | tf_op jit(solution)/shard_map/ppermute | solution.py:394
  16.0 1.9 %collective-permute-start.4 = (bf16[576,128]{1,0:T(8,128)(2,1)S(1)}, bf16[576,128]{1,0:T(8,128)(2,1)S(1)}, u32[]{:S(2)}, u32[]{:S(2)}) collective-permute-start(bf16[576,128]{1,0:T(8,128)(2,1)S(1)} %shard_map.72.refs_2_.refs_0_), channel_id=1, source_target_pairs={{0,2},{1,3},{2,0},{3,1},{4,6},{5,7},{6,4},{7,5},{8,10},{9,11},{10,... | collective-permute-start | bytes 442376 | tf_op jit(solution)/shard_map/ppermute | solution.py:394
  17.9 2.4 %collective-permute-start.5 = (bf16[272,128]{1,0:T(8,128)(2,1)S(1)}, bf16[272,128]{1,0:T(8,128)(2,1)S(1)}, u32[]{:S(2)}, u32[]{:S(2)}) collective-permute-start(bf16[272,128]{1,0:T(8,128)(2,1)S(1)} %shard_map.73), channel_id=1, source_target_pairs={{0,8},{4,12},{8,0},{12,4},{1,9},{5,13},{9,1},{13,5},{2,10},{6,14},... | collective-permute-start | bytes 208904 | tf_op jit(solution)/shard_map/ppermute | solution.py:394
  20.3 4.3 %collective-permute-done.5.refs_2_.refs_3_ = bf16[272,128]{1,0:T(8,128)(2,1)S(1)} collective-permute-done((bf16[272,128]{1,0:T(8,128)(2,1)S(1)}, bf16[272,128]{1,0:T(8,128)(2,1)S(1)}, u32[]{:S(2)}, u32[]{:S(2)}) %collective-permute-start.5) | collective-permute-done | bytes 69664 | tf_op jit(solution)/shard_map/ppermute | solution.py:394
  24.7 1.4 %collective-permute-done.6.refs_2_ = bf16[576,128]{1,0:T(8,128)(2,1)S(1)} collective-permute-done((bf16[576,128]{1,0:T(8,128)(2,1)S(1)}, bf16[576,128]{1,0:T(8,128)(2,1)S(1)}, u32[]{:S(2)}, u32[]{:S(2)}) %collective-permute-start.6) | collective-permute-done | bytes 147488 | tf_op jit(solution)/shard_map/ppermute | solution.py:394
  26.0 1.5 %shard_map.75 = (bf16[336,128]{1,0:T(8,128)(2,1)S(1)}, bf16[256,128]{1,0:T(8,128)(2,1)S(1)}, f32[256,128]{1,0:T(8,128)S(1)}, f32[256,128]{1,0:T(8,128)S(1)}) custom-call(s32[2,64]{1,0:T(2,128)S(1)} %get-tuple-element.31.refs_0_, bf16[576,128]{1,0:T(8,128)(2,1)S(1)} %shard_map.74.refs_1_, bf16[576,128]{1,0:T(8,128)(2,1)S(1)} %collective-permute-done.6.refs_2_, ...), custom_call_target="tpu_custom_call" | custom-call | tf_op jit(solution)/shard_map/pallas_call | solution.py:51
  27.7 1.9 %collective-permute-start.7 = (bf16[256,128]{1,0:T(8,128)(2,1)S(1)}, bf16[256,128]{1,0:T(8,128)(2,1)S(1)}, u32[]{:S(2)}, u32[]{:S(2)}) collective-permute-start(bf16[256,128]{1,0:T(8,128)(2,1)S(1)} %get-tuple-element.36), channel_id=1, source_target_pairs={{0,4},{4,0},{8,12},{12,8},{1,5},{5,1},{9,13},{13,9},{2,6},{6,2},{1... | collective-permute-start | bytes 196616 | tf_op jit(solution)/shard_map/ppermute | solution.py:394
  29.6 3.3 %collective-permute-done.8.refs_1_ = bf16[336,128]{1,0:T(8,128)(2,1)S(1)} collective-permute-done((bf16[336,128]{1,0:T(8,128)(2,1)S(1)}, bf16[336,128]{1,0:T(8,128)(2,1)S(1)}, u32[]{:S(2)}, u32[]{:S(2)}) %collective-permute-start.8) | collective-permute-done | bytes 86048 | tf_op jit(solution)/shard_map/ppermute | solution.py:394
  32.9 1.5 %collective-permute-start.9 = (bf16[336,128]{1,0:T(8,128)(2,1)S(1)}, bf16[336,128]{1,0:T(8,128)(2,1)S(1)}, u32[]{:S(2)}, u32[]{:S(2)}) collective-permute-start(bf16[336,128]{1,0:T(8,128)(2,1)S(1)} %get-tuple-element.40.refs_0_), channel_id=1, source_target_pairs={{0,8},{4,12},{8,0},{12,4},{1,9},{5,13},{9,1},{13,5},{2,10},{6,14},... | collective-permute-start | bytes 258056 | tf_op jit(solution)/shard_map/ppermute | solution.py:394
  34.4 1.5 %collective-permute-start.11 = (bf16[256,128]{1,0:T(8,128)(2,1)S(1)}, bf16[256,128]{1,0:T(8,128)(2,1)S(1)}, u32[]{:S(2)}, u32[]{:S(2)}) collective-permute-start(bf16[256,128]{1,0:T(8,128)(2,1)S(1)} %get-tuple-element.45), channel_id=1, source_target_pairs={{0,8},{4,12},{8,0},{12,4},{1,9},{5,13},{9,1},{13,5},{2,10},{6,14},... | collective-permute-start | bytes 196616 | tf_op jit(solution)/shard_map/ppermute | solution.py:394
  36.0 4.2 %collective-permute-done.9.refs_1_ = bf16[336,128]{1,0:T(8,128)(2,1)S(1)} collective-permute-done((bf16[336,128]{1,0:T(8,128)(2,1)S(1)}, bf16[336,128]{1,0:T(8,128)(2,1)S(1)}, u32[]{:S(2)}, u32[]{:S(2)}) %collective-permute-start.9) | collective-permute-done | bytes 86048 | tf_op jit(solution)/shard_map/ppermute | solution.py:394
  41.9 1.0 %collective-permute-start.12 = (bf16[256,128]{1,0:T(8,128)(2,1)S(1)}, bf16[256,128]{1,0:T(8,128)(2,1)S(1)}, u32[]{:S(2)}, u32[]{:S(2)}) collective-permute-start(bf16[256,128]{1,0:T(8,128)(2,1)S(1)} %shard_map.79.refs_3_), channel_id=1, source_target_pairs={{0,4},{4,0},{8,12},{12,8},{1,5},{5,1},{9,13},{13,9},{2,6},{6,2},{1... | collective-permute-start | bytes 196616 | tf_op jit(solution)/shard_map/ppermute | solution.py:394
  43.3 1.5 %collective-permute-done.10.refs_2_ = bf16[256,128]{1,0:T(8,128)(2,1)S(1)} collective-permute-done((bf16[256,128]{1,0:T(8,128)(2,1)S(1)}, bf16[256,128]{1,0:T(8,128)(2,1)S(1)}, u32[]{:S(2)}, u32[]{:S(2)}) %collective-permute-start.10) | collective-permute-done | bytes 65568 | tf_op jit(solution)/shard_map/ppermute | solution.py:394
  44.8 1.4 %collective-permute-done.12.refs_4_ = bf16[256,128]{1,0:T(8,128)(2,1)S(1)} collective-permute-done((bf16[256,128]{1,0:T(8,128)(2,1)S(1)}, bf16[256,128]{1,0:T(8,128)(2,1)S(1)}, u32[]{:S(2)}, u32[]{:S(2)}) %collective-permute-start.12) | collective-permute-done | bytes 65568 | tf_op jit(solution)/shard_map/ppermute | solution.py:394
  46.2 1.4 %shard_map.81 = (f32[608,128]{1,0:T(8,128)S(1)}, f32[608,128]{1,0:T(8,128)S(1)}) custom-call(s32[2,64]{1,0:T(2,128)S(1)} %get-tuple-element.31.refs_0_, bf16[256,128]{1,0:T(8,128)(2,1)S(1)} %get-tuple-element.44.refs_1_, bf16[256,128]{1,0:T(8,128)(2,1)S(1)} %collective-permute-done.10.refs_2_, bf16[256,128]{1,0:T(8,128)(2,1)S(1)} %shard_map.79.refs_3_, ...), custom_call_target="tpu_custom_call" | custom-call | tf_op jit(solution)/shard_map/pallas_call | solution.py:51
  47.7 1.6 %collective-permute-done.13.refs_1_ = f32[608,128]{1,0:T(8,128)S(1)} collective-permute-done((f32[608,128]{1,0:T(8,128)S(1)}, f32[608,128]{1,0:T(8,128)S(1)}, u32[]{:S(2)}, u32[]{:S(2)}) %collective-permute-start.13) | collective-permute-done | bytes 311328 | tf_op jit(solution)/shard_map/ppermute | solution.py:394
  49.9 1.7 %shard_map.83.refs_2_.refs_3_ = f32[64,64]{1,0:T(8,128)S(1)} custom-call(f32[64,128]{1,0:T(8,128)S(1)} %get-tuple-element.51.refs_0_.refs_2_), custom_call_target="tpu_custom_call" | custom-call | flops 2000000000 | bytes 8000000 | tf_op jit(solution)/shard_map/pallas_call | solution.py:51
  51.6 3.6 %collective-permute-done.14.refs_1_ = bf16[576,128]{1,0:T(8,128)(2,1)S(1)} collective-permute-done((bf16[576,128]{1,0:T(8,128)(2,1)S(1)}, bf16[576,128]{1,0:T(8,128)(2,1)S(1)}, u32[]{:S(2)}, u32[]{:S(2)}) %collective-permute-start.14) | collective-permute-done | bytes 147488 | tf_op jit(solution)/shard_map/ppermute | solution.py:394
  55.4 1.4 %collective-permute-done.15.refs_1_.refs_2_ = bf16[576,128]{1,0:T(8,128)(2,1)S(1)} collective-permute-done((bf16[576,128]{1,0:T(8,128)(2,1)S(1)}, bf16[576,128]{1,0:T(8,128)(2,1)S(1)}, u32[]{:S(2)}, u32[]{:S(2)}) %collective-permute-start.15) | collective-permute-done | bytes 147488 | tf_op jit(solution)/shard_map/ppermute | solution.py:394
  58.0 1.3 %shard_map.87 = (bf16[256,128]{1,0:T(8,128)(2,1)S(1)}, bf16[256,128]{1,0:T(8,128)(2,1)S(1)}, f32[256,128]{1,0:T(8,128)S(1)}, f32[256,128]{1,0:T(8,128)S(1)}, f32[64,64]{1,0:T(8,128)S(1)}) custom-call(s32[2,64]{1,0:T(2,128)S(1)} %get-tuple-element.31.refs_0_, bf16[576,128]{1,0:T(8,128)(2,1)S(1)} %shard_map.84.refs_0_.refs_1_, ...), custom_call_target="tpu_custom_call" | custom-call | tf_op jit(solution)/shard_map/pallas_call | solution.py:51
  59.4 1.2 %collective-permute-start.19 = (bf16[256,128]{1,0:T(8,128)(2,1)S(1)}, bf16[256,128]{1,0:T(8,128)(2,1)S(1)}, u32[]{:S(2)}, u32[]{:S(2)}) collective-permute-start(bf16[256,128]{1,0:T(8,128)(2,1)S(1)} %get-tuple-element.57.refs_0_), channel_id=1, source_target_pairs={{0,4},{4,0},{8,12},{12,8},{1,5},{5,1},{9,13},{13,9},{2,6},{6,2},{1... | collective-permute-start | bytes 196616 | tf_op jit(solution)/shard_map/ppermute | solution.py:394
  61.0 2.5 %collective-permute-start.17 = (bf16[64,128]{1,0:T(8,128)(2,1)S(1)}, bf16[64,128]{1,0:T(8,128)(2,1)S(1)}, u32[]{:S(2)}, u32[]{:S(2)}) collective-permute-start(bf16[64,128]{1,0:T(8,128)(2,1)S(1)} %get-tuple-element.53), channel_id=1, source_target_pairs={{0,8},{4,12},{8,0},{12,4},{1,9},{5,13},{9,1},{13,5},{2,10},{6,14},... | collective-permute-start | bytes 49160 | tf_op jit(solution)/shard_map/ppermute | solution.py:394
  63.5 1.1 %collective-permute-start.18 = (bf16[256,128]{1,0:T(8,128)(2,1)S(1)}, bf16[256,128]{1,0:T(8,128)(2,1)S(1)}, u32[]{:S(2)}, u32[]{:S(2)}) collective-permute-start(bf16[256,128]{1,0:T(8,128)(2,1)S(1)} %get-tuple-element.56), channel_id=1, source_target_pairs={{0,4},{4,0},{8,12},{12,8},{1,5},{5,1},{9,13},{13,9},{2,6},{6,2},{1... | collective-permute-start | bytes 196616 | tf_op jit(solution)/shard_map/ppermute | solution.py:394
  64.6 2.4 %collective-permute-start.20 = (bf16[256,128]{1,0:T(8,128)(2,1)S(1)}, bf16[256,128]{1,0:T(8,128)(2,1)S(1)}, u32[]{:S(2)}, u32[]{:S(2)}) collective-permute-start(bf16[256,128]{1,0:T(8,128)(2,1)S(1)} %shard_map.90), channel_id=1, source_target_pairs={{0,8},{4,12},{8,0},{12,4},{1,9},{5,13},{9,1},{13,5},{2,10},{6,14},... | collective-permute-start | bytes 196616 | tf_op jit(solution)/shard_map/ppermute | solution.py:394
  67.0 2.9 %shard_map.88.refs_2_.refs_7_ = f32[128,64]{1,0:T(8,128)S(1)} custom-call(f32[64,64]{1,0:T(8,128)S(1)} %get-tuple-element.52.refs_0_, bf16[64,128]{1,0:T(8,128)(2,1)S(1)} %collective-permute-done.17.refs_1_, f32[64,128]{1,0:T(8,128)S(1)} %get-tuple-element.51.refs_0_.refs_2_, f32[64,64]{1,0:T(8,128)S(1)} %shard_map.83.refs_2_.refs_3_, ...), custom_call_target="tpu_custom_call" | custom-call | flops 2000000000 | bytes 8000000 | tf_op jit(solution)/shard_map/pallas_call | solution.py:51
  69.9 1.1 %shard_map.89 = f32[64,512]{1,0:T(8,128)} custom-call(f32[64,512]{1,0:T(8,128)S(1)} %copy-done.2, f32[64,512]{1,0:T(8,128)S(1)} %get-tuple-element.43.refs_0_.refs_1_.refs_5_, f32[128,64]{1,0:T(8,128)S(1)} %shard_map.88.refs_2_.refs_7_), custom_call_target="tpu_custom_call" | custom-call | flops 1 | bytes 1 | tf_op jit(solution)/shard_map/pallas_call | solution.py:51
  71.0 1.1 %shard_map.91 = f32[64,512]{1,0:T(8,128)} custom-call(f32[256,128]{1,0:T(8,128)S(1)} %get-tuple-element.55.refs_0_, bf16[256,128]{1,0:T(8,128)(2,1)S(1)} %collective-permute-done.18.refs_1_, bf16[256,128]{1,0:T(8,128)(2,1)S(1)} %collective-permute-done.20.refs_2_, f32[64,512]{1,0:T(8,128)S(1)} %copy-done.2, f32[64,512]{1,0:T(8,128)S(1)} %get-tuple-element.59.refs_4_, ...), custom_call_target="tpu_custom_call" | custom-call | tf_op jit(solution)/shard_map/pallas_call | solution.py:51
  (48 shorter events, 8.4 us)
Async XLA Ops:
  0.6 0.9 %copy-start.1 = (f32[64,512]{1,0:T(8,128)S(1)}, f32[64,512]{1,0:T(8,128)}, u32[]{:S(2)}) copy-start(f32[64,512]{1,0:T(8,128)} %refs_3_.5) | copy-start | bytes 393220
  1.5 7.2 %collective-permute-start.1 = (bf16[256,128]{1,0:T(8,128)(2,1)S(1)}, bf16[256,128]{1,0:T(8,128)(2,1)S(1)}, u32[]{:S(2)}, u32[]{:S(2)}) collective-permute-start(bf16[256,128]{1,0:T(8,128)(2,1)S(1)} %shard_map.69.refs_1_), channel_id=1, source_target_pairs={{0,8},{4,12},{8,0},{12,4},{1,9},{5,13},{9,1},{13,5},{2,10},{6,14},... | collective-permute-start | bytes 196616 | tf_op jit(solution)/shard_map/ppermute | solution.py:394
  5.7 6.5 %collective-permute-start = (bf16[256,128]{1,0:T(8,128)(2,1)S(1)}, bf16[256,128]{1,0:T(8,128)(2,1)S(1)}, u32[]{:S(2)}, u32[]{:S(2)}) collective-permute-start(bf16[256,128]{1,0:T(8,128)(2,1)S(1)} %shard_map.69.refs_1_), channel_id=1, source_target_pairs={{0,4},{4,0},{8,12},{12,8},{1,5},{5,1},{9,13},{13,9},{2,6},{6,2},{1... | collective-permute-start | bytes 196616 | tf_op jit(solution)/shard_map/ppermute | solution.py:394
  7.2 0.7 copy-start.3
  7.9 2.2 %copy-start = (bf16[64,128,128]{2,1,0:T(8,128)(2,1)S(1)}, bf16[64,128,128]{2,1,0:T(8,128)(2,1)}, u32[]{:S(2)}) copy-start(bf16[64,128,128]{2,1,0:T(8,128)(2,1)} %refs_3_.4) | copy-start | bytes 6291460
  7.9 2.2 %copy-start.5 = (s32[64]{0:T(128)S(1)}, s32[64]{0:T(128)}, u32[]{:S(2)}) copy-start(s32[64]{0:T(128)} %refs_0_.5) | copy-start | bytes 772
  7.9 2.2 %copy-start.6 = (s32[64]{0:T(128)S(1)}, s32[64]{0:T(128)}, u32[]{:S(2)}) copy-start(s32[64]{0:T(128)} %refs_1_.1) | copy-start | bytes 772
  8.7 4.3 %collective-permute-start.2 = (bf16[256,128]{1,0:T(8,128)(2,1)S(1)}, bf16[256,128]{1,0:T(8,128)(2,1)S(1)}, u32[]{:S(2)}, u32[]{:S(2)}) collective-permute-start(bf16[256,128]{1,0:T(8,128)(2,1)S(1)} %collective-permute-done.1.refs_3_.refs_2_), channel_id=1, source_target_pairs={{0,4},{4,0},{8,12},{12,8},{1,5},{5,1},{9,13},{13,9},{2,6},{6,2},{1... | collective-permute-start | bytes 196616 | tf_op jit(solution)/shard_map/ppermute | solution.py:394
  12.1 5.8 %copy-start.2 = (f32[64,512]{1,0:T(8,128)S(1)}, f32[64,512]{1,0:T(8,128)}, u32[]{:S(2)}) copy-start(f32[64,512]{1,0:T(8,128)} %refs_3_.5) | copy-start | bytes 393220
  12.1 5.8 %copy-start.4 = (f32[512]{0:T(512)S(1)}, f32[512]{0:T(512)}, u32[]{:S(2)}) copy-start(f32[512]{0:T(512)} %param.6) | copy-start | bytes 6148
  14.3 1.6 %collective-permute-start.3 = (f32[576,128]{1,0:T(8,128)S(1)}, f32[576,128]{1,0:T(8,128)S(1)}, u32[]{:S(2)}, u32[]{:S(2)}) collective-permute-start(f32[576,128]{1,0:T(8,128)S(1)} %get-tuple-element.34), channel_id=1, source_target_pairs={{0,1},{1,0},{2,3},{3,2},{4,5},{5,4},{6,7},{7,6},{8,9},{9,8},{10,11... | collective-permute-start | bytes 884744 | tf_op jit(solution)/shard_map/ppermute | solution.py:394
  16.0 8.6 %collective-permute-start.4 = (bf16[576,128]{1,0:T(8,128)(2,1)S(1)}, bf16[576,128]{1,0:T(8,128)(2,1)S(1)}, u32[]{:S(2)}, u32[]{:S(2)}) collective-permute-start(bf16[576,128]{1,0:T(8,128)(2,1)S(1)} %shard_map.72.refs_2_.refs_0_), channel_id=1, source_target_pairs={{0,2},{1,3},{2,0},{3,1},{4,6},{5,7},{6,4},{7,5},{8,10},{9,11},{10,... | collective-permute-start | bytes 442376 | tf_op jit(solution)/shard_map/ppermute | solution.py:394
  17.9 6.6 %collective-permute-start.5 = (bf16[272,128]{1,0:T(8,128)(2,1)S(1)}, bf16[272,128]{1,0:T(8,128)(2,1)S(1)}, u32[]{:S(2)}, u32[]{:S(2)}) collective-permute-start(bf16[272,128]{1,0:T(8,128)(2,1)S(1)} %shard_map.73), channel_id=1, source_target_pairs={{0,8},{4,12},{8,0},{12,4},{1,9},{5,13},{9,1},{13,5},{2,10},{6,14},... | collective-permute-start | bytes 208904 | tf_op jit(solution)/shard_map/ppermute | solution.py:394
  24.6 1.4 %collective-permute-start.6 = (bf16[576,128]{1,0:T(8,128)(2,1)S(1)}, bf16[576,128]{1,0:T(8,128)(2,1)S(1)}, u32[]{:S(2)}, u32[]{:S(2)}) collective-permute-start(bf16[576,128]{1,0:T(8,128)(2,1)S(1)} %shard_map.74.refs_1_), channel_id=1, source_target_pairs={{0,1},{1,0},{2,3},{3,2},{4,5},{5,4},{6,7},{7,6},{8,9},{9,8},{10,11... | collective-permute-start | bytes 442376 | tf_op jit(solution)/shard_map/ppermute | solution.py:394
  27.5 5.4 %collective-permute-start.8 = (bf16[336,128]{1,0:T(8,128)(2,1)S(1)}, bf16[336,128]{1,0:T(8,128)(2,1)S(1)}, u32[]{:S(2)}, u32[]{:S(2)}) collective-permute-start(bf16[336,128]{1,0:T(8,128)(2,1)S(1)} %get-tuple-element.38.refs_0_), channel_id=1, source_target_pairs={{0,4},{4,0},{8,12},{12,8},{1,5},{5,1},{9,13},{13,9},{2,6},{6,2},{1... | collective-permute-start | bytes 258056 | tf_op jit(solution)/shard_map/ppermute | solution.py:394
  27.7 6.7 %collective-permute-start.7 = (bf16[256,128]{1,0:T(8,128)(2,1)S(1)}, bf16[256,128]{1,0:T(8,128)(2,1)S(1)}, u32[]{:S(2)}, u32[]{:S(2)}) collective-permute-start(bf16[256,128]{1,0:T(8,128)(2,1)S(1)} %get-tuple-element.36), channel_id=1, source_target_pairs={{0,4},{4,0},{8,12},{12,8},{1,5},{5,1},{9,13},{13,9},{2,6},{6,2},{1... | collective-permute-start | bytes 196616 | tf_op jit(solution)/shard_map/ppermute | solution.py:394
  32.9 7.3 %collective-permute-start.9 = (bf16[336,128]{1,0:T(8,128)(2,1)S(1)}, bf16[336,128]{1,0:T(8,128)(2,1)S(1)}, u32[]{:S(2)}, u32[]{:S(2)}) collective-permute-start(bf16[336,128]{1,0:T(8,128)(2,1)S(1)} %get-tuple-element.40.refs_0_), channel_id=1, source_target_pairs={{0,8},{4,12},{8,0},{12,4},{1,9},{5,13},{9,1},{13,5},{2,10},{6,14},... | collective-permute-start | bytes 258056 | tf_op jit(solution)/shard_map/ppermute | solution.py:394
  34.4 7.2 %collective-permute-start.11 = (bf16[256,128]{1,0:T(8,128)(2,1)S(1)}, bf16[256,128]{1,0:T(8,128)(2,1)S(1)}, u32[]{:S(2)}, u32[]{:S(2)}) collective-permute-start(bf16[256,128]{1,0:T(8,128)(2,1)S(1)} %get-tuple-element.45), channel_id=1, source_target_pairs={{0,8},{4,12},{8,0},{12,4},{1,9},{5,13},{9,1},{13,5},{2,10},{6,14},... | collective-permute-start | bytes 196616 | tf_op jit(solution)/shard_map/ppermute | solution.py:394
  40.5 4.3 %collective-permute-start.10 = (bf16[256,128]{1,0:T(8,128)(2,1)S(1)}, bf16[256,128]{1,0:T(8,128)(2,1)S(1)}, u32[]{:S(2)}, u32[]{:S(2)}) collective-permute-start(bf16[256,128]{1,0:T(8,128)(2,1)S(1)} %get-tuple-element.44.refs_1_), channel_id=1, source_target_pairs={{0,4},{4,0},{8,12},{12,8},{1,5},{5,1},{9,13},{13,9},{2,6},{6,2},{1... | collective-permute-start | bytes 196616 | tf_op jit(solution)/shard_map/ppermute | solution.py:394
  41.9 4.3 %collective-permute-start.12 = (bf16[256,128]{1,0:T(8,128)(2,1)S(1)}, bf16[256,128]{1,0:T(8,128)(2,1)S(1)}, u32[]{:S(2)}, u32[]{:S(2)}) collective-permute-start(bf16[256,128]{1,0:T(8,128)(2,1)S(1)} %shard_map.79.refs_3_), channel_id=1, source_target_pairs={{0,4},{4,0},{8,12},{12,8},{1,5},{5,1},{9,13},{13,9},{2,6},{6,2},{1... | collective-permute-start | bytes 196616 | tf_op jit(solution)/shard_map/ppermute | solution.py:394
  47.6 1.7 %collective-permute-start.13 = (f32[608,128]{1,0:T(8,128)S(1)}, f32[608,128]{1,0:T(8,128)S(1)}, u32[]{:S(2)}, u32[]{:S(2)}) collective-permute-start(f32[608,128]{1,0:T(8,128)S(1)} %get-tuple-element.49), channel_id=1, source_target_pairs={{0,1},{1,0},{2,3},{3,2},{4,5},{5,4},{6,7},{7,6},{8,9},{9,8},{10,11... | collective-permute-start | bytes 933896 | tf_op jit(solution)/shard_map/ppermute | solution.py:394
  49.3 6.0 %collective-permute-start.14 = (bf16[576,128]{1,0:T(8,128)(2,1)S(1)}, bf16[576,128]{1,0:T(8,128)(2,1)S(1)}, u32[]{:S(2)}, u32[]{:S(2)}) collective-permute-start(bf16[576,128]{1,0:T(8,128)(2,1)S(1)} %get-tuple-element.50.refs_0_), channel_id=1, source_target_pairs={{0,2},{1,3},{2,0},{3,1},{4,6},{5,7},{6,4},{7,5},{8,10},{9,11},{10,... | collective-permute-start | bytes 442376 | tf_op jit(solution)/shard_map/ppermute | solution.py:394
  55.3 1.4 %collective-permute-start.15 = (bf16[576,128]{1,0:T(8,128)(2,1)S(1)}, bf16[576,128]{1,0:T(8,128)(2,1)S(1)}, u32[]{:S(2)}, u32[]{:S(2)}) collective-permute-start(bf16[576,128]{1,0:T(8,128)(2,1)S(1)} %shard_map.84.refs_0_.refs_1_), channel_id=1, source_target_pairs={{0,1},{1,0},{2,3},{3,2},{4,5},{5,4},{6,7},{7,6},{8,9},{9,8},{10,11... | collective-permute-start | bytes 442376 | tf_op jit(solution)/shard_map/ppermute | solution.py:394
  57.1 3.8 %collective-permute-start.16 = (bf16[64,128]{1,0:T(8,128)(2,1)S(1)}, bf16[64,128]{1,0:T(8,128)(2,1)S(1)}, u32[]{:S(2)}, u32[]{:S(2)}) collective-permute-start(bf16[64,128]{1,0:T(8,128)(2,1)S(1)} %shard_map.85.refs_0_), channel_id=1, source_target_pairs={{0,4},{4,0},{8,12},{12,8},{1,5},{5,1},{9,13},{13,9},{2,6},{6,2},{1... | collective-permute-start | bytes 49160 | tf_op jit(solution)/shard_map/ppermute | solution.py:394
  59.4 5.2 %collective-permute-start.19 = (bf16[256,128]{1,0:T(8,128)(2,1)S(1)}, bf16[256,128]{1,0:T(8,128)(2,1)S(1)}, u32[]{:S(2)}, u32[]{:S(2)}) collective-permute-start(bf16[256,128]{1,0:T(8,128)(2,1)S(1)} %get-tuple-element.57.refs_0_), channel_id=1, source_target_pairs={{0,4},{4,0},{8,12},{12,8},{1,5},{5,1},{9,13},{13,9},{2,6},{6,2},{1... | collective-permute-start | bytes 196616 | tf_op jit(solution)/shard_map/ppermute | solution.py:394
  61.0 6.0 %collective-permute-start.17 = (bf16[64,128]{1,0:T(8,128)(2,1)S(1)}, bf16[64,128]{1,0:T(8,128)(2,1)S(1)}, u32[]{:S(2)}, u32[]{:S(2)}) collective-permute-start(bf16[64,128]{1,0:T(8,128)(2,1)S(1)} %get-tuple-element.53), channel_id=1, source_target_pairs={{0,8},{4,12},{8,0},{12,4},{1,9},{5,13},{9,1},{13,5},{2,10},{6,14},... | collective-permute-start | bytes 49160 | tf_op jit(solution)/shard_map/ppermute | solution.py:394
  63.5 7.5 %collective-permute-start.18 = (bf16[256,128]{1,0:T(8,128)(2,1)S(1)}, bf16[256,128]{1,0:T(8,128)(2,1)S(1)}, u32[]{:S(2)}, u32[]{:S(2)}) collective-permute-start(bf16[256,128]{1,0:T(8,128)(2,1)S(1)} %get-tuple-element.56), channel_id=1, source_target_pairs={{0,4},{4,0},{8,12},{12,8},{1,5},{5,1},{9,13},{13,9},{2,6},{6,2},{1... | collective-permute-start | bytes 196616 | tf_op jit(solution)/shard_map/ppermute | solution.py:394
  64.6 6.3 %collective-permute-start.20 = (bf16[256,128]{1,0:T(8,128)(2,1)S(1)}, bf16[256,128]{1,0:T(8,128)(2,1)S(1)}, u32[]{:S(2)}, u32[]{:S(2)}) collective-permute-start(bf16[256,128]{1,0:T(8,128)(2,1)S(1)} %shard_map.90), channel_id=1, source_target_pairs={{0,8},{4,12},{8,0},{12,4},{1,9},{5,13},{9,1},{13,5},{2,10},{6,14},... | collective-permute-start | bytes 196616 | tf_op jit(solution)/shard_map/ppermute | solution.py:394

commit v15 on v10

--- a/solution.py
+++ b/solution.py
@@ -213,21 +213,21 @@
     out_ref[at + frames :, :] = jnp.where(row == 0, diagonal, 0.0).astype(BF16)
 
 
-def rows_kernel(frames, sent, received, kept, out_refs, gram_refs):
+def rows_kernel(frames, sent, received, kept, out_refs, extra_refs):
     split_at = frames // 2
     data = kept[0].shape[0]
     for out_ref, kept_ref, received_ref in zip(out_refs, kept, received):
         for j in range(data // frames):
             at = rows(j, frames)
             out_ref[at, :] = (kept_ref[at, :] + received_ref[at, :].astype(F32)).astype(BF16)
-    if gram_refs:
+    if extra_refs:
         pair = (sent, received[0])
         high, low = slice(data, data + split_at), slice(data + split_at, data + frames)
         value = sum_rows(pair, high) + sum_rows(pair, low)
         block = jnp.concatenate(split(value), axis=0)
         tile = sum_rows(pair, slice(data + frames, data + frames + DIAG)).astype(BF16)
-        gram_refs[0][...] = value
-        gram_refs[1][...] = tile
+        extra_refs[0][...] = value
+        extra_refs[1][...] = tile
         for out_ref in out_refs:
             out_ref[data : data + frames, :] = block
             out_ref[data + frames :, :] = tile
@@ -484,7 +484,9 @@
             (far[0], received, kept),
         )
         far = tuple(swapped(x, "row", 2 * (p + 1)) for p, x in enumerate(sums))
-        return (keep, near, far, *gram), (norm if last else sums)
+        if last:
+            return (keep, near, far), norm
+        return (keep, near, far, *gram), sums
 
     (cast,) = call(cast_kernel, (cast_type,), (right_side,))
     search = gather(cast, "row")
@@ -532,13 +534,14 @@
         second_pair_kernel,
         (shape((frames, frames)), shape((frames, 2 * frames), BF16)),
         (second, swapped(second, "row", 1)),
+        cost=aside,
     )
     second = others(second, "row")[1:]
-    parts, norm = backward(foot, True)
+    parts, (norm,) = backward(foot, True)
     (coeffs,) = call(
         solve_kernel,
         (shape((2 * frames, frames)),),
-        (gram, second, first, inverse, *norm, diagonal),
+        (gram, second, first, inverse, norm, diagonal),
         cost=aside,
     )
     return tuple(

time: 74.3 us -> 72 us (0.969)
  waiting for transfers between devices: 31.5 us -> 27.4 us
  starting transfers between devices: 24.8 us -> 26.7 us
    ppermute x21, waiting for transfers between devices: 31.5 us -> 27.4 us  [swapped(): lax.ppermute(x, axis, [(i, i ^ flip) for i in range(lax.axis_size(axis))])]
    ppermute x21, starting transfers between devices: 24.8 us -> 26.7 us  [swapped(): lax.ppermute(x, axis, [(i, i ^ flip) for i in range(lax.axis_size(axis))])]
  transfers between devices with their start and end apart: 21 -> 21, of which waited for: 16 -> 15; matrix products, arithmetic and copies ran while one was open for 0% -> 0% of each run, Pallas kernels for 11% -> 13%
where the time goes in v15:
time: 72 us; the launch traced here: 71.9 us
  waiting for transfers between devices  27.4 us (38%)
  starting transfers between devices  26.7 us (37%)
  Pallas kernels  15.4 us (21%)
  local copies, waits for them, and re-layouts  1.6 us (2%)
  between operations  0.82 us (1%)
    ppermute x21, waiting for transfers between devices, swapped(): lax.ppermute(x, axis, [(i, i ^ flip) for i in range(lax.axis_size(axis))])  27.4 us
    ppermute x21, starting transfers between devices, swapped(): lax.ppermute(x, axis, [(i, i ^ flip) for i in range(lax.axis_size(axis))])  26.7 us
    pallas_call x23, Pallas kernels, call(): pl.pallas_call(body, out_shape=flat_outs, in_specs=[space(x) for x in fla...  15.4 us
    unnamed x14, local copies, waits for them, and re-layouts  1.6 us
  transfers between devices with their start and end apart: 21, of which 15 were waited for; matrix products, arithmetic and copies ran while one was open for 0% of the time, Pallas kernels for 13%

profile of v15, /device:TPU:0, one launch (start us, length us, event | category | flops | bytes accessed | tf_op | source)
XLA Modules:
  0.0 71.9 jit_solution(6123981105172446684)
XLA Ops:
  1.5 4.1 %collective-permute-start.1 = (bf16[256,128]{1,0:T(8,128)(2,1)S(1)}, bf16[256,128]{1,0:T(8,128)(2,1)S(1)}, u32[]{:S(2)}, u32[]{:S(2)}) collective-permute-start(bf16[256,128]{1,0:T(8,128)(2,1)S(1)} %shard_map.69.refs_1_), channel_id=1, source_target_pairs={{0,8},{4,12},{8,0},{12,4},{1,9},{5,13},{9,1},{13,5},{2,10},{6,14},... | collective-permute-start | bytes 196616 | tf_op jit(solution)/shard_map/ppermute | solution.py:390
  5.7 1.6 %collective-permute-start = (bf16[256,128]{1,0:T(8,128)(2,1)S(1)}, bf16[256,128]{1,0:T(8,128)(2,1)S(1)}, u32[]{:S(2)}, u32[]{:S(2)}) collective-permute-start(bf16[256,128]{1,0:T(8,128)(2,1)S(1)} %shard_map.69.refs_1_), channel_id=1, source_target_pairs={{0,4},{4,0},{8,12},{12,8},{1,5},{5,1},{9,13},{13,9},{2,6},{6,2},{1... | collective-permute-start | bytes 196616 | tf_op jit(solution)/shard_map/ppermute | solution.py:390
  8.7 1.4 %collective-permute-start.2 = (bf16[256,128]{1,0:T(8,128)(2,1)S(1)}, bf16[256,128]{1,0:T(8,128)(2,1)S(1)}, u32[]{:S(2)}, u32[]{:S(2)}) collective-permute-start(bf16[256,128]{1,0:T(8,128)(2,1)S(1)} %collective-permute-done.1.refs_3_.refs_2_), channel_id=1, source_target_pairs={{0,4},{4,0},{8,12},{12,8},{1,5},{5,1},{9,13},{13,9},{2,6},{6,2},{1... | collective-permute-start | bytes 196616 | tf_op jit(solution)/shard_map/ppermute | solution.py:390
  10.1 2.0 %shard_map.68 = (s32[2,64]{1,0:T(2,128)S(1)}, bf16[64,128,128]{2,1,0:T(8,128)(2,1)S(1)}) custom-call(s32[64]{0:T(128)S(1)} %copy-done.5, s32[64]{0:T(128)S(1)} %copy-done.6, bf16[64,128,128]{2,1,0:T(8,128)(2,1)S(1)} %copy-done), custom_call_target="tpu_custom_call" | custom-call | flops 2000000000 | bytes 8000000 | tf_op jit(solution)/shard_map/pallas_call | solution.py:51
  13.0 1.3 %shard_map.71 = (f32[576,128]{1,0:T(8,128)S(1)}, f32[576,128]{1,0:T(8,128)S(1)}) custom-call(s32[2,64]{1,0:T(2,128)S(1)} %get-tuple-element.31.refs_0_, bf16[256,128]{1,0:T(8,128)(2,1)S(1)} %shard_map.69.refs_1_, bf16[256,128]{1,0:T(8,128)(2,1)S(1)} %collective-permute-done.refs_2_, bf16[256,128]{1,0:T(8,128)(2,1)S(1)} %collective-permute-done.1.refs_3_.refs_2_, ...), custom_call_target="tpu_custom_call" | custom-call | tf_op jit(solution)/shard_map/pallas_call | solution.py:51
  14.4 1.6 %collective-permute-done.3.refs_1_ = f32[576,128]{1,0:T(8,128)S(1)} collective-permute-done((f32[576,128]{1,0:T(8,128)S(1)}, f32[576,128]{1,0:T(8,128)S(1)}, u32[]{:S(2)}, u32[]{:S(2)}) %collective-permute-start.3) | collective-permute-done | bytes 294944 | tf_op jit(solution)/shard_map/ppermute | solution.py:390
  16.0 1.9 %collective-permute-start.4 = (bf16[576,128]{1,0:T(8,128)(2,1)S(1)}, bf16[576,128]{1,0:T(8,128)(2,1)S(1)}, u32[]{:S(2)}, u32[]{:S(2)}) collective-permute-start(bf16[576,128]{1,0:T(8,128)(2,1)S(1)} %shard_map.72.refs_2_.refs_0_), channel_id=1, source_target_pairs={{0,2},{1,3},{2,0},{3,1},{4,6},{5,7},{6,4},{7,5},{8,10},{9,11},{10,... | collective-permute-start | bytes 442376 | tf_op jit(solution)/shard_map/ppermute | solution.py:390
  17.9 2.4 %collective-permute-start.5 = (bf16[272,128]{1,0:T(8,128)(2,1)S(1)}, bf16[272,128]{1,0:T(8,128)(2,1)S(1)}, u32[]{:S(2)}, u32[]{:S(2)}) collective-permute-start(bf16[272,128]{1,0:T(8,128)(2,1)S(1)} %shard_map.73), channel_id=1, source_target_pairs={{0,8},{4,12},{8,0},{12,4},{1,9},{5,13},{9,1},{13,5},{2,10},{6,14},... | collective-permute-start | bytes 208904 | tf_op jit(solution)/shard_map/ppermute | solution.py:390
  20.3 4.3 %collective-permute-done.5.refs_2_.refs_3_ = bf16[272,128]{1,0:T(8,128)(2,1)S(1)} collective-permute-done((bf16[272,128]{1,0:T(8,128)(2,1)S(1)}, bf16[272,128]{1,0:T(8,128)(2,1)S(1)}, u32[]{:S(2)}, u32[]{:S(2)}) %collective-permute-start.5) | collective-permute-done | bytes 69664 | tf_op jit(solution)/shard_map/ppermute | solution.py:390
  24.7 1.4 %collective-permute-done.6.refs_2_ = bf16[576,128]{1,0:T(8,128)(2,1)S(1)} collective-permute-done((bf16[576,128]{1,0:T(8,128)(2,1)S(1)}, bf16[576,128]{1,0:T(8,128)(2,1)S(1)}, u32[]{:S(2)}, u32[]{:S(2)}) %collective-permute-start.6) | collective-permute-done | bytes 147488 | tf_op jit(solution)/shard_map/ppermute | solution.py:390
  26.0 1.5 %shard_map.75 = (bf16[336,128]{1,0:T(8,128)(2,1)S(1)}, bf16[256,128]{1,0:T(8,128)(2,1)S(1)}, f32[256,128]{1,0:T(8,128)S(1)}, f32[256,128]{1,0:T(8,128)S(1)}) custom-call(s32[2,64]{1,0:T(2,128)S(1)} %get-tuple-element.31.refs_0_, bf16[576,128]{1,0:T(8,128)(2,1)S(1)} %shard_map.74.refs_1_, bf16[576,128]{1,0:T(8,128)(2,1)S(1)} %collective-permute-done.6.refs_2_, ...), custom_call_target="tpu_custom_call" | custom-call | tf_op jit(solution)/shard_map/pallas_call | solution.py:51
  27.7 1.9 %collective-permute-start.7 = (bf16[256,128]{1,0:T(8,128)(2,1)S(1)}, bf16[256,128]{1,0:T(8,128)(2,1)S(1)}, u32[]{:S(2)}, u32[]{:S(2)}) collective-permute-start(bf16[256,128]{1,0:T(8,128)(2,1)S(1)} %get-tuple-element.36), channel_id=1, source_target_pairs={{0,4},{4,0},{8,12},{12,8},{1,5},{5,1},{9,13},{13,9},{2,6},{6,2},{1... | collective-permute-start | bytes 196616 | tf_op jit(solution)/shard_map/ppermute | solution.py:390
  29.6 3.3 %collective-permute-done.8.refs_1_ = bf16[336,128]{1,0:T(8,128)(2,1)S(1)} collective-permute-done((bf16[336,128]{1,0:T(8,128)(2,1)S(1)}, bf16[336,128]{1,0:T(8,128)(2,1)S(1)}, u32[]{:S(2)}, u32[]{:S(2)}) %collective-permute-start.8) | collective-permute-done | bytes 86048 | tf_op jit(solution)/shard_map/ppermute | solution.py:390
  32.9 1.5 %collective-permute-start.9 = (bf16[336,128]{1,0:T(8,128)(2,1)S(1)}, bf16[336,128]{1,0:T(8,128)(2,1)S(1)}, u32[]{:S(2)}, u32[]{:S(2)}) collective-permute-start(bf16[336,128]{1,0:T(8,128)(2,1)S(1)} %get-tuple-element.40.refs_0_), channel_id=1, source_target_pairs={{0,8},{4,12},{8,0},{12,4},{1,9},{5,13},{9,1},{13,5},{2,10},{6,14},... | collective-permute-start | bytes 258056 | tf_op jit(solution)/shard_map/ppermute | solution.py:390
  34.4 1.5 %collective-permute-start.11 = (bf16[256,128]{1,0:T(8,128)(2,1)S(1)}, bf16[256,128]{1,0:T(8,128)(2,1)S(1)}, u32[]{:S(2)}, u32[]{:S(2)}) collective-permute-start(bf16[256,128]{1,0:T(8,128)(2,1)S(1)} %get-tuple-element.44), channel_id=1, source_target_pairs={{0,8},{4,12},{8,0},{12,4},{1,9},{5,13},{9,1},{13,5},{2,10},{6,14},... | collective-permute-start | bytes 196616 | tf_op jit(solution)/shard_map/ppermute | solution.py:390
  36.0 4.2 %collective-permute-done.9.refs_1_ = bf16[336,128]{1,0:T(8,128)(2,1)S(1)} collective-permute-done((bf16[336,128]{1,0:T(8,128)(2,1)S(1)}, bf16[336,128]{1,0:T(8,128)(2,1)S(1)}, u32[]{:S(2)}, u32[]{:S(2)}) %collective-permute-start.9) | collective-permute-done | bytes 86048 | tf_op jit(solution)/shard_map/ppermute | solution.py:390
  41.9 1.0 %collective-permute-start.12 = (bf16[256,128]{1,0:T(8,128)(2,1)S(1)}, bf16[256,128]{1,0:T(8,128)(2,1)S(1)}, u32[]{:S(2)}, u32[]{:S(2)}) collective-permute-start(bf16[256,128]{1,0:T(8,128)(2,1)S(1)} %shard_map.79.refs_3_), channel_id=1, source_target_pairs={{0,4},{4,0},{8,12},{12,8},{1,5},{5,1},{9,13},{13,9},{2,6},{6,2},{1... | collective-permute-start | bytes 196616 | tf_op jit(solution)/shard_map/ppermute | solution.py:390
  43.2 1.5 %collective-permute-done.10.refs_2_ = bf16[256,128]{1,0:T(8,128)(2,1)S(1)} collective-permute-done((bf16[256,128]{1,0:T(8,128)(2,1)S(1)}, bf16[256,128]{1,0:T(8,128)(2,1)S(1)}, u32[]{:S(2)}, u32[]{:S(2)}) %collective-permute-start.10) | collective-permute-done | bytes 65568 | tf_op jit(solution)/shard_map/ppermute | solution.py:390
  44.8 1.4 %collective-permute-done.12.refs_4_ = bf16[256,128]{1,0:T(8,128)(2,1)S(1)} collective-permute-done((bf16[256,128]{1,0:T(8,128)(2,1)S(1)}, bf16[256,128]{1,0:T(8,128)(2,1)S(1)}, u32[]{:S(2)}, u32[]{:S(2)}) %collective-permute-start.12) | collective-permute-done | bytes 65568 | tf_op jit(solution)/shard_map/ppermute | solution.py:390
  46.2 1.4 %shard_map.81 = (f32[608,128]{1,0:T(8,128)S(1)}, f32[608,128]{1,0:T(8,128)S(1)}) custom-call(s32[2,64]{1,0:T(2,128)S(1)} %get-tuple-element.31.refs_0_, bf16[256,128]{1,0:T(8,128)(2,1)S(1)} %get-tuple-element.43.refs_1_, bf16[256,128]{1,0:T(8,128)(2,1)S(1)} %collective-permute-done.10.refs_2_, bf16[256,128]{1,0:T(8,128)(2,1)S(1)} %shard_map.79.refs_3_, ...), custom_call_target="tpu_custom_call" | custom-call | tf_op jit(solution)/shard_map/pallas_call | solution.py:51
  47.7 1.6 %collective-permute-done.13.refs_1_ = f32[608,128]{1,0:T(8,128)S(1)} collective-permute-done((f32[608,128]{1,0:T(8,128)S(1)}, f32[608,128]{1,0:T(8,128)S(1)}, u32[]{:S(2)}, u32[]{:S(2)}) %collective-permute-start.13) | collective-permute-done | bytes 311328 | tf_op jit(solution)/shard_map/ppermute | solution.py:390
  49.9 1.7 %shard_map.83.refs_2_.refs_3_ = f32[64,64]{1,0:T(8,128)S(1)} custom-call(f32[64,128]{1,0:T(8,128)S(1)} %get-tuple-element.51.refs_0_.refs_2_), custom_call_target="tpu_custom_call" | custom-call | flops 2000000000 | bytes 8000000 | tf_op jit(solution)/shard_map/pallas_call | solution.py:51
  51.6 3.6 %collective-permute-done.14.refs_1_ = bf16[576,128]{1,0:T(8,128)(2,1)S(1)} collective-permute-done((bf16[576,128]{1,0:T(8,128)(2,1)S(1)}, bf16[576,128]{1,0:T(8,128)(2,1)S(1)}, u32[]{:S(2)}, u32[]{:S(2)}) %collective-permute-start.14) | collective-permute-done | bytes 147488 | tf_op jit(solution)/shard_map/ppermute | solution.py:390
  55.4 1.4 %collective-permute-done.15.refs_2_.refs_1_ = bf16[576,128]{1,0:T(8,128)(2,1)S(1)} collective-permute-done((bf16[576,128]{1,0:T(8,128)(2,1)S(1)}, bf16[576,128]{1,0:T(8,128)(2,1)S(1)}, u32[]{:S(2)}, u32[]{:S(2)}) %collective-permute-start.15) | collective-permute-done | bytes 147488 | tf_op jit(solution)/shard_map/ppermute | solution.py:390
  57.1 1.0 %collective-permute-start.19 = (bf16[64,128]{1,0:T(8,128)(2,1)S(1)}, bf16[64,128]{1,0:T(8,128)(2,1)S(1)}, u32[]{:S(2)}, u32[]{:S(2)}) collective-permute-start(bf16[64,128]{1,0:T(8,128)(2,1)S(1)} %shard_map.87.refs_0_), channel_id=1, source_target_pairs={{0,4},{4,0},{8,12},{12,8},{1,5},{5,1},{9,13},{13,9},{2,6},{6,2},{1... | collective-permute-start | bytes 49160 | tf_op jit(solution)/shard_map/ppermute | solution.py:390
  58.0 1.3 %shard_map.85 = (bf16[256,128]{1,0:T(8,128)(2,1)S(1)}, bf16[256,128]{1,0:T(8,128)(2,1)S(1)}, f32[256,128]{1,0:T(8,128)S(1)}, f32[256,128]{1,0:T(8,128)S(1)}, f32[64,64]{1,0:T(8,128)S(1)}) custom-call(s32[2,64]{1,0:T(2,128)S(1)} %get-tuple-element.31.refs_0_, bf16[576,128]{1,0:T(8,128)(2,1)S(1)} %shard_map.84.refs_1_.refs_0_, ...), custom_call_target="tpu_custom_call" | custom-call | tf_op jit(solution)/shard_map/pallas_call | solution.py:51
  59.3 1.2 %collective-permute-start.17 = (bf16[256,128]{1,0:T(8,128)(2,1)S(1)}, bf16[256,128]{1,0:T(8,128)(2,1)S(1)}, u32[]{:S(2)}, u32[]{:S(2)}) collective-permute-start(bf16[256,128]{1,0:T(8,128)(2,1)S(1)} %get-tuple-element.54.refs_0_), channel_id=1, source_target_pairs={{0,4},{4,0},{8,12},{12,8},{1,5},{5,1},{9,13},{13,9},{2,6},{6,2},{1... | collective-permute-start | bytes 196616 | tf_op jit(solution)/shard_map/ppermute | solution.py:390
  61.0 2.5 %collective-permute-start.20 = (bf16[64,128]{1,0:T(8,128)(2,1)S(1)}, bf16[64,128]{1,0:T(8,128)(2,1)S(1)}, u32[]{:S(2)}, u32[]{:S(2)}) collective-permute-start(bf16[64,128]{1,0:T(8,128)(2,1)S(1)} %get-tuple-element.58), channel_id=1, source_target_pairs={{0,8},{4,12},{8,0},{12,4},{1,9},{5,13},{9,1},{13,5},{2,10},{6,14},... | collective-permute-start | bytes 49160 | tf_op jit(solution)/shard_map/ppermute | solution.py:390
  63.5 1.1 %collective-permute-start.16 = (bf16[256,128]{1,0:T(8,128)(2,1)S(1)}, bf16[256,128]{1,0:T(8,128)(2,1)S(1)}, u32[]{:S(2)}, u32[]{:S(2)}) collective-permute-start(bf16[256,128]{1,0:T(8,128)(2,1)S(1)} %get-tuple-element.53), channel_id=1, source_target_pairs={{0,4},{4,0},{8,12},{12,8},{1,5},{5,1},{9,13},{13,9},{2,6},{6,2},{1... | collective-permute-start | bytes 196616 | tf_op jit(solution)/shard_map/ppermute | solution.py:390
  64.6 2.4 %collective-permute-start.18 = (bf16[256,128]{1,0:T(8,128)(2,1)S(1)}, bf16[256,128]{1,0:T(8,128)(2,1)S(1)}, u32[]{:S(2)}, u32[]{:S(2)}) collective-permute-start(bf16[256,128]{1,0:T(8,128)(2,1)S(1)} %shard_map.86), channel_id=1, source_target_pairs={{0,8},{4,12},{8,0},{12,4},{1,9},{5,13},{9,1},{13,5},{2,10},{6,14},... | collective-permute-start | bytes 196616 | tf_op jit(solution)/shard_map/ppermute | solution.py:390
  67.0 2.9 %shard_map.89.refs_7_ = f32[128,64]{1,0:T(8,128)S(1)} custom-call(f32[64,64]{1,0:T(8,128)S(1)} %get-tuple-element.57.refs_0_, bf16[64,128]{1,0:T(8,128)(2,1)S(1)} %collective-permute-done.20.refs_1_, f32[64,128]{1,0:T(8,128)S(1)} %get-tuple-element.51.refs_0_.refs_2_, f32[64,64]{1,0:T(8,128)S(1)} %shard_map.83.refs_2_.refs_3_, ...), custom_call_target="tpu_custom_call" | custom-call | flops 2000000000 | bytes 8000000 | tf_op jit(solution)/shard_map/pallas_call | solution.py:51
  70.6 1.3 %shard_map.90 = (f32[64,512]{1,0:T(8,128)}, f32[64,512]{1,0:T(8,128)}) custom-call(f32[256,128]{1,0:T(8,128)S(1)} %get-tuple-element.52.refs_0_, bf16[256,128]{1,0:T(8,128)(2,1)S(1)} %collective-permute-done.16.refs_1_, bf16[256,128]{1,0:T(8,128)(2,1)S(1)} %collective-permute-done.18.refs_2_, f32[64,512]{1,0:T(8,128)S(1)} %copy-done.2, ...), custom_call_target="tpu_custom_call" | custom-call | tf_op jit(solution)/shard_map/pallas_call | solution.py:51
  (47 shorter events, 8.1 us)
Async XLA Ops:
  0.6 0.9 %copy-start.1 = (f32[64,512]{1,0:T(8,128)S(1)}, f32[64,512]{1,0:T(8,128)}, u32[]{:S(2)}) copy-start(f32[64,512]{1,0:T(8,128)} %refs_3_.5) | copy-start | bytes 393220
  1.5 7.2 %collective-permute-start.1 = (bf16[256,128]{1,0:T(8,128)(2,1)S(1)}, bf16[256,128]{1,0:T(8,128)(2,1)S(1)}, u32[]{:S(2)}, u32[]{:S(2)}) collective-permute-start(bf16[256,128]{1,0:T(8,128)(2,1)S(1)} %shard_map.69.refs_1_), channel_id=1, source_target_pairs={{0,8},{4,12},{8,0},{12,4},{1,9},{5,13},{9,1},{13,5},{2,10},{6,14},... | collective-permute-start | bytes 196616 | tf_op jit(solution)/shard_map/ppermute | solution.py:390
  5.7 6.5 %collective-permute-start = (bf16[256,128]{1,0:T(8,128)(2,1)S(1)}, bf16[256,128]{1,0:T(8,128)(2,1)S(1)}, u32[]{:S(2)}, u32[]{:S(2)}) collective-permute-start(bf16[256,128]{1,0:T(8,128)(2,1)S(1)} %shard_map.69.refs_1_), channel_id=1, source_target_pairs={{0,4},{4,0},{8,12},{12,8},{1,5},{5,1},{9,13},{13,9},{2,6},{6,2},{1... | collective-permute-start | bytes 196616 | tf_op jit(solution)/shard_map/ppermute | solution.py:390
  7.2 0.7 copy-start.3
  7.9 2.2 %copy-start = (bf16[64,128,128]{2,1,0:T(8,128)(2,1)S(1)}, bf16[64,128,128]{2,1,0:T(8,128)(2,1)}, u32[]{:S(2)}) copy-start(bf16[64,128,128]{2,1,0:T(8,128)(2,1)} %refs_3_.4) | copy-start | bytes 6291460
  7.9 2.2 %copy-start.5 = (s32[64]{0:T(128)S(1)}, s32[64]{0:T(128)}, u32[]{:S(2)}) copy-start(s32[64]{0:T(128)} %refs_0_.4) | copy-start | bytes 772
  7.9 2.2 %copy-start.6 = (s32[64]{0:T(128)S(1)}, s32[64]{0:T(128)}, u32[]{:S(2)}) copy-start(s32[64]{0:T(128)} %refs_1_.1) | copy-start | bytes 772
  8.7 4.3 %collective-permute-start.2 = (bf16[256,128]{1,0:T(8,128)(2,1)S(1)}, bf16[256,128]{1,0:T(8,128)(2,1)S(1)}, u32[]{:S(2)}, u32[]{:S(2)}) collective-permute-start(bf16[256,128]{1,0:T(8,128)(2,1)S(1)} %collective-permute-done.1.refs_3_.refs_2_), channel_id=1, source_target_pairs={{0,4},{4,0},{8,12},{12,8},{1,5},{5,1},{9,13},{13,9},{2,6},{6,2},{1... | collective-permute-start | bytes 196616 | tf_op jit(solution)/shard_map/ppermute | solution.py:390
  12.1 5.8 %copy-start.2 = (f32[64,512]{1,0:T(8,128)S(1)}, f32[64,512]{1,0:T(8,128)}, u32[]{:S(2)}) copy-start(f32[64,512]{1,0:T(8,128)} %refs_3_.5) | copy-start | bytes 393220
  12.1 5.8 %copy-start.4 = (f32[512]{0:T(512)S(1)}, f32[512]{0:T(512)}, u32[]{:S(2)}) copy-start(f32[512]{0:T(512)} %param.6) | copy-start | bytes 6148
  14.3 1.6 %collective-permute-start.3 = (f32[576,128]{1,0:T(8,128)S(1)}, f32[576,128]{1,0:T(8,128)S(1)}, u32[]{:S(2)}, u32[]{:S(2)}) collective-permute-start(f32[576,128]{1,0:T(8,128)S(1)} %get-tuple-element.34), channel_id=1, source_target_pairs={{0,1},{1,0},{2,3},{3,2},{4,5},{5,4},{6,7},{7,6},{8,9},{9,8},{10,11... | collective-permute-start | bytes 884744 | tf_op jit(solution)/shard_map/ppermute | solution.py:390
  16.0 8.6 %collective-permute-start.4 = (bf16[576,128]{1,0:T(8,128)(2,1)S(1)}, bf16[576,128]{1,0:T(8,128)(2,1)S(1)}, u32[]{:S(2)}, u32[]{:S(2)}) collective-permute-start(bf16[576,128]{1,0:T(8,128)(2,1)S(1)} %shard_map.72.refs_2_.refs_0_), channel_id=1, source_target_pairs={{0,2},{1,3},{2,0},{3,1},{4,6},{5,7},{6,4},{7,5},{8,10},{9,11},{10,... | collective-permute-start | bytes 442376 | tf_op jit(solution)/shard_map/ppermute | solution.py:390
  17.9 6.6 %collective-permute-start.5 = (bf16[272,128]{1,0:T(8,128)(2,1)S(1)}, bf16[272,128]{1,0:T(8,128)(2,1)S(1)}, u32[]{:S(2)}, u32[]{:S(2)}) collective-permute-start(bf16[272,128]{1,0:T(8,128)(2,1)S(1)} %shard_map.73), channel_id=1, source_target_pairs={{0,8},{4,12},{8,0},{12,4},{1,9},{5,13},{9,1},{13,5},{2,10},{6,14},... | collective-permute-start | bytes 208904 | tf_op jit(solution)/shard_map/ppermute | solution.py:390
  24.6 1.4 %collective-permute-start.6 = (bf16[576,128]{1,0:T(8,128)(2,1)S(1)}, bf16[576,128]{1,0:T(8,128)(2,1)S(1)}, u32[]{:S(2)}, u32[]{:S(2)}) collective-permute-start(bf16[576,128]{1,0:T(8,128)(2,1)S(1)} %shard_map.74.refs_1_), channel_id=1, source_target_pairs={{0,1},{1,0},{2,3},{3,2},{4,5},{5,4},{6,7},{7,6},{8,9},{9,8},{10,11... | collective-permute-start | bytes 442376 | tf_op jit(solution)/shard_map/ppermute | solution.py:390
  27.5 5.3 %collective-permute-start.8 = (bf16[336,128]{1,0:T(8,128)(2,1)S(1)}, bf16[336,128]{1,0:T(8,128)(2,1)S(1)}, u32[]{:S(2)}, u32[]{:S(2)}) collective-permute-start(bf16[336,128]{1,0:T(8,128)(2,1)S(1)} %get-tuple-element.38.refs_0_), channel_id=1, source_target_pairs={{0,4},{4,0},{8,12},{12,8},{1,5},{5,1},{9,13},{13,9},{2,6},{6,2},{1... | collective-permute-start | bytes 258056 | tf_op jit(solution)/shard_map/ppermute | solution.py:390
  27.7 6.7 %collective-permute-start.7 = (bf16[256,128]{1,0:T(8,128)(2,1)S(1)}, bf16[256,128]{1,0:T(8,128)(2,1)S(1)}, u32[]{:S(2)}, u32[]{:S(2)}) collective-permute-start(bf16[256,128]{1,0:T(8,128)(2,1)S(1)} %get-tuple-element.36), channel_id=1, source_target_pairs={{0,4},{4,0},{8,12},{12,8},{1,5},{5,1},{9,13},{13,9},{2,6},{6,2},{1... | collective-permute-start | bytes 196616 | tf_op jit(solution)/shard_map/ppermute | solution.py:390
  32.9 7.3 %collective-permute-start.9 = (bf16[336,128]{1,0:T(8,128)(2,1)S(1)}, bf16[336,128]{1,0:T(8,128)(2,1)S(1)}, u32[]{:S(2)}, u32[]{:S(2)}) collective-permute-start(bf16[336,128]{1,0:T(8,128)(2,1)S(1)} %get-tuple-element.40.refs_0_), channel_id=1, source_target_pairs={{0,8},{4,12},{8,0},{12,4},{1,9},{5,13},{9,1},{13,5},{2,10},{6,14},... | collective-permute-start | bytes 258056 | tf_op jit(solution)/shard_map/ppermute | solution.py:390
  34.4 7.2 %collective-permute-start.11 = (bf16[256,128]{1,0:T(8,128)(2,1)S(1)}, bf16[256,128]{1,0:T(8,128)(2,1)S(1)}, u32[]{:S(2)}, u32[]{:S(2)}) collective-permute-start(bf16[256,128]{1,0:T(8,128)(2,1)S(1)} %get-tuple-element.44), channel_id=1, source_target_pairs={{0,8},{4,12},{8,0},{12,4},{1,9},{5,13},{9,1},{13,5},{2,10},{6,14},... | collective-permute-start | bytes 196616 | tf_op jit(solution)/shard_map/ppermute | solution.py:390
  40.5 4.3 %collective-permute-start.10 = (bf16[256,128]{1,0:T(8,128)(2,1)S(1)}, bf16[256,128]{1,0:T(8,128)(2,1)S(1)}, u32[]{:S(2)}, u32[]{:S(2)}) collective-permute-start(bf16[256,128]{1,0:T(8,128)(2,1)S(1)} %get-tuple-element.43.refs_1_), channel_id=1, source_target_pairs={{0,4},{4,0},{8,12},{12,8},{1,5},{5,1},{9,13},{13,9},{2,6},{6,2},{1... | collective-permute-start | bytes 196616 | tf_op jit(solution)/shard_map/ppermute | solution.py:390
  41.9 4.3 %collective-permute-start.12 = (bf16[256,128]{1,0:T(8,128)(2,1)S(1)}, bf16[256,128]{1,0:T(8,128)(2,1)S(1)}, u32[]{:S(2)}, u32[]{:S(2)}) collective-permute-start(bf16[256,128]{1,0:T(8,128)(2,1)S(1)} %shard_map.79.refs_3_), channel_id=1, source_target_pairs={{0,4},{4,0},{8,12},{12,8},{1,5},{5,1},{9,13},{13,9},{2,6},{6,2},{1... | collective-permute-start | bytes 196616 | tf_op jit(solution)/shard_map/ppermute | solution.py:390
  47.6 1.7 %collective-permute-start.13 = (f32[608,128]{1,0:T(8,128)S(1)}, f32[608,128]{1,0:T(8,128)S(1)}, u32[]{:S(2)}, u32[]{:S(2)}) collective-permute-start(f32[608,128]{1,0:T(8,128)S(1)} %get-tuple-element.49), channel_id=1, source_target_pairs={{0,1},{1,0},{2,3},{3,2},{4,5},{5,4},{6,7},{7,6},{8,9},{9,8},{10,11... | collective-permute-start | bytes 933896 | tf_op jit(solution)/shard_map/ppermute | solution.py:390
  49.3 6.0 %collective-permute-start.14 = (bf16[576,128]{1,0:T(8,128)(2,1)S(1)}, bf16[576,128]{1,0:T(8,128)(2,1)S(1)}, u32[]{:S(2)}, u32[]{:S(2)}) collective-permute-start(bf16[576,128]{1,0:T(8,128)(2,1)S(1)} %get-tuple-element.50.refs_0_), channel_id=1, source_target_pairs={{0,2},{1,3},{2,0},{3,1},{4,6},{5,7},{6,4},{7,5},{8,10},{9,11},{10,... | collective-permute-start | bytes 442376 | tf_op jit(solution)/shard_map/ppermute | solution.py:390
  55.3 1.4 %collective-permute-start.15 = (bf16[576,128]{1,0:T(8,128)(2,1)S(1)}, bf16[576,128]{1,0:T(8,128)(2,1)S(1)}, u32[]{:S(2)}, u32[]{:S(2)}) collective-permute-start(bf16[576,128]{1,0:T(8,128)(2,1)S(1)} %shard_map.84.refs_1_.refs_0_), channel_id=1, source_target_pairs={{0,1},{1,0},{2,3},{3,2},{4,5},{5,4},{6,7},{7,6},{8,9},{9,8},{10,11... | collective-permute-start | bytes 442376 | tf_op jit(solution)/shard_map/ppermute | solution.py:390
  57.1 3.8 %collective-permute-start.19 = (bf16[64,128]{1,0:T(8,128)(2,1)S(1)}, bf16[64,128]{1,0:T(8,128)(2,1)S(1)}, u32[]{:S(2)}, u32[]{:S(2)}) collective-permute-start(bf16[64,128]{1,0:T(8,128)(2,1)S(1)} %shard_map.87.refs_0_), channel_id=1, source_target_pairs={{0,4},{4,0},{8,12},{12,8},{1,5},{5,1},{9,13},{13,9},{2,6},{6,2},{1... | collective-permute-start | bytes 49160 | tf_op jit(solution)/shard_map/ppermute | solution.py:390
  59.3 5.3 %collective-permute-start.17 = (bf16[256,128]{1,0:T(8,128)(2,1)S(1)}, bf16[256,128]{1,0:T(8,128)(2,1)S(1)}, u32[]{:S(2)}, u32[]{:S(2)}) collective-permute-start(bf16[256,128]{1,0:T(8,128)(2,1)S(1)} %get-tuple-element.54.refs_0_), channel_id=1, source_target_pairs={{0,4},{4,0},{8,12},{12,8},{1,5},{5,1},{9,13},{13,9},{2,6},{6,2},{1... | collective-permute-start | bytes 196616 | tf_op jit(solution)/shard_map/ppermute | solution.py:390
  61.0 6.0 %collective-permute-start.20 = (bf16[64,128]{1,0:T(8,128)(2,1)S(1)}, bf16[64,128]{1,0:T(8,128)(2,1)S(1)}, u32[]{:S(2)}, u32[]{:S(2)}) collective-permute-start(bf16[64,128]{1,0:T(8,128)(2,1)S(1)} %get-tuple-element.58), channel_id=1, source_target_pairs={{0,8},{4,12},{8,0},{12,4},{1,9},{5,13},{9,1},{13,5},{2,10},{6,14},... | collective-permute-start | bytes 49160 | tf_op jit(solution)/shard_map/ppermute | solution.py:390
  63.5 6.4 %collective-permute-start.16 = (bf16[256,128]{1,0:T(8,128)(2,1)S(1)}, bf16[256,128]{1,0:T(8,128)(2,1)S(1)}, u32[]{:S(2)}, u32[]{:S(2)}) collective-permute-start(bf16[256,128]{1,0:T(8,128)(2,1)S(1)} %get-tuple-element.53), channel_id=1, source_target_pairs={{0,4},{4,0},{8,12},{12,8},{1,5},{5,1},{9,13},{13,9},{2,6},{6,2},{1... | collective-permute-start | bytes 196616 | tf_op jit(solution)/shard_map/ppermute | solution.py:390
  64.6 5.9 %collective-permute-start.18 = (bf16[256,128]{1,0:T(8,128)(2,1)S(1)}, bf16[256,128]{1,0:T(8,128)(2,1)S(1)}, u32[]{:S(2)}, u32[]{:S(2)}) collective-permute-start(bf16[256,128]{1,0:T(8,128)(2,1)S(1)} %shard_map.86), channel_id=1, source_target_pairs={{0,8},{4,12},{8,0},{12,4},{1,9},{5,13},{9,1},{13,5},{2,10},{6,14},... | collective-permute-start | bytes 196616 | tf_op jit(solution)/shard_map/ppermute | solution.py:390

commit v16 on v15

--- a/solution.py
+++ b/solution.py
@@ -213,14 +213,16 @@
     out_ref[at + frames :, :] = jnp.where(row == 0, diagonal, 0.0).astype(BF16)
 
 
-def rows_kernel(frames, sent, received, kept, out_refs, extra_refs):
+def rows_kernel(frames, sent, received, kept, later, out_refs, extra_refs):
     split_at = frames // 2
     data = kept[0].shape[0]
     for out_ref, kept_ref, received_ref in zip(out_refs, kept, received):
         for j in range(data // frames):
             at = rows(j, frames)
             out_ref[at, :] = (kept_ref[at, :] + received_ref[at, :].astype(F32)).astype(BF16)
-    if extra_refs:
+    if later:
+        extra_refs[0][...] = later[0][...]
+    else:
         pair = (sent, received[0])
         high, low = slice(data, data + split_at), slice(data + split_at, data + frames)
         value = sum_rows(pair, high) + sum_rows(pair, low)
@@ -373,7 +375,7 @@
     out_ref[n:, :] = gamma
 
 
-def final_kernel(keep, near, far, v_ref, image_ref, next_ref, prior, coeffs_ref, x_ref, r_ref):
+def final_kernel(keep, far, near, v_ref, image_ref, next_ref, prior, coeffs_ref, x_ref, r_ref):
     n = v_ref.shape[0]
     coeffs = coeffs_ref[...]
     for j in range(keep.shape[0] // n):
@@ -472,20 +474,20 @@
             ],
         )
         received = tuple(swapped(x, "row", 1) for x in far)
-        near = swapped(near, "row", 1)
         sums, gram = call(
             lambda *refs: rows_kernel(frames, *refs),
             (
                 (shape((size + extra, BLOCK), BF16),) * pairs,
-                ()
+                (cast_type,)
                 if last
                 else (shape((frames // 2, 2 * frames)), shape((DIAG, 2 * frames), BF16)),
             ),
-            (far[0], received, kept),
+            (far[0], received, kept, (near,) if last else ()),
         )
         far = tuple(swapped(x, "row", 2 * (p + 1)) for p, x in enumerate(sums))
+        near = swapped(gram[0] if last else near, "row", 1)
         if last:
-            return (keep, near, far), norm
+            return (keep, far, near), norm
         return (keep, near, far, *gram), sums
 
     (cast,) = call(cast_kernel, (cast_type,), (right_side,))

time: 72 us -> 72.2 us (level)
  transfers between devices with their start and end apart: 21 -> 21, of which waited for: 15 -> 16; matrix products, arithmetic and copies ran while one was open for 0% -> 0% of each run, Pallas kernels for 13% -> 13%
where the time goes in v16:
time: 72.2 us; the launch traced here: 72 us
  waiting for transfers between devices  27.3 us (38%)
  starting transfers between devices  26.9 us (37%)
  Pallas kernels  15.4 us (21%)
  local copies, waits for them, and re-layouts  1.6 us (2%)
  between operations  0.82 us (1%)
    ppermute x21, waiting for transfers between devices, swapped(): lax.ppermute(x, axis, [(i, i ^ flip) for i in range(lax.axis_size(axis))])  27.3 us
    ppermute x21, starting transfers between devices, swapped(): lax.ppermute(x, axis, [(i, i ^ flip) for i in range(lax.axis_size(axis))])  26.9 us
    pallas_call x23, Pallas kernels, call(): pl.pallas_call(body, out_shape=flat_outs, in_specs=[space(x) for x in fla...  15.4 us
    unnamed x14, local copies, waits for them, and re-layouts  1.6 us
  transfers between devices with their start and end apart: 21, of which 16 were waited for; matrix products, arithmetic and copies ran while one was open for 0% of the time, Pallas kernels for 13%

profile of v16, /device:TPU:0, one launch (start us, length us, event | category | flops | bytes accessed | tf_op | source)
XLA Modules:
  0.0 72.0 jit_solution(13097763337074284840)
XLA Ops:
  1.5 4.1 %collective-permute-start.1 = (bf16[256,128]{1,0:T(8,128)(2,1)S(1)}, bf16[256,128]{1,0:T(8,128)(2,1)S(1)}, u32[]{:S(2)}, u32[]{:S(2)}) collective-permute-start(bf16[256,128]{1,0:T(8,128)(2,1)S(1)} %shard_map.69.refs_1_), channel_id=1, source_target_pairs={{0,8},{4,12},{8,0},{12,4},{1,9},{5,13},{9,1},{13,5},{2,10},{6,14},... | collective-permute-start | bytes 196616 | tf_op jit(solution)/shard_map/ppermute | solution.py:392
  5.7 1.6 %collective-permute-start = (bf16[256,128]{1,0:T(8,128)(2,1)S(1)}, bf16[256,128]{1,0:T(8,128)(2,1)S(1)}, u32[]{:S(2)}, u32[]{:S(2)}) collective-permute-start(bf16[256,128]{1,0:T(8,128)(2,1)S(1)} %shard_map.69.refs_1_), channel_id=1, source_target_pairs={{0,4},{4,0},{8,12},{12,8},{1,5},{5,1},{9,13},{13,9},{2,6},{6,2},{1... | collective-permute-start | bytes 196616 | tf_op jit(solution)/shard_map/ppermute | solution.py:392
  8.7 1.4 %collective-permute-start.2 = (bf16[256,128]{1,0:T(8,128)(2,1)S(1)}, bf16[256,128]{1,0:T(8,128)(2,1)S(1)}, u32[]{:S(2)}, u32[]{:S(2)}) collective-permute-start(bf16[256,128]{1,0:T(8,128)(2,1)S(1)} %collective-permute-done.1.refs_3_.refs_2_), channel_id=1, source_target_pairs={{0,4},{4,0},{8,12},{12,8},{1,5},{5,1},{9,13},{13,9},{2,6},{6,2},{1... | collective-permute-start | bytes 196616 | tf_op jit(solution)/shard_map/ppermute | solution.py:392
  10.1 2.0 %shard_map.68 = (s32[2,64]{1,0:T(2,128)S(1)}, bf16[64,128,128]{2,1,0:T(8,128)(2,1)S(1)}) custom-call(s32[64]{0:T(128)S(1)} %copy-done.5, s32[64]{0:T(128)S(1)} %copy-done.6, bf16[64,128,128]{2,1,0:T(8,128)(2,1)S(1)} %copy-done), custom_call_target="tpu_custom_call" | custom-call | flops 2000000000 | bytes 8000000 | tf_op jit(solution)/shard_map/pallas_call | solution.py:51
  13.0 1.3 %shard_map.71 = (f32[576,128]{1,0:T(8,128)S(1)}, f32[576,128]{1,0:T(8,128)S(1)}) custom-call(s32[2,64]{1,0:T(2,128)S(1)} %get-tuple-element.33.refs_0_, bf16[256,128]{1,0:T(8,128)(2,1)S(1)} %shard_map.69.refs_1_, bf16[256,128]{1,0:T(8,128)(2,1)S(1)} %collective-permute-done.refs_2_, bf16[256,128]{1,0:T(8,128)(2,1)S(1)} %collective-permute-done.1.refs_3_.refs_2_, ...), custom_call_target="tpu_custom_call" | custom-call | tf_op jit(solution)/shard_map/pallas_call | solution.py:51
  14.4 1.6 %collective-permute-done.3.refs_1_ = f32[576,128]{1,0:T(8,128)S(1)} collective-permute-done((f32[576,128]{1,0:T(8,128)S(1)}, f32[576,128]{1,0:T(8,128)S(1)}, u32[]{:S(2)}, u32[]{:S(2)}) %collective-permute-start.3) | collective-permute-done | bytes 294944 | tf_op jit(solution)/shard_map/ppermute | solution.py:392
  16.0 1.9 %collective-permute-start.4 = (bf16[576,128]{1,0:T(8,128)(2,1)S(1)}, bf16[576,128]{1,0:T(8,128)(2,1)S(1)}, u32[]{:S(2)}, u32[]{:S(2)}) collective-permute-start(bf16[576,128]{1,0:T(8,128)(2,1)S(1)} %shard_map.72.refs_2_.refs_0_), channel_id=1, source_target_pairs={{0,2},{1,3},{2,0},{3,1},{4,6},{5,7},{6,4},{7,5},{8,10},{9,11},{10,... | collective-permute-start | bytes 442376 | tf_op jit(solution)/shard_map/ppermute | solution.py:392
  17.9 2.4 %collective-permute-start.5 = (bf16[272,128]{1,0:T(8,128)(2,1)S(1)}, bf16[272,128]{1,0:T(8,128)(2,1)S(1)}, u32[]{:S(2)}, u32[]{:S(2)}) collective-permute-start(bf16[272,128]{1,0:T(8,128)(2,1)S(1)} %shard_map.73), channel_id=1, source_target_pairs={{0,8},{4,12},{8,0},{12,4},{1,9},{5,13},{9,1},{13,5},{2,10},{6,14},... | collective-permute-start | bytes 208904 | tf_op jit(solution)/shard_map/ppermute | solution.py:392
  20.3 4.3 %collective-permute-done.5.refs_2_.refs_3_ = bf16[272,128]{1,0:T(8,128)(2,1)S(1)} collective-permute-done((bf16[272,128]{1,0:T(8,128)(2,1)S(1)}, bf16[272,128]{1,0:T(8,128)(2,1)S(1)}, u32[]{:S(2)}, u32[]{:S(2)}) %collective-permute-start.5) | collective-permute-done | bytes 69664 | tf_op jit(solution)/shard_map/ppermute | solution.py:392
  24.7 1.4 %collective-permute-done.6.refs_2_ = bf16[576,128]{1,0:T(8,128)(2,1)S(1)} collective-permute-done((bf16[576,128]{1,0:T(8,128)(2,1)S(1)}, bf16[576,128]{1,0:T(8,128)(2,1)S(1)}, u32[]{:S(2)}, u32[]{:S(2)}) %collective-permute-start.6) | collective-permute-done | bytes 147488 | tf_op jit(solution)/shard_map/ppermute | solution.py:392
  26.0 1.5 %shard_map.75 = (bf16[336,128]{1,0:T(8,128)(2,1)S(1)}, bf16[256,128]{1,0:T(8,128)(2,1)S(1)}, f32[256,128]{1,0:T(8,128)S(1)}, f32[256,128]{1,0:T(8,128)S(1)}) custom-call(s32[2,64]{1,0:T(2,128)S(1)} %get-tuple-element.33.refs_0_, bf16[576,128]{1,0:T(8,128)(2,1)S(1)} %shard_map.74.refs_1_, bf16[576,128]{1,0:T(8,128)(2,1)S(1)} %collective-permute-done.6.refs_2_, ...), custom_call_target="tpu_custom_call" | custom-call | tf_op jit(solution)/shard_map/pallas_call | solution.py:51
  27.7 1.9 %collective-permute-start.7 = (bf16[256,128]{1,0:T(8,128)(2,1)S(1)}, bf16[256,128]{1,0:T(8,128)(2,1)S(1)}, u32[]{:S(2)}, u32[]{:S(2)}) collective-permute-start(bf16[256,128]{1,0:T(8,128)(2,1)S(1)} %get-tuple-element.38), channel_id=1, source_target_pairs={{0,4},{4,0},{8,12},{12,8},{1,5},{5,1},{9,13},{13,9},{2,6},{6,2},{1... | collective-permute-start | bytes 196616 | tf_op jit(solution)/shard_map/ppermute | solution.py:392
  29.6 3.3 %collective-permute-done.8.refs_1_ = bf16[336,128]{1,0:T(8,128)(2,1)S(1)} collective-permute-done((bf16[336,128]{1,0:T(8,128)(2,1)S(1)}, bf16[336,128]{1,0:T(8,128)(2,1)S(1)}, u32[]{:S(2)}, u32[]{:S(2)}) %collective-permute-start.8) | collective-permute-done | bytes 86048 | tf_op jit(solution)/shard_map/ppermute | solution.py:392
  32.9 1.5 %collective-permute-start.9 = (bf16[336,128]{1,0:T(8,128)(2,1)S(1)}, bf16[336,128]{1,0:T(8,128)(2,1)S(1)}, u32[]{:S(2)}, u32[]{:S(2)}) collective-permute-start(bf16[336,128]{1,0:T(8,128)(2,1)S(1)} %get-tuple-element.42.refs_0_), channel_id=1, source_target_pairs={{0,8},{4,12},{8,0},{12,4},{1,9},{5,13},{9,1},{13,5},{2,10},{6,14},... | collective-permute-start | bytes 258056 | tf_op jit(solution)/shard_map/ppermute | solution.py:392
  34.4 1.5 %collective-permute-start.11 = (bf16[256,128]{1,0:T(8,128)(2,1)S(1)}, bf16[256,128]{1,0:T(8,128)(2,1)S(1)}, u32[]{:S(2)}, u32[]{:S(2)}) collective-permute-start(bf16[256,128]{1,0:T(8,128)(2,1)S(1)} %get-tuple-element.46), channel_id=1, source_target_pairs={{0,8},{4,12},{8,0},{12,4},{1,9},{5,13},{9,1},{13,5},{2,10},{6,14},... | collective-permute-start | bytes 196616 | tf_op jit(solution)/shard_map/ppermute | solution.py:392
  36.0 4.2 %collective-permute-done.9.refs_1_ = bf16[336,128]{1,0:T(8,128)(2,1)S(1)} collective-permute-done((bf16[336,128]{1,0:T(8,128)(2,1)S(1)}, bf16[336,128]{1,0:T(8,128)(2,1)S(1)}, u32[]{:S(2)}, u32[]{:S(2)}) %collective-permute-start.9) | collective-permute-done | bytes 86048 | tf_op jit(solution)/shard_map/ppermute | solution.py:392
  41.9 1.0 %collective-permute-start.12 = (bf16[256,128]{1,0:T(8,128)(2,1)S(1)}, bf16[256,128]{1,0:T(8,128)(2,1)S(1)}, u32[]{:S(2)}, u32[]{:S(2)}) collective-permute-start(bf16[256,128]{1,0:T(8,128)(2,1)S(1)} %shard_map.79.refs_3_), channel_id=1, source_target_pairs={{0,4},{4,0},{8,12},{12,8},{1,5},{5,1},{9,13},{13,9},{2,6},{6,2},{1... | collective-permute-start | bytes 196616 | tf_op jit(solution)/shard_map/ppermute | solution.py:392
  43.3 1.5 %collective-permute-done.10.refs_2_ = bf16[256,128]{1,0:T(8,128)(2,1)S(1)} collective-permute-done((bf16[256,128]{1,0:T(8,128)(2,1)S(1)}, bf16[256,128]{1,0:T(8,128)(2,1)S(1)}, u32[]{:S(2)}, u32[]{:S(2)}) %collective-permute-start.10) | collective-permute-done | bytes 65568 | tf_op jit(solution)/shard_map/ppermute | solution.py:392
  44.8 1.4 %collective-permute-done.12.refs_4_ = bf16[256,128]{1,0:T(8,128)(2,1)S(1)} collective-permute-done((bf16[256,128]{1,0:T(8,128)(2,1)S(1)}, bf16[256,128]{1,0:T(8,128)(2,1)S(1)}, u32[]{:S(2)}, u32[]{:S(2)}) %collective-permute-start.12) | collective-permute-done | bytes 65568 | tf_op jit(solution)/shard_map/ppermute | solution.py:392
  46.2 1.4 %shard_map.81 = (f32[608,128]{1,0:T(8,128)S(1)}, f32[608,128]{1,0:T(8,128)S(1)}) custom-call(s32[2,64]{1,0:T(2,128)S(1)} %get-tuple-element.33.refs_0_, bf16[256,128]{1,0:T(8,128)(2,1)S(1)} %get-tuple-element.45.refs_1_, bf16[256,128]{1,0:T(8,128)(2,1)S(1)} %collective-permute-done.10.refs_2_, bf16[256,128]{1,0:T(8,128)(2,1)S(1)} %shard_map.79.refs_3_, ...), custom_call_target="tpu_custom_call" | custom-call | tf_op jit(solution)/shard_map/pallas_call | solution.py:51
  47.7 1.6 %collective-permute-done.13.refs_1_ = f32[608,128]{1,0:T(8,128)S(1)} collective-permute-done((f32[608,128]{1,0:T(8,128)S(1)}, f32[608,128]{1,0:T(8,128)S(1)}, u32[]{:S(2)}, u32[]{:S(2)}) %collective-permute-start.13) | collective-permute-done | bytes 311328 | tf_op jit(solution)/shard_map/ppermute | solution.py:392
  49.9 1.7 %shard_map.83.refs_2_.refs_3_ = f32[64,64]{1,0:T(8,128)S(1)} custom-call(f32[64,128]{1,0:T(8,128)S(1)} %get-tuple-element.53.refs_0_.refs_2_), custom_call_target="tpu_custom_call" | custom-call | flops 2000000000 | bytes 8000000 | tf_op jit(solution)/shard_map/pallas_call | solution.py:51
  51.6 3.6 %collective-permute-done.14.refs_1_ = bf16[576,128]{1,0:T(8,128)(2,1)S(1)} collective-permute-done((bf16[576,128]{1,0:T(8,128)(2,1)S(1)}, bf16[576,128]{1,0:T(8,128)(2,1)S(1)}, u32[]{:S(2)}, u32[]{:S(2)}) %collective-permute-start.14) | collective-permute-done | bytes 147488 | tf_op jit(solution)/shard_map/ppermute | solution.py:392
  55.4 1.4 %collective-permute-done.15.refs_2_.refs_1_ = bf16[576,128]{1,0:T(8,128)(2,1)S(1)} collective-permute-done((bf16[576,128]{1,0:T(8,128)(2,1)S(1)}, bf16[576,128]{1,0:T(8,128)(2,1)S(1)}, u32[]{:S(2)}, u32[]{:S(2)}) %collective-permute-start.15) | collective-permute-done | bytes 147488 | tf_op jit(solution)/shard_map/ppermute | solution.py:392
  57.1 1.0 %collective-permute-start.19 = (bf16[64,128]{1,0:T(8,128)(2,1)S(1)}, bf16[64,128]{1,0:T(8,128)(2,1)S(1)}, u32[]{:S(2)}, u32[]{:S(2)}) collective-permute-start(bf16[64,128]{1,0:T(8,128)(2,1)S(1)} %shard_map.87.refs_0_), channel_id=1, source_target_pairs={{0,4},{4,0},{8,12},{12,8},{1,5},{5,1},{9,13},{13,9},{2,6},{6,2},{1... | collective-permute-start | bytes 49160 | tf_op jit(solution)/shard_map/ppermute | solution.py:392
  58.0 1.3 %shard_map.85 = (bf16[256,128]{1,0:T(8,128)(2,1)S(1)}, bf16[256,128]{1,0:T(8,128)(2,1)S(1)}, f32[256,128]{1,0:T(8,128)S(1)}, f32[256,128]{1,0:T(8,128)S(1)}, f32[64,64]{1,0:T(8,128)S(1)}) custom-call(s32[2,64]{1,0:T(2,128)S(1)} %get-tuple-element.33.refs_0_, bf16[576,128]{1,0:T(8,128)(2,1)S(1)} %shard_map.84.refs_1_.refs_0_, ...), custom_call_target="tpu_custom_call" | custom-call | tf_op jit(solution)/shard_map/pallas_call | solution.py:51
  59.4 1.2 %collective-permute-start.16 = (bf16[256,128]{1,0:T(8,128)(2,1)S(1)}, bf16[256,128]{1,0:T(8,128)(2,1)S(1)}, u32[]{:S(2)}, u32[]{:S(2)}) collective-permute-start(bf16[256,128]{1,0:T(8,128)(2,1)S(1)} %get-tuple-element.55.refs_0_), channel_id=1, source_target_pairs={{0,4},{4,0},{8,12},{12,8},{1,5},{5,1},{9,13},{13,9},{2,6},{6,2},{1... | collective-permute-start | bytes 196616 | tf_op jit(solution)/shard_map/ppermute | solution.py:392
  61.0 2.5 %collective-permute-start.20 = (bf16[64,128]{1,0:T(8,128)(2,1)S(1)}, bf16[64,128]{1,0:T(8,128)(2,1)S(1)}, u32[]{:S(2)}, u32[]{:S(2)}) collective-permute-start(bf16[64,128]{1,0:T(8,128)(2,1)S(1)} %get-tuple-element.62), channel_id=1, source_target_pairs={{0,8},{4,12},{8,0},{12,4},{1,9},{5,13},{9,1},{13,5},{2,10},{6,14},... | collective-permute-start | bytes 49160 | tf_op jit(solution)/shard_map/ppermute | solution.py:392
  63.7 2.7 %collective-permute-start.17 = (bf16[256,128]{1,0:T(8,128)(2,1)S(1)}, bf16[256,128]{1,0:T(8,128)(2,1)S(1)}, u32[]{:S(2)}, u32[]{:S(2)}) collective-permute-start(bf16[256,128]{1,0:T(8,128)(2,1)S(1)} %get-tuple-element.58), channel_id=1, source_target_pairs={{0,8},{4,12},{8,0},{12,4},{1,9},{5,13},{9,1},{13,5},{2,10},{6,14},... | collective-permute-start | bytes 196616 | tf_op jit(solution)/shard_map/ppermute | solution.py:392
  66.4 0.9 %collective-permute-start.18 = (bf16[256,128]{1,0:T(8,128)(2,1)S(1)}, bf16[256,128]{1,0:T(8,128)(2,1)S(1)}, u32[]{:S(2)}, u32[]{:S(2)}) collective-permute-start(bf16[256,128]{1,0:T(8,128)(2,1)S(1)} %get-tuple-element.59), channel_id=1, source_target_pairs={{0,4},{4,0},{8,12},{12,8},{1,5},{5,1},{9,13},{13,9},{2,6},{6,2},{1... | collective-permute-start | bytes 196616 | tf_op jit(solution)/shard_map/ppermute | solution.py:392
  67.4 2.9 %shard_map.89.refs_7_ = f32[128,64]{1,0:T(8,128)S(1)} custom-call(f32[64,64]{1,0:T(8,128)S(1)} %get-tuple-element.61.refs_0_, bf16[64,128]{1,0:T(8,128)(2,1)S(1)} %collective-permute-done.20.refs_1_, f32[64,128]{1,0:T(8,128)S(1)} %get-tuple-element.53.refs_0_.refs_2_, f32[64,64]{1,0:T(8,128)S(1)} %shard_map.83.refs_2_.refs_3_, ...), custom_call_target="tpu_custom_call" | custom-call | flops 2000000000 | bytes 8000000 | tf_op jit(solution)/shard_map/pallas_call | solution.py:51
  70.7 1.3 %shard_map.90 = (f32[64,512]{1,0:T(8,128)}, f32[64,512]{1,0:T(8,128)}) custom-call(f32[256,128]{1,0:T(8,128)S(1)} %get-tuple-element.54.refs_0_, bf16[256,128]{1,0:T(8,128)(2,1)S(1)} %collective-permute-done.17.refs_1_, bf16[256,128]{1,0:T(8,128)(2,1)S(1)} %collective-permute-done.18.refs_2_, f32[64,512]{1,0:T(8,128)S(1)} %copy-done.2, ...), custom_call_target="tpu_custom_call" | custom-call | tf_op jit(solution)/shard_map/pallas_call | solution.py:51
  (47 shorter events, 8.0 us)
Async XLA Ops:
  0.6 0.9 %copy-start.1 = (f32[64,512]{1,0:T(8,128)S(1)}, f32[64,512]{1,0:T(8,128)}, u32[]{:S(2)}) copy-start(f32[64,512]{1,0:T(8,128)} %refs_3_.5) | copy-start | bytes 393220
  1.5 7.2 %collective-permute-start.1 = (bf16[256,128]{1,0:T(8,128)(2,1)S(1)}, bf16[256,128]{1,0:T(8,128)(2,1)S(1)}, u32[]{:S(2)}, u32[]{:S(2)}) collective-permute-start(bf16[256,128]{1,0:T(8,128)(2,1)S(1)} %shard_map.69.refs_1_), channel_id=1, source_target_pairs={{0,8},{4,12},{8,0},{12,4},{1,9},{5,13},{9,1},{13,5},{2,10},{6,14},... | collective-permute-start | bytes 196616 | tf_op jit(solution)/shard_map/ppermute | solution.py:392
  5.7 6.5 %collective-permute-start = (bf16[256,128]{1,0:T(8,128)(2,1)S(1)}, bf16[256,128]{1,0:T(8,128)(2,1)S(1)}, u32[]{:S(2)}, u32[]{:S(2)}) collective-permute-start(bf16[256,128]{1,0:T(8,128)(2,1)S(1)} %shard_map.69.refs_1_), channel_id=1, source_target_pairs={{0,4},{4,0},{8,12},{12,8},{1,5},{5,1},{9,13},{13,9},{2,6},{6,2},{1... | collective-permute-start | bytes 196616 | tf_op jit(solution)/shard_map/ppermute | solution.py:392
  7.2 0.7 copy-start.3
  7.9 2.2 %copy-start = (bf16[64,128,128]{2,1,0:T(8,128)(2,1)S(1)}, bf16[64,128,128]{2,1,0:T(8,128)(2,1)}, u32[]{:S(2)}) copy-start(bf16[64,128,128]{2,1,0:T(8,128)(2,1)} %refs_3_.4) | copy-start | bytes 6291460
  7.9 2.2 %copy-start.5 = (s32[64]{0:T(128)S(1)}, s32[64]{0:T(128)}, u32[]{:S(2)}) copy-start(s32[64]{0:T(128)} %refs_0_.4) | copy-start | bytes 772
  7.9 2.2 %copy-start.6 = (s32[64]{0:T(128)S(1)}, s32[64]{0:T(128)}, u32[]{:S(2)}) copy-start(s32[64]{0:T(128)} %refs_1_.1) | copy-start | bytes 772
  8.7 4.3 %collective-permute-start.2 = (bf16[256,128]{1,0:T(8,128)(2,1)S(1)}, bf16[256,128]{1,0:T(8,128)(2,1)S(1)}, u32[]{:S(2)}, u32[]{:S(2)}) collective-permute-start(bf16[256,128]{1,0:T(8,128)(2,1)S(1)} %collective-permute-done.1.refs_3_.refs_2_), channel_id=1, source_target_pairs={{0,4},{4,0},{8,12},{12,8},{1,5},{5,1},{9,13},{13,9},{2,6},{6,2},{1... | collective-permute-start | bytes 196616 | tf_op jit(solution)/shard_map/ppermute | solution.py:392
  12.1 5.8 %copy-start.2 = (f32[64,512]{1,0:T(8,128)S(1)}, f32[64,512]{1,0:T(8,128)}, u32[]{:S(2)}) copy-start(f32[64,512]{1,0:T(8,128)} %refs_3_.5) | copy-start | bytes 393220
  12.1 5.8 %copy-start.4 = (f32[512]{0:T(512)S(1)}, f32[512]{0:T(512)}, u32[]{:S(2)}) copy-start(f32[512]{0:T(512)} %param.6) | copy-start | bytes 6148
  14.3 1.6 %collective-permute-start.3 = (f32[576,128]{1,0:T(8,128)S(1)}, f32[576,128]{1,0:T(8,128)S(1)}, u32[]{:S(2)}, u32[]{:S(2)}) collective-permute-start(f32[576,128]{1,0:T(8,128)S(1)} %get-tuple-element.36), channel_id=1, source_target_pairs={{0,1},{1,0},{2,3},{3,2},{4,5},{5,4},{6,7},{7,6},{8,9},{9,8},{10,11... | collective-permute-start | bytes 884744 | tf_op jit(solution)/shard_map/ppermute | solution.py:392
  16.0 8.6 %collective-permute-start.4 = (bf16[576,128]{1,0:T(8,128)(2,1)S(1)}, bf16[576,128]{1,0:T(8,128)(2,1)S(1)}, u32[]{:S(2)}, u32[]{:S(2)}) collective-permute-start(bf16[576,128]{1,0:T(8,128)(2,1)S(1)} %shard_map.72.refs_2_.refs_0_), channel_id=1, source_target_pairs={{0,2},{1,3},{2,0},{3,1},{4,6},{5,7},{6,4},{7,5},{8,10},{9,11},{10,... | collective-permute-start | bytes 442376 | tf_op jit(solution)/shard_map/ppermute | solution.py:392
  17.9 6.6 %collective-permute-start.5 = (bf16[272,128]{1,0:T(8,128)(2,1)S(1)}, bf16[272,128]{1,0:T(8,128)(2,1)S(1)}, u32[]{:S(2)}, u32[]{:S(2)}) collective-permute-start(bf16[272,128]{1,0:T(8,128)(2,1)S(1)} %shard_map.73), channel_id=1, source_target_pairs={{0,8},{4,12},{8,0},{12,4},{1,9},{5,13},{9,1},{13,5},{2,10},{6,14},... | collective-permute-start | bytes 208904 | tf_op jit(solution)/shard_map/ppermute | solution.py:392
  24.6 1.4 %collective-permute-start.6 = (bf16[576,128]{1,0:T(8,128)(2,1)S(1)}, bf16[576,128]{1,0:T(8,128)(2,1)S(1)}, u32[]{:S(2)}, u32[]{:S(2)}) collective-permute-start(bf16[576,128]{1,0:T(8,128)(2,1)S(1)} %shard_map.74.refs_1_), channel_id=1, source_target_pairs={{0,1},{1,0},{2,3},{3,2},{4,5},{5,4},{6,7},{7,6},{8,9},{9,8},{10,11... | collective-permute-start | bytes 442376 | tf_op jit(solution)/shard_map/ppermute | solution.py:392
  27.5 5.4 %collective-permute-start.8 = (bf16[336,128]{1,0:T(8,128)(2,1)S(1)}, bf16[336,128]{1,0:T(8,128)(2,1)S(1)}, u32[]{:S(2)}, u32[]{:S(2)}) collective-permute-start(bf16[336,128]{1,0:T(8,128)(2,1)S(1)} %get-tuple-element.40.refs_0_), channel_id=1, source_target_pairs={{0,4},{4,0},{8,12},{12,8},{1,5},{5,1},{9,13},{13,9},{2,6},{6,2},{1... | collective-permute-start | bytes 258056 | tf_op jit(solution)/shard_map/ppermute | solution.py:392
  27.7 6.7 %collective-permute-start.7 = (bf16[256,128]{1,0:T(8,128)(2,1)S(1)}, bf16[256,128]{1,0:T(8,128)(2,1)S(1)}, u32[]{:S(2)}, u32[]{:S(2)}) collective-permute-start(bf16[256,128]{1,0:T(8,128)(2,1)S(1)} %get-tuple-element.38), channel_id=1, source_target_pairs={{0,4},{4,0},{8,12},{12,8},{1,5},{5,1},{9,13},{13,9},{2,6},{6,2},{1... | collective-permute-start | bytes 196616 | tf_op jit(solution)/shard_map/ppermute | solution.py:392
  32.9 7.3 %collective-permute-start.9 = (bf16[336,128]{1,0:T(8,128)(2,1)S(1)}, bf16[336,128]{1,0:T(8,128)(2,1)S(1)}, u32[]{:S(2)}, u32[]{:S(2)}) collective-permute-start(bf16[336,128]{1,0:T(8,128)(2,1)S(1)} %get-tuple-element.42.refs_0_), channel_id=1, source_target_pairs={{0,8},{4,12},{8,0},{12,4},{1,9},{5,13},{9,1},{13,5},{2,10},{6,14},... | collective-permute-start | bytes 258056 | tf_op jit(solution)/shard_map/ppermute | solution.py:392
  34.4 7.2 %collective-permute-start.11 = (bf16[256,128]{1,0:T(8,128)(2,1)S(1)}, bf16[256,128]{1,0:T(8,128)(2,1)S(1)}, u32[]{:S(2)}, u32[]{:S(2)}) collective-permute-start(bf16[256,128]{1,0:T(8,128)(2,1)S(1)} %get-tuple-element.46), channel_id=1, source_target_pairs={{0,8},{4,12},{8,0},{12,4},{1,9},{5,13},{9,1},{13,5},{2,10},{6,14},... | collective-permute-start | bytes 196616 | tf_op jit(solution)/shard_map/ppermute | solution.py:392
  40.5 4.3 %collective-permute-start.10 = (bf16[256,128]{1,0:T(8,128)(2,1)S(1)}, bf16[256,128]{1,0:T(8,128)(2,1)S(1)}, u32[]{:S(2)}, u32[]{:S(2)}) collective-permute-start(bf16[256,128]{1,0:T(8,128)(2,1)S(1)} %get-tuple-element.45.refs_1_), channel_id=1, source_target_pairs={{0,4},{4,0},{8,12},{12,8},{1,5},{5,1},{9,13},{13,9},{2,6},{6,2},{1... | collective-permute-start | bytes 196616 | tf_op jit(solution)/shard_map/ppermute | solution.py:392
  41.9 4.3 %collective-permute-start.12 = (bf16[256,128]{1,0:T(8,128)(2,1)S(1)}, bf16[256,128]{1,0:T(8,128)(2,1)S(1)}, u32[]{:S(2)}, u32[]{:S(2)}) collective-permute-start(bf16[256,128]{1,0:T(8,128)(2,1)S(1)} %shard_map.79.refs_3_), channel_id=1, source_target_pairs={{0,4},{4,0},{8,12},{12,8},{1,5},{5,1},{9,13},{13,9},{2,6},{6,2},{1... | collective-permute-start | bytes 196616 | tf_op jit(solution)/shard_map/ppermute | solution.py:392
  47.6 1.7 %collective-permute-start.13 = (f32[608,128]{1,0:T(8,128)S(1)}, f32[608,128]{1,0:T(8,128)S(1)}, u32[]{:S(2)}, u32[]{:S(2)}) collective-permute-start(f32[608,128]{1,0:T(8,128)S(1)} %get-tuple-element.51), channel_id=1, source_target_pairs={{0,1},{1,0},{2,3},{3,2},{4,5},{5,4},{6,7},{7,6},{8,9},{9,8},{10,11... | collective-permute-start | bytes 933896 | tf_op jit(solution)/shard_map/ppermute | solution.py:392
  49.3 6.0 %collective-permute-start.14 = (bf16[576,128]{1,0:T(8,128)(2,1)S(1)}, bf16[576,128]{1,0:T(8,128)(2,1)S(1)}, u32[]{:S(2)}, u32[]{:S(2)}) collective-permute-start(bf16[576,128]{1,0:T(8,128)(2,1)S(1)} %get-tuple-element.52.refs_0_), channel_id=1, source_target_pairs={{0,2},{1,3},{2,0},{3,1},{4,6},{5,7},{6,4},{7,5},{8,10},{9,11},{10,... | collective-permute-start | bytes 442376 | tf_op jit(solution)/shard_map/ppermute | solution.py:392
  55.3 1.4 %collective-permute-start.15 = (bf16[576,128]{1,0:T(8,128)(2,1)S(1)}, bf16[576,128]{1,0:T(8,128)(2,1)S(1)}, u32[]{:S(2)}, u32[]{:S(2)}) collective-permute-start(bf16[576,128]{1,0:T(8,128)(2,1)S(1)} %shard_map.84.refs_1_.refs_0_), channel_id=1, source_target_pairs={{0,1},{1,0},{2,3},{3,2},{4,5},{5,4},{6,7},{7,6},{8,9},{9,8},{10,11... | collective-permute-start | bytes 442376 | tf_op jit(solution)/shard_map/ppermute | solution.py:392
  57.1 3.8 %collective-permute-start.19 = (bf16[64,128]{1,0:T(8,128)(2,1)S(1)}, bf16[64,128]{1,0:T(8,128)(2,1)S(1)}, u32[]{:S(2)}, u32[]{:S(2)}) collective-permute-start(bf16[64,128]{1,0:T(8,128)(2,1)S(1)} %shard_map.87.refs_0_), channel_id=1, source_target_pairs={{0,4},{4,0},{8,12},{12,8},{1,5},{5,1},{9,13},{13,9},{2,6},{6,2},{1... | collective-permute-start | bytes 49160 | tf_op jit(solution)/shard_map/ppermute | solution.py:392
  59.4 4.3 %collective-permute-start.16 = (bf16[256,128]{1,0:T(8,128)(2,1)S(1)}, bf16[256,128]{1,0:T(8,128)(2,1)S(1)}, u32[]{:S(2)}, u32[]{:S(2)}) collective-permute-start(bf16[256,128]{1,0:T(8,128)(2,1)S(1)} %get-tuple-element.55.refs_0_), channel_id=1, source_target_pairs={{0,4},{4,0},{8,12},{12,8},{1,5},{5,1},{9,13},{13,9},{2,6},{6,2},{1... | collective-permute-start | bytes 196616 | tf_op jit(solution)/shard_map/ppermute | solution.py:392
  61.0 6.4 %collective-permute-start.20 = (bf16[64,128]{1,0:T(8,128)(2,1)S(1)}, bf16[64,128]{1,0:T(8,128)(2,1)S(1)}, u32[]{:S(2)}, u32[]{:S(2)}) collective-permute-start(bf16[64,128]{1,0:T(8,128)(2,1)S(1)} %get-tuple-element.62), channel_id=1, source_target_pairs={{0,8},{4,12},{8,0},{12,4},{1,9},{5,13},{9,1},{13,5},{2,10},{6,14},... | collective-permute-start | bytes 49160 | tf_op jit(solution)/shard_map/ppermute | solution.py:392
  63.7 6.6 %collective-permute-start.17 = (bf16[256,128]{1,0:T(8,128)(2,1)S(1)}, bf16[256,128]{1,0:T(8,128)(2,1)S(1)}, u32[]{:S(2)}, u32[]{:S(2)}) collective-permute-start(bf16[256,128]{1,0:T(8,128)(2,1)S(1)} %get-tuple-element.58), channel_id=1, source_target_pairs={{0,8},{4,12},{8,0},{12,4},{1,9},{5,13},{9,1},{13,5},{2,10},{6,14},... | collective-permute-start | bytes 196616 | tf_op jit(solution)/shard_map/ppermute | solution.py:392
  66.4 4.3 %collective-permute-start.18 = (bf16[256,128]{1,0:T(8,128)(2,1)S(1)}, bf16[256,128]{1,0:T(8,128)(2,1)S(1)}, u32[]{:S(2)}, u32[]{:S(2)}) collective-permute-start(bf16[256,128]{1,0:T(8,128)(2,1)S(1)} %get-tuple-element.59), channel_id=1, source_target_pairs={{0,4},{4,0},{8,12},{12,8},{1,5},{5,1},{9,13},{13,9},{2,6},{6,2},{1... | collective-permute-start | bytes 196616 | tf_op jit(solution)/shard_map/ppermute | solution.py:392

commit v17 on v16

--- a/solution.py
+++ b/solution.py
@@ -7,7 +7,7 @@
 
 BLOCK = 128
 TILE = 8
-AHEAD = 4
+AHEAD = 3
 DIAG = 16
 F32, BF16 = jnp.float32, jnp.bfloat16
 FP32 = lax.Precision.HIGHEST

time: 72.2 us -> 72.2 us (level)
  waiting for transfers between devices: 27.3 us -> 26.2 us
  Pallas kernels: 15.4 us -> 16.5 us
    pallas_call x23, Pallas kernels: 15.4 us -> 16.5 us  [call(): pl.pallas_call(body, out_shape=flat_outs, in_specs=[space(x) for x in fla...]
    ppermute x21, waiting for transfers between devices: 27.3 us -> 26.2 us  [swapped(): lax.ppermute(x, axis, [(i, i ^ flip) for i in range(lax.axis_size(axis))])]
  transfers between devices with their start and end apart: 21 -> 21, of which waited for: 16 -> 15; matrix products, arithmetic and copies ran while one was open for 0% -> 0% of each run, Pallas kernels for 13% -> 15%
where the time goes in v17:
time: 72.2 us; the launch traced here: 72 us
  starting transfers between devices  26.9 us (37%)
  waiting for transfers between devices  26.2 us (36%)
  Pallas kernels  16.5 us (23%)
  local copies, waits for them, and re-layouts  1.6 us (2%)
  between operations  0.83 us (1%)
    ppermute x21, starting transfers between devices, swapped(): lax.ppermute(x, axis, [(i, i ^ flip) for i in range(lax.axis_size(axis))])  26.9 us
    ppermute x21, waiting for transfers between devices, swapped(): lax.ppermute(x, axis, [(i, i ^ flip) for i in range(lax.axis_size(axis))])  26.2 us
    pallas_call x23, Pallas kernels, call(): pl.pallas_call(body, out_shape=flat_outs, in_specs=[space(x) for x in fla...  16.5 us
    unnamed x14, local copies, waits for them, and re-layouts  1.6 us
  transfers between devices with their start and end apart: 21, of which 15 were waited for; matrix products, arithmetic and copies ran while one was open for 0% of the time, Pallas kernels for 15%

profile of v17, /device:TPU:0, one launch (start us, length us, event | category | flops | bytes accessed | tf_op | source)
XLA Modules:
  0.0 72.0 jit_solution(13925547772324600464)
XLA Ops:
  1.5 4.1 %collective-permute-start.1 = (bf16[256,128]{1,0:T(8,128)(2,1)S(1)}, bf16[256,128]{1,0:T(8,128)(2,1)S(1)}, u32[]{:S(2)}, u32[]{:S(2)}) collective-permute-start(bf16[256,128]{1,0:T(8,128)(2,1)S(1)} %shard_map.69.refs_1_), channel_id=1, source_target_pairs={{0,8},{4,12},{8,0},{12,4},{1,9},{5,13},{9,1},{13,5},{2,10},{6,14},... | collective-permute-start | bytes 196616 | tf_op jit(solution)/shard_map/ppermute | solution.py:392
  5.7 1.6 %collective-permute-start = (bf16[256,128]{1,0:T(8,128)(2,1)S(1)}, bf16[256,128]{1,0:T(8,128)(2,1)S(1)}, u32[]{:S(2)}, u32[]{:S(2)}) collective-permute-start(bf16[256,128]{1,0:T(8,128)(2,1)S(1)} %shard_map.69.refs_1_), channel_id=1, source_target_pairs={{0,4},{4,0},{8,12},{12,8},{1,5},{5,1},{9,13},{13,9},{2,6},{6,2},{1... | collective-permute-start | bytes 196616 | tf_op jit(solution)/shard_map/ppermute | solution.py:392
  8.7 1.4 %collective-permute-start.2 = (bf16[256,128]{1,0:T(8,128)(2,1)S(1)}, bf16[256,128]{1,0:T(8,128)(2,1)S(1)}, u32[]{:S(2)}, u32[]{:S(2)}) collective-permute-start(bf16[256,128]{1,0:T(8,128)(2,1)S(1)} %collective-permute-done.1.refs_3_.refs_2_), channel_id=1, source_target_pairs={{0,4},{4,0},{8,12},{12,8},{1,5},{5,1},{9,13},{13,9},{2,6},{6,2},{1... | collective-permute-start | bytes 196616 | tf_op jit(solution)/shard_map/ppermute | solution.py:392
  10.1 2.0 %shard_map.68 = (s32[2,64]{1,0:T(2,128)S(1)}, bf16[64,128,128]{2,1,0:T(8,128)(2,1)S(1)}) custom-call(s32[64]{0:T(128)S(1)} %copy-done.5, s32[64]{0:T(128)S(1)} %copy-done.6, bf16[64,128,128]{2,1,0:T(8,128)(2,1)S(1)} %copy-done), custom_call_target="tpu_custom_call" | custom-call | flops 2000000000 | bytes 8000000 | tf_op jit(solution)/shard_map/pallas_call | solution.py:51
  13.0 1.3 %shard_map.71 = (f32[576,128]{1,0:T(8,128)S(1)}, f32[576,128]{1,0:T(8,128)S(1)}) custom-call(s32[2,64]{1,0:T(2,128)S(1)} %get-tuple-element.33.refs_0_, bf16[256,128]{1,0:T(8,128)(2,1)S(1)} %shard_map.69.refs_1_, bf16[256,128]{1,0:T(8,128)(2,1)S(1)} %collective-permute-done.refs_2_, bf16[256,128]{1,0:T(8,128)(2,1)S(1)} %collective-permute-done.1.refs_3_.refs_2_, ...), custom_call_target="tpu_custom_call" | custom-call | tf_op jit(solution)/shard_map/pallas_call | solution.py:51
  14.4 1.6 %collective-permute-done.3.refs_1_ = f32[576,128]{1,0:T(8,128)S(1)} collective-permute-done((f32[576,128]{1,0:T(8,128)S(1)}, f32[576,128]{1,0:T(8,128)S(1)}, u32[]{:S(2)}, u32[]{:S(2)}) %collective-permute-start.3) | collective-permute-done | bytes 294944 | tf_op jit(solution)/shard_map/ppermute | solution.py:392
  16.0 1.9 %collective-permute-start.4 = (bf16[576,128]{1,0:T(8,128)(2,1)S(1)}, bf16[576,128]{1,0:T(8,128)(2,1)S(1)}, u32[]{:S(2)}, u32[]{:S(2)}) collective-permute-start(bf16[576,128]{1,0:T(8,128)(2,1)S(1)} %shard_map.72.refs_2_.refs_0_), channel_id=1, source_target_pairs={{0,2},{1,3},{2,0},{3,1},{4,6},{5,7},{6,4},{7,5},{8,10},{9,11},{10,... | collective-permute-start | bytes 442376 | tf_op jit(solution)/shard_map/ppermute | solution.py:392
  17.9 2.4 %collective-permute-start.5 = (bf16[272,128]{1,0:T(8,128)(2,1)S(1)}, bf16[272,128]{1,0:T(8,128)(2,1)S(1)}, u32[]{:S(2)}, u32[]{:S(2)}) collective-permute-start(bf16[272,128]{1,0:T(8,128)(2,1)S(1)} %shard_map.73), channel_id=1, source_target_pairs={{0,8},{4,12},{8,0},{12,4},{1,9},{5,13},{9,1},{13,5},{2,10},{6,14},... | collective-permute-start | bytes 208904 | tf_op jit(solution)/shard_map/ppermute | solution.py:392
  20.3 4.3 %collective-permute-done.5.refs_2_.refs_3_ = bf16[272,128]{1,0:T(8,128)(2,1)S(1)} collective-permute-done((bf16[272,128]{1,0:T(8,128)(2,1)S(1)}, bf16[272,128]{1,0:T(8,128)(2,1)S(1)}, u32[]{:S(2)}, u32[]{:S(2)}) %collective-permute-start.5) | collective-permute-done | bytes 69664 | tf_op jit(solution)/shard_map/ppermute | solution.py:392
  24.7 1.4 %collective-permute-done.6.refs_2_ = bf16[576,128]{1,0:T(8,128)(2,1)S(1)} collective-permute-done((bf16[576,128]{1,0:T(8,128)(2,1)S(1)}, bf16[576,128]{1,0:T(8,128)(2,1)S(1)}, u32[]{:S(2)}, u32[]{:S(2)}) %collective-permute-start.6) | collective-permute-done | bytes 147488 | tf_op jit(solution)/shard_map/ppermute | solution.py:392
  26.0 1.5 %shard_map.75 = (bf16[336,128]{1,0:T(8,128)(2,1)S(1)}, bf16[256,128]{1,0:T(8,128)(2,1)S(1)}, f32[256,128]{1,0:T(8,128)S(1)}, f32[256,128]{1,0:T(8,128)S(1)}) custom-call(s32[2,64]{1,0:T(2,128)S(1)} %get-tuple-element.33.refs_0_, bf16[576,128]{1,0:T(8,128)(2,1)S(1)} %shard_map.74.refs_1_, bf16[576,128]{1,0:T(8,128)(2,1)S(1)} %collective-permute-done.6.refs_2_, ...), custom_call_target="tpu_custom_call" | custom-call | tf_op jit(solution)/shard_map/pallas_call | solution.py:51
  27.7 1.9 %collective-permute-start.7 = (bf16[256,128]{1,0:T(8,128)(2,1)S(1)}, bf16[256,128]{1,0:T(8,128)(2,1)S(1)}, u32[]{:S(2)}, u32[]{:S(2)}) collective-permute-start(bf16[256,128]{1,0:T(8,128)(2,1)S(1)} %get-tuple-element.38), channel_id=1, source_target_pairs={{0,4},{4,0},{8,12},{12,8},{1,5},{5,1},{9,13},{13,9},{2,6},{6,2},{1... | collective-permute-start | bytes 196616 | tf_op jit(solution)/shard_map/ppermute | solution.py:392
  29.6 3.3 %collective-permute-done.8.refs_1_ = bf16[336,128]{1,0:T(8,128)(2,1)S(1)} collective-permute-done((bf16[336,128]{1,0:T(8,128)(2,1)S(1)}, bf16[336,128]{1,0:T(8,128)(2,1)S(1)}, u32[]{:S(2)}, u32[]{:S(2)}) %collective-permute-start.8) | collective-permute-done | bytes 86048 | tf_op jit(solution)/shard_map/ppermute | solution.py:392
  32.9 1.5 %collective-permute-start.9 = (bf16[336,128]{1,0:T(8,128)(2,1)S(1)}, bf16[336,128]{1,0:T(8,128)(2,1)S(1)}, u32[]{:S(2)}, u32[]{:S(2)}) collective-permute-start(bf16[336,128]{1,0:T(8,128)(2,1)S(1)} %get-tuple-element.42.refs_0_), channel_id=1, source_target_pairs={{0,8},{4,12},{8,0},{12,4},{1,9},{5,13},{9,1},{13,5},{2,10},{6,14},... | collective-permute-start | bytes 258056 | tf_op jit(solution)/shard_map/ppermute | solution.py:392
  34.4 1.5 %collective-permute-start.11 = (bf16[256,128]{1,0:T(8,128)(2,1)S(1)}, bf16[256,128]{1,0:T(8,128)(2,1)S(1)}, u32[]{:S(2)}, u32[]{:S(2)}) collective-permute-start(bf16[256,128]{1,0:T(8,128)(2,1)S(1)} %get-tuple-element.46), channel_id=1, source_target_pairs={{0,8},{4,12},{8,0},{12,4},{1,9},{5,13},{9,1},{13,5},{2,10},{6,14},... | collective-permute-start | bytes 196616 | tf_op jit(solution)/shard_map/ppermute | solution.py:392
  36.0 4.2 %collective-permute-done.9.refs_1_ = bf16[336,128]{1,0:T(8,128)(2,1)S(1)} collective-permute-done((bf16[336,128]{1,0:T(8,128)(2,1)S(1)}, bf16[336,128]{1,0:T(8,128)(2,1)S(1)}, u32[]{:S(2)}, u32[]{:S(2)}) %collective-permute-start.9) | collective-permute-done | bytes 86048 | tf_op jit(solution)/shard_map/ppermute | solution.py:392
  41.9 1.0 %collective-permute-start.12 = (bf16[256,128]{1,0:T(8,128)(2,1)S(1)}, bf16[256,128]{1,0:T(8,128)(2,1)S(1)}, u32[]{:S(2)}, u32[]{:S(2)}) collective-permute-start(bf16[256,128]{1,0:T(8,128)(2,1)S(1)} %shard_map.79.refs_3_), channel_id=1, source_target_pairs={{0,4},{4,0},{8,12},{12,8},{1,5},{5,1},{9,13},{13,9},{2,6},{6,2},{1... | collective-permute-start | bytes 196616 | tf_op jit(solution)/shard_map/ppermute | solution.py:392
  43.3 1.5 %collective-permute-done.10.refs_2_ = bf16[256,128]{1,0:T(8,128)(2,1)S(1)} collective-permute-done((bf16[256,128]{1,0:T(8,128)(2,1)S(1)}, bf16[256,128]{1,0:T(8,128)(2,1)S(1)}, u32[]{:S(2)}, u32[]{:S(2)}) %collective-permute-start.10) | collective-permute-done | bytes 65568 | tf_op jit(solution)/shard_map/ppermute | solution.py:392
  44.8 1.4 %collective-permute-done.12.refs_4_ = bf16[256,128]{1,0:T(8,128)(2,1)S(1)} collective-permute-done((bf16[256,128]{1,0:T(8,128)(2,1)S(1)}, bf16[256,128]{1,0:T(8,128)(2,1)S(1)}, u32[]{:S(2)}, u32[]{:S(2)}) %collective-permute-start.12) | collective-permute-done | bytes 65568 | tf_op jit(solution)/shard_map/ppermute | solution.py:392
  46.2 1.4 %shard_map.81 = (f32[608,128]{1,0:T(8,128)S(1)}, f32[608,128]{1,0:T(8,128)S(1)}) custom-call(s32[2,64]{1,0:T(2,128)S(1)} %get-tuple-element.33.refs_0_, bf16[256,128]{1,0:T(8,128)(2,1)S(1)} %get-tuple-element.45.refs_1_, bf16[256,128]{1,0:T(8,128)(2,1)S(1)} %collective-permute-done.10.refs_2_, bf16[256,128]{1,0:T(8,128)(2,1)S(1)} %shard_map.79.refs_3_, ...), custom_call_target="tpu_custom_call" | custom-call | tf_op jit(solution)/shard_map/pallas_call | solution.py:51
  47.7 1.6 %collective-permute-done.13.refs_1_ = f32[608,128]{1,0:T(8,128)S(1)} collective-permute-done((f32[608,128]{1,0:T(8,128)S(1)}, f32[608,128]{1,0:T(8,128)S(1)}, u32[]{:S(2)}, u32[]{:S(2)}) %collective-permute-start.13) | collective-permute-done | bytes 311328 | tf_op jit(solution)/shard_map/ppermute | solution.py:392
  49.9 2.4 %shard_map.83.refs_2_.refs_3_ = f32[64,64]{1,0:T(8,128)S(1)} custom-call(f32[64,128]{1,0:T(8,128)S(1)} %get-tuple-element.53.refs_0_.refs_2_), custom_call_target="tpu_custom_call" | custom-call | flops 2000000000 | bytes 8000000 | tf_op jit(solution)/shard_map/pallas_call | solution.py:51
  52.3 3.0 %collective-permute-done.14.refs_1_ = bf16[576,128]{1,0:T(8,128)(2,1)S(1)} collective-permute-done((bf16[576,128]{1,0:T(8,128)(2,1)S(1)}, bf16[576,128]{1,0:T(8,128)(2,1)S(1)}, u32[]{:S(2)}, u32[]{:S(2)}) %collective-permute-start.14) | collective-permute-done | bytes 147488 | tf_op jit(solution)/shard_map/ppermute | solution.py:392
  55.4 1.4 %collective-permute-done.15.refs_2_.refs_1_ = bf16[576,128]{1,0:T(8,128)(2,1)S(1)} collective-permute-done((bf16[576,128]{1,0:T(8,128)(2,1)S(1)}, bf16[576,128]{1,0:T(8,128)(2,1)S(1)}, u32[]{:S(2)}, u32[]{:S(2)}) %collective-permute-start.15) | collective-permute-done | bytes 147488 | tf_op jit(solution)/shard_map/ppermute | solution.py:392
  57.1 1.0 %collective-permute-start.19 = (bf16[64,128]{1,0:T(8,128)(2,1)S(1)}, bf16[64,128]{1,0:T(8,128)(2,1)S(1)}, u32[]{:S(2)}, u32[]{:S(2)}) collective-permute-start(bf16[64,128]{1,0:T(8,128)(2,1)S(1)} %shard_map.87.refs_0_), channel_id=1, source_target_pairs={{0,4},{4,0},{8,12},{12,8},{1,5},{5,1},{9,13},{13,9},{2,6},{6,2},{1... | collective-permute-start | bytes 49160 | tf_op jit(solution)/shard_map/ppermute | solution.py:392
  58.0 1.3 %shard_map.85 = (bf16[256,128]{1,0:T(8,128)(2,1)S(1)}, bf16[256,128]{1,0:T(8,128)(2,1)S(1)}, f32[256,128]{1,0:T(8,128)S(1)}, f32[256,128]{1,0:T(8,128)S(1)}, f32[64,64]{1,0:T(8,128)S(1)}) custom-call(s32[2,64]{1,0:T(2,128)S(1)} %get-tuple-element.33.refs_0_, bf16[576,128]{1,0:T(8,128)(2,1)S(1)} %shard_map.84.refs_1_.refs_0_, ...), custom_call_target="tpu_custom_call" | custom-call | tf_op jit(solution)/shard_map/pallas_call | solution.py:51
  59.4 1.2 %collective-permute-start.16 = (bf16[256,128]{1,0:T(8,128)(2,1)S(1)}, bf16[256,128]{1,0:T(8,128)(2,1)S(1)}, u32[]{:S(2)}, u32[]{:S(2)}) collective-permute-start(bf16[256,128]{1,0:T(8,128)(2,1)S(1)} %get-tuple-element.55.refs_0_), channel_id=1, source_target_pairs={{0,4},{4,0},{8,12},{12,8},{1,5},{5,1},{9,13},{13,9},{2,6},{6,2},{1... | collective-permute-start | bytes 196616 | tf_op jit(solution)/shard_map/ppermute | solution.py:392
  61.0 2.5 %collective-permute-start.20 = (bf16[64,128]{1,0:T(8,128)(2,1)S(1)}, bf16[64,128]{1,0:T(8,128)(2,1)S(1)}, u32[]{:S(2)}, u32[]{:S(2)}) collective-permute-start(bf16[64,128]{1,0:T(8,128)(2,1)S(1)} %get-tuple-element.62), channel_id=1, source_target_pairs={{0,8},{4,12},{8,0},{12,4},{1,9},{5,13},{9,1},{13,5},{2,10},{6,14},... | collective-permute-start | bytes 49160 | tf_op jit(solution)/shard_map/ppermute | solution.py:392
  63.7 2.7 %collective-permute-start.17 = (bf16[256,128]{1,0:T(8,128)(2,1)S(1)}, bf16[256,128]{1,0:T(8,128)(2,1)S(1)}, u32[]{:S(2)}, u32[]{:S(2)}) collective-permute-start(bf16[256,128]{1,0:T(8,128)(2,1)S(1)} %get-tuple-element.58), channel_id=1, source_target_pairs={{0,8},{4,12},{8,0},{12,4},{1,9},{5,13},{9,1},{13,5},{2,10},{6,14},... | collective-permute-start | bytes 196616 | tf_op jit(solution)/shard_map/ppermute | solution.py:392
  66.4 0.9 %collective-permute-start.18 = (bf16[256,128]{1,0:T(8,128)(2,1)S(1)}, bf16[256,128]{1,0:T(8,128)(2,1)S(1)}, u32[]{:S(2)}, u32[]{:S(2)}) collective-permute-start(bf16[256,128]{1,0:T(8,128)(2,1)S(1)} %get-tuple-element.59), channel_id=1, source_target_pairs={{0,4},{4,0},{8,12},{12,8},{1,5},{5,1},{9,13},{13,9},{2,6},{6,2},{1... | collective-permute-start | bytes 196616 | tf_op jit(solution)/shard_map/ppermute | solution.py:392
  67.4 3.3 %shard_map.89.refs_7_ = f32[128,64]{1,0:T(8,128)S(1)} custom-call(f32[64,64]{1,0:T(8,128)S(1)} %get-tuple-element.61.refs_0_, bf16[64,128]{1,0:T(8,128)(2,1)S(1)} %collective-permute-done.20.refs_1_, f32[64,128]{1,0:T(8,128)S(1)} %get-tuple-element.53.refs_0_.refs_2_, f32[64,64]{1,0:T(8,128)S(1)} %shard_map.83.refs_2_.refs_3_, ...), custom_call_target="tpu_custom_call" | custom-call | flops 2000000000 | bytes 8000000 | tf_op jit(solution)/shard_map/pallas_call | solution.py:51
  70.7 1.3 %shard_map.90 = (f32[64,512]{1,0:T(8,128)}, f32[64,512]{1,0:T(8,128)}) custom-call(f32[256,128]{1,0:T(8,128)S(1)} %get-tuple-element.54.refs_0_, bf16[256,128]{1,0:T(8,128)(2,1)S(1)} %collective-permute-done.17.refs_1_, bf16[256,128]{1,0:T(8,128)(2,1)S(1)} %collective-permute-done.18.refs_2_, f32[64,512]{1,0:T(8,128)S(1)} %copy-done.2, ...), custom_call_target="tpu_custom_call" | custom-call | tf_op jit(solution)/shard_map/pallas_call | solution.py:51
  (47 shorter events, 7.6 us)
Async XLA Ops:
  0.6 0.9 %copy-start.1 = (f32[64,512]{1,0:T(8,128)S(1)}, f32[64,512]{1,0:T(8,128)}, u32[]{:S(2)}) copy-start(f32[64,512]{1,0:T(8,128)} %refs_3_.5) | copy-start | bytes 393220
  1.5 7.2 %collective-permute-start.1 = (bf16[256,128]{1,0:T(8,128)(2,1)S(1)}, bf16[256,128]{1,0:T(8,128)(2,1)S(1)}, u32[]{:S(2)}, u32[]{:S(2)}) collective-permute-start(bf16[256,128]{1,0:T(8,128)(2,1)S(1)} %shard_map.69.refs_1_), channel_id=1, source_target_pairs={{0,8},{4,12},{8,0},{12,4},{1,9},{5,13},{9,1},{13,5},{2,10},{6,14},... | collective-permute-start | bytes 196616 | tf_op jit(solution)/shard_map/ppermute | solution.py:392
  5.7 6.5 %collective-permute-start = (bf16[256,128]{1,0:T(8,128)(2,1)S(1)}, bf16[256,128]{1,0:T(8,128)(2,1)S(1)}, u32[]{:S(2)}, u32[]{:S(2)}) collective-permute-start(bf16[256,128]{1,0:T(8,128)(2,1)S(1)} %shard_map.69.refs_1_), channel_id=1, source_target_pairs={{0,4},{4,0},{8,12},{12,8},{1,5},{5,1},{9,13},{13,9},{2,6},{6,2},{1... | collective-permute-start | bytes 196616 | tf_op jit(solution)/shard_map/ppermute | solution.py:392
  7.2 0.7 copy-start.3
  7.9 2.2 %copy-start = (bf16[64,128,128]{2,1,0:T(8,128)(2,1)S(1)}, bf16[64,128,128]{2,1,0:T(8,128)(2,1)}, u32[]{:S(2)}) copy-start(bf16[64,128,128]{2,1,0:T(8,128)(2,1)} %refs_3_.4) | copy-start | bytes 6291460
  7.9 2.2 %copy-start.5 = (s32[64]{0:T(128)S(1)}, s32[64]{0:T(128)}, u32[]{:S(2)}) copy-start(s32[64]{0:T(128)} %refs_0_.4) | copy-start | bytes 772
  7.9 2.2 %copy-start.6 = (s32[64]{0:T(128)S(1)}, s32[64]{0:T(128)}, u32[]{:S(2)}) copy-start(s32[64]{0:T(128)} %refs_1_.1) | copy-start | bytes 772
  8.7 4.3 %collective-permute-start.2 = (bf16[256,128]{1,0:T(8,128)(2,1)S(1)}, bf16[256,128]{1,0:T(8,128)(2,1)S(1)}, u32[]{:S(2)}, u32[]{:S(2)}) collective-permute-start(bf16[256,128]{1,0:T(8,128)(2,1)S(1)} %collective-permute-done.1.refs_3_.refs_2_), channel_id=1, source_target_pairs={{0,4},{4,0},{8,12},{12,8},{1,5},{5,1},{9,13},{13,9},{2,6},{6,2},{1... | collective-permute-start | bytes 196616 | tf_op jit(solution)/shard_map/ppermute | solution.py:392
  12.1 5.8 %copy-start.2 = (f32[64,512]{1,0:T(8,128)S(1)}, f32[64,512]{1,0:T(8,128)}, u32[]{:S(2)}) copy-start(f32[64,512]{1,0:T(8,128)} %refs_3_.5) | copy-start | bytes 393220
  12.1 5.8 %copy-start.4 = (f32[512]{0:T(512)S(1)}, f32[512]{0:T(512)}, u32[]{:S(2)}) copy-start(f32[512]{0:T(512)} %param.6) | copy-start | bytes 6148
  14.3 1.6 %collective-permute-start.3 = (f32[576,128]{1,0:T(8,128)S(1)}, f32[576,128]{1,0:T(8,128)S(1)}, u32[]{:S(2)}, u32[]{:S(2)}) collective-permute-start(f32[576,128]{1,0:T(8,128)S(1)} %get-tuple-element.36), channel_id=1, source_target_pairs={{0,1},{1,0},{2,3},{3,2},{4,5},{5,4},{6,7},{7,6},{8,9},{9,8},{10,11... | collective-permute-start | bytes 884744 | tf_op jit(solution)/shard_map/ppermute | solution.py:392
  16.0 8.6 %collective-permute-start.4 = (bf16[576,128]{1,0:T(8,128)(2,1)S(1)}, bf16[576,128]{1,0:T(8,128)(2,1)S(1)}, u32[]{:S(2)}, u32[]{:S(2)}) collective-permute-start(bf16[576,128]{1,0:T(8,128)(2,1)S(1)} %shard_map.72.refs_2_.refs_0_), channel_id=1, source_target_pairs={{0,2},{1,3},{2,0},{3,1},{4,6},{5,7},{6,4},{7,5},{8,10},{9,11},{10,... | collective-permute-start | bytes 442376 | tf_op jit(solution)/shard_map/ppermute | solution.py:392
  17.9 6.6 %collective-permute-start.5 = (bf16[272,128]{1,0:T(8,128)(2,1)S(1)}, bf16[272,128]{1,0:T(8,128)(2,1)S(1)}, u32[]{:S(2)}, u32[]{:S(2)}) collective-permute-start(bf16[272,128]{1,0:T(8,128)(2,1)S(1)} %shard_map.73), channel_id=1, source_target_pairs={{0,8},{4,12},{8,0},{12,4},{1,9},{5,13},{9,1},{13,5},{2,10},{6,14},... | collective-permute-start | bytes 208904 | tf_op jit(solution)/shard_map/ppermute | solution.py:392
  24.6 1.4 %collective-permute-start.6 = (bf16[576,128]{1,0:T(8,128)(2,1)S(1)}, bf16[576,128]{1,0:T(8,128)(2,1)S(1)}, u32[]{:S(2)}, u32[]{:S(2)}) collective-permute-start(bf16[576,128]{1,0:T(8,128)(2,1)S(1)} %shard_map.74.refs_1_), channel_id=1, source_target_pairs={{0,1},{1,0},{2,3},{3,2},{4,5},{5,4},{6,7},{7,6},{8,9},{9,8},{10,11... | collective-permute-start | bytes 442376 | tf_op jit(solution)/shard_map/ppermute | solution.py:392
  27.5 5.3 %collective-permute-start.8 = (bf16[336,128]{1,0:T(8,128)(2,1)S(1)}, bf16[336,128]{1,0:T(8,128)(2,1)S(1)}, u32[]{:S(2)}, u32[]{:S(2)}) collective-permute-start(bf16[336,128]{1,0:T(8,128)(2,1)S(1)} %get-tuple-element.40.refs_0_), channel_id=1, source_target_pairs={{0,4},{4,0},{8,12},{12,8},{1,5},{5,1},{9,13},{13,9},{2,6},{6,2},{1... | collective-permute-start | bytes 258056 | tf_op jit(solution)/shard_map/ppermute | solution.py:392
  27.7 6.7 %collective-permute-start.7 = (bf16[256,128]{1,0:T(8,128)(2,1)S(1)}, bf16[256,128]{1,0:T(8,128)(2,1)S(1)}, u32[]{:S(2)}, u32[]{:S(2)}) collective-permute-start(bf16[256,128]{1,0:T(8,128)(2,1)S(1)} %get-tuple-element.38), channel_id=1, source_target_pairs={{0,4},{4,0},{8,12},{12,8},{1,5},{5,1},{9,13},{13,9},{2,6},{6,2},{1... | collective-permute-start | bytes 196616 | tf_op jit(solution)/shard_map/ppermute | solution.py:392
  32.9 7.3 %collective-permute-start.9 = (bf16[336,128]{1,0:T(8,128)(2,1)S(1)}, bf16[336,128]{1,0:T(8,128)(2,1)S(1)}, u32[]{:S(2)}, u32[]{:S(2)}) collective-permute-start(bf16[336,128]{1,0:T(8,128)(2,1)S(1)} %get-tuple-element.42.refs_0_), channel_id=1, source_target_pairs={{0,8},{4,12},{8,0},{12,4},{1,9},{5,13},{9,1},{13,5},{2,10},{6,14},... | collective-permute-start | bytes 258056 | tf_op jit(solution)/shard_map/ppermute | solution.py:392
  34.4 7.2 %collective-permute-start.11 = (bf16[256,128]{1,0:T(8,128)(2,1)S(1)}, bf16[256,128]{1,0:T(8,128)(2,1)S(1)}, u32[]{:S(2)}, u32[]{:S(2)}) collective-permute-start(bf16[256,128]{1,0:T(8,128)(2,1)S(1)} %get-tuple-element.46), channel_id=1, source_target_pairs={{0,8},{4,12},{8,0},{12,4},{1,9},{5,13},{9,1},{13,5},{2,10},{6,14},... | collective-permute-start | bytes 196616 | tf_op jit(solution)/shard_map/ppermute | solution.py:392
  40.5 4.3 %collective-permute-start.10 = (bf16[256,128]{1,0:T(8,128)(2,1)S(1)}, bf16[256,128]{1,0:T(8,128)(2,1)S(1)}, u32[]{:S(2)}, u32[]{:S(2)}) collective-permute-start(bf16[256,128]{1,0:T(8,128)(2,1)S(1)} %get-tuple-element.45.refs_1_), channel_id=1, source_target_pairs={{0,4},{4,0},{8,12},{12,8},{1,5},{5,1},{9,13},{13,9},{2,6},{6,2},{1... | collective-permute-start | bytes 196616 | tf_op jit(solution)/shard_map/ppermute | solution.py:392
  41.9 4.3 %collective-permute-start.12 = (bf16[256,128]{1,0:T(8,128)(2,1)S(1)}, bf16[256,128]{1,0:T(8,128)(2,1)S(1)}, u32[]{:S(2)}, u32[]{:S(2)}) collective-permute-start(bf16[256,128]{1,0:T(8,128)(2,1)S(1)} %shard_map.79.refs_3_), channel_id=1, source_target_pairs={{0,4},{4,0},{8,12},{12,8},{1,5},{5,1},{9,13},{13,9},{2,6},{6,2},{1... | collective-permute-start | bytes 196616 | tf_op jit(solution)/shard_map/ppermute | solution.py:392
  47.6 1.7 %collective-permute-start.13 = (f32[608,128]{1,0:T(8,128)S(1)}, f32[608,128]{1,0:T(8,128)S(1)}, u32[]{:S(2)}, u32[]{:S(2)}) collective-permute-start(f32[608,128]{1,0:T(8,128)S(1)} %get-tuple-element.51), channel_id=1, source_target_pairs={{0,1},{1,0},{2,3},{3,2},{4,5},{5,4},{6,7},{7,6},{8,9},{9,8},{10,11... | collective-permute-start | bytes 933896 | tf_op jit(solution)/shard_map/ppermute | solution.py:392
  49.3 6.0 %collective-permute-start.14 = (bf16[576,128]{1,0:T(8,128)(2,1)S(1)}, bf16[576,128]{1,0:T(8,128)(2,1)S(1)}, u32[]{:S(2)}, u32[]{:S(2)}) collective-permute-start(bf16[576,128]{1,0:T(8,128)(2,1)S(1)} %get-tuple-element.52.refs_0_), channel_id=1, source_target_pairs={{0,2},{1,3},{2,0},{3,1},{4,6},{5,7},{6,4},{7,5},{8,10},{9,11},{10,... | collective-permute-start | bytes 442376 | tf_op jit(solution)/shard_map/ppermute | solution.py:392
  55.3 1.4 %collective-permute-start.15 = (bf16[576,128]{1,0:T(8,128)(2,1)S(1)}, bf16[576,128]{1,0:T(8,128)(2,1)S(1)}, u32[]{:S(2)}, u32[]{:S(2)}) collective-permute-start(bf16[576,128]{1,0:T(8,128)(2,1)S(1)} %shard_map.84.refs_1_.refs_0_), channel_id=1, source_target_pairs={{0,1},{1,0},{2,3},{3,2},{4,5},{5,4},{6,7},{7,6},{8,9},{9,8},{10,11... | collective-permute-start | bytes 442376 | tf_op jit(solution)/shard_map/ppermute | solution.py:392
  57.1 3.8 %collective-permute-start.19 = (bf16[64,128]{1,0:T(8,128)(2,1)S(1)}, bf16[64,128]{1,0:T(8,128)(2,1)S(1)}, u32[]{:S(2)}, u32[]{:S(2)}) collective-permute-start(bf16[64,128]{1,0:T(8,128)(2,1)S(1)} %shard_map.87.refs_0_), channel_id=1, source_target_pairs={{0,4},{4,0},{8,12},{12,8},{1,5},{5,1},{9,13},{13,9},{2,6},{6,2},{1... | collective-permute-start | bytes 49160 | tf_op jit(solution)/shard_map/ppermute | solution.py:392
  59.4 4.3 %collective-permute-start.16 = (bf16[256,128]{1,0:T(8,128)(2,1)S(1)}, bf16[256,128]{1,0:T(8,128)(2,1)S(1)}, u32[]{:S(2)}, u32[]{:S(2)}) collective-permute-start(bf16[256,128]{1,0:T(8,128)(2,1)S(1)} %get-tuple-element.55.refs_0_), channel_id=1, source_target_pairs={{0,4},{4,0},{8,12},{12,8},{1,5},{5,1},{9,13},{13,9},{2,6},{6,2},{1... | collective-permute-start | bytes 196616 | tf_op jit(solution)/shard_map/ppermute | solution.py:392
  61.0 6.4 %collective-permute-start.20 = (bf16[64,128]{1,0:T(8,128)(2,1)S(1)}, bf16[64,128]{1,0:T(8,128)(2,1)S(1)}, u32[]{:S(2)}, u32[]{:S(2)}) collective-permute-start(bf16[64,128]{1,0:T(8,128)(2,1)S(1)} %get-tuple-element.62), channel_id=1, source_target_pairs={{0,8},{4,12},{8,0},{12,4},{1,9},{5,13},{9,1},{13,5},{2,10},{6,14},... | collective-permute-start | bytes 49160 | tf_op jit(solution)/shard_map/ppermute | solution.py:392
  63.7 7.0 %collective-permute-start.17 = (bf16[256,128]{1,0:T(8,128)(2,1)S(1)}, bf16[256,128]{1,0:T(8,128)(2,1)S(1)}, u32[]{:S(2)}, u32[]{:S(2)}) collective-permute-start(bf16[256,128]{1,0:T(8,128)(2,1)S(1)} %get-tuple-element.58), channel_id=1, source_target_pairs={{0,8},{4,12},{8,0},{12,4},{1,9},{5,13},{9,1},{13,5},{2,10},{6,14},... | collective-permute-start | bytes 196616 | tf_op jit(solution)/shard_map/ppermute | solution.py:392
  66.4 4.3 %collective-permute-start.18 = (bf16[256,128]{1,0:T(8,128)(2,1)S(1)}, bf16[256,128]{1,0:T(8,128)(2,1)S(1)}, u32[]{:S(2)}, u32[]{:S(2)}) collective-permute-start(bf16[256,128]{1,0:T(8,128)(2,1)S(1)} %get-tuple-element.59), channel_id=1, source_target_pairs={{0,4},{4,0},{8,12},{12,8},{1,5},{5,1},{9,13},{13,9},{2,6},{6,2},{1... | collective-permute-start | bytes 196616 | tf_op jit(solution)/shard_map/ppermute | solution.py:392
